TPU v7x, 512 devices: a whole 4x8x8 slice. The times are simulated.
512 devices in a mesh: win: 32 (over x, z), grp: 16 (over y, core).
Axes of the slice: x: 4, y: 8, z: 8, core: 2. Of those that a mesh axis runs over, the one named last changes fastest.
Arguments:
- query_rows: bfloat16 [65536, 1024], P(('grp', 'win')), may hold values from -5 to 5
- key_rows: bfloat16 [65536, 1024], P(('grp', 'win')), may hold values from -5 to 5
- value_rows: bfloat16 [65536, 1024], P(('grp', 'win')), may hold values from -6 to 6
- out_grad: bfloat16 [65536, 1024], P(('grp', 'win')), may hold values from -48 to 48
- far_blocks: int32 [1024, 8], P(('grp', 'win')), may hold values from 0 to 1023, as said below
Outputs:
- attended: bfloat16 [65536, 1024], P(('grp', 'win'))
- query_grad: bfloat16 [65536, 1024], P(('grp', 'win'))
- key_grad: bfloat16 [65536, 1024], P(('grp', 'win'))
- value_grad: bfloat16 [65536, 1024], P(('grp', 'win'))
Inputs may be any that keep to these rules, and one draw needn't show every extreme that they name: far_blocks[b] names 8 blocks on devices with the win index of block b; the entries of the 2 rows of one device name exactly 1 block of every window group, its own included; a block may be named more than once.
All inputs are finite; a program needn't handle non-finite values.
Results may differ from a plain program's by a relative error of at most 0.024.
Values may be sent and summed in bfloat16 or wider, within the bound.
No kernel may reach another device: no remote copies, remote signals or barrier semaphores. Data moves between devices by JAX's collectives and lax.ppermute only.
A program may use at most 128 MiB of HBM per device.

v0:
```python
import math

import jax
import jax.numpy as jnp
from jax import lax
from jax.sharding import PartitionSpec as P

HEADS = 8
HEAD_DIM = 128
BLOCK = 64
GTOK = 1


def owner_rank(block_lists, stride):
    owners = block_lists // stride
    width_entries = block_lists.shape[1]
    before = jnp.arange(width_entries)[:, None] < jnp.arange(width_entries)[None, :]
    same_owner = owners[:, :, None] == owners[:, None, :]
    order_rank = jnp.sum((same_owner & before[None]).astype(jnp.int32), axis=1)
    return (owners, order_rank)


def attend(query_part, near_key, near_value, near_mask, far_key, far_value, grad_part):
    scaling = 1.0 / math.sqrt(query_part.shape[-1])
    near_scores = (
        jnp.einsum("bqhd,khd->bhqk", query_part, near_key, preferred_element_type=jnp.float32)
        * scaling
    )
    near_scores = jnp.where(near_mask[None, None, None, :], near_scores, -jnp.inf)
    far_scores = (
        jnp.einsum("bqhd,bkhd->bhqk", query_part, far_key, preferred_element_type=jnp.float32)
        * scaling
    )
    row_max = jnp.maximum(jnp.max(near_scores, axis=-1), jnp.max(far_scores, axis=-1))
    near_exp = jnp.exp(near_scores - row_max[..., None])
    far_exp = jnp.exp(far_scores - row_max[..., None])
    row_sum = jnp.sum(near_exp, axis=-1) + jnp.sum(far_exp, axis=-1)
    near_weight = near_exp / row_sum[..., None]
    far_weight = far_exp / row_sum[..., None]
    near_half = near_weight.astype(jnp.bfloat16)
    far_half = far_weight.astype(jnp.bfloat16)
    attended = (
        jnp.einsum("bhqk,khd->bqhd", near_half, near_value, preferred_element_type=jnp.float32)
        + jnp.einsum("bhqk,bkhd->bqhd", far_half, far_value, preferred_element_type=jnp.float32)
    ).astype(jnp.bfloat16)
    row_delta = jnp.sum(
        grad_part.astype(jnp.float32) * attended.astype(jnp.float32), axis=-1
    ).transpose(0, 2, 1)
    near_dprod = jnp.einsum(
        "bqhd,khd->bhqk", grad_part, near_value, preferred_element_type=jnp.float32
    )
    far_dprod = jnp.einsum(
        "bqhd,bkhd->bhqk", grad_part, far_value, preferred_element_type=jnp.float32
    )
    near_sgrad = (near_weight * (near_dprod - row_delta[..., None])).astype(jnp.bfloat16)
    far_sgrad = (far_weight * (far_dprod - row_delta[..., None])).astype(jnp.bfloat16)
    query_grad = (
        scaling
        * (
            jnp.einsum("bhqk,khd->bqhd", near_sgrad, near_key, preferred_element_type=jnp.float32)
            + jnp.einsum("bhqk,bkhd->bqhd", far_sgrad, far_key, preferred_element_type=jnp.float32)
        )
    ).astype(jnp.bfloat16)
    near_kgrad = scaling * jnp.einsum(
        "bhqk,bqhd->khd", near_sgrad, query_part, preferred_element_type=jnp.float32
    )
    near_vgrad = jnp.einsum(
        "bhqk,bqhd->khd", near_half, grad_part, preferred_element_type=jnp.float32
    )
    return (
        attended,
        query_grad,
        near_kgrad,
        near_vgrad,
        far_sgrad,
        far_half,
        row_max,
        row_sum,
        row_delta,
    )


def per_device(query_rows, key_rows, value_rows, out_grad, far_blocks):
    tok_dev, features = query_rows.shape
    blk_dev, far_count = far_blocks.shape
    groups = lax.axis_size("grp")
    windows = lax.axis_size("win")
    my_group = lax.axis_index("grp")
    my_window = lax.axis_index("win")
    entries = blk_dev * far_count
    slot_cap = entries // groups
    slot_total = groups * slot_cap
    scaling = 1.0 / math.sqrt(HEAD_DIM)
    glob_key, glob_value = (
        lax.all_gather(key_rows[:GTOK], "win", axis=0, tiled=True),
        lax.all_gather(value_rows[:GTOK], "win", axis=0, tiled=True),
    )
    listed = lax.all_gather(far_blocks, "grp", axis=0, tiled=True).reshape(groups, entries)
    own_owner, own_rank = owner_rank(far_blocks.reshape(1, entries), windows * blk_dev)
    slot_index = own_owner[0] * slot_cap + own_rank[0]
    peer_owner, peer_rank = owner_rank(listed, windows * blk_dev)
    inner_block = listed % blk_dev
    matches = (
        (peer_owner == my_group)[:, :, None, None]
        & (peer_rank[:, :, None, None] == jnp.arange(slot_cap)[None, None, :, None])
        & (inner_block[:, :, None, None] == jnp.arange(blk_dev)[None, None, None, :])
    )
    picker = (
        jnp.sum(matches.astype(jnp.int32), axis=1).reshape(slot_total, blk_dev).astype(jnp.bfloat16)
    )
    key_blocks = key_rows.reshape(blk_dev, BLOCK, features)
    value_blocks = value_rows.reshape(blk_dev, BLOCK, features)
    send_key = jnp.einsum("sj,jkd->skd", picker, key_blocks, preferred_element_type=jnp.bfloat16)
    send_value = jnp.einsum(
        "sj,jkd->skd", picker, value_blocks, preferred_element_type=jnp.bfloat16
    )
    got_key, got_value = (
        lax.all_to_all(
            send_key.reshape(groups, slot_cap, BLOCK, features),
            "grp",
            split_axis=0,
            concat_axis=0,
            tiled=True,
        ),
        lax.all_to_all(
            send_value.reshape(groups, slot_cap, BLOCK, features),
            "grp",
            split_axis=0,
            concat_axis=0,
            tiled=True,
        ),
    )
    far_key = jnp.take(got_key.reshape(slot_total, BLOCK, features), slot_index, axis=0).reshape(
        blk_dev, far_count * BLOCK, HEADS, HEAD_DIM
    )
    far_value = jnp.take(
        got_value.reshape(slot_total, BLOCK, features), slot_index, axis=0
    ).reshape(blk_dev, far_count * BLOCK, HEADS, HEAD_DIM)
    query_part = query_rows.reshape(blk_dev, BLOCK, HEADS, HEAD_DIM)
    grad_part = out_grad.reshape(blk_dev, BLOCK, HEADS, HEAD_DIM)
    near_key = jnp.concatenate([key_rows, glob_key], axis=0).reshape(
        tok_dev + windows * GTOK, HEADS, HEAD_DIM
    )
    near_value = jnp.concatenate([value_rows, glob_value], axis=0).reshape(
        tok_dev + windows * GTOK, HEADS, HEAD_DIM
    )
    near_mask = jnp.concatenate(
        [jnp.ones((tok_dev,), jnp.bool_), jnp.arange(windows * GTOK) // GTOK != my_window]
    )
    results = attend(query_part, near_key, near_value, near_mask, far_key, far_value, grad_part)
    (
        attended,
        query_grad,
        near_kgrad,
        near_vgrad,
        far_sgrad,
        far_half,
        row_max,
        row_sum,
        row_delta,
    ) = results
    glob_kgrad, glob_vgrad = (
        lax.psum_scatter(
            near_kgrad[tok_dev:].reshape(windows * GTOK, features).astype(jnp.bfloat16),
            "win",
            scatter_dimension=0,
            tiled=True,
        ).astype(jnp.float32),
        lax.psum_scatter(
            near_vgrad[tok_dev:].reshape(windows * GTOK, features).astype(jnp.bfloat16),
            "win",
            scatter_dimension=0,
            tiled=True,
        ).astype(jnp.float32),
    )
    far_kgrad = (
        (
            scaling
            * jnp.einsum(
                "bhqk,bqhd->bkhd", far_sgrad, query_part, preferred_element_type=jnp.float32
            )
        )
        .astype(jnp.bfloat16)
        .reshape(entries, BLOCK, features)
    )
    far_vgrad = (
        jnp.einsum("bhqk,bqhd->bkhd", far_half, grad_part, preferred_element_type=jnp.float32)
        .astype(jnp.bfloat16)
        .reshape(entries, BLOCK, features)
    )
    spread = (jnp.arange(slot_total)[:, None] == slot_index[None, :]).astype(jnp.bfloat16)
    back_key = jnp.einsum("se,ekd->skd", spread, far_kgrad, preferred_element_type=jnp.bfloat16)
    back_value = jnp.einsum("se,ekd->skd", spread, far_vgrad, preferred_element_type=jnp.bfloat16)
    ret_key, ret_value = (
        lax.all_to_all(
            back_key.reshape(groups, slot_cap, BLOCK, features),
            "grp",
            split_axis=0,
            concat_axis=0,
            tiled=True,
        ),
        lax.all_to_all(
            back_value.reshape(groups, slot_cap, BLOCK, features),
            "grp",
            split_axis=0,
            concat_axis=0,
            tiled=True,
        ),
    )
    tile_kgrad = ret_key.reshape(slot_total, BLOCK, features)
    tile_vgrad = ret_value.reshape(slot_total, BLOCK, features)
    own_kfar = jnp.einsum(
        "sj,skd->jkd", picker, tile_kgrad, preferred_element_type=jnp.float32
    ).reshape(tok_dev, features)
    own_vfar = jnp.einsum(
        "sj,skd->jkd", picker, tile_vgrad, preferred_element_type=jnp.float32
    ).reshape(tok_dev, features)
    key_sum = near_kgrad[:tok_dev].reshape(tok_dev, features) + own_kfar
    value_sum = near_vgrad[:tok_dev].reshape(tok_dev, features) + own_vfar
    key_grad = jnp.concatenate([key_sum[:GTOK] + glob_kgrad, key_sum[GTOK:]], axis=0).astype(
        jnp.bfloat16
    )
    value_grad = jnp.concatenate([value_sum[:GTOK] + glob_vgrad, value_sum[GTOK:]], axis=0).astype(
        jnp.bfloat16
    )
    return (
        attended.reshape(tok_dev, features),
        query_grad.reshape(tok_dev, features),
        key_grad,
        value_grad,
    )


def solution(mesh):
    in_specs = (
        P(("grp", "win"), None),
        P(("grp", "win"), None),
        P(("grp", "win"), None),
        P(("grp", "win"), None),
        P(("grp", "win"), None),
    )
    out_specs = (
        P(("grp", "win"), None),
        P(("grp", "win"), None),
        P(("grp", "win"), None),
        P(("grp", "win"), None),
    )
    return jax.shard_map(
        per_device, mesh=mesh, in_specs=in_specs, out_specs=out_specs, check_vma=False
    )
```

profile of v0, /device:TPU:1, one launch (start us, length us, event | category | flops | bytes accessed | tf_op | source)
XLA Modules:
  0.0 453.2 jit_solution(11606252146306635005)
XLA Ops:
  7.2 21.2 %all-gather.2 = s32[16,2,8]{2,1,0:T(2,128)S(1)} all-gather(s32[1,2,8]{2,1,0:T(2,128)} %bitcast.236), channel_id=1, replica_groups=mesh['win'=32,'grp'=16] {'grp'}, dimensions={0}, use_global_device_ids=true | all-gather | bytes 1088 | tf_op jit(solution)/shard_map/all_gather | solution.py:98
  28.8 1.7 convolution_bitcast_fusion
  30.5 2.5 copy.304
  33.0 3.8 all-to-all-start.1
  37.6 2.5 copy.295
  40.1 45.7 %all-to-all-done.1 = bf16[16,1,64,1024]{3,2,1,0:T(8,128)(2,1)S(1)} async-done(((bf16[16,1,64,1024]{3,2,1,0:T(8,128)(2,1)}), bf16[16,1,64,1024]{3,2,1,0:T(8,128)(2,1)S(1)}, u32[]{:S(2)}, u32[]{:S(2)}) %all-to-all-start.1) | async-done | bytes 2097184 | tf_op jit(solution)/shard_map/all_to_all | solution.py:125
  85.8 5.0 %all-to-all-start = ((bf16[16,1,64,1024]{3,2,1,0:T(8,128)(2,1)}), bf16[16,1,64,1024]{3,2,1,0:T(8,128)(2,1)}, u32[]{:S(2)}, u32[]{:S(2)}) async-start(bf16[16,1,64,1024]{3,2,1,0:T(8,128)(2,1)} %copy.295), calls=%async_computation | async-start | bytes 4194304 | tf_op jit(solution)/shard_map/all_to_all | solution.py:118
  91.7 43.3 %all-gather = bf16[32,1,1024]{2,1,0:T(2,128)(2,1)S(1)} all-gather(bf16[1,1,1024]{2,1,0:T(2,128)(2,1)S(1)} %slice_bitcast_fusion.1), channel_id=1, replica_groups=mesh['win'=32,'grp'=16] {'win'}, dimensions={0}, use_global_device_ids=true | all-gather | bytes 67584 | tf_op jit(solution)/shard_map/all_gather | solution.py:96
  135.0 0.8 fusion.80
  137.5 33.0 %all-gather.1 = bf16[32,1,1024]{2,1,0:T(2,128)(2,1)S(1)} all-gather(bf16[1,1,1024]{2,1,0:T(2,128)(2,1)S(1)} %slice_bitcast_fusion), channel_id=1, replica_groups=mesh['win'=32,'grp'=16] {'win'}, dimensions={0}, use_global_device_ids=true | all-gather | bytes 67584 | tf_op jit(solution)/shard_map/all_gather | solution.py:95
  170.7 0.8 fusion.79
  171.5 1.3 fusion.65
  173.1 2.0 gather_fusion.1
  175.1 3.7 gather_fusion
  178.8 2.0 broadcast_select_fusion
  181.5 0.9 bitcast_reduce_fusion
  186.2 1.4 multiply_reduce_fusion
  187.5 1.1 fusion.4
  188.7 1.1 copy-done.9
  189.7 0.8 fusion.28
  190.6 2.7 copy.321
  193.2 4.2 reshape.490
  197.4 3.1 fusion.22
  200.5 2.5 copy.323
  203.0 21.5 %all-to-all-start.2 = ((bf16[16,1,64,1024]{3,2,1,0:T(8,128)(2,1)}), bf16[16,1,64,1024]{3,2,1,0:T(8,128)(2,1)}, u32[]{:S(2)}, u32[]{:S(2)}) async-start(bf16[16,1,64,1024]{3,2,1,0:T(8,128)(2,1)} %copy.323), calls=%async_computation.2 | async-start | bytes 4194304 | tf_op jit(solution)/shard_map/all_to_all | solution.py:195
  224.5 2.0 convert_bitcast_fusion
  226.5 2.7 copy.332
  229.2 4.2 reshape.495
  233.4 3.1 fusion.25
  236.5 2.5 copy.334
  239.0 34.5 %all-to-all-done.2 = bf16[16,1,64,1024]{3,2,1,0:T(8,128)(2,1)} async-done(((bf16[16,1,64,1024]{3,2,1,0:T(8,128)(2,1)}), bf16[16,1,64,1024]{3,2,1,0:T(8,128)(2,1)}, u32[]{:S(2)}, u32[]{:S(2)}) %all-to-all-start.2) | async-done | bytes 2097184 | tf_op jit(solution)/shard_map/all_to_all | solution.py:195
  273.5 5.0 %all-to-all-start.3 = ((bf16[16,1,64,1024]{3,2,1,0:T(8,128)(2,1)}), bf16[16,1,64,1024]{3,2,1,0:T(8,128)(2,1)}, u32[]{:S(2)}, u32[]{:S(2)}) async-start(bf16[16,1,64,1024]{3,2,1,0:T(8,128)(2,1)} %copy.334), calls=%async_computation.3 | async-start | bytes 4194304 | tf_op jit(solution)/shard_map/all_to_all | solution.py:202
  278.6 1.7 copy.309
  280.3 1.8 copy.367
  282.0 1.3 dynamic-slice
  283.3 1.4 fusion.62
  285.6 0.8 copy-done.2
  287.2 0.8 copy-done.5
  290.6 0.8 copy.350
  291.5 0.8 copy.351
  292.3 0.9 copy_bitcast_fusion
  293.2 2.9 fusion.2
  296.5 31.1 %all-to-all-done.3 = bf16[16,1,64,1024]{3,2,1,0:T(8,128)(2,1)} async-done(((bf16[16,1,64,1024]{3,2,1,0:T(8,128)(2,1)}), bf16[16,1,64,1024]{3,2,1,0:T(8,128)(2,1)}, u32[]{:S(2)}, u32[]{:S(2)}) %all-to-all-start.3) | async-done | bytes 2097184 | tf_op jit(solution)/shard_map/all_to_all | solution.py:202
  327.6 2.9 fusion
  331.2 111.2 %all-reduce.6.cloned.1.call-done = (bf16[32,1024]{0,1:T(8,128)(2,1)}, bf16[32,1024]{0,1:T(8,128)(2,1)}) async-done(((bf16[32,1024]{0,1:T(8,128)(2,1)}, bf16[32,1024]{0,1:T(8,128)(2,1)}), (bf16[32,1024]{0,1:T(8,128)(2,1)}, bf16[32,1024]{0,1:T(8,128)(2,1)})) %all-reduce.6.cloned.1.call-update) | async-done | bytes 131088
  442.4 1.9 fusion.59
  444.5 0.9 copy.340
  445.5 0.9 copy.341
  (94 shorter events, 14.0 us)
Async XLA Ops:
  33.0 3.8 copy-start.8
  33.0 52.8 %all-to-all-start.1 = ((bf16[16,1,64,1024]{3,2,1,0:T(8,128)(2,1)}), bf16[16,1,64,1024]{3,2,1,0:T(8,128)(2,1)S(1)}, u32[]{:S(2)}, u32[]{:S(2)}) async-start(bf16[16,1,64,1024]{3,2,1,0:T(8,128)(2,1)} %copy.304), calls=%async_computation.1 | async-start | bytes 4194304 | tf_op jit(solution)/shard_map/all_to_all | solution.py:125
  40.1 50.7 %copy-start.15 = (s32[2,8]{1,0:T(2,128)S(1)}, s32[2,8]{1,0:T(2,128)}, u32[]{:S(2)}) copy-start(s32[2,8]{1,0:T(2,128)} %param.11) | copy-start | bytes 196
  40.1 50.8 %copy-start.12 = (bf16[128,1024]{1,0:T(8,128)(2,1)S(1)}, bf16[128,1024]{1,0:T(8,128)(2,1)}, u32[]{:S(2)}) copy-start(bf16[128,1024]{1,0:T(8,128)(2,1)} %param.10) | copy-start | bytes 786436
  40.1 51.6 %copy-start.7 = (bf16[128,1024]{1,0:T(8,128)(2,1)S(1)}, bf16[128,1024]{1,0:T(8,128)(2,1)}, u32[]{:S(2)}) copy-start(bf16[128,1024]{1,0:T(8,128)(2,1)} %param.9) | copy-start | bytes 786436
  85.8 89.3 %all-to-all-start = ((bf16[16,1,64,1024]{3,2,1,0:T(8,128)(2,1)}), bf16[16,1,64,1024]{3,2,1,0:T(8,128)(2,1)}, u32[]{:S(2)}, u32[]{:S(2)}) async-start(bf16[16,1,64,1024]{3,2,1,0:T(8,128)(2,1)} %copy.295), calls=%async_computation | async-start | bytes 4194304 | tf_op jit(solution)/shard_map/all_to_all | solution.py:118
  90.8 45.8 %copy-start.13 = (bf16[128,1024]{1,0:T(8,128)(2,1)S(1)}, bf16[128,1024]{1,0:T(8,128)(2,1)}, u32[]{:S(2)}) copy-start(bf16[128,1024]{1,0:T(8,128)(2,1)} %param.7) | copy-start | bytes 786436
  175.1 3.7 copy-start
  184.0 1.7 copy-start.1
  184.0 1.2 copy-start.11
  185.2 0.9 copy-start.3
  188.7 1.1 copy-start.9
  203.0 70.5 %all-to-all-start.2 = ((bf16[16,1,64,1024]{3,2,1,0:T(8,128)(2,1)}), bf16[16,1,64,1024]{3,2,1,0:T(8,128)(2,1)}, u32[]{:S(2)}, u32[]{:S(2)}) async-start(bf16[16,1,64,1024]{3,2,1,0:T(8,128)(2,1)} %copy.323), calls=%async_computation.2 | async-start | bytes 4194304 | tf_op jit(solution)/shard_map/all_to_all | solution.py:195
  273.5 54.0 %all-to-all-start.3 = ((bf16[16,1,64,1024]{3,2,1,0:T(8,128)(2,1)}), bf16[16,1,64,1024]{3,2,1,0:T(8,128)(2,1)}, u32[]{:S(2)}, u32[]{:S(2)}) async-start(bf16[16,1,64,1024]{3,2,1,0:T(8,128)(2,1)} %copy.334), calls=%async_computation.3 | async-start | bytes 4194304 | tf_op jit(solution)/shard_map/all_to_all | solution.py:202
  278.5 163.9 %all-reduce.6.cloned.1.call-start = ((), (), s32[]{:S(2)}) async-start(), calls=%async_computation.4 | async-start | bytes 1048576
  284.7 1.7 copy-start.4
  285.5 0.8 copy-start.2
  286.4 1.6 copy-start.6
  287.1 0.8 copy-start.5
  287.1 1.5 copy-start.10
  288.6 0.9 copy-start.14
  288.6 1.1 slice-start
  289.3 1.1 slice-start.1
Sparse Core Ops, SparseCore 0:
  292.5 149.9 all-reduce.5
where the time goes:
time: 458 us; the launch traced here: 453 us
  waiting for transfers between devices  223 us (49%)
  blocking collectives  97.6 us (21%)
  local copies, waits for them, and re-layouts  48.7 us (11%)
  starting transfers between devices  35.3 us (8%)
  matrix products  25.9 us (6%)
  between operations  14.5 us (3%)
  other arithmetic  8.54 us (2%)
    unnamed x2, waiting for transfers between devices  111 us
    all_to_all x1, waiting for transfers between devices, per_device(): lax.all_to_all(send_value.reshape(groups, slot_cap, BLOCK, features), 'gr...  45.7 us
    all_gather x1, blocking collectives, per_device(): lax.all_gather(value_rows[:GTOK], 'win', axis=0, tiled=True)  43.3 us
    all_to_all x1, waiting for transfers between devices, per_device(): lax.all_to_all(back_key.reshape(groups, slot_cap, BLOCK, features), 'grp'...  34.5 us
    all_gather x1, blocking collectives, per_device(): lax.all_gather(key_rows[:GTOK], 'win', axis=0, tiled=True)  33 us
    all_to_all x1, waiting for transfers between devices, per_device(): lax.all_to_all(back_value.reshape(groups, slot_cap, BLOCK, features), 'gr...  31.1 us
    all_to_all x1, starting transfers between devices, per_device(): lax.all_to_all(back_key.reshape(groups, slot_cap, BLOCK, features), 'grp'...  21.5 us
    all_gather x1, blocking collectives, per_device(): lax.all_gather(far_blocks, 'grp', axis=0, tiled=True)  21.2 us
  transfers between devices with their start and end apart: 5, of which 4 were waited for; matrix products, arithmetic and copies ran while one was open for 10% of the time, Pallas kernels for 0%

commit v1 on v0

v1 whole, which is shorter than its diff:
```python
import functools
import math

import jax
import jax.numpy as jnp
from jax import lax
from jax.experimental import pallas as pl
from jax.experimental.pallas import tpu as pltpu
from jax.sharding import Mesh
from jax.sharding import PartitionSpec as P

HEAD_DIM = 128
BLOCK = 64
TOK = 128
BLK = 2
FAR = 8
NX, NZ, NY, NC = 4, 8, 8, 2
WINDOWS = NX * NZ
HALF = 512
HEADS = HALF // HEAD_DIM
NEAR = 256
FKEYS = FAR * BLOCK
SCALE = 1.0 / math.sqrt(HEAD_DIM)
EXP_SCALE = SCALE * math.log2(math.e)
BF16 = jnp.bfloat16
F32 = jnp.float32


def dot_nt(a, b):
    return lax.dot_general(a, b, (((1,), (1,)), ((), ())), preferred_element_type=F32)


def dot_nn(a, b):
    return lax.dot_general(a, b, (((1,), (0,)), ((), ())), preferred_element_type=F32)


def dot_tn(a, b):
    return lax.dot_general(a, b, (((0,), (0,)), ((), ())), preferred_element_type=F32)


def attend_kernel(*refs):
    pos, far_own, far_peer, qdo_own, qdo_peer, glob = refs[:6]
    sources = refs[6:22]
    res_own, res_peer, base, gglob = refs[22:26]
    parts = refs[26:40]
    slots, near, fgrad, table = refs[40:]
    my_y, my_c, my_w = pos[0], pos[1], pos[2]
    for who, far in enumerate((far_own, far_peer)):
        for row in range(BLK):
            for entry in range(FAR):
                block = far[row, entry]
                group = lax.shift_right_logical(block, 6)
                offset = lax.bitwise_and(lax.shift_right_logical(group, 1) - my_y, NY - 1)
                chain = lax.bitwise_xor(lax.bitwise_and(group, 1), my_c)
                inner = lax.bitwise_and(block, 1)
                table[who, chain * NY + offset] = (row * FAR + entry) * 2 + inner
    for source in range(2 * NY):
        for who in range(2):
            code = table[who, source]
            slot = lax.shift_right_logical(code, 1)
            inner = lax.bitwise_and(code, 1)
            at = pl.ds(pl.multiple_of(slot * BLOCK, BLOCK), BLOCK)
            rows = pl.ds(pl.multiple_of(inner * BLOCK, BLOCK), BLOCK)
            for kind in range(2):
                slots[kind, who, at, :] = sources[source][kind, rows, :]
    for who in range(2):
        for kind in range(2):
            near[kind, who, :TOK, :] = sources[who * NY][kind]
            first = (who * 2 + kind) * HALF
            near[kind, who, TOK : TOK + WINDOWS, :] = glob[:, first : first + HALF]
            near[kind, who, TOK + WINDOWS :, :] = jnp.zeros((NEAR - TOK - WINDOWS, HALF), BF16)
    column = lax.broadcasted_iota(jnp.int32, (TOK, NEAR), 1)
    hidden = (column >= TOK + WINDOWS) | (column == TOK + my_w)

    def head_step(head, carry):
        lanes = pl.ds(pl.multiple_of(head * HEAD_DIM, HEAD_DIM), HEAD_DIM)
        for who, (qdo, res) in enumerate(((qdo_own, res_own), (qdo_peer, res_peer))):
            query = qdo[0, :, lanes]
            grad = qdo[1, :, lanes]
            near_key = near[0, who, :, lanes]
            near_value = near[1, who, :, lanes]
            near_score = jnp.where(hidden, -1e30, dot_nt(query, near_key))
            near_dprod = dot_nt(grad, near_value)
            halves, near_dscore = [], []
            near_half = []
            for row in range(BLK):
                rows = slice(row * BLOCK, (row + 1) * BLOCK)
                keys = slice(row * FKEYS, (row + 1) * FKEYS)
                far_key = slots[0, who, keys, lanes]
                far_value = slots[1, who, keys, lanes]
                far_score = dot_nt(query[rows], far_key)
                ns = near_score[rows]
                top = jnp.maximum(
                    jnp.max(ns, axis=1, keepdims=True), jnp.max(far_score, axis=1, keepdims=True)
                )
                near_exp = jnp.exp2((ns - top) * EXP_SCALE)
                far_exp = jnp.exp2((far_score - top) * EXP_SCALE)
                total = jnp.sum(near_exp, axis=1, keepdims=True) + jnp.sum(
                    far_exp, axis=1, keepdims=True
                )
                inverse = 1.0 / total
                near_weight = near_exp * inverse
                far_weight = far_exp * inverse
                nh = near_weight.astype(BF16)
                fh = far_weight.astype(BF16)
                out = (dot_nn(nh, near_value) + dot_nn(fh, far_value)).astype(BF16)
                res[0, rows, lanes] = out
                g = grad[rows]
                delta = jnp.sum(g.astype(F32) * out.astype(F32), axis=1, keepdims=True)
                far_dprod = dot_nt(g, far_value)
                nd = (near_weight * (near_dprod[rows] - delta)).astype(BF16)
                fd = (far_weight * (far_dprod - delta)).astype(BF16)
                dq = (dot_nn(nd, near_key) + dot_nn(fd, far_key)) * SCALE
                res[1, rows, lanes] = dq.astype(BF16)
                fgrad[0, who, keys, lanes] = (dot_tn(fd, query[rows]) * SCALE).astype(BF16)
                fgrad[1, who, keys, lanes] = dot_tn(fh, g).astype(BF16)
                near_half.append(nh)
                near_dscore.append(nd)
            near_kgrad = dot_tn(jnp.concatenate(near_dscore, axis=0), query) * SCALE
            near_vgrad = dot_tn(jnp.concatenate(near_half, axis=0), grad)
            for kind, value in enumerate((near_kgrad, near_vgrad)):
                base[who, kind, :, lanes] = value[:TOK]
                first = (who * 2 + kind) * HALF
                cols = pl.ds(pl.multiple_of(first + head * HEAD_DIM, HEAD_DIM), HEAD_DIM)
                gglob[:, cols] = value[TOK : TOK + WINDOWS].astype(BF16)
        return carry

    lax.fori_loop(0, HEADS, head_step, 0)

    for source in range(2 * NY):
        for kind in range(2):
            for inner in range(BLK):
                rows = slice(inner * BLOCK, (inner + 1) * BLOCK)
                value = None
                for who in range(2):
                    code = table[who, source]
                    slot = lax.shift_right_logical(code, 1)
                    at = pl.ds(pl.multiple_of(slot * BLOCK, BLOCK), BLOCK)
                    here = (lax.bitwise_and(code, 1) == inner).astype(F32)
                    term = fgrad[kind, who, at, :].astype(F32) * here
                    value = term if value is None else value + term
                if source % NY == 0:
                    base[source // NY, kind, rows, :] += value
                else:
                    index = source - 1 - source // NY
                    parts[index][kind, rows, :] = value.astype(BF16)


def attend(pos, far_own, far_peer, qdo_own, qdo_peer, glob, sources):
    smem = pl.BlockSpec(memory_space=pltpu.SMEM)
    vmem = pl.BlockSpec(memory_space=pltpu.VMEM)
    piece = jax.ShapeDtypeStruct((2, TOK, HALF), BF16)
    return pl.pallas_call(
        attend_kernel,
        out_shape=[
            piece,
            piece,
            jax.ShapeDtypeStruct((2, 2, TOK, HALF), F32),
            jax.ShapeDtypeStruct((WINDOWS, 4 * HALF), BF16),
        ]
        + [piece] * 14,
        in_specs=[smem] * 3 + [vmem] * 19,
        out_specs=[vmem] * 18,
        scratch_shapes=[
            pltpu.VMEM((2, 2, BLK * FKEYS, HALF), BF16),
            pltpu.VMEM((2, 2, NEAR, HALF), BF16),
            pltpu.VMEM((2, 2, BLK * FKEYS, HALF), BF16),
            pltpu.SMEM((2, 2 * NY), jnp.int32),
        ],
        compiler_params=pltpu.CompilerParams(vmem_limit_bytes=44 * 1024 * 1024),
        cost_estimate=pl.CostEstimate(
            flops=1_200_000_000, bytes_accessed=12_000_000, transcendentals=800_000
        ),
    )(pos, far_own, far_peer, qdo_own, qdo_peer, glob, *sources)


UP = [(i, (i + 1) % NY) for i in range(NY)]
DOWN = [(i, (i - 1) % NY) for i in range(NY)]
SWAP = [(0, 1), (1, 0)]


def per_device(query_rows, key_rows, value_rows, out_grad, far_blocks):
    my_y = lax.axis_index("y")
    my_c = lax.axis_index("c")
    my_w = lax.axis_index("x") * NZ + lax.axis_index("z")
    swap = functools.partial(lax.ppermute, axis_name="c", perm=SWAP)
    up = functools.partial(lax.ppermute, axis_name="y", perm=UP)
    down = functools.partial(lax.ppermute, axis_name="y", perm=DOWN)
    low = my_c == 0

    def split(first, second):
        mine = [jnp.where(low, a[:, :HALF], a[:, HALF:]) for a in (first, second)]
        other = [jnp.where(low, a[:, HALF:], a[:, :HALF]) for a in (first, second)]
        return jnp.stack(mine), jnp.stack(other)

    kv_own, kv_send = split(key_rows, value_rows)
    qdo_own, qdo_send = split(query_rows, out_grad)
    kv_peer = swap(kv_send)
    sources = [None] * 16
    sources[0], sources[NY] = kv_own, kv_peer
    chains = [
        (0, up, 4, -1),
        (0, down, 3, 1),
        (NY, up, 3, -1),
        (NY, down, 4, 1),
    ]
    held = [kv_own, kv_own, kv_peer, kv_peer]
    for step in range(1, 5):
        for i, (first, move, count, sign) in enumerate(chains):
            if step <= count:
                held[i] = move(held[i])
                sources[first + (sign * step) % NY] = held[i]
    qdo_peer = swap(qdo_send)
    far_peer = swap(far_blocks)
    row = jnp.concatenate([kv_own[0, 0], kv_own[1, 0], kv_peer[0, 0], kv_peer[1, 0]])
    glob = lax.all_to_all(
        jnp.broadcast_to(row, (WINDOWS, 4 * HALF)), ("x", "z"), 0, 0, tiled=True
    )
    pos = jnp.stack([my_y, my_c, my_w]).astype(jnp.int32)
    res_own, res_peer, base, gglob, *parts = attend(
        pos, far_blocks, far_peer, qdo_own, qdo_peer, glob, sources
    )
    part = parts[:7], parts[7:]

    held = [
        part[0][4 - 1],
        part[0][5 - 1],
        part[1][3 - 1],
        part[1][4 - 1],
    ]
    at = [4, 5, 3, 4]
    for step in range(1, 5):
        for i, (first, move, count, sign) in enumerate(chains):
            if step <= count:
                held[i] = move(held[i])
                at[i] = (at[i] + sign) % NY
                if at[i]:
                    mine = part[first // NY][at[i] - 1]
                    held[i] = (held[i].astype(F32) + mine.astype(F32)).astype(BF16)
    gback = lax.all_to_all(gglob, ("x", "z"), 0, 0, tiled=True)
    gsum = jnp.sum(gback.astype(F32), axis=0).reshape(2, 2, 1, HALF)
    res_back = swap(res_peer)
    first_row = lax.broadcasted_iota(jnp.int32, (1, TOK, 1), 1) == 0

    def finish(who):
        total = base[who] + held[2 * who].astype(F32) + held[2 * who + 1].astype(F32)
        return (total + jnp.where(first_row, gsum[who], 0.0)).astype(BF16)

    peer_grad = swap(finish(1))
    own_grad = finish(0)

    def join(mine, other):
        return jnp.where(
            low,
            jnp.concatenate([mine, other], axis=1),
            jnp.concatenate([other, mine], axis=1),
        )

    return (
        join(res_own[0], res_back[0]),
        join(res_own[1], res_back[1]),
        join(own_grad[0], peer_grad[0]),
        join(own_grad[1], peer_grad[1]),
    )


def solution(mesh):
    fine = Mesh(mesh.devices.reshape(NX, NZ, NY, NC), ("x", "z", "y", "c"))
    spec = P(("y", "c", "x", "z"), None)
    return jax.shard_map(
        per_device, mesh=fine, in_specs=(spec,) * 5, out_specs=(spec,) * 4, check_vma=False
    )
```

time: 458 us -> 192 us (0.42)
  waiting for transfers between devices: 223 us -> 17.2 us
  blocking collectives: 97.6 us -> 0 us
  starting transfers between devices: 35.3 us -> 124 us
  local copies, waits for them, and re-layouts: 48.7 us -> 21.3 us
  matrix products: 25.9 us -> 0 us
  Pallas kernels: 0 us -> 15.4 us
  between operations: 14.5 us -> 1.61 us
    ppermute x0 -> x33, starting transfers between devices: none -> 111 us  [the longest x28 85.5 us: per_device(): held[i] = move(held[i])]
    unnamed x2 -> x0, waiting for transfers between devices: 111 us -> none
    all_to_all x4 -> x2, waiting for transfers between devices: 111 us -> 8.07 us  [the longest x1 8.07 us: per_device(): lax.all_to_all(jnp.broadcast_to(row, (WINDOWS, 4 * HALF)), ('x', 'z'), 0,...]
    all_gather x3 -> x0, blocking collectives: 97.6 us -> none  [the longest x1 43.3 us: per_device(): lax.all_gather(value_rows[:GTOK], 'win', axis=0, tiled=True)]
    dot_general x16 -> x0, matrix products: 23.3 us -> none  [the longest x1 3.1 us: per_device(): jnp.einsum('se,ekd->skd', spread, far_kgrad, preferred_element_type=jnp.b...]
    reshape x13 -> x0, local copies, waits for them, and re-layouts: 22.2 us -> none  [the longest x1 4.21 us: per_device(): far_vgrad = jnp.einsum('bhqk,bqhd->bkhd', far_half, grad_part, preferred_...]
    all_to_all x4 -> x2, starting transfers between devices: 35.2 us -> 13.1 us  [the longest x1 9.25 us: per_device(): lax.all_to_all(jnp.broadcast_to(row, (WINDOWS, 4 * HALF)), ('x', 'z'), 0,...]
    pallas_call x0 -> x1, Pallas kernels: none -> 15.4 us  [attend(): pl.pallas_call(attend_kernel, out_shape=[piece, piece, jax.ShapeDtypeStru...]
  transfers between devices with their start and end apart: 5 -> 35, of which waited for: 4 -> 5; matrix products, arithmetic and copies ran while one was open for 10% -> 6% of each run, Pallas kernels for 0% -> 0%
where the time goes in v1:
time: 192 us; the launch traced here: 191 us
  starting transfers between devices  124 us (65%)
  local copies, waits for them, and re-layouts  21.3 us (11%)
  waiting for transfers between devices  17.2 us (9%)
  Pallas kernels  15.4 us (8%)
  other arithmetic  11 us (6%)
    ppermute x28, starting transfers between devices, per_device(): held[i] = move(held[i])  85.5 us
    unnamed x87, local copies, waits for them, and re-layouts  19.5 us
    pallas_call x1, Pallas kernels, attend(): pl.pallas_call(attend_kernel, out_shape=[piece, piece, jax.ShapeDtypeStru...  15.4 us
    all_to_all x1, starting transfers between devices, per_device(): lax.all_to_all(jnp.broadcast_to(row, (WINDOWS, 4 * HALF)), ('x', 'z'), 0,...  9.25 us
    ppermute x28, waiting for transfers between devices, per_device(): held[i] = move(held[i])  8.94 us
    ppermute x1, starting transfers between devices, per_device(): kv_peer = swap(kv_send)  8.79 us
    all_to_all x1, waiting for transfers between devices, per_device(): lax.all_to_all(jnp.broadcast_to(row, (WINDOWS, 4 * HALF)), ('x', 'z'), 0,...  8.07 us
    ppermute x1, starting transfers between devices, per_device(): peer_grad = swap(finish(1))  5.67 us
  transfers between devices with their start and end apart: 35, of which 5 were waited for; matrix products, arithmetic and copies ran while one was open for 6% of the time, Pallas kernels for 0%

profile of v1, /device:TPU:1, one launch (start us, length us, event | category | flops | bytes accessed | tf_op | source)
XLA Modules:
  0.0 190.9 jit_solution(1182086220148030155)
XLA Ops:
  0.6 1.0 select_bitcast_fusion.3
  1.8 8.8 %collective-permute-start.2 = (bf16[2,128,512]{2,1,0:T(8,128)(2,1)S(1)}, bf16[2,128,512]{2,1,0:T(8,128)(2,1)S(1)}, u32[]{:S(2)}, u32[]{:S(2)}) collective-permute-start(bf16[2,128,512]{2,1,0:T(8,128)(2,1)S(1)} %pad_maximum_fusion.2), channel_id=1, source_target_pairs={{0,1},{1,0},{2,3},{3,2},{4,5},{5,4},{6,7},{7,6},{8,9},{9,8},{10,11... | collective-permute-start | bytes 786440 | tf_op jit(solution)/shard_map/ppermute | solution.py:198
  10.6 2.1 %collective-permute-start.6 = (bf16[2,128,512]{2,1,0:T(8,128)(2,1)S(1)}, bf16[2,128,512]{2,1,0:T(8,128)(2,1)S(1)}, u32[]{:S(2)}, u32[]{:S(2)}) collective-permute-start(bf16[2,128,512]{2,1,0:T(8,128)(2,1)S(1)} %pad_maximum_fusion.3.refs_6_), channel_id=1, source_target_pairs={{0,2},{2,4},{4,6},{6,8},{8,10},{10,12},{12,14},{14,0},{1,3},{3,5},... | collective-permute-start | bytes 786440 | tf_op jit(solution)/shard_map/ppermute | solution.py:211
  12.7 4.6 %collective-permute-start.10 = (bf16[2,128,512]{2,1,0:T(8,128)(2,1)S(1)}, bf16[2,128,512]{2,1,0:T(8,128)(2,1)S(1)}, u32[]{:S(2)}, u32[]{:S(2)}) collective-permute-start(bf16[2,128,512]{2,1,0:T(8,128)(2,1)S(1)} %collective-permute-done.2.refs_14_), channel_id=1, source_target_pairs={{0,14},{2,0},{4,2},{6,4},{8,6},{10,8},{12,10},{14,12},{1,15},{3,1}... | collective-permute-start | bytes 786440 | tf_op jit(solution)/shard_map/ppermute | solution.py:211
  17.3 1.9 %collective-permute-start.3 = (bf16[2,128,512]{2,1,0:T(8,128)(2,1)S(1)}, bf16[2,128,512]{2,1,0:T(8,128)(2,1)S(1)}, u32[]{:S(2)}, u32[]{:S(2)}) collective-permute-start(bf16[2,128,512]{2,1,0:T(8,128)(2,1)S(1)} %pad_maximum_fusion.3.refs_6_), channel_id=1, source_target_pairs={{0,14},{2,0},{4,2},{6,4},{8,6},{10,8},{12,10},{14,12},{1,15},{3,1}... | collective-permute-start | bytes 786440 | tf_op jit(solution)/shard_map/ppermute | solution.py:211
  19.2 2.5 %collective-permute-start = (s32[2,8]{1,0:T(2,128)S(1)}, s32[2,8]{1,0:T(2,128)S(1)}, u32[]{:S(2)}, u32[]{:S(2)}) collective-permute-start(s32[2,8]{1,0:T(2,128)S(1)} %copy-done.30), channel_id=1, source_target_pairs={{0,1},{1,0},{2,3},{3,2},{4,5},{5,4},{6,7},{7,6},{8,9},{9,8},{10,11... | collective-permute-start | bytes 200 | tf_op jit(solution)/shard_map/ppermute | solution.py:214
  22.4 3.6 %collective-permute-start.14 = (bf16[2,128,512]{2,1,0:T(8,128)(2,1)S(1)}, bf16[2,128,512]{2,1,0:T(8,128)(2,1)S(1)}, u32[]{:S(2)}, u32[]{:S(2)}) collective-permute-start(bf16[2,128,512]{2,1,0:T(8,128)(2,1)S(1)} %collective-permute-done.2.refs_14_), channel_id=1, source_target_pairs={{0,2},{2,4},{4,6},{6,8},{8,10},{10,12},{12,14},{14,0},{1,3},{3,5},... | collective-permute-start | bytes 786440 | tf_op jit(solution)/shard_map/ppermute | solution.py:211
  26.1 1.9 %collective-permute-start.7 = (bf16[2,128,512]{2,1,0:T(8,128)(2,1)S(1)}, bf16[2,128,512]{2,1,0:T(8,128)(2,1)S(1)}, u32[]{:S(2)}, u32[]{:S(2)}) collective-permute-start(bf16[2,128,512]{2,1,0:T(8,128)(2,1)S(1)} %collective-permute-done.6.refs_13_), channel_id=1, source_target_pairs={{0,2},{2,4},{4,6},{6,8},{8,10},{10,12},{12,14},{14,0},{1,3},{3,5},... | collective-permute-start | bytes 786440 | tf_op jit(solution)/shard_map/ppermute | solution.py:211
  28.0 4.6 %collective-permute-start.11 = (bf16[2,128,512]{2,1,0:T(8,128)(2,1)S(1)}, bf16[2,128,512]{2,1,0:T(8,128)(2,1)S(1)}, u32[]{:S(2)}, u32[]{:S(2)}) collective-permute-start(bf16[2,128,512]{2,1,0:T(8,128)(2,1)S(1)} %collective-permute-done.10.refs_15_), channel_id=1, source_target_pairs={{0,14},{2,0},{4,2},{6,4},{8,6},{10,8},{12,10},{14,12},{1,15},{3,1}... | collective-permute-start | bytes 786440 | tf_op jit(solution)/shard_map/ppermute | solution.py:211
  33.3 1.9 %collective-permute-start.4 = (bf16[2,128,512]{2,1,0:T(8,128)(2,1)S(1)}, bf16[2,128,512]{2,1,0:T(8,128)(2,1)S(1)}, u32[]{:S(2)}, u32[]{:S(2)}) collective-permute-start(bf16[2,128,512]{2,1,0:T(8,128)(2,1)S(1)} %collective-permute-done.3.refs_7_), channel_id=1, source_target_pairs={{0,14},{2,0},{4,2},{6,4},{8,6},{10,8},{12,10},{14,12},{1,15},{3,1}... | collective-permute-start | bytes 786440 | tf_op jit(solution)/shard_map/ppermute | solution.py:211
  35.2 3.8 %collective-permute-done.7.refs_12_ = bf16[2,128,512]{2,1,0:T(8,128)(2,1)S(1)} collective-permute-done((bf16[2,128,512]{2,1,0:T(8,128)(2,1)S(1)}, bf16[2,128,512]{2,1,0:T(8,128)(2,1)S(1)}, u32[]{:S(2)}, u32[]{:S(2)}) %collective-permute-start.7) | collective-permute-done | bytes 262176 | tf_op jit(solution)/shard_map/ppermute | solution.py:211
  39.0 2.4 %collective-permute-start.8 = (bf16[2,128,512]{2,1,0:T(8,128)(2,1)S(1)}, bf16[2,128,512]{2,1,0:T(8,128)(2,1)S(1)}, u32[]{:S(2)}, u32[]{:S(2)}) collective-permute-start(bf16[2,128,512]{2,1,0:T(8,128)(2,1)S(1)} %collective-permute-done.7.refs_12_), channel_id=1, source_target_pairs={{0,2},{2,4},{4,6},{6,8},{8,10},{10,12},{12,14},{14,0},{1,3},{3,5},... | collective-permute-start | bytes 786440 | tf_op jit(solution)/shard_map/ppermute | solution.py:211
  41.5 2.1 %collective-permute-start.15 = (bf16[2,128,512]{2,1,0:T(8,128)(2,1)S(1)}, bf16[2,128,512]{2,1,0:T(8,128)(2,1)S(1)}, u32[]{:S(2)}, u32[]{:S(2)}) collective-permute-start(bf16[2,128,512]{2,1,0:T(8,128)(2,1)S(1)} %collective-permute-done.14.refs_21_), channel_id=1, source_target_pairs={{0,2},{2,4},{4,6},{6,8},{8,10},{10,12},{12,14},{14,0},{1,3},{3,5},... | collective-permute-start | bytes 786440 | tf_op jit(solution)/shard_map/ppermute | solution.py:211
  43.6 4.4 %collective-permute-start.12 = (bf16[2,128,512]{2,1,0:T(8,128)(2,1)S(1)}, bf16[2,128,512]{2,1,0:T(8,128)(2,1)S(1)}, u32[]{:S(2)}, u32[]{:S(2)}) collective-permute-start(bf16[2,128,512]{2,1,0:T(8,128)(2,1)S(1)} %collective-permute-done.11.refs_16_), channel_id=1, source_target_pairs={{0,14},{2,0},{4,2},{6,4},{8,6},{10,8},{12,10},{14,12},{1,15},{3,1}... | collective-permute-start | bytes 786440 | tf_op jit(solution)/shard_map/ppermute | solution.py:211
  48.8 3.5 %collective-permute-start.1 = (bf16[2,128,512]{2,1,0:T(8,128)(2,1)}, bf16[2,128,512]{2,1,0:T(8,128)(2,1)}, u32[]{:S(2)}, u32[]{:S(2)}) collective-permute-start(bf16[2,128,512]{2,1,0:T(8,128)(2,1)} %pad_maximum_fusion.1), channel_id=1, source_target_pairs={{0,1},{1,0},{2,3},{3,2},{4,5},{5,4},{6,7},{7,6},{8,9},{9,8},{10,11... | collective-permute-start | bytes 786440 | tf_op jit(solution)/shard_map/ppermute | solution.py:213
  52.4 2.9 %collective-permute-start.5 = (bf16[2,128,512]{2,1,0:T(8,128)(2,1)S(1)}, bf16[2,128,512]{2,1,0:T(8,128)(2,1)}, u32[]{:S(2)}, u32[]{:S(2)}) collective-permute-start(bf16[2,128,512]{2,1,0:T(8,128)(2,1)S(1)} %collective-permute-done.4.refs_8_), channel_id=1, source_target_pairs={{0,14},{2,0},{4,2},{6,4},{8,6},{10,8},{12,10},{14,12},{1,15},{3,1}... | collective-permute-start | bytes 786440 | tf_op jit(solution)/shard_map/ppermute | solution.py:211
  55.2 2.4 %collective-permute-start.9 = (bf16[2,128,512]{2,1,0:T(8,128)(2,1)S(1)}, bf16[2,128,512]{2,1,0:T(8,128)(2,1)}, u32[]{:S(2)}, u32[]{:S(2)}) collective-permute-start(bf16[2,128,512]{2,1,0:T(8,128)(2,1)S(1)} %collective-permute-done.8.refs_11_), channel_id=1, source_target_pairs={{0,2},{2,4},{4,6},{6,8},{8,10},{10,12},{12,14},{14,0},{1,3},{3,5},... | collective-permute-start | bytes 786440 | tf_op jit(solution)/shard_map/ppermute | solution.py:211
  57.7 1.9 %collective-permute-start.16 = (bf16[2,128,512]{2,1,0:T(8,128)(2,1)S(1)}, bf16[2,128,512]{2,1,0:T(8,128)(2,1)}, u32[]{:S(2)}, u32[]{:S(2)}) collective-permute-start(bf16[2,128,512]{2,1,0:T(8,128)(2,1)S(1)} %collective-permute-done.15.refs_20_), channel_id=1, source_target_pairs={{0,2},{2,4},{4,6},{6,8},{8,10},{10,12},{12,14},{14,0},{1,3},{3,5},... | collective-permute-start | bytes 786440 | tf_op jit(solution)/shard_map/ppermute | solution.py:211
  60.3 4.6 %collective-permute-start.13 = (bf16[2,128,512]{2,1,0:T(8,128)(2,1)S(1)}, bf16[2,128,512]{2,1,0:T(8,128)(2,1)}, u32[]{:S(2)}, u32[]{:S(2)}) collective-permute-start(bf16[2,128,512]{2,1,0:T(8,128)(2,1)S(1)} %collective-permute-done.12.refs_17_), channel_id=1, source_target_pairs={{0,14},{2,0},{4,2},{6,4},{8,6},{10,8},{12,10},{14,12},{1,15},{3,1}... | collective-permute-start | bytes 786440 | tf_op jit(solution)/shard_map/ppermute | solution.py:211
  66.3 1.4 reduce.9
  68.4 9.2 %all-to-all-start = ((bf16[32,2,1024]{2,1,0:T(2,128)(2,1)}), bf16[32,2,1024]{2,1,0:T(2,128)(2,1)S(1)}, u32[]{:S(2)}, u32[]{:S(2)}) async-start(bf16[32,2,1024]{2,1,0:T(2,128)(2,1)} %reshape.47), calls=%async_computation | async-start | bytes 262144 | tf_op jit(solution)/shard_map/all_to_all | solution.py:216
  77.8 1.0 pad_maximum_fusion.refs_3_
  78.8 8.1 %all-to-all-done = bf16[32,2,1024]{2,1,0:T(2,128)(2,1)S(1)} async-done(((bf16[32,2,1024]{2,1,0:T(2,128)(2,1)}), bf16[32,2,1024]{2,1,0:T(2,128)(2,1)S(1)}, u32[]{:S(2)}, u32[]{:S(2)}) %all-to-all-start) | async-done | bytes 131104 | tf_op jit(solution)/shard_map/all_to_all | solution.py:216
  87.6 1.1 copy.13
  89.7 0.9 copy-done.9
  90.7 0.9 copy-done.11
  91.6 15.4 %shard_map.84 = (bf16[2,128,512]{2,1,0:T(8,128)(2,1)S(1)}, bf16[2,128,512]{2,1,0:T(8,128)(2,1)S(1)}, f32[2,2,128,512]{3,2,1,0:T(8,128)S(1)}, bf16[32,2048]{1,0:T...) custom-call(s32[3]{0:T(128)S(1)} %pad_add_fusion.refs_0_, ...), custom_call_target="tpu_custom_call" | custom-call | flops 1200000000 | bytes 12000000 | tf_op jit(solution)/shard_map/pallas_call | solution.py:153
  119.6 3.8 %all-to-all-start.1 = ((bf16[32,2,1024]{2,1,0:T(2,128)(2,1)}), bf16[32,2,1024]{2,1,0:T(2,128)(2,1)S(1)}, u32[]{:S(2)}, u32[]{:S(2)}) async-start(bf16[32,2,1024]{2,1,0:T(2,128)(2,1)} %reshape.49), calls=%async_computation.1 | async-start | bytes 262144 | tf_op jit(solution)/shard_map/all_to_all | solution.py:240
  123.5 1.9 %collective-permute-start.25 = (bf16[2,128,512]{2,1,0:T(8,128)(2,1)}, bf16[2,128,512]{2,1,0:T(8,128)(2,1)S(1)}, u32[]{:S(2)}, u32[]{:S(2)}) collective-permute-start(bf16[2,128,512]{2,1,0:T(8,128)(2,1)} %copy-done.37), channel_id=1, source_target_pairs={{0,2},{2,4},{4,6},{6,8},{8,10},{10,12},{12,14},{14,0},{1,3},{3,5},... | collective-permute-start | bytes 786440 | tf_op jit(solution)/shard_map/ppermute | solution.py:235
  125.4 4.6 %collective-permute-start.28 = (bf16[2,128,512]{2,1,0:T(8,128)(2,1)}, bf16[2,128,512]{2,1,0:T(8,128)(2,1)S(1)}, u32[]{:S(2)}, u32[]{:S(2)}) collective-permute-start(bf16[2,128,512]{2,1,0:T(8,128)(2,1)} %copy-done.36), channel_id=1, source_target_pairs={{0,14},{2,0},{4,2},{6,4},{8,6},{10,8},{12,10},{14,12},{1,15},{3,1}... | collective-permute-start | bytes 786440 | tf_op jit(solution)/shard_map/ppermute | solution.py:235
  130.0 1.9 %collective-permute-start.18 = (bf16[2,128,512]{2,1,0:T(8,128)(2,1)}, bf16[2,128,512]{2,1,0:T(8,128)(2,1)S(1)}, u32[]{:S(2)}, u32[]{:S(2)}) collective-permute-start(bf16[2,128,512]{2,1,0:T(8,128)(2,1)} %copy-done.35), channel_id=1, source_target_pairs={{0,2},{2,4},{4,6},{6,8},{8,10},{10,12},{12,14},{14,0},{1,3},{3,5},... | collective-permute-start | bytes 786440 | tf_op jit(solution)/shard_map/ppermute | solution.py:235
  131.9 4.6 %collective-permute-start.22 = (bf16[2,128,512]{2,1,0:T(8,128)(2,1)S(1)}, bf16[2,128,512]{2,1,0:T(8,128)(2,1)S(1)}, u32[]{:S(2)}, u32[]{:S(2)}) collective-permute-start(bf16[2,128,512]{2,1,0:T(8,128)(2,1)S(1)} %copy-done.34), channel_id=1, source_target_pairs={{0,14},{2,0},{4,2},{6,4},{8,6},{10,8},{12,10},{14,12},{1,15},{3,1}... | collective-permute-start | bytes 786440 | tf_op jit(solution)/shard_map/ppermute | solution.py:235
  136.5 5.3 %collective-permute-start.17 = (bf16[2,128,512]{2,1,0:T(8,128)(2,1)S(1)}, bf16[2,128,512]{2,1,0:T(8,128)(2,1)}, u32[]{:S(2)}, u32[]{:S(2)}) collective-permute-start(bf16[2,128,512]{2,1,0:T(8,128)(2,1)S(1)} %copy-done.32), channel_id=1, source_target_pairs={{0,1},{1,0},{2,3},{3,2},{4,5},{5,4},{6,7},{7,6},{8,9},{9,8},{10,11... | collective-permute-start | bytes 786440 | tf_op jit(solution)/shard_map/ppermute | solution.py:242
  142.9 1.9 %collective-permute-start.26 = (bf16[2,128,512]{2,1,0:T(8,128)(2,1)S(1)}, bf16[2,128,512]{2,1,0:T(8,128)(2,1)S(1)}, u32[]{:S(2)}, u32[]{:S(2)}) collective-permute-start(bf16[2,128,512]{2,1,0:T(8,128)(2,1)S(1)} %add_convert_fusion.4), channel_id=1, source_target_pairs={{0,2},{2,4},{4,6},{6,8},{8,10},{10,12},{12,14},{14,0},{1,3},{3,5},... | collective-permute-start | bytes 786440 | tf_op jit(solution)/shard_map/ppermute | solution.py:235
  144.9 4.6 %collective-permute-start.29 = (bf16[2,128,512]{2,1,0:T(8,128)(2,1)S(1)}, bf16[2,128,512]{2,1,0:T(8,128)(2,1)S(1)}, u32[]{:S(2)}, u32[]{:S(2)}) collective-permute-start(bf16[2,128,512]{2,1,0:T(8,128)(2,1)S(1)} %add_convert_fusion.2), channel_id=1, source_target_pairs={{0,14},{2,0},{4,2},{6,4},{8,6},{10,8},{12,10},{14,12},{1,15},{3,1}... | collective-permute-start | bytes 786440 | tf_op jit(solution)/shard_map/ppermute | solution.py:235
  149.6 1.9 %collective-permute-start.19 = (bf16[2,128,512]{2,1,0:T(8,128)(2,1)S(1)}, bf16[2,128,512]{2,1,0:T(8,128)(2,1)S(1)}, u32[]{:S(2)}, u32[]{:S(2)}) collective-permute-start(bf16[2,128,512]{2,1,0:T(8,128)(2,1)S(1)} %add_convert_fusion.9), channel_id=1, source_target_pairs={{0,2},{2,4},{4,6},{6,8},{8,10},{10,12},{12,14},{14,0},{1,3},{3,5},... | collective-permute-start | bytes 786440 | tf_op jit(solution)/shard_map/ppermute | solution.py:235
  151.6 4.6 %collective-permute-start.23 = (bf16[2,128,512]{2,1,0:T(8,128)(2,1)S(1)}, bf16[2,128,512]{2,1,0:T(8,128)(2,1)S(1)}, u32[]{:S(2)}, u32[]{:S(2)}) collective-permute-start(bf16[2,128,512]{2,1,0:T(8,128)(2,1)S(1)} %add_convert_fusion.6), channel_id=1, source_target_pairs={{0,14},{2,0},{4,2},{6,4},{8,6},{10,8},{12,10},{14,12},{1,15},{3,1}... | collective-permute-start | bytes 786440 | tf_op jit(solution)/shard_map/ppermute | solution.py:235
  156.3 1.9 %collective-permute-start.27 = (bf16[2,128,512]{2,1,0:T(8,128)(2,1)S(1)}, bf16[2,128,512]{2,1,0:T(8,128)(2,1)S(1)}, u32[]{:S(2)}, u32[]{:S(2)}) collective-permute-start(bf16[2,128,512]{2,1,0:T(8,128)(2,1)S(1)} %add_convert_fusion.3), channel_id=1, source_target_pairs={{0,2},{2,4},{4,6},{6,8},{8,10},{10,12},{12,14},{14,0},{1,3},{3,5},... | collective-permute-start | bytes 786440 | tf_op jit(solution)/shard_map/ppermute | solution.py:235
  158.3 4.6 %collective-permute-start.30 = (bf16[2,128,512]{2,1,0:T(8,128)(2,1)S(1)}, bf16[2,128,512]{2,1,0:T(8,128)(2,1)S(1)}, u32[]{:S(2)}, u32[]{:S(2)}) collective-permute-start(bf16[2,128,512]{2,1,0:T(8,128)(2,1)S(1)} %add_convert_fusion.1), channel_id=1, source_target_pairs={{0,14},{2,0},{4,2},{6,4},{8,6},{10,8},{12,10},{14,12},{1,15},{3,1}... | collective-permute-start | bytes 786440 | tf_op jit(solution)/shard_map/ppermute | solution.py:235
  163.0 1.9 %collective-permute-start.20 = (bf16[2,128,512]{2,1,0:T(8,128)(2,1)S(1)}, bf16[2,128,512]{2,1,0:T(8,128)(2,1)S(1)}, u32[]{:S(2)}, u32[]{:S(2)}) collective-permute-start(bf16[2,128,512]{2,1,0:T(8,128)(2,1)S(1)} %add_convert_fusion.8), channel_id=1, source_target_pairs={{0,2},{2,4},{4,6},{6,8},{8,10},{10,12},{12,14},{14,0},{1,3},{3,5},... | collective-permute-start | bytes 786440 | tf_op jit(solution)/shard_map/ppermute | solution.py:235
  165.0 4.6 %collective-permute-start.24 = (bf16[2,128,512]{2,1,0:T(8,128)(2,1)S(1)}, bf16[2,128,512]{2,1,0:T(8,128)(2,1)S(1)}, u32[]{:S(2)}, u32[]{:S(2)}) collective-permute-start(bf16[2,128,512]{2,1,0:T(8,128)(2,1)S(1)} %add_convert_fusion.5), channel_id=1, source_target_pairs={{0,14},{2,0},{4,2},{6,4},{8,6},{10,8},{12,10},{14,12},{1,15},{3,1}... | collective-permute-start | bytes 786440 | tf_op jit(solution)/shard_map/ppermute | solution.py:235
  169.7 2.7 %collective-permute-start.31 = (bf16[2,128,512]{2,1,0:T(8,128)(2,1)S(1)}, bf16[2,128,512]{2,1,0:T(8,128)(2,1)S(1)}, u32[]{:S(2)}, u32[]{:S(2)}) collective-permute-start(bf16[2,128,512]{2,1,0:T(8,128)(2,1)S(1)} %add_convert_fusion), channel_id=1, source_target_pairs={{0,14},{2,0},{4,2},{6,4},{8,6},{10,8},{12,10},{14,12},{1,15},{3,1}... | collective-permute-start | bytes 786440 | tf_op jit(solution)/shard_map/ppermute | solution.py:235
  173.3 2.5 %collective-permute-start.21 = (bf16[2,128,512]{2,1,0:T(8,128)(2,1)}, bf16[2,128,512]{2,1,0:T(8,128)(2,1)}, u32[]{:S(2)}, u32[]{:S(2)}) collective-permute-start(bf16[2,128,512]{2,1,0:T(8,128)(2,1)} %add_convert_fusion.7), channel_id=1, source_target_pairs={{0,2},{2,4},{4,6},{6,8},{8,10},{10,12},{12,14},{14,0},{1,3},{3,5},... | collective-permute-start | bytes 786440 | tf_op jit(solution)/shard_map/ppermute | solution.py:235
  175.8 1.0 slice_bitcast_fusion.4
  176.9 2.2 %collective-permute-done.31 = bf16[2,128,512]{2,1,0:T(8,128)(2,1)S(1)} collective-permute-done((bf16[2,128,512]{2,1,0:T(8,128)(2,1)S(1)}, bf16[2,128,512]{2,1,0:T(8,128)(2,1)S(1)}, u32[]{:S(2)}, u32[]{:S(2)}) %collective-permute-start.31) | collective-permute-done | bytes 262176 | tf_op jit(solution)/shard_map/ppermute | solution.py:235
  179.0 2.9 %collective-permute-done.21 = bf16[2,128,512]{2,1,0:T(8,128)(2,1)} collective-permute-done((bf16[2,128,512]{2,1,0:T(8,128)(2,1)}, bf16[2,128,512]{2,1,0:T(8,128)(2,1)}, u32[]{:S(2)}, u32[]{:S(2)}) %collective-permute-start.21) | collective-permute-done | bytes 262176 | tf_op jit(solution)/shard_map/ppermute | solution.py:235
  181.9 1.2 fusion.5
  183.1 5.7 %collective-permute-start.32 = (bf16[2,128,512]{2,1,0:T(8,128)(2,1)S(1)}, bf16[2,128,512]{2,1,0:T(8,128)(2,1)S(1)}, u32[]{:S(2)}, u32[]{:S(2)}) collective-permute-start(bf16[2,128,512]{2,1,0:T(8,128)(2,1)S(1)} %get-tuple-element.43), channel_id=1, source_target_pairs={{0,1},{1,0},{2,3},{3,2},{4,5},{5,4},{6,7},{7,6},{8,9},{9,8},{10,11... | collective-permute-start | bytes 786440 | tf_op jit(solution)/shard_map/ppermute | solution.py:249
  (149 shorter events, 24.0 us)
Async XLA Ops:
  1.8 10.9 %collective-permute-start.2 = (bf16[2,128,512]{2,1,0:T(8,128)(2,1)S(1)}, bf16[2,128,512]{2,1,0:T(8,128)(2,1)S(1)}, u32[]{:S(2)}, u32[]{:S(2)}) collective-permute-start(bf16[2,128,512]{2,1,0:T(8,128)(2,1)S(1)} %pad_maximum_fusion.2), channel_id=1, source_target_pairs={{0,1},{1,0},{2,3},{3,2},{4,5},{5,4},{6,7},{7,6},{8,9},{9,8},{10,11... | collective-permute-start | bytes 786440 | tf_op jit(solution)/shard_map/ppermute | solution.py:198
  10.6 8.7 %copy-start.30 = (s32[2,8]{1,0:T(2,128)S(1)}, s32[2,8]{1,0:T(2,128)}, u32[]{:S(2)}) copy-start(s32[2,8]{1,0:T(2,128)} %refs_1_.1) | copy-start | bytes 196
  10.6 11.1 %copy-start.39 = (bf16[128,1024]{1,0:T(8,128)(2,1)S(1)}, bf16[128,1024]{1,0:T(8,128)(2,1)}, u32[]{:S(2)}) copy-start(bf16[128,1024]{1,0:T(8,128)(2,1)} %param.5) | copy-start | bytes 786436
  10.6 22.0 %copy-start.40 = (bf16[128,1024]{1,0:T(8,128)(2,1)S(1)}, bf16[128,1024]{1,0:T(8,128)(2,1)}, u32[]{:S(2)}) copy-start(bf16[128,1024]{1,0:T(8,128)(2,1)} %param.8) | copy-start | bytes 786436
  10.6 15.4 %collective-permute-start.6 = (bf16[2,128,512]{2,1,0:T(8,128)(2,1)S(1)}, bf16[2,128,512]{2,1,0:T(8,128)(2,1)S(1)}, u32[]{:S(2)}, u32[]{:S(2)}) collective-permute-start(bf16[2,128,512]{2,1,0:T(8,128)(2,1)S(1)} %pad_maximum_fusion.3.refs_6_), channel_id=1, source_target_pairs={{0,2},{2,4},{4,6},{6,8},{8,10},{10,12},{12,14},{14,0},{1,3},{3,5},... | collective-permute-start | bytes 786440 | tf_op jit(solution)/shard_map/ppermute | solution.py:211
  12.7 15.3 %collective-permute-start.10 = (bf16[2,128,512]{2,1,0:T(8,128)(2,1)S(1)}, bf16[2,128,512]{2,1,0:T(8,128)(2,1)S(1)}, u32[]{:S(2)}, u32[]{:S(2)}) collective-permute-start(bf16[2,128,512]{2,1,0:T(8,128)(2,1)S(1)} %collective-permute-done.2.refs_14_), channel_id=1, source_target_pairs={{0,14},{2,0},{4,2},{6,4},{8,6},{10,8},{12,10},{14,12},{1,15},{3,1}... | collective-permute-start | bytes 786440 | tf_op jit(solution)/shard_map/ppermute | solution.py:211
  17.3 16.0 %collective-permute-start.3 = (bf16[2,128,512]{2,1,0:T(8,128)(2,1)S(1)}, bf16[2,128,512]{2,1,0:T(8,128)(2,1)S(1)}, u32[]{:S(2)}, u32[]{:S(2)}) collective-permute-start(bf16[2,128,512]{2,1,0:T(8,128)(2,1)S(1)} %pad_maximum_fusion.3.refs_6_), channel_id=1, source_target_pairs={{0,14},{2,0},{4,2},{6,4},{8,6},{10,8},{12,10},{14,12},{1,15},{3,1}... | collective-permute-start | bytes 786440 | tf_op jit(solution)/shard_map/ppermute | solution.py:211
  19.2 29.5 %collective-permute-start = (s32[2,8]{1,0:T(2,128)S(1)}, s32[2,8]{1,0:T(2,128)S(1)}, u32[]{:S(2)}, u32[]{:S(2)}) collective-permute-start(s32[2,8]{1,0:T(2,128)S(1)} %copy-done.30), channel_id=1, source_target_pairs={{0,1},{1,0},{2,3},{3,2},{4,5},{5,4},{6,7},{7,6},{8,9},{9,8},{10,11... | collective-permute-start | bytes 200 | tf_op jit(solution)/shard_map/ppermute | solution.py:214
  22.4 19.1 %collective-permute-start.14 = (bf16[2,128,512]{2,1,0:T(8,128)(2,1)S(1)}, bf16[2,128,512]{2,1,0:T(8,128)(2,1)S(1)}, u32[]{:S(2)}, u32[]{:S(2)}) collective-permute-start(bf16[2,128,512]{2,1,0:T(8,128)(2,1)S(1)} %collective-permute-done.2.refs_14_), channel_id=1, source_target_pairs={{0,2},{2,4},{4,6},{6,8},{8,10},{10,12},{12,14},{14,0},{1,3},{3,5},... | collective-permute-start | bytes 786440 | tf_op jit(solution)/shard_map/ppermute | solution.py:211
  26.1 13.0 %collective-permute-start.7 = (bf16[2,128,512]{2,1,0:T(8,128)(2,1)S(1)}, bf16[2,128,512]{2,1,0:T(8,128)(2,1)S(1)}, u32[]{:S(2)}, u32[]{:S(2)}) collective-permute-start(bf16[2,128,512]{2,1,0:T(8,128)(2,1)S(1)} %collective-permute-done.6.refs_13_), channel_id=1, source_target_pairs={{0,2},{2,4},{4,6},{6,8},{8,10},{10,12},{12,14},{14,0},{1,3},{3,5},... | collective-permute-start | bytes 786440 | tf_op jit(solution)/shard_map/ppermute | solution.py:211
  28.0 15.6 %collective-permute-start.11 = (bf16[2,128,512]{2,1,0:T(8,128)(2,1)S(1)}, bf16[2,128,512]{2,1,0:T(8,128)(2,1)S(1)}, u32[]{:S(2)}, u32[]{:S(2)}) collective-permute-start(bf16[2,128,512]{2,1,0:T(8,128)(2,1)S(1)} %collective-permute-done.10.refs_15_), channel_id=1, source_target_pairs={{0,14},{2,0},{4,2},{6,4},{8,6},{10,8},{12,10},{14,12},{1,15},{3,1}... | collective-permute-start | bytes 786440 | tf_op jit(solution)/shard_map/ppermute | solution.py:211
  33.3 19.1 %collective-permute-start.4 = (bf16[2,128,512]{2,1,0:T(8,128)(2,1)S(1)}, bf16[2,128,512]{2,1,0:T(8,128)(2,1)S(1)}, u32[]{:S(2)}, u32[]{:S(2)}) collective-permute-start(bf16[2,128,512]{2,1,0:T(8,128)(2,1)S(1)} %collective-permute-done.3.refs_7_), channel_id=1, source_target_pairs={{0,14},{2,0},{4,2},{6,4},{8,6},{10,8},{12,10},{14,12},{1,15},{3,1}... | collective-permute-start | bytes 786440 | tf_op jit(solution)/shard_map/ppermute | solution.py:211
  39.0 16.2 %collective-permute-start.8 = (bf16[2,128,512]{2,1,0:T(8,128)(2,1)S(1)}, bf16[2,128,512]{2,1,0:T(8,128)(2,1)S(1)}, u32[]{:S(2)}, u32[]{:S(2)}) collective-permute-start(bf16[2,128,512]{2,1,0:T(8,128)(2,1)S(1)} %collective-permute-done.7.refs_12_), channel_id=1, source_target_pairs={{0,2},{2,4},{4,6},{6,8},{8,10},{10,12},{12,14},{14,0},{1,3},{3,5},... | collective-permute-start | bytes 786440 | tf_op jit(solution)/shard_map/ppermute | solution.py:211
  41.5 16.2 %collective-permute-start.15 = (bf16[2,128,512]{2,1,0:T(8,128)(2,1)S(1)}, bf16[2,128,512]{2,1,0:T(8,128)(2,1)S(1)}, u32[]{:S(2)}, u32[]{:S(2)}) collective-permute-start(bf16[2,128,512]{2,1,0:T(8,128)(2,1)S(1)} %collective-permute-done.14.refs_21_), channel_id=1, source_target_pairs={{0,2},{2,4},{4,6},{6,8},{8,10},{10,12},{12,14},{14,0},{1,3},{3,5},... | collective-permute-start | bytes 786440 | tf_op jit(solution)/shard_map/ppermute | solution.py:211
  43.6 16.7 %collective-permute-start.12 = (bf16[2,128,512]{2,1,0:T(8,128)(2,1)S(1)}, bf16[2,128,512]{2,1,0:T(8,128)(2,1)S(1)}, u32[]{:S(2)}, u32[]{:S(2)}) collective-permute-start(bf16[2,128,512]{2,1,0:T(8,128)(2,1)S(1)} %collective-permute-done.11.refs_16_), channel_id=1, source_target_pairs={{0,14},{2,0},{4,2},{6,4},{8,6},{10,8},{12,10},{14,12},{1,15},{3,1}... | collective-permute-start | bytes 786440 | tf_op jit(solution)/shard_map/ppermute | solution.py:211
  48.8 39.9 %collective-permute-start.1 = (bf16[2,128,512]{2,1,0:T(8,128)(2,1)}, bf16[2,128,512]{2,1,0:T(8,128)(2,1)}, u32[]{:S(2)}, u32[]{:S(2)}) collective-permute-start(bf16[2,128,512]{2,1,0:T(8,128)(2,1)} %pad_maximum_fusion.1), channel_id=1, source_target_pairs={{0,1},{1,0},{2,3},{3,2},{4,5},{5,4},{6,7},{7,6},{8,9},{9,8},{10,11... | collective-permute-start | bytes 786440 | tf_op jit(solution)/shard_map/ppermute | solution.py:213
  52.3 15.3 %copy-start.2 = (bf16[2,128,512]{2,1,0:T(8,128)(2,1)}, bf16[2,128,512]{2,1,0:T(8,128)(2,1)S(1)}, u32[]{:S(2)}) copy-start(bf16[2,128,512]{2,1,0:T(8,128)(2,1)S(1)} %collective-permute-done.4.refs_8_) | copy-start | bytes 786436
  52.4 36.4 %collective-permute-start.5 = (bf16[2,128,512]{2,1,0:T(8,128)(2,1)S(1)}, bf16[2,128,512]{2,1,0:T(8,128)(2,1)}, u32[]{:S(2)}, u32[]{:S(2)}) collective-permute-start(bf16[2,128,512]{2,1,0:T(8,128)(2,1)S(1)} %collective-permute-done.4.refs_8_), channel_id=1, source_target_pairs={{0,14},{2,0},{4,2},{6,4},{8,6},{10,8},{12,10},{14,12},{1,15},{3,1}... | collective-permute-start | bytes 786440 | tf_op jit(solution)/shard_map/ppermute | solution.py:211
  55.2 12.5 %copy-start.4 = (bf16[2,128,512]{2,1,0:T(8,128)(2,1)}, bf16[2,128,512]{2,1,0:T(8,128)(2,1)S(1)}, u32[]{:S(2)}) copy-start(bf16[2,128,512]{2,1,0:T(8,128)(2,1)S(1)} %collective-permute-done.8.refs_11_) | copy-start | bytes 786436
  55.2 33.5 %collective-permute-start.9 = (bf16[2,128,512]{2,1,0:T(8,128)(2,1)S(1)}, bf16[2,128,512]{2,1,0:T(8,128)(2,1)}, u32[]{:S(2)}, u32[]{:S(2)}) collective-permute-start(bf16[2,128,512]{2,1,0:T(8,128)(2,1)S(1)} %collective-permute-done.8.refs_11_), channel_id=1, source_target_pairs={{0,2},{2,4},{4,6},{6,8},{8,10},{10,12},{12,14},{14,0},{1,3},{3,5},... | collective-permute-start | bytes 786440 | tf_op jit(solution)/shard_map/ppermute | solution.py:211
  57.7 31.1 %collective-permute-start.16 = (bf16[2,128,512]{2,1,0:T(8,128)(2,1)S(1)}, bf16[2,128,512]{2,1,0:T(8,128)(2,1)}, u32[]{:S(2)}, u32[]{:S(2)}) collective-permute-start(bf16[2,128,512]{2,1,0:T(8,128)(2,1)S(1)} %collective-permute-done.15.refs_20_), channel_id=1, source_target_pairs={{0,2},{2,4},{4,6},{6,8},{8,10},{10,12},{12,14},{14,0},{1,3},{3,5},... | collective-permute-start | bytes 786440 | tf_op jit(solution)/shard_map/ppermute | solution.py:211
  60.3 28.4 %collective-permute-start.13 = (bf16[2,128,512]{2,1,0:T(8,128)(2,1)S(1)}, bf16[2,128,512]{2,1,0:T(8,128)(2,1)}, u32[]{:S(2)}, u32[]{:S(2)}) collective-permute-start(bf16[2,128,512]{2,1,0:T(8,128)(2,1)S(1)} %collective-permute-done.12.refs_17_), channel_id=1, source_target_pairs={{0,14},{2,0},{4,2},{6,4},{8,6},{10,8},{12,10},{14,12},{1,15},{3,1}... | collective-permute-start | bytes 786440 | tf_op jit(solution)/shard_map/ppermute | solution.py:211
  68.4 18.4 %all-to-all-start = ((bf16[32,2,1024]{2,1,0:T(2,128)(2,1)}), bf16[32,2,1024]{2,1,0:T(2,128)(2,1)S(1)}, u32[]{:S(2)}, u32[]{:S(2)}) async-start(bf16[32,2,1024]{2,1,0:T(2,128)(2,1)} %reshape.47), calls=%async_computation | async-start | bytes 262144 | tf_op jit(solution)/shard_map/all_to_all | solution.py:216
  118.2 13.7 %copy-start.34 = (bf16[2,128,512]{2,1,0:T(8,128)(2,1)S(1)}, bf16[2,128,512]{2,1,0:T(8,128)(2,1)}, u32[]{:S(2)}) copy-start(bf16[2,128,512]{2,1,0:T(8,128)(2,1)} %copy-done.33) | copy-start | bytes 786436
  118.9 17.6 %copy-start.32 = (bf16[2,128,512]{2,1,0:T(8,128)(2,1)S(1)}, bf16[2,128,512]{2,1,0:T(8,128)(2,1)}, u32[]{:S(2)}) copy-start(bf16[2,128,512]{2,1,0:T(8,128)(2,1)} %copy-done.31) | copy-start | bytes 786436
  118.9 22.9 %copy-start.29 = (bf16[2,128,512]{2,1,0:T(8,128)(2,1)S(1)}, bf16[2,128,512]{2,1,0:T(8,128)(2,1)}, u32[]{:S(2)}) copy-start(bf16[2,128,512]{2,1,0:T(8,128)(2,1)} %copy-done.28) | copy-start | bytes 786436
  119.6 22.2 %all-to-all-start.1 = ((bf16[32,2,1024]{2,1,0:T(2,128)(2,1)}), bf16[32,2,1024]{2,1,0:T(2,128)(2,1)S(1)}, u32[]{:S(2)}, u32[]{:S(2)}) async-start(bf16[32,2,1024]{2,1,0:T(2,128)(2,1)} %reshape.49), calls=%async_computation.1 | async-start | bytes 262144 | tf_op jit(solution)/shard_map/all_to_all | solution.py:240
  123.5 18.7 %collective-permute-start.25 = (bf16[2,128,512]{2,1,0:T(8,128)(2,1)}, bf16[2,128,512]{2,1,0:T(8,128)(2,1)S(1)}, u32[]{:S(2)}, u32[]{:S(2)}) collective-permute-start(bf16[2,128,512]{2,1,0:T(8,128)(2,1)} %copy-done.37), channel_id=1, source_target_pairs={{0,2},{2,4},{4,6},{6,8},{8,10},{10,12},{12,14},{14,0},{1,3},{3,5},... | collective-permute-start | bytes 786440 | tf_op jit(solution)/shard_map/ppermute | solution.py:235
  125.4 19.4 %collective-permute-start.28 = (bf16[2,128,512]{2,1,0:T(8,128)(2,1)}, bf16[2,128,512]{2,1,0:T(8,128)(2,1)S(1)}, u32[]{:S(2)}, u32[]{:S(2)}) collective-permute-start(bf16[2,128,512]{2,1,0:T(8,128)(2,1)} %copy-done.36), channel_id=1, source_target_pairs={{0,14},{2,0},{4,2},{6,4},{8,6},{10,8},{12,10},{14,12},{1,15},{3,1}... | collective-permute-start | bytes 786440 | tf_op jit(solution)/shard_map/ppermute | solution.py:235
  130.0 19.5 %collective-permute-start.18 = (bf16[2,128,512]{2,1,0:T(8,128)(2,1)}, bf16[2,128,512]{2,1,0:T(8,128)(2,1)S(1)}, u32[]{:S(2)}, u32[]{:S(2)}) collective-permute-start(bf16[2,128,512]{2,1,0:T(8,128)(2,1)} %copy-done.35), channel_id=1, source_target_pairs={{0,2},{2,4},{4,6},{6,8},{8,10},{10,12},{12,14},{14,0},{1,3},{3,5},... | collective-permute-start | bytes 786440 | tf_op jit(solution)/shard_map/ppermute | solution.py:235
  131.9 19.6 %collective-permute-start.22 = (bf16[2,128,512]{2,1,0:T(8,128)(2,1)S(1)}, bf16[2,128,512]{2,1,0:T(8,128)(2,1)S(1)}, u32[]{:S(2)}, u32[]{:S(2)}) collective-permute-start(bf16[2,128,512]{2,1,0:T(8,128)(2,1)S(1)} %copy-done.34), channel_id=1, source_target_pairs={{0,14},{2,0},{4,2},{6,4},{8,6},{10,8},{12,10},{14,12},{1,15},{3,1}... | collective-permute-start | bytes 786440 | tf_op jit(solution)/shard_map/ppermute | solution.py:235
  136.5 39.3 %collective-permute-start.17 = (bf16[2,128,512]{2,1,0:T(8,128)(2,1)S(1)}, bf16[2,128,512]{2,1,0:T(8,128)(2,1)}, u32[]{:S(2)}, u32[]{:S(2)}) collective-permute-start(bf16[2,128,512]{2,1,0:T(8,128)(2,1)S(1)} %copy-done.32), channel_id=1, source_target_pairs={{0,1},{1,0},{2,3},{3,2},{4,5},{5,4},{6,7},{7,6},{8,9},{9,8},{10,11... | collective-permute-start | bytes 786440 | tf_op jit(solution)/shard_map/ppermute | solution.py:242
  142.9 13.3 %collective-permute-start.26 = (bf16[2,128,512]{2,1,0:T(8,128)(2,1)S(1)}, bf16[2,128,512]{2,1,0:T(8,128)(2,1)S(1)}, u32[]{:S(2)}, u32[]{:S(2)}) collective-permute-start(bf16[2,128,512]{2,1,0:T(8,128)(2,1)S(1)} %add_convert_fusion.4), channel_id=1, source_target_pairs={{0,2},{2,4},{4,6},{6,8},{8,10},{10,12},{12,14},{14,0},{1,3},{3,5},... | collective-permute-start | bytes 786440 | tf_op jit(solution)/shard_map/ppermute | solution.py:235
  144.8 4.7 %copy-start.23 = (bf16[2,128,512]{2,1,0:T(8,128)(2,1)S(1)}, bf16[2,128,512]{2,1,0:T(8,128)(2,1)}, u32[]{:S(2)}) copy-start(bf16[2,128,512]{2,1,0:T(8,128)(2,1)} %copy-done.22) | copy-start | bytes 786436
  144.9 13.3 %collective-permute-start.29 = (bf16[2,128,512]{2,1,0:T(8,128)(2,1)S(1)}, bf16[2,128,512]{2,1,0:T(8,128)(2,1)S(1)}, u32[]{:S(2)}, u32[]{:S(2)}) collective-permute-start(bf16[2,128,512]{2,1,0:T(8,128)(2,1)S(1)} %add_convert_fusion.2), channel_id=1, source_target_pairs={{0,14},{2,0},{4,2},{6,4},{8,6},{10,8},{12,10},{14,12},{1,15},{3,1}... | collective-permute-start | bytes 786440 | tf_op jit(solution)/shard_map/ppermute | solution.py:235
  149.6 13.3 %collective-permute-start.19 = (bf16[2,128,512]{2,1,0:T(8,128)(2,1)S(1)}, bf16[2,128,512]{2,1,0:T(8,128)(2,1)S(1)}, u32[]{:S(2)}, u32[]{:S(2)}) collective-permute-start(bf16[2,128,512]{2,1,0:T(8,128)(2,1)S(1)} %add_convert_fusion.9), channel_id=1, source_target_pairs={{0,2},{2,4},{4,6},{6,8},{8,10},{10,12},{12,14},{14,0},{1,3},{3,5},... | collective-permute-start | bytes 786440 | tf_op jit(solution)/shard_map/ppermute | solution.py:235
  151.5 4.7 %copy-start.19 = (bf16[2,128,512]{2,1,0:T(8,128)(2,1)S(1)}, bf16[2,128,512]{2,1,0:T(8,128)(2,1)}, u32[]{:S(2)}) copy-start(bf16[2,128,512]{2,1,0:T(8,128)(2,1)} %copy-done.18) | copy-start | bytes 786436
  151.6 13.3 %collective-permute-start.23 = (bf16[2,128,512]{2,1,0:T(8,128)(2,1)S(1)}, bf16[2,128,512]{2,1,0:T(8,128)(2,1)S(1)}, u32[]{:S(2)}, u32[]{:S(2)}) collective-permute-start(bf16[2,128,512]{2,1,0:T(8,128)(2,1)S(1)} %add_convert_fusion.6), channel_id=1, source_target_pairs={{0,14},{2,0},{4,2},{6,4},{8,6},{10,8},{12,10},{14,12},{1,15},{3,1}... | collective-permute-start | bytes 786440 | tf_op jit(solution)/shard_map/ppermute | solution.py:235
  156.3 20.5 %collective-permute-start.27 = (bf16[2,128,512]{2,1,0:T(8,128)(2,1)S(1)}, bf16[2,128,512]{2,1,0:T(8,128)(2,1)S(1)}, u32[]{:S(2)}, u32[]{:S(2)}) collective-permute-start(bf16[2,128,512]{2,1,0:T(8,128)(2,1)S(1)} %add_convert_fusion.3), channel_id=1, source_target_pairs={{0,2},{2,4},{4,6},{6,8},{8,10},{10,12},{12,14},{14,0},{1,3},{3,5},... | collective-permute-start | bytes 786440 | tf_op jit(solution)/shard_map/ppermute | solution.py:235
  158.2 4.7 %copy-start.15 = (bf16[2,128,512]{2,1,0:T(8,128)(2,1)S(1)}, bf16[2,128,512]{2,1,0:T(8,128)(2,1)}, u32[]{:S(2)}) copy-start(bf16[2,128,512]{2,1,0:T(8,128)(2,1)} %copy-done.14) | copy-start | bytes 786436
  158.3 11.3 %collective-permute-start.30 = (bf16[2,128,512]{2,1,0:T(8,128)(2,1)S(1)}, bf16[2,128,512]{2,1,0:T(8,128)(2,1)S(1)}, u32[]{:S(2)}, u32[]{:S(2)}) collective-permute-start(bf16[2,128,512]{2,1,0:T(8,128)(2,1)S(1)} %add_convert_fusion.1), channel_id=1, source_target_pairs={{0,14},{2,0},{4,2},{6,4},{8,6},{10,8},{12,10},{14,12},{1,15},{3,1}... | collective-permute-start | bytes 786440 | tf_op jit(solution)/shard_map/ppermute | solution.py:235
  163.0 9.5 %collective-permute-start.20 = (bf16[2,128,512]{2,1,0:T(8,128)(2,1)S(1)}, bf16[2,128,512]{2,1,0:T(8,128)(2,1)S(1)}, u32[]{:S(2)}, u32[]{:S(2)}) collective-permute-start(bf16[2,128,512]{2,1,0:T(8,128)(2,1)S(1)} %add_convert_fusion.8), channel_id=1, source_target_pairs={{0,2},{2,4},{4,6},{6,8},{8,10},{10,12},{12,14},{14,0},{1,3},{3,5},... | collective-permute-start | bytes 786440 | tf_op jit(solution)/shard_map/ppermute | solution.py:235
  165.0 4.7 %copy-start.7 = (bf16[2,128,512]{2,1,0:T(8,128)(2,1)S(1)}, bf16[2,128,512]{2,1,0:T(8,128)(2,1)}, u32[]{:S(2)}) copy-start(bf16[2,128,512]{2,1,0:T(8,128)(2,1)} %copy-done.6) | copy-start | bytes 786436
  165.0 11.8 %collective-permute-start.24 = (bf16[2,128,512]{2,1,0:T(8,128)(2,1)S(1)}, bf16[2,128,512]{2,1,0:T(8,128)(2,1)S(1)}, u32[]{:S(2)}, u32[]{:S(2)}) collective-permute-start(bf16[2,128,512]{2,1,0:T(8,128)(2,1)S(1)} %add_convert_fusion.5), channel_id=1, source_target_pairs={{0,14},{2,0},{4,2},{6,4},{8,6},{10,8},{12,10},{14,12},{1,15},{3,1}... | collective-permute-start | bytes 786440 | tf_op jit(solution)/shard_map/ppermute | solution.py:235
  169.6 2.8 %copy-start.1 = (bf16[2,128,512]{2,1,0:T(8,128)(2,1)S(1)}, bf16[2,128,512]{2,1,0:T(8,128)(2,1)}, u32[]{:S(2)}) copy-start(bf16[2,128,512]{2,1,0:T(8,128)(2,1)} %copy-done) | copy-start | bytes 786436
  169.7 9.3 %collective-permute-start.31 = (bf16[2,128,512]{2,1,0:T(8,128)(2,1)S(1)}, bf16[2,128,512]{2,1,0:T(8,128)(2,1)S(1)}, u32[]{:S(2)}, u32[]{:S(2)}) collective-permute-start(bf16[2,128,512]{2,1,0:T(8,128)(2,1)S(1)} %add_convert_fusion), channel_id=1, source_target_pairs={{0,14},{2,0},{4,2},{6,4},{8,6},{10,8},{12,10},{14,12},{1,15},{3,1}... | collective-permute-start | bytes 786440 | tf_op jit(solution)/shard_map/ppermute | solution.py:235
  173.3 8.6 %collective-permute-start.21 = (bf16[2,128,512]{2,1,0:T(8,128)(2,1)}, bf16[2,128,512]{2,1,0:T(8,128)(2,1)}, u32[]{:S(2)}, u32[]{:S(2)}) collective-permute-start(bf16[2,128,512]{2,1,0:T(8,128)(2,1)} %add_convert_fusion.7), channel_id=1, source_target_pairs={{0,2},{2,4},{4,6},{6,8},{8,10},{10,12},{12,14},{14,0},{1,3},{3,5},... | collective-permute-start | bytes 786440 | tf_op jit(solution)/shard_map/ppermute | solution.py:235
  183.1 6.8 %collective-permute-start.32 = (bf16[2,128,512]{2,1,0:T(8,128)(2,1)S(1)}, bf16[2,128,512]{2,1,0:T(8,128)(2,1)S(1)}, u32[]{:S(2)}, u32[]{:S(2)}) collective-permute-start(bf16[2,128,512]{2,1,0:T(8,128)(2,1)S(1)} %get-tuple-element.43), channel_id=1, source_target_pairs={{0,1},{1,0},{2,3},{3,2},{4,5},{5,4},{6,7},{7,6},{8,9},{9,8},{10,11... | collective-permute-start | bytes 786440 | tf_op jit(solution)/shard_map/ppermute | solution.py:249
  (28 other events, 26.7 us)

commit v2 on v1

--- a/solution.py
+++ b/solution.py
@@ -19,6 +19,8 @@
 HALF = 512
 HEADS = HALF // HEAD_DIM
 NEAR = 256
+GROWS = 4 * HEADS
+SEND_ORDER = [11, 12, 5, 4, 14, 13, 2, 3, 9, 10, 7, 6, 15, 1, 8, 0]
 FKEYS = FAR * BLOCK
 SCALE = 1.0 / math.sqrt(HEAD_DIM)
 EXP_SCALE = SCALE * math.log2(math.e)
@@ -41,19 +43,28 @@
 def attend_kernel(*refs):
     pos, far_own, far_peer, qdo_own, qdo_peer, glob = refs[:6]
     sources = refs[6:22]
-    res_own, res_peer, base, gglob = refs[22:26]
+    outputs = refs[22:26]
     parts = refs[26:40]
-    slots, near, fgrad, table = refs[40:]
-    my_y, my_c, my_w = pos[0], pos[1], pos[2]
+    slots, near, fgrad, gwide, res_own, res_peer, base, gglob, spare, table, in_sem, out_sem = refs[40:]
+    my_y, my_c, my_w, my_sign = pos[0], pos[1], pos[2], pos[3]
     for who, far in enumerate((far_own, far_peer)):
         for row in range(BLK):
             for entry in range(FAR):
                 block = far[row, entry]
                 group = lax.shift_right_logical(block, 6)
-                offset = lax.bitwise_and(lax.shift_right_logical(group, 1) - my_y, NY - 1)
+                offset = lax.bitwise_and(
+                    (lax.shift_right_logical(group, 1) - my_y) * my_sign, NY - 1
+                )
                 chain = lax.bitwise_xor(lax.bitwise_and(group, 1), my_c)
                 inner = lax.bitwise_and(block, 1)
                 table[who, chain * NY + offset] = (row * FAR + entry) * 2 + inner
+    copies = []
+    for who in range(2):
+        copies.append(
+            pltpu.make_async_copy(
+                sources[who * NY], near.at[:, who, :TOK, :], in_sem.at[len(copies)]
+            )
+        )
     for source in range(2 * NY):
         for who in range(2):
             code = table[who, source]
@@ -61,16 +72,28 @@
             inner = lax.bitwise_and(code, 1)
             at = pl.ds(pl.multiple_of(slot * BLOCK, BLOCK), BLOCK)
             rows = pl.ds(pl.multiple_of(inner * BLOCK, BLOCK), BLOCK)
-            for kind in range(2):
-                slots[kind, who, at, :] = sources[source][kind, rows, :]
+            copies.append(
+                pltpu.make_async_copy(
+                    sources[source].at[:, rows, :],
+                    slots.at[:, who, at, :],
+                    in_sem.at[len(copies)],
+                )
+            )
+    for copy in copies:
+        copy.start()
+    gwide[...] = glob[...].astype(F32).reshape(WINDOWS * GROWS, HEAD_DIM)
     for who in range(2):
         for kind in range(2):
-            near[kind, who, :TOK, :] = sources[who * NY][kind]
-            first = (who * 2 + kind) * HALF
-            near[kind, who, TOK : TOK + WINDOWS, :] = glob[:, first : first + HALF]
+            for head in range(HEADS):
+                first = (who * 2 + kind) * HEADS + head
+                near[kind, who, TOK : TOK + WINDOWS, head * HEAD_DIM : (head + 1) * HEAD_DIM] = (
+                    gwide[pl.ds(first, WINDOWS, stride=GROWS), :].astype(BF16)
+                )
             near[kind, who, TOK + WINDOWS :, :] = jnp.zeros((NEAR - TOK - WINDOWS, HALF), BF16)
     column = lax.broadcasted_iota(jnp.int32, (TOK, NEAR), 1)
     hidden = (column >= TOK + WINDOWS) | (column == TOK + my_w)
+    for copy in copies:
+        copy.wait()
 
     def head_step(head, carry):
         lanes = pl.ds(pl.multiple_of(head * HEAD_DIM, HEAD_DIM), HEAD_DIM)
@@ -120,14 +143,23 @@
             near_vgrad = dot_tn(jnp.concatenate(near_half, axis=0), grad)
             for kind, value in enumerate((near_kgrad, near_vgrad)):
                 base[who, kind, :, lanes] = value[:TOK]
-                first = (who * 2 + kind) * HALF
-                cols = pl.ds(pl.multiple_of(first + head * HEAD_DIM, HEAD_DIM), HEAD_DIM)
-                gglob[:, cols] = value[TOK : TOK + WINDOWS].astype(BF16)
+                first = (who * 2 + kind) * HEADS + head
+                gwide[pl.ds(first, WINDOWS, stride=GROWS), :] = value[TOK : TOK + WINDOWS]
         return carry
 
     lax.fori_loop(0, HEADS, head_step, 0)
-
-    for source in range(2 * NY):
+    gglob[...] = gwide[...].reshape(WINDOWS, GROWS, HEAD_DIM).astype(BF16)
+    copies = []
+
+    def send(value, output):
+        copy = pltpu.make_async_copy(value, output, out_sem.at[len(copies)])
+        copy.start()
+        copies.append(copy)
+
+    send(gglob, outputs[3])
+    send(res_peer, outputs[1])
+    send(res_own, outputs[0])
+    for source in SEND_ORDER:
         for kind in range(2):
             for inner in range(BLK):
                 rows = slice(inner * BLOCK, (inner + 1) * BLOCK)
@@ -142,13 +174,19 @@
                 if source % NY == 0:
                     base[source // NY, kind, rows, :] += value
                 else:
-                    index = source - 1 - source // NY
-                    parts[index][kind, rows, :] = value.astype(BF16)
+                    spare[source - 1 - source // NY, kind, rows, :] = value.astype(BF16)
+        if source % NY:
+            index = source - 1 - source // NY
+            send(spare.at[index], parts[index])
+    send(base, outputs[2])
+    for copy in copies:
+        copy.wait()
 
 
 def attend(pos, far_own, far_peer, qdo_own, qdo_peer, glob, sources):
     smem = pl.BlockSpec(memory_space=pltpu.SMEM)
     vmem = pl.BlockSpec(memory_space=pltpu.VMEM)
+    anywhere = pl.BlockSpec(memory_space=pl.ANY)
     piece = jax.ShapeDtypeStruct((2, TOK, HALF), BF16)
     return pl.pallas_call(
         attend_kernel,
@@ -156,27 +194,39 @@
             piece,
             piece,
             jax.ShapeDtypeStruct((2, 2, TOK, HALF), F32),
-            jax.ShapeDtypeStruct((WINDOWS, 4 * HALF), BF16),
+            jax.ShapeDtypeStruct((WINDOWS, GROWS, HEAD_DIM), BF16),
         ]
         + [piece] * 14,
-        in_specs=[smem] * 3 + [vmem] * 19,
-        out_specs=[vmem] * 18,
+        in_specs=[smem] * 3 + [vmem] * 3 + [anywhere] * 16,
+        out_specs=[anywhere] * 18,
         scratch_shapes=[
             pltpu.VMEM((2, 2, BLK * FKEYS, HALF), BF16),
             pltpu.VMEM((2, 2, NEAR, HALF), BF16),
             pltpu.VMEM((2, 2, BLK * FKEYS, HALF), BF16),
+            pltpu.VMEM((WINDOWS * GROWS, HEAD_DIM), F32),
+            pltpu.VMEM((2, TOK, HALF), BF16),
+            pltpu.VMEM((2, TOK, HALF), BF16),
+            pltpu.VMEM((2, 2, TOK, HALF), F32),
+            pltpu.VMEM((WINDOWS, GROWS, HEAD_DIM), BF16),
+            pltpu.VMEM((2 * NY - 2, 2, TOK, HALF), BF16),
             pltpu.SMEM((2, 2 * NY), jnp.int32),
+            pltpu.SemaphoreType.DMA((2 + 4 * NY,)),
+            pltpu.SemaphoreType.DMA((2 + 2 * NY,)),
         ],
-        compiler_params=pltpu.CompilerParams(vmem_limit_bytes=44 * 1024 * 1024),
+        compiler_params=pltpu.CompilerParams(vmem_limit_bytes=60 * 1024 * 1024),
         cost_estimate=pl.CostEstimate(
             flops=1_200_000_000, bytes_accessed=12_000_000, transcendentals=800_000
         ),
     )(pos, far_own, far_peer, qdo_own, qdo_peer, glob, *sources)
 
 
-UP = [(i, (i + 1) % NY) for i in range(NY)]
-DOWN = [(i, (i - 1) % NY) for i in range(NY)]
+EVEN = [(i, i ^ 1) for i in range(NY)]
+ODD = [(i, (((i + 1) ^ 1) - 1) % NY) for i in range(NY)]
 SWAP = [(0, 1), (1, 0)]
+
+
+def plus(a, b):
+    return (a.astype(F32) + b.astype(F32)).astype(BF16)
 
 
 def per_device(query_rows, key_rows, value_rows, out_grad, far_blocks):
@@ -184,8 +234,8 @@
     my_c = lax.axis_index("c")
     my_w = lax.axis_index("x") * NZ + lax.axis_index("z")
     swap = functools.partial(lax.ppermute, axis_name="c", perm=SWAP)
-    up = functools.partial(lax.ppermute, axis_name="y", perm=UP)
-    down = functools.partial(lax.ppermute, axis_name="y", perm=DOWN)
+    even = functools.partial(lax.ppermute, axis_name="y", perm=EVEN)
+    odd = functools.partial(lax.ppermute, axis_name="y", perm=ODD)
     low = my_c == 0
 
     def split(first, second):
@@ -195,59 +245,46 @@
 
     kv_own, kv_send = split(key_rows, value_rows)
     qdo_own, qdo_send = split(query_rows, out_grad)
-    kv_peer = swap(kv_send)
-    sources = [None] * 16
-    sources[0], sources[NY] = kv_own, kv_peer
-    chains = [
-        (0, up, 4, -1),
-        (0, down, 3, 1),
-        (NY, up, 3, -1),
-        (NY, down, 4, 1),
-    ]
-    held = [kv_own, kv_own, kv_peer, kv_peer]
-    for step in range(1, 5):
-        for i, (first, move, count, sign) in enumerate(chains):
-            if step <= count:
-                held[i] = move(held[i])
-                sources[first + (sign * step) % NY] = held[i]
+    a, b = {0: kv_own}, {0: swap(kv_send)}
+    row = jnp.concatenate([a[0][:, 0], b[0][:, 0]]).reshape(GROWS, HEAD_DIM)
+    glob = lax.all_to_all(
+        jnp.broadcast_to(row, (WINDOWS, GROWS, HEAD_DIM)), ("x", "z"), 0, 0, tiled=True
+    )
+    a[1], b[-1] = even(a[0]), odd(b[0])
+    a[-1], b[1] = odd(a[0]), even(b[0])
+    a[-2], b[2] = odd(a[1]), even(b[-1])
+    a[2], b[-2] = even(a[-1]), odd(b[1])
+    a[3], b[-3] = even(a[-2]), odd(b[2])
     qdo_peer = swap(qdo_send)
     far_peer = swap(far_blocks)
-    row = jnp.concatenate([kv_own[0, 0], kv_own[1, 0], kv_peer[0, 0], kv_peer[1, 0]])
-    glob = lax.all_to_all(
-        jnp.broadcast_to(row, (WINDOWS, 4 * HALF)), ("x", "z"), 0, 0, tiled=True
-    )
-    pos = jnp.stack([my_y, my_c, my_w]).astype(jnp.int32)
+    glob, a[2], a[3], b[-2], b[-3] = lax.optimization_barrier((glob, a[2], a[3], b[-2], b[-3]))
+    a[-3], b[3] = odd(a[2]), even(b[-2])
+    a[-4], b[4] = odd(a[3]), even(b[-3])
+    sources = [x[r] if r in x else x[r - NY] for x in (a, b) for r in range(NY)]
+    pos = jnp.stack([my_y, my_c, my_w, 1 - 2 * (my_y % 2)]).astype(jnp.int32)
     res_own, res_peer, base, gglob, *parts = attend(
         pos, far_blocks, far_peer, qdo_own, qdo_peer, glob, sources
     )
-    part = parts[:7], parts[7:]
-
-    held = [
-        part[0][4 - 1],
-        part[0][5 - 1],
-        part[1][3 - 1],
-        part[1][4 - 1],
-    ]
-    at = [4, 5, 3, 4]
-    for step in range(1, 5):
-        for i, (first, move, count, sign) in enumerate(chains):
-            if step <= count:
-                held[i] = move(held[i])
-                at[i] = (at[i] + sign) % NY
-                if at[i]:
-                    mine = part[first // NY][at[i] - 1]
-                    held[i] = (held[i].astype(F32) + mine.astype(F32)).astype(BF16)
+    a = {r: parts[r % NY - 1] for r in range(-4, 4) if r}
+    b = {r: parts[NY - 2 + r % NY] for r in range(-3, 5) if r}
     gback = lax.all_to_all(gglob, ("x", "z"), 0, 0, tiled=True)
+    b[-2], a[2] = plus(b[-2], even(b[3])), plus(a[2], odd(a[-3]))
+    b[-3], a[3] = plus(b[-3], even(b[4])), plus(a[3], odd(a[-4]))
+    b[1], a[-1] = plus(b[1], odd(b[-2])), plus(a[-1], even(a[2]))
+    b[2], a[-2] = plus(b[2], odd(b[-3])), plus(a[-2], even(a[3]))
+    b[-1], a[1] = plus(b[-1], even(b[2])), plus(a[1], odd(a[-2]))
+    far_own = odd(a[-1]), even(a[1])
+    far_peer = even(b[1]), odd(b[-1])
     gsum = jnp.sum(gback.astype(F32), axis=0).reshape(2, 2, 1, HALF)
     res_back = swap(res_peer)
     first_row = lax.broadcasted_iota(jnp.int32, (1, TOK, 1), 1) == 0
 
-    def finish(who):
-        total = base[who] + held[2 * who].astype(F32) + held[2 * who + 1].astype(F32)
+    def finish(who, far):
+        total = base[who] + far[0].astype(F32) + far[1].astype(F32)
         return (total + jnp.where(first_row, gsum[who], 0.0)).astype(BF16)
 
-    peer_grad = swap(finish(1))
-    own_grad = finish(0)
+    peer_grad = swap(finish(1, far_peer))
+    own_grad = finish(0, far_own)
 
     def join(mine, other):
         return jnp.where(

time: 192 us -> 179 us (0.932)
  local copies, waits for them, and re-layouts: 21.3 us -> 3.49 us
  other arithmetic: 11 us -> 6.11 us
  waiting for transfers between devices: 17.2 us -> 21.6 us
  Pallas kernels: 15.4 us -> 18.6 us
  starting transfers between devices: 124 us -> 126 us
    unnamed x87 -> x72, local copies, waits for them, and re-layouts: 19.5 us -> 1.74 us
    ppermute x30, waiting for transfers between devices: 9.13 us -> 21.6 us  [the longest x2 5.36 us: per_device(): b[2], a[-2] = (plus(b[2], odd(b[-3])), plus(a[-2], even(a[3])))]
    all_to_all x1, waiting for transfers between devices: 8.07 us -> 0.01 us  [per_device(): lax.all_to_all(jnp.broadcast_to(row, (WINDOWS, GROWS, HEAD_DIM)), ('x', '...]
    ppermute x30, starting transfers between devices: 100 us -> 92.4 us  [the longest x1 8.79 us: per_device(): a, b = ({0: kv_own}, {0: swap(kv_send)})]
    all_to_all x1, starting transfers between devices: 3.84 us -> 9.7 us  [per_device(): gback = lax.all_to_all(gglob, ('x', 'z'), 0, 0, tiled=True)]
    pallas_call x1, Pallas kernels: 15.4 us -> 18.6 us  [attend(): pl.pallas_call(attend_kernel, out_shape=[piece, piece, jax.ShapeDtypeStru...]
    ppermute x1, starting transfers between devices: 5.29 us -> 7.22 us  [per_device(): res_back = swap(res_peer)]
    another operation x8 -> x9, other arithmetic: 4.18 us -> 2.62 us  [split(): return (jnp.stack(mine), jnp.stack(other))]
  transfers between devices with their start and end apart: 35 -> 35, of which waited for: 5 -> 10; matrix products, arithmetic and copies ran while one was open for 6% -> 3% of each run, Pallas kernels for 0% -> 0%
where the time goes in v2:
time: 179 us; the launch traced here: 178 us
  starting transfers between devices  126 us (70%)
  waiting for transfers between devices  21.6 us (12%)
  Pallas kernels  18.6 us (10%)
  other arithmetic  6.11 us (3%)
  local copies, waits for them, and re-layouts  3.49 us (2%)
    pallas_call x1, Pallas kernels, attend(): pl.pallas_call(attend_kernel, out_shape=[piece, piece, jax.ShapeDtypeStru...  18.6 us
    all_to_all x1, starting transfers between devices, per_device(): lax.all_to_all(jnp.broadcast_to(row, (WINDOWS, GROWS, HEAD_DIM)), ('x', '...  10.3 us
    all_to_all x1, starting transfers between devices, per_device(): gback = lax.all_to_all(gglob, ('x', 'z'), 0, 0, tiled=True)  9.7 us
    ppermute x1, starting transfers between devices, per_device(): a, b = ({0: kv_own}, {0: swap(kv_send)})  8.79 us
    ppermute x2, starting transfers between devices, per_device(): a[2], b[-2] = (even(a[-1]), odd(b[1]))  7.78 us
    ppermute x2, starting transfers between devices, per_device(): a[-4], b[4] = (odd(a[3]), even(b[-3]))  7.27 us
    ppermute x1, starting transfers between devices, per_device(): res_back = swap(res_peer)  7.22 us
    ppermute x2, starting transfers between devices, per_device(): b[-2], a[2] = (plus(b[-2], even(b[3])), plus(a[2], odd(a[-3])))  7.1 us
  transfers between devices with their start and end apart: 35, of which 10 were waited for; matrix products, arithmetic and copies ran while one was open for 3% of the time, Pallas kernels for 0%

profile of v2, /device:TPU:1, one launch (start us, length us, event | category | flops | bytes accessed | tf_op | source)
XLA Modules:
  0.0 177.7 jit_solution(11331878240497386581)
XLA Ops:
  0.6 1.0 select_bitcast_fusion.2
  1.8 8.8 %collective-permute-start.2 = (bf16[2,128,512]{2,1,0:T(8,128)(2,1)S(1)}, bf16[2,128,512]{2,1,0:T(8,128)(2,1)S(1)}, u32[]{:S(2)}, u32[]{:S(2)}) collective-permute-start(bf16[2,128,512]{2,1,0:T(8,128)(2,1)S(1)} %pad_maximum_fusion.3), channel_id=1, source_target_pairs={{0,1},{1,0},{2,3},{3,2},{4,5},{5,4},{6,7},{7,6},{8,9},{9,8},{10,11... | collective-permute-start | bytes 786440 | tf_op jit(solution)/shard_map/ppermute | solution.py:248
  10.6 2.1 %collective-permute-start.5 = (bf16[2,128,512]{2,1,0:T(8,128)(2,1)S(1)}, bf16[2,128,512]{2,1,0:T(8,128)(2,1)S(1)}, u32[]{:S(2)}, u32[]{:S(2)}) collective-permute-start(bf16[2,128,512]{2,1,0:T(8,128)(2,1)S(1)} %pad_maximum_fusion.refs_6_), channel_id=1, source_target_pairs={{0,2},{2,0},{4,6},{6,4},{8,10},{10,8},{12,14},{14,12},{1,3},{3,1},... | collective-permute-start | bytes 786440 | tf_op jit(solution)/shard_map/ppermute | solution.py:253
  12.7 1.9 %collective-permute-start.10 = (bf16[2,128,512]{2,1,0:T(8,128)(2,1)S(1)}, bf16[2,128,512]{2,1,0:T(8,128)(2,1)S(1)}, u32[]{:S(2)}, u32[]{:S(2)}) collective-permute-start(bf16[2,128,512]{2,1,0:T(8,128)(2,1)S(1)} %collective-permute-done.2.refs_14_), channel_id=1, source_target_pairs={{0,14},{2,4},{4,2},{6,8},{8,6},{10,12},{12,10},{14,0},{1,15},{3,5}... | collective-permute-start | bytes 786440 | tf_op jit(solution)/shard_map/ppermute | solution.py:253
  14.6 4.6 %collective-permute-start.3 = (bf16[2,128,512]{2,1,0:T(8,128)(2,1)S(1)}, bf16[2,128,512]{2,1,0:T(8,128)(2,1)S(1)}, u32[]{:S(2)}, u32[]{:S(2)}) collective-permute-start(bf16[2,128,512]{2,1,0:T(8,128)(2,1)S(1)} %pad_maximum_fusion.refs_6_), channel_id=1, source_target_pairs={{0,14},{2,4},{4,2},{6,8},{8,6},{10,12},{12,10},{14,0},{1,15},{3,5}... | collective-permute-start | bytes 786440 | tf_op jit(solution)/shard_map/ppermute | solution.py:254
  19.2 2.2 %collective-permute-start.8 = (bf16[2,128,512]{2,1,0:T(8,128)(2,1)S(1)}, bf16[2,128,512]{2,1,0:T(8,128)(2,1)S(1)}, u32[]{:S(2)}, u32[]{:S(2)}) collective-permute-start(bf16[2,128,512]{2,1,0:T(8,128)(2,1)S(1)} %collective-permute-done.2.refs_14_), channel_id=1, source_target_pairs={{0,2},{2,0},{4,6},{6,4},{8,10},{10,8},{12,14},{14,12},{1,3},{3,1},... | collective-permute-start | bytes 786440 | tf_op jit(solution)/shard_map/ppermute | solution.py:254
  21.4 1.9 %collective-permute-start.6 = (bf16[2,128,512]{2,1,0:T(8,128)(2,1)S(1)}, bf16[2,128,512]{2,1,0:T(8,128)(2,1)S(1)}, u32[]{:S(2)}, u32[]{:S(2)}) collective-permute-start(bf16[2,128,512]{2,1,0:T(8,128)(2,1)S(1)} %collective-permute-done.5.refs_7_), channel_id=1, source_target_pairs={{0,14},{2,4},{4,2},{6,8},{8,6},{10,12},{12,10},{14,0},{1,15},{3,5}... | collective-permute-start | bytes 786440 | tf_op jit(solution)/shard_map/ppermute | solution.py:255
  23.7 2.8 %collective-permute-start.11 = (bf16[2,128,512]{2,1,0:T(8,128)(2,1)S(1)}, bf16[2,128,512]{2,1,0:T(8,128)(2,1)S(1)}, u32[]{:S(2)}, u32[]{:S(2)}) collective-permute-start(bf16[2,128,512]{2,1,0:T(8,128)(2,1)S(1)} %collective-permute-done.10.refs_21_), channel_id=1, source_target_pairs={{0,2},{2,0},{4,6},{6,4},{8,10},{10,8},{12,14},{14,12},{1,3},{3,1},... | collective-permute-start | bytes 786440 | tf_op jit(solution)/shard_map/ppermute | solution.py:255
  27.3 10.3 %all-to-all-start = ((bf16[32,16,128]{2,1,0:T(8,128)(2,1)}), bf16[32,16,128]{2,1,0:T(8,128)(2,1)S(1)}, u32[]{:S(2)}, u32[]{:S(2)}) async-start(bf16[32,16,128]{2,1,0:T(8,128)(2,1)} %broadcast_in_dim.38), calls=%async_computation | async-start | bytes 262144 | tf_op jit(solution)/shard_map/all_to_all | solution.py:250
  37.7 3.4 %collective-permute-start.4 = (bf16[2,128,512]{2,1,0:T(8,128)(2,1)S(1)}, bf16[2,128,512]{2,1,0:T(8,128)(2,1)S(1)}, u32[]{:S(2)}, u32[]{:S(2)}) collective-permute-start(bf16[2,128,512]{2,1,0:T(8,128)(2,1)S(1)} %collective-permute-done.3.refs_13_), channel_id=1, source_target_pairs={{0,2},{2,0},{4,6},{6,4},{8,10},{10,8},{12,14},{14,12},{1,3},{3,1},... | collective-permute-start | bytes 786440 | tf_op jit(solution)/shard_map/ppermute | solution.py:256
  41.1 1.9 %collective-permute-start.7 = (bf16[2,128,512]{2,1,0:T(8,128)(2,1)S(1)}, bf16[2,128,512]{2,1,0:T(8,128)(2,1)S(1)}, u32[]{:S(2)}, u32[]{:S(2)}) collective-permute-start(bf16[2,128,512]{2,1,0:T(8,128)(2,1)S(1)} %collective-permute-done.6.refs_12_), channel_id=1, source_target_pairs={{0,2},{2,0},{4,6},{6,4},{8,10},{10,8},{12,14},{14,12},{1,3},{3,1},... | collective-permute-start | bytes 786440 | tf_op jit(solution)/shard_map/ppermute | solution.py:257
  43.0 4.4 %collective-permute-start.9 = (bf16[2,128,512]{2,1,0:T(8,128)(2,1)S(1)}, bf16[2,128,512]{2,1,0:T(8,128)(2,1)S(1)}, u32[]{:S(2)}, u32[]{:S(2)}) collective-permute-start(bf16[2,128,512]{2,1,0:T(8,128)(2,1)S(1)} %collective-permute-done.8.refs_15_), channel_id=1, source_target_pairs={{0,14},{2,4},{4,2},{6,8},{8,6},{10,12},{12,10},{14,0},{1,15},{3,5}... | collective-permute-start | bytes 786440 | tf_op jit(solution)/shard_map/ppermute | solution.py:256
  47.4 2.1 %collective-permute-start.12 = (bf16[2,128,512]{2,1,0:T(8,128)(2,1)S(1)}, bf16[2,128,512]{2,1,0:T(8,128)(2,1)S(1)}, u32[]{:S(2)}, u32[]{:S(2)}) collective-permute-start(bf16[2,128,512]{2,1,0:T(8,128)(2,1)S(1)} %collective-permute-done.11.refs_16_), channel_id=1, source_target_pairs={{0,14},{2,4},{4,2},{6,8},{8,6},{10,12},{12,10},{14,0},{1,15},{3,5}... | collective-permute-start | bytes 786440 | tf_op jit(solution)/shard_map/ppermute | solution.py:257
  50.3 4.8 %collective-permute-start.1 = (bf16[2,128,512]{2,1,0:T(8,128)(2,1)}, bf16[2,128,512]{2,1,0:T(8,128)(2,1)S(1)}, u32[]{:S(2)}, u32[]{:S(2)}) collective-permute-start(bf16[2,128,512]{2,1,0:T(8,128)(2,1)} %pad_maximum_fusion.2), channel_id=1, source_target_pairs={{0,1},{1,0},{2,3},{3,2},{4,5},{5,4},{6,7},{7,6},{8,9},{9,8},{10,11... | collective-permute-start | bytes 786440 | tf_op jit(solution)/shard_map/ppermute | solution.py:258
  55.1 1.9 %collective-permute-start = (s32[2,8]{1,0:T(2,128)S(1)}, s32[2,8]{1,0:T(2,128)S(1)}, u32[]{:S(2)}, u32[]{:S(2)}) collective-permute-start(s32[2,8]{1,0:T(2,128)S(1)} %copy-done.33), channel_id=1, source_target_pairs={{0,1},{1,0},{2,3},{3,2},{4,5},{5,4},{6,7},{7,6},{8,9},{9,8},{10,11... | collective-permute-start | bytes 200 | tf_op jit(solution)/shard_map/ppermute | solution.py:259
  57.9 3.9 %collective-permute-start.13 = (bf16[2,128,512]{2,1,0:T(8,128)(2,1)S(1)}, bf16[2,128,512]{2,1,0:T(8,128)(2,1)S(1)}, u32[]{:S(2)}, u32[]{:S(2)}) collective-permute-start(bf16[2,128,512]{2,1,0:T(8,128)(2,1)S(1)} %collective-permute-done.7.refs_9_), channel_id=1, source_target_pairs={{0,14},{2,4},{4,2},{6,8},{8,6},{10,12},{12,10},{14,0},{1,15},{3,5}... | collective-permute-start | bytes 786440 | tf_op jit(solution)/shard_map/ppermute | solution.py:262
  61.8 2.6 %collective-permute-start.14 = (bf16[2,128,512]{2,1,0:T(8,128)(2,1)S(1)}, bf16[2,128,512]{2,1,0:T(8,128)(2,1)S(1)}, u32[]{:S(2)}, u32[]{:S(2)}) collective-permute-start(bf16[2,128,512]{2,1,0:T(8,128)(2,1)S(1)} %collective-permute-done.4.refs_8_), channel_id=1, source_target_pairs={{0,14},{2,4},{4,2},{6,8},{8,6},{10,12},{12,10},{14,0},{1,15},{3,5}... | collective-permute-start | bytes 786440 | tf_op jit(solution)/shard_map/ppermute | solution.py:261
  64.4 1.9 %collective-permute-start.15 = (bf16[2,128,512]{2,1,0:T(8,128)(2,1)S(1)}, bf16[2,128,512]{2,1,0:T(8,128)(2,1)S(1)}, u32[]{:S(2)}, u32[]{:S(2)}) collective-permute-start(bf16[2,128,512]{2,1,0:T(8,128)(2,1)S(1)} %collective-permute-done.9.refs_20_), channel_id=1, source_target_pairs={{0,2},{2,0},{4,6},{6,4},{8,10},{10,8},{12,14},{14,12},{1,3},{3,1},... | collective-permute-start | bytes 786440 | tf_op jit(solution)/shard_map/ppermute | solution.py:261
  66.3 3.4 %collective-permute-start.16 = (bf16[2,128,512]{2,1,0:T(8,128)(2,1)S(1)}, bf16[2,128,512]{2,1,0:T(8,128)(2,1)S(1)}, u32[]{:S(2)}, u32[]{:S(2)}) collective-permute-start(bf16[2,128,512]{2,1,0:T(8,128)(2,1)S(1)} %collective-permute-done.12.refs_19_), channel_id=1, source_target_pairs={{0,2},{2,0},{4,6},{6,4},{8,10},{10,8},{12,14},{14,12},{1,3},{3,1},... | collective-permute-start | bytes 786440 | tf_op jit(solution)/shard_map/ppermute | solution.py:262
  71.1 2.1 %collective-permute-done.14.refs_11_ = bf16[2,128,512]{2,1,0:T(8,128)(2,1)S(1)} collective-permute-done((bf16[2,128,512]{2,1,0:T(8,128)(2,1)S(1)}, bf16[2,128,512]{2,1,0:T(8,128)(2,1)S(1)}, u32[]{:S(2)}, u32[]{:S(2)}) %collective-permute-start.14) | collective-permute-done | bytes 262176 | tf_op jit(solution)/shard_map/ppermute | solution.py:261
  73.2 3.3 %collective-permute-done.16.refs_18_ = bf16[2,128,512]{2,1,0:T(8,128)(2,1)S(1)} collective-permute-done((bf16[2,128,512]{2,1,0:T(8,128)(2,1)S(1)}, bf16[2,128,512]{2,1,0:T(8,128)(2,1)S(1)}, u32[]{:S(2)}, u32[]{:S(2)}) %collective-permute-start.16) | collective-permute-done | bytes 262176 | tf_op jit(solution)/shard_map/ppermute | solution.py:262
  77.3 18.6 %shard_map.84 = (bf16[2,128,512]{2,1,0:T(8,128)(2,1)}, bf16[2,128,512]{2,1,0:T(8,128)(2,1)}, f32[2,2,128,512]{3,2,1,0:T(8,128)}, bf16[32,16,128]{2,1,0:T(8,128)(...) custom-call(s32[4]{0:T(128)} %pad_add_fusion.refs_0_, ...), custom_call_target="tpu_custom_call" | custom-call | flops 1200000000 | bytes 12000000 | tf_op jit(solution)/shard_map/pallas_call | solution.py:191
  95.9 9.7 %all-to-all-start.1 = ((bf16[32,16,128]{2,1,0:T(8,128)(2,1)}), bf16[32,16,128]{2,1,0:T(8,128)(2,1)S(1)}, u32[]{:S(2)}, u32[]{:S(2)}) async-start(bf16[32,16,128]{2,1,0:T(8,128)(2,1)} %get-tuple-element.42), calls=%async_computation.1 | async-start | bytes 262144 | tf_op jit(solution)/shard_map/all_to_all | solution.py:270
  105.6 3.2 %collective-permute-start.25 = (bf16[2,128,512]{2,1,0:T(8,128)(2,1)}, bf16[2,128,512]{2,1,0:T(8,128)(2,1)S(1)}, u32[]{:S(2)}, u32[]{:S(2)}) collective-permute-start(bf16[2,128,512]{2,1,0:T(8,128)(2,1)} %get-tuple-element.45), channel_id=1, source_target_pairs={{0,2},{2,0},{4,6},{6,4},{8,10},{10,8},{12,14},{14,12},{1,3},{3,1},... | collective-permute-start | bytes 786440 | tf_op jit(solution)/shard_map/ppermute | solution.py:271
  108.9 2.1 %collective-permute-start.28 = (bf16[2,128,512]{2,1,0:T(8,128)(2,1)}, bf16[2,128,512]{2,1,0:T(8,128)(2,1)S(1)}, u32[]{:S(2)}, u32[]{:S(2)}) collective-permute-start(bf16[2,128,512]{2,1,0:T(8,128)(2,1)} %get-tuple-element.49), channel_id=1, source_target_pairs={{0,2},{2,0},{4,6},{6,4},{8,10},{10,8},{12,14},{14,12},{1,3},{3,1},... | collective-permute-start | bytes 786440 | tf_op jit(solution)/shard_map/ppermute | solution.py:272
  110.9 3.9 %collective-permute-start.18 = (bf16[2,128,512]{2,1,0:T(8,128)(2,1)}, bf16[2,128,512]{2,1,0:T(8,128)(2,1)S(1)}, u32[]{:S(2)}, u32[]{:S(2)}) collective-permute-start(bf16[2,128,512]{2,1,0:T(8,128)(2,1)} %get-tuple-element.37), channel_id=1, source_target_pairs={{0,14},{2,4},{4,2},{6,8},{8,6},{10,12},{12,10},{14,0},{1,15},{3,5}... | collective-permute-start | bytes 786440 | tf_op jit(solution)/shard_map/ppermute | solution.py:271
  114.8 2.6 %collective-permute-start.21 = (bf16[2,128,512]{2,1,0:T(8,128)(2,1)}, bf16[2,128,512]{2,1,0:T(8,128)(2,1)S(1)}, u32[]{:S(2)}, u32[]{:S(2)}) collective-permute-start(bf16[2,128,512]{2,1,0:T(8,128)(2,1)} %get-tuple-element.41), channel_id=1, source_target_pairs={{0,14},{2,4},{4,2},{6,8},{8,6},{10,12},{12,10},{14,0},{1,15},{3,5}... | collective-permute-start | bytes 786440 | tf_op jit(solution)/shard_map/ppermute | solution.py:272
  117.4 7.2 %collective-permute-start.17 = (bf16[2,128,512]{2,1,0:T(8,128)(2,1)}, bf16[2,128,512]{2,1,0:T(8,128)(2,1)}, u32[]{:S(2)}, u32[]{:S(2)}) collective-permute-start(bf16[2,128,512]{2,1,0:T(8,128)(2,1)} %get-tuple-element.33), channel_id=1, source_target_pairs={{0,1},{1,0},{2,3},{3,2},{4,5},{5,4},{6,7},{7,6},{8,9},{9,8},{10,11... | collective-permute-start | bytes 786440 | tf_op jit(solution)/shard_map/ppermute | solution.py:279
  124.8 0.8 copy-done.28
  125.7 4.1 %collective-permute-start.26 = (bf16[2,128,512]{2,1,0:T(8,128)(2,1)S(1)}, bf16[2,128,512]{2,1,0:T(8,128)(2,1)S(1)}, u32[]{:S(2)}, u32[]{:S(2)}) collective-permute-start(bf16[2,128,512]{2,1,0:T(8,128)(2,1)S(1)} %add_convert_fusion.4), channel_id=1, source_target_pairs={{0,14},{2,4},{4,2},{6,8},{8,6},{10,12},{12,10},{14,0},{1,15},{3,5}... | collective-permute-start | bytes 786440 | tf_op jit(solution)/shard_map/ppermute | solution.py:273
  129.9 2.4 %collective-permute-start.29 = (bf16[2,128,512]{2,1,0:T(8,128)(2,1)S(1)}, bf16[2,128,512]{2,1,0:T(8,128)(2,1)S(1)}, u32[]{:S(2)}, u32[]{:S(2)}) collective-permute-start(bf16[2,128,512]{2,1,0:T(8,128)(2,1)S(1)} %add_convert_fusion.2), channel_id=1, source_target_pairs={{0,14},{2,4},{4,2},{6,8},{8,6},{10,12},{12,10},{14,0},{1,15},{3,5}... | collective-permute-start | bytes 786440 | tf_op jit(solution)/shard_map/ppermute | solution.py:274
  132.4 1.9 %collective-permute-start.19 = (bf16[2,128,512]{2,1,0:T(8,128)(2,1)S(1)}, bf16[2,128,512]{2,1,0:T(8,128)(2,1)S(1)}, u32[]{:S(2)}, u32[]{:S(2)}) collective-permute-start(bf16[2,128,512]{2,1,0:T(8,128)(2,1)S(1)} %add_convert_fusion.9), channel_id=1, source_target_pairs={{0,2},{2,0},{4,6},{6,4},{8,10},{10,8},{12,14},{14,12},{1,3},{3,1},... | collective-permute-start | bytes 786440 | tf_op jit(solution)/shard_map/ppermute | solution.py:273
  134.4 3.4 %collective-permute-start.22 = (bf16[2,128,512]{2,1,0:T(8,128)(2,1)S(1)}, bf16[2,128,512]{2,1,0:T(8,128)(2,1)S(1)}, u32[]{:S(2)}, u32[]{:S(2)}) collective-permute-start(bf16[2,128,512]{2,1,0:T(8,128)(2,1)S(1)} %add_convert_fusion.7), channel_id=1, source_target_pairs={{0,2},{2,0},{4,6},{6,4},{8,10},{10,8},{12,14},{14,12},{1,3},{3,1},... | collective-permute-start | bytes 786440 | tf_op jit(solution)/shard_map/ppermute | solution.py:274
  137.9 1.9 %collective-permute-start.27 = (bf16[2,128,512]{2,1,0:T(8,128)(2,1)S(1)}, bf16[2,128,512]{2,1,0:T(8,128)(2,1)S(1)}, u32[]{:S(2)}, u32[]{:S(2)}) collective-permute-start(bf16[2,128,512]{2,1,0:T(8,128)(2,1)S(1)} %add_convert_fusion.3), channel_id=1, source_target_pairs={{0,2},{2,0},{4,6},{6,4},{8,10},{10,8},{12,14},{14,12},{1,3},{3,1},... | collective-permute-start | bytes 786440 | tf_op jit(solution)/shard_map/ppermute | solution.py:277
  139.8 2.5 %collective-permute-done.29 = bf16[2,128,512]{2,1,0:T(8,128)(2,1)S(1)} collective-permute-done((bf16[2,128,512]{2,1,0:T(8,128)(2,1)S(1)}, bf16[2,128,512]{2,1,0:T(8,128)(2,1)S(1)}, u32[]{:S(2)}, u32[]{:S(2)}) %collective-permute-start.29) | collective-permute-done | bytes 262176 | tf_op jit(solution)/shard_map/ppermute | solution.py:274
  142.4 1.9 %collective-permute-start.30 = (bf16[2,128,512]{2,1,0:T(8,128)(2,1)S(1)}, bf16[2,128,512]{2,1,0:T(8,128)(2,1)S(1)}, u32[]{:S(2)}, u32[]{:S(2)}) collective-permute-start(bf16[2,128,512]{2,1,0:T(8,128)(2,1)S(1)} %add_convert_fusion.1), channel_id=1, source_target_pairs={{0,2},{2,0},{4,6},{6,4},{8,10},{10,8},{12,14},{14,12},{1,3},{3,1},... | collective-permute-start | bytes 786440 | tf_op jit(solution)/shard_map/ppermute | solution.py:275
  144.3 2.9 %collective-permute-done.22 = bf16[2,128,512]{2,1,0:T(8,128)(2,1)S(1)} collective-permute-done((bf16[2,128,512]{2,1,0:T(8,128)(2,1)S(1)}, bf16[2,128,512]{2,1,0:T(8,128)(2,1)S(1)}, u32[]{:S(2)}, u32[]{:S(2)}) %collective-permute-start.22) | collective-permute-done | bytes 262176 | tf_op jit(solution)/shard_map/ppermute | solution.py:274
  147.3 4.1 %collective-permute-start.23 = (bf16[2,128,512]{2,1,0:T(8,128)(2,1)S(1)}, bf16[2,128,512]{2,1,0:T(8,128)(2,1)S(1)}, u32[]{:S(2)}, u32[]{:S(2)}) collective-permute-start(bf16[2,128,512]{2,1,0:T(8,128)(2,1)S(1)} %add_convert_fusion.6), channel_id=1, source_target_pairs={{0,14},{2,4},{4,2},{6,8},{8,6},{10,12},{12,10},{14,0},{1,15},{3,5}... | collective-permute-start | bytes 786440 | tf_op jit(solution)/shard_map/ppermute | solution.py:275
  151.5 2.6 %collective-permute-start.20 = (bf16[2,128,512]{2,1,0:T(8,128)(2,1)S(1)}, bf16[2,128,512]{2,1,0:T(8,128)(2,1)S(1)}, u32[]{:S(2)}, u32[]{:S(2)}) collective-permute-start(bf16[2,128,512]{2,1,0:T(8,128)(2,1)S(1)} %add_convert_fusion.8), channel_id=1, source_target_pairs={{0,14},{2,4},{4,2},{6,8},{8,6},{10,12},{12,10},{14,0},{1,15},{3,5}... | collective-permute-start | bytes 786440 | tf_op jit(solution)/shard_map/ppermute | solution.py:276
  154.0 4.4 %collective-permute-done.30 = bf16[2,128,512]{2,1,0:T(8,128)(2,1)S(1)} collective-permute-done((bf16[2,128,512]{2,1,0:T(8,128)(2,1)S(1)}, bf16[2,128,512]{2,1,0:T(8,128)(2,1)S(1)}, u32[]{:S(2)}, u32[]{:S(2)}) %collective-permute-start.30) | collective-permute-done | bytes 262176 | tf_op jit(solution)/shard_map/ppermute | solution.py:275
  158.5 4.2 %collective-permute-start.31 = (bf16[2,128,512]{2,1,0:T(8,128)(2,1)S(1)}, bf16[2,128,512]{2,1,0:T(8,128)(2,1)S(1)}, u32[]{:S(2)}, u32[]{:S(2)}) collective-permute-start(bf16[2,128,512]{2,1,0:T(8,128)(2,1)S(1)} %add_convert_fusion), channel_id=1, source_target_pairs={{0,14},{2,4},{4,2},{6,8},{8,6},{10,12},{12,10},{14,0},{1,15},{3,5}... | collective-permute-start | bytes 786440 | tf_op jit(solution)/shard_map/ppermute | solution.py:277
  162.8 1.9 %collective-permute-start.24 = (bf16[2,128,512]{2,1,0:T(8,128)(2,1)S(1)}, bf16[2,128,512]{2,1,0:T(8,128)(2,1)S(1)}, u32[]{:S(2)}, u32[]{:S(2)}) collective-permute-start(bf16[2,128,512]{2,1,0:T(8,128)(2,1)S(1)} %add_convert_fusion.5), channel_id=1, source_target_pairs={{0,2},{2,0},{4,6},{6,4},{8,10},{10,8},{12,14},{14,12},{1,3},{3,1},... | collective-permute-start | bytes 786440 | tf_op jit(solution)/shard_map/ppermute | solution.py:276
  164.8 1.0 slice_bitcast_fusion.4
  165.8 2.3 %collective-permute-done.31 = bf16[2,128,512]{2,1,0:T(8,128)(2,1)S(1)} collective-permute-done((bf16[2,128,512]{2,1,0:T(8,128)(2,1)S(1)}, bf16[2,128,512]{2,1,0:T(8,128)(2,1)S(1)}, u32[]{:S(2)}, u32[]{:S(2)}) %collective-permute-start.31) | collective-permute-done | bytes 262176 | tf_op jit(solution)/shard_map/ppermute | solution.py:277
  168.1 2.7 %collective-permute-done.24 = bf16[2,128,512]{2,1,0:T(8,128)(2,1)S(1)} collective-permute-done((bf16[2,128,512]{2,1,0:T(8,128)(2,1)S(1)}, bf16[2,128,512]{2,1,0:T(8,128)(2,1)S(1)}, u32[]{:S(2)}, u32[]{:S(2)}) %collective-permute-start.24) | collective-permute-done | bytes 262176 | tf_op jit(solution)/shard_map/ppermute | solution.py:276
  171.1 4.5 %collective-permute-start.32 = (bf16[2,128,512]{2,1,0:T(8,128)(2,1)S(1)}, bf16[2,128,512]{2,1,0:T(8,128)(2,1)S(1)}, u32[]{:S(2)}, u32[]{:S(2)}) collective-permute-start(bf16[2,128,512]{2,1,0:T(8,128)(2,1)S(1)} %get-tuple-element.51), channel_id=1, source_target_pairs={{0,1},{1,0},{2,3},{3,2},{4,5},{5,4},{6,7},{7,6},{8,9},{9,8},{10,11... | collective-permute-start | bytes 786440 | tf_op jit(solution)/shard_map/ppermute | solution.py:286
  175.6 0.9 maximum_select_fusion
  176.8 0.9 maximum_select_fusion.2
  (131 shorter events, 6.3 us)
Async XLA Ops:
  1.8 10.9 %collective-permute-start.2 = (bf16[2,128,512]{2,1,0:T(8,128)(2,1)S(1)}, bf16[2,128,512]{2,1,0:T(8,128)(2,1)S(1)}, u32[]{:S(2)}, u32[]{:S(2)}) collective-permute-start(bf16[2,128,512]{2,1,0:T(8,128)(2,1)S(1)} %pad_maximum_fusion.3), channel_id=1, source_target_pairs={{0,1},{1,0},{2,3},{3,2},{4,5},{5,4},{6,7},{7,6},{8,9},{9,8},{10,11... | collective-permute-start | bytes 786440 | tf_op jit(solution)/shard_map/ppermute | solution.py:248
  10.6 16.0 %copy-start = (bf16[2,128,512]{2,1,0:T(8,128)(2,1)}, bf16[2,128,512]{2,1,0:T(8,128)(2,1)S(1)}, u32[]{:S(2)}) copy-start(bf16[2,128,512]{2,1,0:T(8,128)(2,1)S(1)} %pad_maximum_fusion.refs_6_) | copy-start | bytes 786436
  10.6 15.9 %copy-start.30 = (bf16[128,1024]{1,0:T(8,128)(2,1)S(1)}, bf16[128,1024]{1,0:T(8,128)(2,1)}, u32[]{:S(2)}) copy-start(bf16[128,1024]{1,0:T(8,128)(2,1)} %param.5) | copy-start | bytes 786436
  10.6 10.8 %collective-permute-start.5 = (bf16[2,128,512]{2,1,0:T(8,128)(2,1)S(1)}, bf16[2,128,512]{2,1,0:T(8,128)(2,1)S(1)}, u32[]{:S(2)}, u32[]{:S(2)}) collective-permute-start(bf16[2,128,512]{2,1,0:T(8,128)(2,1)S(1)} %pad_maximum_fusion.refs_6_), channel_id=1, source_target_pairs={{0,2},{2,0},{4,6},{6,4},{8,10},{10,8},{12,14},{14,12},{1,3},{3,1},... | collective-permute-start | bytes 786440 | tf_op jit(solution)/shard_map/ppermute | solution.py:253
  12.7 13.9 %copy-start.3 = (bf16[2,128,512]{2,1,0:T(8,128)(2,1)}, bf16[2,128,512]{2,1,0:T(8,128)(2,1)S(1)}, u32[]{:S(2)}) copy-start(bf16[2,128,512]{2,1,0:T(8,128)(2,1)S(1)} %collective-permute-done.2.refs_14_) | copy-start | bytes 786436
  12.7 11.0 %collective-permute-start.10 = (bf16[2,128,512]{2,1,0:T(8,128)(2,1)S(1)}, bf16[2,128,512]{2,1,0:T(8,128)(2,1)S(1)}, u32[]{:S(2)}, u32[]{:S(2)}) collective-permute-start(bf16[2,128,512]{2,1,0:T(8,128)(2,1)S(1)} %collective-permute-done.2.refs_14_), channel_id=1, source_target_pairs={{0,14},{2,4},{4,2},{6,8},{8,6},{10,12},{12,10},{14,0},{1,15},{3,5}... | collective-permute-start | bytes 786440 | tf_op jit(solution)/shard_map/ppermute | solution.py:253
  14.6 23.0 %collective-permute-start.3 = (bf16[2,128,512]{2,1,0:T(8,128)(2,1)S(1)}, bf16[2,128,512]{2,1,0:T(8,128)(2,1)S(1)}, u32[]{:S(2)}, u32[]{:S(2)}) collective-permute-start(bf16[2,128,512]{2,1,0:T(8,128)(2,1)S(1)} %pad_maximum_fusion.refs_6_), channel_id=1, source_target_pairs={{0,14},{2,4},{4,2},{6,8},{8,6},{10,12},{12,10},{14,0},{1,15},{3,5}... | collective-permute-start | bytes 786440 | tf_op jit(solution)/shard_map/ppermute | solution.py:254
  19.2 23.7 %collective-permute-start.8 = (bf16[2,128,512]{2,1,0:T(8,128)(2,1)S(1)}, bf16[2,128,512]{2,1,0:T(8,128)(2,1)S(1)}, u32[]{:S(2)}, u32[]{:S(2)}) collective-permute-start(bf16[2,128,512]{2,1,0:T(8,128)(2,1)S(1)} %collective-permute-done.2.refs_14_), channel_id=1, source_target_pairs={{0,2},{2,0},{4,6},{6,4},{8,10},{10,8},{12,14},{14,12},{1,3},{3,1},... | collective-permute-start | bytes 786440 | tf_op jit(solution)/shard_map/ppermute | solution.py:254
  21.4 19.6 %collective-permute-start.6 = (bf16[2,128,512]{2,1,0:T(8,128)(2,1)S(1)}, bf16[2,128,512]{2,1,0:T(8,128)(2,1)S(1)}, u32[]{:S(2)}, u32[]{:S(2)}) collective-permute-start(bf16[2,128,512]{2,1,0:T(8,128)(2,1)S(1)} %collective-permute-done.5.refs_7_), channel_id=1, source_target_pairs={{0,14},{2,4},{4,2},{6,8},{8,6},{10,12},{12,10},{14,0},{1,15},{3,5}... | collective-permute-start | bytes 786440 | tf_op jit(solution)/shard_map/ppermute | solution.py:255
  23.7 26.6 %copy-start.5 = (bf16[2,128,512]{2,1,0:T(8,128)(2,1)}, bf16[2,128,512]{2,1,0:T(8,128)(2,1)S(1)}, u32[]{:S(2)}) copy-start(bf16[2,128,512]{2,1,0:T(8,128)(2,1)S(1)} %collective-permute-done.10.refs_21_) | copy-start | bytes 786436
  23.7 23.7 %collective-permute-start.11 = (bf16[2,128,512]{2,1,0:T(8,128)(2,1)S(1)}, bf16[2,128,512]{2,1,0:T(8,128)(2,1)S(1)}, u32[]{:S(2)}, u32[]{:S(2)}) collective-permute-start(bf16[2,128,512]{2,1,0:T(8,128)(2,1)S(1)} %collective-permute-done.10.refs_21_), channel_id=1, source_target_pairs={{0,2},{2,0},{4,6},{6,4},{8,10},{10,8},{12,14},{14,12},{1,3},{3,1},... | collective-permute-start | bytes 786440 | tf_op jit(solution)/shard_map/ppermute | solution.py:255
  26.6 22.9 %copy-start.31 = (bf16[128,1024]{1,0:T(8,128)(2,1)S(1)}, bf16[128,1024]{1,0:T(8,128)(2,1)}, u32[]{:S(2)}) copy-start(bf16[128,1024]{1,0:T(8,128)(2,1)} %param.8) | copy-start | bytes 786436
  27.3 29.7 %all-to-all-start = ((bf16[32,16,128]{2,1,0:T(8,128)(2,1)}), bf16[32,16,128]{2,1,0:T(8,128)(2,1)S(1)}, u32[]{:S(2)}, u32[]{:S(2)}) async-start(bf16[32,16,128]{2,1,0:T(8,128)(2,1)} %broadcast_in_dim.38), calls=%async_computation | async-start | bytes 262144 | tf_op jit(solution)/shard_map/all_to_all | solution.py:250
  37.7 17.4 %collective-permute-start.4 = (bf16[2,128,512]{2,1,0:T(8,128)(2,1)S(1)}, bf16[2,128,512]{2,1,0:T(8,128)(2,1)S(1)}, u32[]{:S(2)}, u32[]{:S(2)}) collective-permute-start(bf16[2,128,512]{2,1,0:T(8,128)(2,1)S(1)} %collective-permute-done.3.refs_13_), channel_id=1, source_target_pairs={{0,2},{2,0},{4,6},{6,4},{8,10},{10,8},{12,14},{14,12},{1,3},{3,1},... | collective-permute-start | bytes 786440 | tf_op jit(solution)/shard_map/ppermute | solution.py:256
  41.0 30.0 %copy-start.8 = (bf16[2,128,512]{2,1,0:T(8,128)(2,1)}, bf16[2,128,512]{2,1,0:T(8,128)(2,1)S(1)}, u32[]{:S(2)}) copy-start(bf16[2,128,512]{2,1,0:T(8,128)(2,1)S(1)} %collective-permute-done.6.refs_12_) | copy-start | bytes 786436
  41.1 16.0 %collective-permute-start.7 = (bf16[2,128,512]{2,1,0:T(8,128)(2,1)S(1)}, bf16[2,128,512]{2,1,0:T(8,128)(2,1)S(1)}, u32[]{:S(2)}, u32[]{:S(2)}) collective-permute-start(bf16[2,128,512]{2,1,0:T(8,128)(2,1)S(1)} %collective-permute-done.6.refs_12_), channel_id=1, source_target_pairs={{0,2},{2,0},{4,6},{6,4},{8,10},{10,8},{12,14},{14,12},{1,3},{3,1},... | collective-permute-start | bytes 786440 | tf_op jit(solution)/shard_map/ppermute | solution.py:257
  43.0 14.1 %collective-permute-start.9 = (bf16[2,128,512]{2,1,0:T(8,128)(2,1)S(1)}, bf16[2,128,512]{2,1,0:T(8,128)(2,1)S(1)}, u32[]{:S(2)}, u32[]{:S(2)}) collective-permute-start(bf16[2,128,512]{2,1,0:T(8,128)(2,1)S(1)} %collective-permute-done.8.refs_15_), channel_id=1, source_target_pairs={{0,14},{2,4},{4,2},{6,8},{8,6},{10,12},{12,10},{14,0},{1,15},{3,5}... | collective-permute-start | bytes 786440 | tf_op jit(solution)/shard_map/ppermute | solution.py:256
  47.4 23.6 %copy-start.9 = (bf16[2,128,512]{2,1,0:T(8,128)(2,1)}, bf16[2,128,512]{2,1,0:T(8,128)(2,1)S(1)}, u32[]{:S(2)}) copy-start(bf16[2,128,512]{2,1,0:T(8,128)(2,1)S(1)} %collective-permute-done.11.refs_16_) | copy-start | bytes 786436
  47.4 10.4 %collective-permute-start.12 = (bf16[2,128,512]{2,1,0:T(8,128)(2,1)S(1)}, bf16[2,128,512]{2,1,0:T(8,128)(2,1)S(1)}, u32[]{:S(2)}, u32[]{:S(2)}) collective-permute-start(bf16[2,128,512]{2,1,0:T(8,128)(2,1)S(1)} %collective-permute-done.11.refs_16_), channel_id=1, source_target_pairs={{0,14},{2,4},{4,2},{6,8},{8,6},{10,12},{12,10},{14,0},{1,15},{3,5}... | collective-permute-start | bytes 786440 | tf_op jit(solution)/shard_map/ppermute | solution.py:257
  50.3 20.7 %collective-permute-start.1 = (bf16[2,128,512]{2,1,0:T(8,128)(2,1)}, bf16[2,128,512]{2,1,0:T(8,128)(2,1)S(1)}, u32[]{:S(2)}, u32[]{:S(2)}) collective-permute-start(bf16[2,128,512]{2,1,0:T(8,128)(2,1)} %pad_maximum_fusion.2), channel_id=1, source_target_pairs={{0,1},{1,0},{2,3},{3,2},{4,5},{5,4},{6,7},{7,6},{8,9},{9,8},{10,11... | collective-permute-start | bytes 786440 | tf_op jit(solution)/shard_map/ppermute | solution.py:258
  55.1 15.9 %copy-start.10 = (bf16[2,128,512]{2,1,0:T(8,128)(2,1)}, bf16[2,128,512]{2,1,0:T(8,128)(2,1)S(1)}, u32[]{:S(2)}) copy-start(bf16[2,128,512]{2,1,0:T(8,128)(2,1)S(1)} %collective-permute-done.4.refs_8_) | copy-start | bytes 786436
  55.1 11.2 %collective-permute-start = (s32[2,8]{1,0:T(2,128)S(1)}, s32[2,8]{1,0:T(2,128)S(1)}, u32[]{:S(2)}, u32[]{:S(2)}) collective-permute-start(s32[2,8]{1,0:T(2,128)S(1)} %copy-done.33), channel_id=1, source_target_pairs={{0,1},{1,0},{2,3},{3,2},{4,5},{5,4},{6,7},{7,6},{8,9},{9,8},{10,11... | collective-permute-start | bytes 200 | tf_op jit(solution)/shard_map/ppermute | solution.py:259
  57.1 14.0 %copy-start.2 = (bf16[32,16,128]{2,1,0:T(8,128)(2,1)}, bf16[32,16,128]{2,1,0:T(8,128)(2,1)S(1)}, u32[]{:S(2)}) copy-start(bf16[32,16,128]{2,1,0:T(8,128)(2,1)S(1)} %all-to-all-done.refs_5_) | copy-start | bytes 393220
  57.1 19.5 %copy-start.11 = (bf16[2,128,512]{2,1,0:T(8,128)(2,1)}, bf16[2,128,512]{2,1,0:T(8,128)(2,1)S(1)}, u32[]{:S(2)}) copy-start(bf16[2,128,512]{2,1,0:T(8,128)(2,1)S(1)} %collective-permute-done.7.refs_9_) | copy-start | bytes 786436
  57.1 19.4 %copy-start.12 = (bf16[2,128,512]{2,1,0:T(8,128)(2,1)}, bf16[2,128,512]{2,1,0:T(8,128)(2,1)S(1)}, u32[]{:S(2)}) copy-start(bf16[2,128,512]{2,1,0:T(8,128)(2,1)S(1)} %collective-permute-done.9.refs_20_) | copy-start | bytes 786436
  57.9 18.7 %copy-start.14 = (bf16[2,128,512]{2,1,0:T(8,128)(2,1)}, bf16[2,128,512]{2,1,0:T(8,128)(2,1)S(1)}, u32[]{:S(2)}) copy-start(bf16[2,128,512]{2,1,0:T(8,128)(2,1)S(1)} %collective-permute-done.12.refs_19_) | copy-start | bytes 786436
  57.9 13.2 %collective-permute-start.13 = (bf16[2,128,512]{2,1,0:T(8,128)(2,1)S(1)}, bf16[2,128,512]{2,1,0:T(8,128)(2,1)S(1)}, u32[]{:S(2)}, u32[]{:S(2)}) collective-permute-start(bf16[2,128,512]{2,1,0:T(8,128)(2,1)S(1)} %collective-permute-done.7.refs_9_), channel_id=1, source_target_pairs={{0,14},{2,4},{4,2},{6,8},{8,6},{10,12},{12,10},{14,0},{1,15},{3,5}... | collective-permute-start | bytes 786440 | tf_op jit(solution)/shard_map/ppermute | solution.py:262
  61.8 11.4 %collective-permute-start.14 = (bf16[2,128,512]{2,1,0:T(8,128)(2,1)S(1)}, bf16[2,128,512]{2,1,0:T(8,128)(2,1)S(1)}, u32[]{:S(2)}, u32[]{:S(2)}) collective-permute-start(bf16[2,128,512]{2,1,0:T(8,128)(2,1)S(1)} %collective-permute-done.4.refs_8_), channel_id=1, source_target_pairs={{0,14},{2,4},{4,2},{6,8},{8,6},{10,12},{12,10},{14,0},{1,15},{3,5}... | collective-permute-start | bytes 786440 | tf_op jit(solution)/shard_map/ppermute | solution.py:261
  64.4 8.8 %collective-permute-start.15 = (bf16[2,128,512]{2,1,0:T(8,128)(2,1)S(1)}, bf16[2,128,512]{2,1,0:T(8,128)(2,1)S(1)}, u32[]{:S(2)}, u32[]{:S(2)}) collective-permute-start(bf16[2,128,512]{2,1,0:T(8,128)(2,1)S(1)} %collective-permute-done.9.refs_20_), channel_id=1, source_target_pairs={{0,2},{2,0},{4,6},{6,4},{8,10},{10,8},{12,14},{14,12},{1,3},{3,1},... | collective-permute-start | bytes 786440 | tf_op jit(solution)/shard_map/ppermute | solution.py:261
  66.3 10.2 %collective-permute-start.16 = (bf16[2,128,512]{2,1,0:T(8,128)(2,1)S(1)}, bf16[2,128,512]{2,1,0:T(8,128)(2,1)S(1)}, u32[]{:S(2)}, u32[]{:S(2)}) collective-permute-start(bf16[2,128,512]{2,1,0:T(8,128)(2,1)S(1)} %collective-permute-done.12.refs_19_), channel_id=1, source_target_pairs={{0,2},{2,0},{4,6},{6,4},{8,10},{10,8},{12,14},{14,12},{1,3},{3,1},... | collective-permute-start | bytes 786440 | tf_op jit(solution)/shard_map/ppermute | solution.py:262
  95.9 28.8 %copy-start.32 = (bf16[2,128,512]{2,1,0:T(8,128)(2,1)S(1)}, bf16[2,128,512]{2,1,0:T(8,128)(2,1)}, u32[]{:S(2)}) copy-start(bf16[2,128,512]{2,1,0:T(8,128)(2,1)} %get-tuple-element.32) | copy-start | bytes 786436
  95.9 28.8 %all-to-all-start.1 = ((bf16[32,16,128]{2,1,0:T(8,128)(2,1)}), bf16[32,16,128]{2,1,0:T(8,128)(2,1)S(1)}, u32[]{:S(2)}, u32[]{:S(2)}) async-start(bf16[32,16,128]{2,1,0:T(8,128)(2,1)} %get-tuple-element.42), calls=%async_computation.1 | async-start | bytes 262144 | tf_op jit(solution)/shard_map/all_to_all | solution.py:270
  105.6 19.1 %collective-permute-start.25 = (bf16[2,128,512]{2,1,0:T(8,128)(2,1)}, bf16[2,128,512]{2,1,0:T(8,128)(2,1)S(1)}, u32[]{:S(2)}, u32[]{:S(2)}) collective-permute-start(bf16[2,128,512]{2,1,0:T(8,128)(2,1)} %get-tuple-element.45), channel_id=1, source_target_pairs={{0,2},{2,0},{4,6},{6,4},{8,10},{10,8},{12,14},{14,12},{1,3},{3,1},... | collective-permute-start | bytes 786440 | tf_op jit(solution)/shard_map/ppermute | solution.py:271
  108.9 20.9 %collective-permute-start.28 = (bf16[2,128,512]{2,1,0:T(8,128)(2,1)}, bf16[2,128,512]{2,1,0:T(8,128)(2,1)S(1)}, u32[]{:S(2)}, u32[]{:S(2)}) collective-permute-start(bf16[2,128,512]{2,1,0:T(8,128)(2,1)} %get-tuple-element.49), channel_id=1, source_target_pairs={{0,2},{2,0},{4,6},{6,4},{8,10},{10,8},{12,14},{14,12},{1,3},{3,1},... | collective-permute-start | bytes 786440 | tf_op jit(solution)/shard_map/ppermute | solution.py:272
  110.9 21.4 %collective-permute-start.18 = (bf16[2,128,512]{2,1,0:T(8,128)(2,1)}, bf16[2,128,512]{2,1,0:T(8,128)(2,1)S(1)}, u32[]{:S(2)}, u32[]{:S(2)}) collective-permute-start(bf16[2,128,512]{2,1,0:T(8,128)(2,1)} %get-tuple-element.37), channel_id=1, source_target_pairs={{0,14},{2,4},{4,2},{6,8},{8,6},{10,12},{12,10},{14,0},{1,15},{3,5}... | collective-permute-start | bytes 786440 | tf_op jit(solution)/shard_map/ppermute | solution.py:271
  114.8 19.5 %collective-permute-start.21 = (bf16[2,128,512]{2,1,0:T(8,128)(2,1)}, bf16[2,128,512]{2,1,0:T(8,128)(2,1)S(1)}, u32[]{:S(2)}, u32[]{:S(2)}) collective-permute-start(bf16[2,128,512]{2,1,0:T(8,128)(2,1)} %get-tuple-element.41), channel_id=1, source_target_pairs={{0,14},{2,4},{4,2},{6,8},{8,6},{10,12},{12,10},{14,0},{1,15},{3,5}... | collective-permute-start | bytes 786440 | tf_op jit(solution)/shard_map/ppermute | solution.py:272
  117.4 47.4 %collective-permute-start.17 = (bf16[2,128,512]{2,1,0:T(8,128)(2,1)}, bf16[2,128,512]{2,1,0:T(8,128)(2,1)}, u32[]{:S(2)}, u32[]{:S(2)}) collective-permute-start(bf16[2,128,512]{2,1,0:T(8,128)(2,1)} %get-tuple-element.33), channel_id=1, source_target_pairs={{0,1},{1,0},{2,3},{3,2},{4,5},{5,4},{6,7},{7,6},{8,9},{9,8},{10,11... | collective-permute-start | bytes 786440 | tf_op jit(solution)/shard_map/ppermute | solution.py:279
  125.7 12.1 %collective-permute-start.26 = (bf16[2,128,512]{2,1,0:T(8,128)(2,1)S(1)}, bf16[2,128,512]{2,1,0:T(8,128)(2,1)S(1)}, u32[]{:S(2)}, u32[]{:S(2)}) collective-permute-start(bf16[2,128,512]{2,1,0:T(8,128)(2,1)S(1)} %add_convert_fusion.4), channel_id=1, source_target_pairs={{0,14},{2,4},{4,2},{6,8},{8,6},{10,12},{12,10},{14,0},{1,15},{3,5}... | collective-permute-start | bytes 786440 | tf_op jit(solution)/shard_map/ppermute | solution.py:273
  129.9 12.5 %collective-permute-start.29 = (bf16[2,128,512]{2,1,0:T(8,128)(2,1)S(1)}, bf16[2,128,512]{2,1,0:T(8,128)(2,1)S(1)}, u32[]{:S(2)}, u32[]{:S(2)}) collective-permute-start(bf16[2,128,512]{2,1,0:T(8,128)(2,1)S(1)} %add_convert_fusion.2), channel_id=1, source_target_pairs={{0,14},{2,4},{4,2},{6,8},{8,6},{10,12},{12,10},{14,0},{1,15},{3,5}... | collective-permute-start | bytes 786440 | tf_op jit(solution)/shard_map/ppermute | solution.py:274
  132.4 18.9 %collective-permute-start.19 = (bf16[2,128,512]{2,1,0:T(8,128)(2,1)S(1)}, bf16[2,128,512]{2,1,0:T(8,128)(2,1)S(1)}, u32[]{:S(2)}, u32[]{:S(2)}) collective-permute-start(bf16[2,128,512]{2,1,0:T(8,128)(2,1)S(1)} %add_convert_fusion.9), channel_id=1, source_target_pairs={{0,2},{2,0},{4,6},{6,4},{8,10},{10,8},{12,14},{14,12},{1,3},{3,1},... | collective-permute-start | bytes 786440 | tf_op jit(solution)/shard_map/ppermute | solution.py:273
  134.4 12.8 %collective-permute-start.22 = (bf16[2,128,512]{2,1,0:T(8,128)(2,1)S(1)}, bf16[2,128,512]{2,1,0:T(8,128)(2,1)S(1)}, u32[]{:S(2)}, u32[]{:S(2)}) collective-permute-start(bf16[2,128,512]{2,1,0:T(8,128)(2,1)S(1)} %add_convert_fusion.7), channel_id=1, source_target_pairs={{0,2},{2,0},{4,6},{6,4},{8,10},{10,8},{12,14},{14,12},{1,3},{3,1},... | collective-permute-start | bytes 786440 | tf_op jit(solution)/shard_map/ppermute | solution.py:274
  137.9 27.9 %collective-permute-start.27 = (bf16[2,128,512]{2,1,0:T(8,128)(2,1)S(1)}, bf16[2,128,512]{2,1,0:T(8,128)(2,1)S(1)}, u32[]{:S(2)}, u32[]{:S(2)}) collective-permute-start(bf16[2,128,512]{2,1,0:T(8,128)(2,1)S(1)} %add_convert_fusion.3), channel_id=1, source_target_pairs={{0,2},{2,0},{4,6},{6,4},{8,10},{10,8},{12,14},{14,12},{1,3},{3,1},... | collective-permute-start | bytes 786440 | tf_op jit(solution)/shard_map/ppermute | solution.py:277
  142.4 16.0 %collective-permute-start.30 = (bf16[2,128,512]{2,1,0:T(8,128)(2,1)S(1)}, bf16[2,128,512]{2,1,0:T(8,128)(2,1)S(1)}, u32[]{:S(2)}, u32[]{:S(2)}) collective-permute-start(bf16[2,128,512]{2,1,0:T(8,128)(2,1)S(1)} %add_convert_fusion.1), channel_id=1, source_target_pairs={{0,2},{2,0},{4,6},{6,4},{8,10},{10,8},{12,14},{14,12},{1,3},{3,1},... | collective-permute-start | bytes 786440 | tf_op jit(solution)/shard_map/ppermute | solution.py:275
  147.3 15.4 %collective-permute-start.23 = (bf16[2,128,512]{2,1,0:T(8,128)(2,1)S(1)}, bf16[2,128,512]{2,1,0:T(8,128)(2,1)S(1)}, u32[]{:S(2)}, u32[]{:S(2)}) collective-permute-start(bf16[2,128,512]{2,1,0:T(8,128)(2,1)S(1)} %add_convert_fusion.6), channel_id=1, source_target_pairs={{0,14},{2,4},{4,2},{6,8},{8,6},{10,12},{12,10},{14,0},{1,15},{3,5}... | collective-permute-start | bytes 786440 | tf_op jit(solution)/shard_map/ppermute | solution.py:275
  151.5 14.3 %collective-permute-start.20 = (bf16[2,128,512]{2,1,0:T(8,128)(2,1)S(1)}, bf16[2,128,512]{2,1,0:T(8,128)(2,1)S(1)}, u32[]{:S(2)}, u32[]{:S(2)}) collective-permute-start(bf16[2,128,512]{2,1,0:T(8,128)(2,1)S(1)} %add_convert_fusion.8), channel_id=1, source_target_pairs={{0,14},{2,4},{4,2},{6,8},{8,6},{10,12},{12,10},{14,0},{1,15},{3,5}... | collective-permute-start | bytes 786440 | tf_op jit(solution)/shard_map/ppermute | solution.py:276
  158.5 9.6 %collective-permute-start.31 = (bf16[2,128,512]{2,1,0:T(8,128)(2,1)S(1)}, bf16[2,128,512]{2,1,0:T(8,128)(2,1)S(1)}, u32[]{:S(2)}, u32[]{:S(2)}) collective-permute-start(bf16[2,128,512]{2,1,0:T(8,128)(2,1)S(1)} %add_convert_fusion), channel_id=1, source_target_pairs={{0,14},{2,4},{4,2},{6,8},{8,6},{10,12},{12,10},{14,0},{1,15},{3,5}... | collective-permute-start | bytes 786440 | tf_op jit(solution)/shard_map/ppermute | solution.py:277
  162.8 8.0 %collective-permute-start.24 = (bf16[2,128,512]{2,1,0:T(8,128)(2,1)S(1)}, bf16[2,128,512]{2,1,0:T(8,128)(2,1)S(1)}, u32[]{:S(2)}, u32[]{:S(2)}) collective-permute-start(bf16[2,128,512]{2,1,0:T(8,128)(2,1)S(1)} %add_convert_fusion.5), channel_id=1, source_target_pairs={{0,2},{2,0},{4,6},{6,4},{8,10},{10,8},{12,14},{14,12},{1,3},{3,1},... | collective-permute-start | bytes 786440 | tf_op jit(solution)/shard_map/ppermute | solution.py:276
  171.1 5.7 %collective-permute-start.32 = (bf16[2,128,512]{2,1,0:T(8,128)(2,1)S(1)}, bf16[2,128,512]{2,1,0:T(8,128)(2,1)S(1)}, u32[]{:S(2)}, u32[]{:S(2)}) collective-permute-start(bf16[2,128,512]{2,1,0:T(8,128)(2,1)S(1)} %get-tuple-element.51), channel_id=1, source_target_pairs={{0,1},{1,0},{2,3},{3,2},{4,5},{5,4},{6,7},{7,6},{8,9},{9,8},{10,11... | collective-permute-start | bytes 786440 | tf_op jit(solution)/shard_map/ppermute | solution.py:286
  (22 other events, 109.6 us)

commit v3 on v2

--- a/solution.py
+++ b/solution.py
@@ -20,7 +20,7 @@
 HEADS = HALF // HEAD_DIM
 NEAR = 256
 GROWS = 4 * HEADS
-SEND_ORDER = [11, 12, 5, 4, 14, 13, 2, 3, 9, 10, 7, 6, 15, 1, 8, 0]
+ROUNDS = ((0,), (1,), (-1, -2), (2, 3), (-3, -4))
 FKEYS = FAR * BLOCK
 SCALE = 1.0 / math.sqrt(HEAD_DIM)
 EXP_SCALE = SCALE * math.log2(math.e)
@@ -40,12 +40,22 @@
     return lax.dot_general(a, b, (((0,), (0,)), ((), ())), preferred_element_type=F32)
 
 
+def at_step(chain, step):
+    return chain * NY + (-step if chain else step) % NY
+
+
 def attend_kernel(*refs):
     pos, far_own, far_peer, qdo_own, qdo_peer, glob = refs[:6]
-    sources = refs[6:22]
-    outputs = refs[22:26]
-    parts = refs[26:40]
-    slots, near, fgrad, gwide, res_own, res_peer, base, gglob, spare, table, in_sem, out_sem = refs[40:]
+    arrays = refs[6:16]
+    outputs = refs[16:20]
+    parts = refs[20:28]
+    slots, near, fgrad, gwide, res_own, res_peer, base, gglob, spare, table, in_sem, out_sem = refs[28:]
+    sources = [None] * (2 * NY)
+    for chain in range(2):
+        for round_, steps in enumerate(ROUNDS):
+            for i, step in enumerate(steps):
+                array = arrays[chain * len(ROUNDS) + round_]
+                sources[at_step(chain, step)] = array.at[i] if len(steps) > 1 else array
     my_y, my_c, my_w, my_sign = pos[0], pos[1], pos[2], pos[3]
     for who, far in enumerate((far_own, far_peer)):
         for row in range(BLK):
@@ -159,35 +169,40 @@
     send(gglob, outputs[3])
     send(res_peer, outputs[1])
     send(res_own, outputs[0])
-    for source in SEND_ORDER:
-        for kind in range(2):
-            for inner in range(BLK):
-                rows = slice(inner * BLOCK, (inner + 1) * BLOCK)
-                value = None
-                for who in range(2):
-                    code = table[who, source]
-                    slot = lax.shift_right_logical(code, 1)
-                    at = pl.ds(pl.multiple_of(slot * BLOCK, BLOCK), BLOCK)
-                    here = (lax.bitwise_and(code, 1) == inner).astype(F32)
-                    term = fgrad[kind, who, at, :].astype(F32) * here
-                    value = term if value is None else value + term
-                if source % NY == 0:
-                    base[source // NY, kind, rows, :] += value
-                else:
-                    spare[source - 1 - source // NY, kind, rows, :] = value.astype(BF16)
-        if source % NY:
-            index = source - 1 - source // NY
-            send(spare.at[index], parts[index])
+    for round_ in (4, 3, 2, 1, 0):
+        for chain in (1, 0):
+            for step in ROUNDS[round_]:
+                source = at_step(chain, step)
+                for kind in range(2):
+                    for inner in range(BLK):
+                        rows = slice(inner * BLOCK, (inner + 1) * BLOCK)
+                        value = None
+                        for who in range(2):
+                            code = table[who, source]
+                            slot = lax.shift_right_logical(code, 1)
+                            at = pl.ds(pl.multiple_of(slot * BLOCK, BLOCK), BLOCK)
+                            here = (lax.bitwise_and(code, 1) == inner).astype(F32)
+                            term = fgrad[kind, who, at, :].astype(F32) * here
+                            value = term if value is None else value + term
+                        if round_ == 0:
+                            base[chain, kind, rows, :] += value
+                        else:
+                            spare[source, kind, rows, :] = value.astype(BF16)
+                if round_:
+                    part = parts[chain * 4 + round_ - 1]
+                    where = part.at[ROUNDS[round_].index(step)] if round_ > 1 else part
+                    send(spare.at[source], where)
     send(base, outputs[2])
     for copy in copies:
         copy.wait()
 
 
-def attend(pos, far_own, far_peer, qdo_own, qdo_peer, glob, sources):
+def attend(pos, far_own, far_peer, qdo_own, qdo_peer, glob, arrays):
     smem = pl.BlockSpec(memory_space=pltpu.SMEM)
     vmem = pl.BlockSpec(memory_space=pltpu.VMEM)
     anywhere = pl.BlockSpec(memory_space=pl.ANY)
     piece = jax.ShapeDtypeStruct((2, TOK, HALF), BF16)
+    double = jax.ShapeDtypeStruct((2, 2, TOK, HALF), BF16)
     return pl.pallas_call(
         attend_kernel,
         out_shape=[
@@ -196,9 +211,9 @@
             jax.ShapeDtypeStruct((2, 2, TOK, HALF), F32),
             jax.ShapeDtypeStruct((WINDOWS, GROWS, HEAD_DIM), BF16),
         ]
-        + [piece] * 14,
-        in_specs=[smem] * 3 + [vmem] * 3 + [anywhere] * 16,
-        out_specs=[anywhere] * 18,
+        + [piece, double, double, double] * 2,
+        in_specs=[smem] * 3 + [vmem] * 3 + [anywhere] * 10,
+        out_specs=[anywhere] * 12,
         scratch_shapes=[
             pltpu.VMEM((2, 2, BLK * FKEYS, HALF), BF16),
             pltpu.VMEM((2, 2, NEAR, HALF), BF16),
@@ -208,7 +223,7 @@
             pltpu.VMEM((2, TOK, HALF), BF16),
             pltpu.VMEM((2, 2, TOK, HALF), F32),
             pltpu.VMEM((WINDOWS, GROWS, HEAD_DIM), BF16),
-            pltpu.VMEM((2 * NY - 2, 2, TOK, HALF), BF16),
+            pltpu.VMEM((2 * NY, 2, TOK, HALF), BF16),
             pltpu.SMEM((2, 2 * NY), jnp.int32),
             pltpu.SemaphoreType.DMA((2 + 4 * NY,)),
             pltpu.SemaphoreType.DMA((2 + 2 * NY,)),
@@ -217,7 +232,7 @@
         cost_estimate=pl.CostEstimate(
             flops=1_200_000_000, bytes_accessed=12_000_000, transcendentals=800_000
         ),
-    )(pos, far_own, far_peer, qdo_own, qdo_peer, glob, *sources)
+    )(pos, far_own, far_peer, qdo_own, qdo_peer, glob, *arrays)
 
 
 EVEN = [(i, i ^ 1) for i in range(NY)]
@@ -245,36 +260,43 @@
 
     kv_own, kv_send = split(key_rows, value_rows)
     qdo_own, qdo_send = split(query_rows, out_grad)
-    a, b = {0: kv_own}, {0: swap(kv_send)}
+    moves = (even, odd), (odd, even)
+    a, b = [kv_own], [swap(kv_send)]
     row = jnp.concatenate([a[0][:, 0], b[0][:, 0]]).reshape(GROWS, HEAD_DIM)
+    chains = list(zip((a, b), moves))
+    for held, (first, second) in chains:
+        held.append(first(held[0]))
+    row, a[1], b[1] = lax.optimization_barrier((row, a[1], b[1]))
     glob = lax.all_to_all(
         jnp.broadcast_to(row, (WINDOWS, GROWS, HEAD_DIM)), ("x", "z"), 0, 0, tiled=True
     )
-    a[1], b[-1] = even(a[0]), odd(b[0])
-    a[-1], b[1] = odd(a[0]), even(b[0])
-    a[-2], b[2] = odd(a[1]), even(b[-1])
-    a[2], b[-2] = even(a[-1]), odd(b[1])
-    a[3], b[-3] = even(a[-2]), odd(b[2])
+    for held, (first, second) in chains:
+        held.append(second(jnp.stack(held)))
+    for held, (first, second) in chains:
+        held.append(first(held[2]))
+    glob, a[3], b[3] = lax.optimization_barrier((glob, a[3], b[3]))
     qdo_peer = swap(qdo_send)
     far_peer = swap(far_blocks)
-    glob, a[2], a[3], b[-2], b[-3] = lax.optimization_barrier((glob, a[2], a[3], b[-2], b[-3]))
-    a[-3], b[3] = odd(a[2]), even(b[-2])
-    a[-4], b[4] = odd(a[3]), even(b[-3])
-    sources = [x[r] if r in x else x[r - NY] for x in (a, b) for r in range(NY)]
+    for held, (first, second) in chains:
+        held.append(second(held[3]))
     pos = jnp.stack([my_y, my_c, my_w, 1 - 2 * (my_y % 2)]).astype(jnp.int32)
     res_own, res_peer, base, gglob, *parts = attend(
-        pos, far_blocks, far_peer, qdo_own, qdo_peer, glob, sources
+        pos, far_blocks, far_peer, qdo_own, qdo_peer, glob, a + b
     )
-    a = {r: parts[r % NY - 1] for r in range(-4, 4) if r}
-    b = {r: parts[NY - 2 + r % NY] for r in range(-3, 5) if r}
+    chains = [(parts[4:], moves[1]), (parts[:4], moves[0])]
+    back = [second(terms[3]) for terms, (first, second) in chains]
+    gglob, *back = lax.optimization_barrier((gglob, *back))
     gback = lax.all_to_all(gglob, ("x", "z"), 0, 0, tiled=True)
-    b[-2], a[2] = plus(b[-2], even(b[3])), plus(a[2], odd(a[-3]))
-    b[-3], a[3] = plus(b[-3], even(b[4])), plus(a[3], odd(a[-4]))
-    b[1], a[-1] = plus(b[1], odd(b[-2])), plus(a[-1], even(a[2]))
-    b[2], a[-2] = plus(b[2], odd(b[-3])), plus(a[-2], even(a[3]))
-    b[-1], a[1] = plus(b[-1], even(b[2])), plus(a[1], odd(a[-2]))
-    far_own = odd(a[-1]), even(a[1])
-    far_peer = even(b[1]), odd(b[-1])
+    back = [
+        first(plus(terms[2], got)) for got, (terms, (first, second)) in zip(back, chains)
+    ]
+    back = [
+        second(plus(terms[1], got)) for got, (terms, (first, second)) in zip(back, chains)
+    ]
+    last = [
+        first(plus(terms[0], got[1])) for got, (terms, (first, second)) in zip(back, chains)
+    ]
+    far_peer, far_own = [(x[0], y) for x, y in zip(back, last)]
     gsum = jnp.sum(gback.astype(F32), axis=0).reshape(2, 2, 1, HALF)
     res_back = swap(res_peer)
     first_row = lax.broadcasted_iota(jnp.int32, (1, TOK, 1), 1) == 0

time: 179 us -> 170 us (0.950)
  starting transfers between devices: 126 us -> 84 us
  waiting for transfers between devices: 21.6 us -> 50.4 us
  other arithmetic: 6.11 us -> 10.2 us
    ppermute x29 -> x17, starting transfers between devices: 87.8 us -> 49.6 us  [the longest x1 8.79 us: per_device(): a, b = ([kv_own], [swap(kv_send)])]
    ppermute x29 -> x17, waiting for transfers between devices: 21.4 us -> 41.8 us  [the longest x2 11 us: per_device(): back = [second(terms[3]) for terms, (first, second) in chains]]
    all_to_all x1, waiting for transfers between devices: 0.01 us -> 8.48 us  [per_device(): lax.all_to_all(jnp.broadcast_to(row, (WINDOWS, GROWS, HEAD_DIM)), ('x', '...]
    all_to_all x1, starting transfers between devices: 9.7 us -> 3.98 us  [per_device(): gback = lax.all_to_all(gglob, ('x', 'z'), 0, 0, tiled=True)]
    convert_element_type x10 -> x6, other arithmetic: 0.68 us -> 3.68 us  [plus(): return (a.astype(F32) + b.astype(F32)).astype(BF16)]
    ppermute x1, starting transfers between devices: 4.54 us -> 6.99 us  [per_device(): peer_grad = swap(finish(1, far_peer))]
    ppermute x1, starting transfers between devices: 7.22 us -> 5.42 us  [per_device(): res_back = swap(res_peer)]
  transfers between devices with their start and end apart: 35 -> 23, of which waited for: 10 -> 13; matrix products, arithmetic and copies ran while one was open for 3% -> 5% of each run, Pallas kernels for 0% -> 0%
where the time goes in v3:
time: 170 us; the launch traced here: 168 us
  starting transfers between devices  84 us (49%)
  waiting for transfers between devices  50.4 us (30%)
  Pallas kernels  18.7 us (11%)
  other arithmetic  10.2 us (6%)
  local copies, waits for them, and re-layouts  3.89 us (2%)
    pallas_call x1, Pallas kernels, attend(): pl.pallas_call(attend_kernel, out_shape=[piece, piece, jax.ShapeDtypeStru...  18.7 us
    ppermute x2, waiting for transfers between devices, per_device(): back = [second(terms[3]) for terms, (first, second) in chains]  11 us
    ppermute x2, waiting for transfers between devices, per_device(): held.append(second(jnp.stack(held)))  10.7 us
    all_to_all x1, starting transfers between devices, per_device(): lax.all_to_all(jnp.broadcast_to(row, (WINDOWS, GROWS, HEAD_DIM)), ('x', '...  9.75 us
    ppermute x2, waiting for transfers between devices, per_device(): held.append(first(held[0]))  9.01 us
    ppermute x1, starting transfers between devices, per_device(): a, b = ([kv_own], [swap(kv_send)])  8.79 us
    all_to_all x1, waiting for transfers between devices, per_device(): lax.all_to_all(jnp.broadcast_to(row, (WINDOWS, GROWS, HEAD_DIM)), ('x', '...  8.48 us
    ppermute x1, starting transfers between devices, per_device(): peer_grad = swap(finish(1, far_peer))  6.99 us
  transfers between devices with their start and end apart: 23, of which 13 were waited for; matrix products, arithmetic and copies ran while one was open for 5% of the time, Pallas kernels for 0%

profile of v3, /device:TPU:1, one launch (start us, length us, event | category | flops | bytes accessed | tf_op | source)
XLA Modules:
  0.0 168.5 jit_solution(18354816874632018811)
XLA Ops:
  0.6 1.0 select_bitcast_fusion.2
  1.8 8.8 %collective-permute-start.2 = (bf16[2,128,512]{2,1,0:T(8,128)(2,1)S(1)}, bf16[2,128,512]{2,1,0:T(8,128)(2,1)S(1)}, u32[]{:S(2)}, u32[]{:S(2)}) collective-permute-start(bf16[2,128,512]{2,1,0:T(8,128)(2,1)S(1)} %pad_maximum_fusion.5), channel_id=1, source_target_pairs={{0,1},{1,0},{2,3},{3,2},{4,5},{5,4},{6,7},{7,6},{8,9},{9,8},{10,11... | collective-permute-start | bytes 786440 | tf_op jit(solution)/shard_map/ppermute | solution.py:264
  10.6 1.9 %collective-permute-start.3 = (bf16[2,128,512]{2,1,0:T(8,128)(2,1)S(1)}, bf16[2,128,512]{2,1,0:T(8,128)(2,1)S(1)}, u32[]{:S(2)}, u32[]{:S(2)}) collective-permute-start(bf16[2,128,512]{2,1,0:T(8,128)(2,1)S(1)} %get-tuple-element.57.refs_6_), channel_id=1, source_target_pairs={{0,2},{2,0},{4,6},{6,4},{8,10},{10,8},{12,14},{14,12},{1,3},{3,1},... | collective-permute-start | bytes 786440 | tf_op jit(solution)/shard_map/ppermute | solution.py:268
  12.6 1.9 %collective-permute-start.4 = (bf16[2,128,512]{2,1,0:T(8,128)(2,1)S(1)}, bf16[2,128,512]{2,1,0:T(8,128)(2,1)S(1)}, u32[]{:S(2)}, u32[]{:S(2)}) collective-permute-start(bf16[2,128,512]{2,1,0:T(8,128)(2,1)S(1)} %collective-permute-done.2.refs_11_), channel_id=1, source_target_pairs={{0,14},{2,4},{4,2},{6,8},{8,6},{10,12},{12,10},{14,0},{1,15},{3,5}... | collective-permute-start | bytes 786440 | tf_op jit(solution)/shard_map/ppermute | solution.py:268
  14.6 5.9 %collective-permute-done.3.refs_7_ = bf16[2,128,512]{2,1,0:T(8,128)(2,1)S(1)} collective-permute-done((bf16[2,128,512]{2,1,0:T(8,128)(2,1)S(1)}, bf16[2,128,512]{2,1,0:T(8,128)(2,1)S(1)}, u32[]{:S(2)}, u32[]{:S(2)}) %collective-permute-start.3) | collective-permute-done | bytes 262176 | tf_op jit(solution)/shard_map/ppermute | solution.py:268
  20.4 3.2 %collective-permute-done.4.refs_12_ = bf16[2,128,512]{2,1,0:T(8,128)(2,1)S(1)} collective-permute-done((bf16[2,128,512]{2,1,0:T(8,128)(2,1)S(1)}, bf16[2,128,512]{2,1,0:T(8,128)(2,1)S(1)}, u32[]{:S(2)}, u32[]{:S(2)}) %collective-permute-start.4) | collective-permute-done | bytes 262176 | tf_op jit(solution)/shard_map/ppermute | solution.py:268
  23.7 0.7 copy-done.4
  24.3 1.9 %collective-permute-start.7 = (bf16[2,2,128,512]{3,2,1,0:T(8,128)(2,1)S(1)}, bf16[2,2,128,512]{3,2,1,0:T(8,128)(2,1)S(1)}, u32[]{:S(2)}, u32[]{:S(2)}) collective-permute-start(bf16[2,2,128,512]{3,2,1,0:T(8,128)(2,1)S(1)} %pad_maximum_fusion.1), channel_id=1, source_target_pairs={{0,2},{2,0},{4,6},{6,4},{8,10},{10,8},{12,14},{14,12},{1,3},{3,1},... | collective-permute-start | bytes 1572872 | tf_op jit(solution)/shard_map/ppermute | solution.py:274
  26.3 2.3 %collective-permute-start.5 = (bf16[2,2,128,512]{3,2,1,0:T(8,128)(2,1)S(1)}, bf16[2,2,128,512]{3,2,1,0:T(8,128)(2,1)S(1)}, u32[]{:S(2)}, u32[]{:S(2)}) collective-permute-start(bf16[2,2,128,512]{3,2,1,0:T(8,128)(2,1)S(1)} %pad_maximum_fusion), channel_id=1, source_target_pairs={{0,14},{2,4},{4,2},{6,8},{8,6},{10,12},{12,10},{14,0},{1,15},{3,5}... | collective-permute-start | bytes 1572872 | tf_op jit(solution)/shard_map/ppermute | solution.py:274
  28.6 10.3 %collective-permute-done.7.refs_13_ = bf16[2,2,128,512]{3,2,1,0:T(8,128)(2,1)S(1)} collective-permute-done((bf16[2,2,128,512]{3,2,1,0:T(8,128)(2,1)S(1)}, bf16[2,2,128,512]{3,2,1,0:T(8,128)(2,1)S(1)}, u32[]{:S(2)}, u32[]{:S(2)}) %collective-permute-start.7) | collective-permute-done | bytes 524320 | tf_op jit(solution)/shard_map/ppermute | solution.py:274
  38.9 2.3 %collective-permute-start.8 = (bf16[2,2,128,512]{3,2,1,0:T(8,128)(2,1)S(1)}, bf16[2,2,128,512]{3,2,1,0:T(8,128)(2,1)S(1)}, u32[]{:S(2)}, u32[]{:S(2)}) collective-permute-start(bf16[2,2,128,512]{3,2,1,0:T(8,128)(2,1)S(1)} %collective-permute-done.7.refs_13_), channel_id=1, source_target_pairs={{0,14},{2,4},{4,2},{6,8},{8,6},{10,12},{12,10},{14,0},{1,15},{3,5}... | collective-permute-start | bytes 1572872 | tf_op jit(solution)/shard_map/ppermute | solution.py:276
  41.7 2.4 %collective-permute-start.6 = (bf16[2,2,128,512]{3,2,1,0:T(8,128)(2,1)S(1)}, bf16[2,2,128,512]{3,2,1,0:T(8,128)(2,1)S(1)}, u32[]{:S(2)}, u32[]{:S(2)}) collective-permute-start(bf16[2,2,128,512]{3,2,1,0:T(8,128)(2,1)S(1)} %collective-permute-done.5.refs_8_), channel_id=1, source_target_pairs={{0,2},{2,0},{4,6},{6,4},{8,10},{10,8},{12,14},{14,12},{1,3},{3,1},... | collective-permute-start | bytes 1572872 | tf_op jit(solution)/shard_map/ppermute | solution.py:276
  44.1 0.7 broadcast_in_dim.38
  44.7 9.8 %all-to-all-start = ((bf16[32,16,128]{2,1,0:T(8,128)(2,1)}), bf16[32,16,128]{2,1,0:T(8,128)(2,1)S(1)}, u32[]{:S(2)}, u32[]{:S(2)}) async-start(bf16[32,16,128]{2,1,0:T(8,128)(2,1)} %broadcast_in_dim.38), calls=%async_computation | async-start | bytes 262144 | tf_op jit(solution)/shard_map/all_to_all | solution.py:270
  54.5 0.7 select_bitcast_fusion.5
  55.2 8.5 %all-to-all-done.refs_5_ = bf16[32,16,128]{2,1,0:T(8,128)(2,1)S(1)} async-done(((bf16[32,16,128]{2,1,0:T(8,128)(2,1)}), bf16[32,16,128]{2,1,0:T(8,128)(2,1)S(1)}, u32[]{:S(2)}, u32[]{:S(2)}) %all-to-all-start) | async-done | bytes 131104 | tf_op jit(solution)/shard_map/all_to_all | solution.py:270
  63.7 3.5 %collective-permute-start.10 = (bf16[2,2,128,512]{3,2,1,0:T(8,128)(2,1)S(1)}, bf16[2,2,128,512]{3,2,1,0:T(8,128)(2,1)S(1)}, u32[]{:S(2)}, u32[]{:S(2)}) collective-permute-start(bf16[2,2,128,512]{3,2,1,0:T(8,128)(2,1)S(1)} %collective-permute-done.8.refs_14_), channel_id=1, source_target_pairs={{0,2},{2,0},{4,6},{6,4},{8,10},{10,8},{12,14},{14,12},{1,3},{3,1},... | collective-permute-start | bytes 1572872 | tf_op jit(solution)/shard_map/ppermute | solution.py:281
  67.2 3.3 %collective-permute-start.9 = (bf16[2,2,128,512]{3,2,1,0:T(8,128)(2,1)S(1)}, bf16[2,2,128,512]{3,2,1,0:T(8,128)(2,1)S(1)}, u32[]{:S(2)}, u32[]{:S(2)}) collective-permute-start(bf16[2,2,128,512]{3,2,1,0:T(8,128)(2,1)S(1)} %collective-permute-done.6.refs_9_), channel_id=1, source_target_pairs={{0,14},{2,4},{4,2},{6,8},{8,6},{10,12},{12,10},{14,0},{1,15},{3,5}... | collective-permute-start | bytes 1572872 | tf_op jit(solution)/shard_map/ppermute | solution.py:281
  70.5 1.0 select_bitcast_fusion.4
  71.6 6.3 %collective-permute-start.1 = (bf16[2,128,512]{2,1,0:T(8,128)(2,1)S(1)}, bf16[2,128,512]{2,1,0:T(8,128)(2,1)S(1)}, u32[]{:S(2)}, u32[]{:S(2)}) collective-permute-start(bf16[2,128,512]{2,1,0:T(8,128)(2,1)S(1)} %pad_maximum_fusion.4), channel_id=1, source_target_pairs={{0,1},{1,0},{2,3},{3,2},{4,5},{5,4},{6,7},{7,6},{8,9},{9,8},{10,11... | collective-permute-start | bytes 786440 | tf_op jit(solution)/shard_map/ppermute | solution.py:278
  78.0 1.9 %collective-permute-start = (s32[2,8]{1,0:T(2,128)S(1)}, s32[2,8]{1,0:T(2,128)S(1)}, u32[]{:S(2)}, u32[]{:S(2)}) collective-permute-start(s32[2,8]{1,0:T(2,128)S(1)} %copy-done.22), channel_id=1, source_target_pairs={{0,1},{1,0},{2,3},{3,2},{4,5},{5,4},{6,7},{7,6},{8,9},{9,8},{10,11... | collective-permute-start | bytes 200 | tf_op jit(solution)/shard_map/ppermute | solution.py:279
  79.9 0.7 pad_maximum_fusion.3.refs_3_
  80.7 0.7 pad_add_fusion.refs_0_
  82.2 0.8 copy-done.10
  83.0 18.7 %shard_map.84 = (bf16[2,128,512]{2,1,0:T(8,128)(2,1)}, bf16[2,128,512]{2,1,0:T(8,128)(2,1)}, f32[2,2,128,512]{3,2,1,0:T(8,128)}, bf16[32,16,128]{2,1,0:T(8,128)(...) custom-call(s32[4]{0:T(128)} %pad_add_fusion.refs_0_, ...), custom_call_target="tpu_custom_call" | custom-call | flops 1200000000 | bytes 12000000 | tf_op jit(solution)/shard_map/pallas_call | solution.py:206
  101.7 1.9 %collective-permute-start.12 = (bf16[2,2,128,512]{3,2,1,0:T(8,128)(2,1)}, bf16[2,2,128,512]{3,2,1,0:T(8,128)(2,1)S(1)}, u32[]{:S(2)}, u32[]{:S(2)}) collective-permute-start(bf16[2,2,128,512]{3,2,1,0:T(8,128)(2,1)} %get-tuple-element.37), channel_id=1, source_target_pairs={{0,2},{2,0},{4,6},{6,4},{8,10},{10,8},{12,14},{14,12},{1,3},{3,1},... | collective-permute-start | bytes 1572872 | tf_op jit(solution)/shard_map/ppermute | solution.py:287
  103.7 3.4 %collective-permute-start.13 = (bf16[2,2,128,512]{3,2,1,0:T(8,128)(2,1)}, bf16[2,2,128,512]{3,2,1,0:T(8,128)(2,1)S(1)}, u32[]{:S(2)}, u32[]{:S(2)}) collective-permute-start(bf16[2,2,128,512]{3,2,1,0:T(8,128)(2,1)} %get-tuple-element.38), channel_id=1, source_target_pairs={{0,14},{2,4},{4,2},{6,8},{8,6},{10,12},{12,10},{14,0},{1,15},{3,5}... | collective-permute-start | bytes 1572872 | tf_op jit(solution)/shard_map/ppermute | solution.py:287
  107.1 7.9 %collective-permute-done.12 = bf16[2,2,128,512]{3,2,1,0:T(8,128)(2,1)S(1)} collective-permute-done((bf16[2,2,128,512]{3,2,1,0:T(8,128)(2,1)}, bf16[2,2,128,512]{3,2,1,0:T(8,128)(2,1)S(1)}, u32[]{:S(2)}, u32[]{:S(2)}) %collective-permute-start.12) | collective-permute-done | bytes 524320 | tf_op jit(solution)/shard_map/ppermute | solution.py:287
  114.9 3.1 %collective-permute-done.13 = bf16[2,2,128,512]{3,2,1,0:T(8,128)(2,1)S(1)} collective-permute-done((bf16[2,2,128,512]{3,2,1,0:T(8,128)(2,1)}, bf16[2,2,128,512]{3,2,1,0:T(8,128)(2,1)S(1)}, u32[]{:S(2)}, u32[]{:S(2)}) %collective-permute-start.13) | collective-permute-done | bytes 524320 | tf_op jit(solution)/shard_map/ppermute | solution.py:287
  118.1 1.2 add_convert_fusion.1
  119.3 3.5 %collective-permute-start.17 = (bf16[2,2,128,512]{3,2,1,0:T(8,128)(2,1)S(1)}, bf16[2,2,128,512]{3,2,1,0:T(8,128)(2,1)S(1)}, u32[]{:S(2)}, u32[]{:S(2)}) collective-permute-start(bf16[2,2,128,512]{3,2,1,0:T(8,128)(2,1)S(1)} %add_convert_fusion.1), channel_id=1, source_target_pairs={{0,14},{2,4},{4,2},{6,8},{8,6},{10,12},{12,10},{14,0},{1,15},{3,5}... | collective-permute-start | bytes 1572872 | tf_op jit(solution)/shard_map/ppermute | solution.py:291
  123.0 2.1 %collective-permute-start.14 = (bf16[2,2,128,512]{3,2,1,0:T(8,128)(2,1)S(1)}, bf16[2,2,128,512]{3,2,1,0:T(8,128)(2,1)S(1)}, u32[]{:S(2)}, u32[]{:S(2)}) collective-permute-start(bf16[2,2,128,512]{3,2,1,0:T(8,128)(2,1)S(1)} %add_convert_fusion.3), channel_id=1, source_target_pairs={{0,2},{2,0},{4,6},{6,4},{8,10},{10,8},{12,14},{14,12},{1,3},{3,1},... | collective-permute-start | bytes 1572872 | tf_op jit(solution)/shard_map/ppermute | solution.py:291
  125.0 5.4 %collective-permute-start.11 = (bf16[2,128,512]{2,1,0:T(8,128)(2,1)S(1)}, bf16[2,128,512]{2,1,0:T(8,128)(2,1)S(1)}, u32[]{:S(2)}, u32[]{:S(2)}) collective-permute-start(bf16[2,128,512]{2,1,0:T(8,128)(2,1)S(1)} %copy-done.24), channel_id=1, source_target_pairs={{0,1},{1,0},{2,3},{3,2},{4,5},{5,4},{6,7},{7,6},{8,9},{9,8},{10,11... | collective-permute-start | bytes 786440 | tf_op jit(solution)/shard_map/ppermute | solution.py:301
  130.5 2.1 %collective-permute-done.17 = bf16[2,2,128,512]{3,2,1,0:T(8,128)(2,1)S(1)} collective-permute-done((bf16[2,2,128,512]{3,2,1,0:T(8,128)(2,1)S(1)}, bf16[2,2,128,512]{3,2,1,0:T(8,128)(2,1)S(1)}, u32[]{:S(2)}, u32[]{:S(2)}) %collective-permute-start.17) | collective-permute-done | bytes 524320 | tf_op jit(solution)/shard_map/ppermute | solution.py:291
  132.8 1.9 %collective-permute-start.18 = (bf16[2,2,128,512]{3,2,1,0:T(8,128)(2,1)S(1)}, bf16[2,2,128,512]{3,2,1,0:T(8,128)(2,1)S(1)}, u32[]{:S(2)}, u32[]{:S(2)}) collective-permute-start(bf16[2,2,128,512]{3,2,1,0:T(8,128)(2,1)S(1)} %add_convert_fusion), channel_id=1, source_target_pairs={{0,2},{2,0},{4,6},{6,4},{8,10},{10,8},{12,14},{14,12},{1,3},{3,1},... | collective-permute-start | bytes 1572872 | tf_op jit(solution)/shard_map/ppermute | solution.py:294
  135.1 3.3 %collective-permute-start.15 = (bf16[2,2,128,512]{3,2,1,0:T(8,128)(2,1)S(1)}, bf16[2,2,128,512]{3,2,1,0:T(8,128)(2,1)S(1)}, u32[]{:S(2)}, u32[]{:S(2)}) collective-permute-start(bf16[2,2,128,512]{3,2,1,0:T(8,128)(2,1)S(1)} %add_convert_fusion.2), channel_id=1, source_target_pairs={{0,14},{2,4},{4,2},{6,8},{8,6},{10,12},{12,10},{14,0},{1,15},{3,5}... | collective-permute-start | bytes 1572872 | tf_op jit(solution)/shard_map/ppermute | solution.py:294
  138.4 0.7 slice_bitcast_fusion.6
  139.2 4.0 %all-to-all-start.1 = ((bf16[32,16,128]{2,1,0:T(8,128)(2,1)}), bf16[32,16,128]{2,1,0:T(8,128)(2,1)S(1)}, u32[]{:S(2)}, u32[]{:S(2)}) async-start(bf16[32,16,128]{2,1,0:T(8,128)(2,1)} %get-tuple-element.41), calls=%async_computation.1 | async-start | bytes 262144 | tf_op jit(solution)/shard_map/all_to_all | solution.py:289
  143.2 3.9 %collective-permute-done.18 = bf16[2,2,128,512]{3,2,1,0:T(8,128)(2,1)S(1)} collective-permute-done((bf16[2,2,128,512]{3,2,1,0:T(8,128)(2,1)S(1)}, bf16[2,2,128,512]{3,2,1,0:T(8,128)(2,1)S(1)}, u32[]{:S(2)}, u32[]{:S(2)}) %collective-permute-start.18) | collective-permute-done | bytes 524320 | tf_op jit(solution)/shard_map/ppermute | solution.py:294
  147.1 1.0 fusion
  148.1 2.6 %collective-permute-start.19 = (bf16[2,128,512]{2,1,0:T(8,128)(2,1)S(1)}, bf16[2,128,512]{2,1,0:T(8,128)(2,1)S(1)}, u32[]{:S(2)}, u32[]{:S(2)}) collective-permute-start(bf16[2,128,512]{2,1,0:T(8,128)(2,1)S(1)} %fusion), channel_id=1, source_target_pairs={{0,14},{2,4},{4,2},{6,8},{8,6},{10,12},{12,10},{14,0},{1,15},{3,5}... | collective-permute-start | bytes 786440 | tf_op jit(solution)/shard_map/ppermute | solution.py:297
  150.7 1.0 fusion.1
  151.7 2.7 %collective-permute-start.16 = (bf16[2,128,512]{2,1,0:T(8,128)(2,1)S(1)}, bf16[2,128,512]{2,1,0:T(8,128)(2,1)S(1)}, u32[]{:S(2)}, u32[]{:S(2)}) collective-permute-start(bf16[2,128,512]{2,1,0:T(8,128)(2,1)S(1)} %fusion.1), channel_id=1, source_target_pairs={{0,2},{2,0},{4,6},{6,4},{8,10},{10,8},{12,14},{14,12},{1,3},{3,1},... | collective-permute-start | bytes 786440 | tf_op jit(solution)/shard_map/ppermute | solution.py:297
  154.5 2.3 %collective-permute-done.19 = bf16[2,128,512]{2,1,0:T(8,128)(2,1)S(1)} collective-permute-done((bf16[2,128,512]{2,1,0:T(8,128)(2,1)S(1)}, bf16[2,128,512]{2,1,0:T(8,128)(2,1)S(1)}, u32[]{:S(2)}, u32[]{:S(2)}) %collective-permute-start.19) | collective-permute-done | bytes 262176 | tf_op jit(solution)/shard_map/ppermute | solution.py:297
  156.7 2.4 %collective-permute-done.16 = bf16[2,128,512]{2,1,0:T(8,128)(2,1)S(1)} collective-permute-done((bf16[2,128,512]{2,1,0:T(8,128)(2,1)S(1)}, bf16[2,128,512]{2,1,0:T(8,128)(2,1)S(1)}, u32[]{:S(2)}, u32[]{:S(2)}) %collective-permute-start.16) | collective-permute-done | bytes 262176 | tf_op jit(solution)/shard_map/ppermute | solution.py:297
  159.4 7.0 %collective-permute-start.20 = (bf16[2,128,512]{2,1,0:T(8,128)(2,1)S(1)}, bf16[2,128,512]{2,1,0:T(8,128)(2,1)S(1)}, u32[]{:S(2)}, u32[]{:S(2)}) collective-permute-start(bf16[2,128,512]{2,1,0:T(8,128)(2,1)S(1)} %get-tuple-element.47), channel_id=1, source_target_pairs={{0,1},{1,0},{2,3},{3,2},{4,5},{5,4},{6,7},{7,6},{8,9},{9,8},{10,11... | collective-permute-start | bytes 786440 | tf_op jit(solution)/shard_map/ppermute | solution.py:308
  166.4 0.9 maximum_select_fusion
  167.6 0.9 maximum_select_fusion.2
  (85 shorter events, 3.0 us)
Async XLA Ops:
  0.6 1.1 copy-start.19
  1.8 10.8 %collective-permute-start.2 = (bf16[2,128,512]{2,1,0:T(8,128)(2,1)S(1)}, bf16[2,128,512]{2,1,0:T(8,128)(2,1)S(1)}, u32[]{:S(2)}, u32[]{:S(2)}) collective-permute-start(bf16[2,128,512]{2,1,0:T(8,128)(2,1)S(1)} %pad_maximum_fusion.5), channel_id=1, source_target_pairs={{0,1},{1,0},{2,3},{3,2},{4,5},{5,4},{6,7},{7,6},{8,9},{9,8},{10,11... | collective-permute-start | bytes 786440 | tf_op jit(solution)/shard_map/ppermute | solution.py:264
  10.6 13.0 %copy-start.1 = (bf16[2,128,512]{2,1,0:T(8,128)(2,1)}, bf16[2,128,512]{2,1,0:T(8,128)(2,1)S(1)}, u32[]{:S(2)}) copy-start(bf16[2,128,512]{2,1,0:T(8,128)(2,1)S(1)} %get-tuple-element.57.refs_6_) | copy-start | bytes 786436
  10.6 9.8 %collective-permute-start.3 = (bf16[2,128,512]{2,1,0:T(8,128)(2,1)S(1)}, bf16[2,128,512]{2,1,0:T(8,128)(2,1)S(1)}, u32[]{:S(2)}, u32[]{:S(2)}) collective-permute-start(bf16[2,128,512]{2,1,0:T(8,128)(2,1)S(1)} %get-tuple-element.57.refs_6_), channel_id=1, source_target_pairs={{0,2},{2,0},{4,6},{6,4},{8,10},{10,8},{12,14},{14,12},{1,3},{3,1},... | collective-permute-start | bytes 786440 | tf_op jit(solution)/shard_map/ppermute | solution.py:268
  12.6 11.1 %copy-start = (bf16[2,128,512]{2,1,0:T(8,128)(2,1)}, bf16[2,128,512]{2,1,0:T(8,128)(2,1)S(1)}, u32[]{:S(2)}) copy-start(bf16[2,128,512]{2,1,0:T(8,128)(2,1)S(1)} %collective-permute-done.2.refs_11_) | copy-start | bytes 786436
  12.6 11.0 %collective-permute-start.4 = (bf16[2,128,512]{2,1,0:T(8,128)(2,1)S(1)}, bf16[2,128,512]{2,1,0:T(8,128)(2,1)S(1)}, u32[]{:S(2)}, u32[]{:S(2)}) collective-permute-start(bf16[2,128,512]{2,1,0:T(8,128)(2,1)S(1)} %collective-permute-done.2.refs_11_), channel_id=1, source_target_pairs={{0,14},{2,4},{4,2},{6,8},{8,6},{10,12},{12,10},{14,0},{1,15},{3,5}... | collective-permute-start | bytes 786440 | tf_op jit(solution)/shard_map/ppermute | solution.py:268
  20.4 5.8 %copy-start.3 = (bf16[2,128,512]{2,1,0:T(8,128)(2,1)}, bf16[2,128,512]{2,1,0:T(8,128)(2,1)S(1)}, u32[]{:S(2)}) copy-start(bf16[2,128,512]{2,1,0:T(8,128)(2,1)S(1)} %collective-permute-done.3.refs_7_) | copy-start | bytes 786436
  23.6 0.7 copy-start.4
  24.3 14.5 %collective-permute-start.7 = (bf16[2,2,128,512]{3,2,1,0:T(8,128)(2,1)S(1)}, bf16[2,2,128,512]{3,2,1,0:T(8,128)(2,1)S(1)}, u32[]{:S(2)}, u32[]{:S(2)}) collective-permute-start(bf16[2,2,128,512]{3,2,1,0:T(8,128)(2,1)S(1)} %pad_maximum_fusion.1), channel_id=1, source_target_pairs={{0,2},{2,0},{4,6},{6,4},{8,10},{10,8},{12,14},{14,12},{1,3},{3,1},... | collective-permute-start | bytes 1572872 | tf_op jit(solution)/shard_map/ppermute | solution.py:274
  26.3 28.2 %copy-start.20 = (bf16[128,1024]{1,0:T(8,128)(2,1)S(1)}, bf16[128,1024]{1,0:T(8,128)(2,1)}, u32[]{:S(2)}) copy-start(bf16[128,1024]{1,0:T(8,128)(2,1)} %param.5) | copy-start | bytes 786436
  26.3 15.3 %collective-permute-start.5 = (bf16[2,2,128,512]{3,2,1,0:T(8,128)(2,1)S(1)}, bf16[2,2,128,512]{3,2,1,0:T(8,128)(2,1)S(1)}, u32[]{:S(2)}, u32[]{:S(2)}) collective-permute-start(bf16[2,2,128,512]{3,2,1,0:T(8,128)(2,1)S(1)} %pad_maximum_fusion), channel_id=1, source_target_pairs={{0,14},{2,4},{4,2},{6,8},{8,6},{10,12},{12,10},{14,0},{1,15},{3,5}... | collective-permute-start | bytes 1572872 | tf_op jit(solution)/shard_map/ppermute | solution.py:274
  38.9 32.7 %copy-start.5 = (bf16[2,2,128,512]{3,2,1,0:T(8,128)(2,1)}, bf16[2,2,128,512]{3,2,1,0:T(8,128)(2,1)S(1)}, u32[]{:S(2)}) copy-start(bf16[2,2,128,512]{3,2,1,0:T(8,128)(2,1)S(1)} %collective-permute-done.7.refs_13_) | copy-start | bytes 1572868
  38.9 24.8 %collective-permute-start.8 = (bf16[2,2,128,512]{3,2,1,0:T(8,128)(2,1)S(1)}, bf16[2,2,128,512]{3,2,1,0:T(8,128)(2,1)S(1)}, u32[]{:S(2)}, u32[]{:S(2)}) collective-permute-start(bf16[2,2,128,512]{3,2,1,0:T(8,128)(2,1)S(1)} %collective-permute-done.7.refs_13_), channel_id=1, source_target_pairs={{0,14},{2,4},{4,2},{6,8},{8,6},{10,12},{12,10},{14,0},{1,15},{3,5}... | collective-permute-start | bytes 1572872 | tf_op jit(solution)/shard_map/ppermute | solution.py:276
  41.7 29.9 %copy-start.6 = (bf16[2,2,128,512]{3,2,1,0:T(8,128)(2,1)}, bf16[2,2,128,512]{3,2,1,0:T(8,128)(2,1)S(1)}, u32[]{:S(2)}) copy-start(bf16[2,2,128,512]{3,2,1,0:T(8,128)(2,1)S(1)} %collective-permute-done.5.refs_8_) | copy-start | bytes 1572868
  41.7 22.0 %collective-permute-start.6 = (bf16[2,2,128,512]{3,2,1,0:T(8,128)(2,1)S(1)}, bf16[2,2,128,512]{3,2,1,0:T(8,128)(2,1)S(1)}, u32[]{:S(2)}, u32[]{:S(2)}) collective-permute-start(bf16[2,2,128,512]{3,2,1,0:T(8,128)(2,1)S(1)} %collective-permute-done.5.refs_8_), channel_id=1, source_target_pairs={{0,2},{2,0},{4,6},{6,4},{8,10},{10,8},{12,14},{14,12},{1,3},{3,1},... | collective-permute-start | bytes 1572872 | tf_op jit(solution)/shard_map/ppermute | solution.py:276
  44.7 18.9 %all-to-all-start = ((bf16[32,16,128]{2,1,0:T(8,128)(2,1)}), bf16[32,16,128]{2,1,0:T(8,128)(2,1)S(1)}, u32[]{:S(2)}, u32[]{:S(2)}) async-start(bf16[32,16,128]{2,1,0:T(8,128)(2,1)} %broadcast_in_dim.38), calls=%async_computation | async-start | bytes 262144 | tf_op jit(solution)/shard_map/all_to_all | solution.py:270
  63.7 7.9 %copy-start.14 = (bf16[32,16,128]{2,1,0:T(8,128)(2,1)}, bf16[32,16,128]{2,1,0:T(8,128)(2,1)S(1)}, u32[]{:S(2)}) copy-start(bf16[32,16,128]{2,1,0:T(8,128)(2,1)S(1)} %all-to-all-done.refs_5_) | copy-start | bytes 393220
  63.7 7.9 %copy-start.15 = (bf16[1,128,512]{2,1,0:T(8,128)(2,1)S(1)}, bf16[1,128,512]{2,1,0:T(8,128)(2,1)}, u32[]{:S(2)}) copy-start(bf16[1,128,512]{2,1,0:T(8,128)(2,1)} %get-tuple-element.62) | copy-start | bytes 393220
  63.7 7.9 %copy-start.7 = (bf16[2,2,128,512]{3,2,1,0:T(8,128)(2,1)}, bf16[2,2,128,512]{3,2,1,0:T(8,128)(2,1)S(1)}, u32[]{:S(2)}) copy-start(bf16[2,2,128,512]{3,2,1,0:T(8,128)(2,1)S(1)} %collective-permute-done.8.refs_14_) | copy-start | bytes 1572868
  63.7 17.7 %copy-start.8 = (bf16[2,2,128,512]{3,2,1,0:T(8,128)(2,1)}, bf16[2,2,128,512]{3,2,1,0:T(8,128)(2,1)S(1)}, u32[]{:S(2)}) copy-start(bf16[2,2,128,512]{3,2,1,0:T(8,128)(2,1)S(1)} %collective-permute-done.6.refs_9_) | copy-start | bytes 1572868
  63.7 17.7 %collective-permute-start.10 = (bf16[2,2,128,512]{3,2,1,0:T(8,128)(2,1)S(1)}, bf16[2,2,128,512]{3,2,1,0:T(8,128)(2,1)S(1)}, u32[]{:S(2)}, u32[]{:S(2)}) collective-permute-start(bf16[2,2,128,512]{3,2,1,0:T(8,128)(2,1)S(1)} %collective-permute-done.8.refs_14_), channel_id=1, source_target_pairs={{0,2},{2,0},{4,6},{6,4},{8,10},{10,8},{12,14},{14,12},{1,3},{3,1},... | collective-permute-start | bytes 1572872 | tf_op jit(solution)/shard_map/ppermute | solution.py:281
  67.2 14.2 %collective-permute-start.9 = (bf16[2,2,128,512]{3,2,1,0:T(8,128)(2,1)S(1)}, bf16[2,2,128,512]{3,2,1,0:T(8,128)(2,1)S(1)}, u32[]{:S(2)}, u32[]{:S(2)}) collective-permute-start(bf16[2,2,128,512]{3,2,1,0:T(8,128)(2,1)S(1)} %collective-permute-done.6.refs_9_), channel_id=1, source_target_pairs={{0,14},{2,4},{4,2},{6,8},{8,6},{10,12},{12,10},{14,0},{1,15},{3,5}... | collective-permute-start | bytes 1572872 | tf_op jit(solution)/shard_map/ppermute | solution.py:281
  71.6 6.4 %copy-start.22 = (s32[2,8]{1,0:T(2,128)S(1)}, s32[2,8]{1,0:T(2,128)}, u32[]{:S(2)}) copy-start(s32[2,8]{1,0:T(2,128)} %refs_1_.1) | copy-start | bytes 196
  71.6 9.7 %collective-permute-start.1 = (bf16[2,128,512]{2,1,0:T(8,128)(2,1)S(1)}, bf16[2,128,512]{2,1,0:T(8,128)(2,1)S(1)}, u32[]{:S(2)}, u32[]{:S(2)}) collective-permute-start(bf16[2,128,512]{2,1,0:T(8,128)(2,1)S(1)} %pad_maximum_fusion.4), channel_id=1, source_target_pairs={{0,1},{1,0},{2,3},{3,2},{4,5},{5,4},{6,7},{7,6},{8,9},{9,8},{10,11... | collective-permute-start | bytes 786440 | tf_op jit(solution)/shard_map/ppermute | solution.py:278
  78.0 3.3 %collective-permute-start = (s32[2,8]{1,0:T(2,128)S(1)}, s32[2,8]{1,0:T(2,128)S(1)}, u32[]{:S(2)}, u32[]{:S(2)}) collective-permute-start(s32[2,8]{1,0:T(2,128)S(1)} %copy-done.22), channel_id=1, source_target_pairs={{0,1},{1,0},{2,3},{3,2},{4,5},{5,4},{6,7},{7,6},{8,9},{9,8},{10,11... | collective-permute-start | bytes 200 | tf_op jit(solution)/shard_map/ppermute | solution.py:279
  81.3 0.6 copy-start.23
  81.3 0.7 copy-start.18
  81.4 0.9 copy-start.9
  82.2 0.8 copy-start.10
  101.7 13.2 %collective-permute-start.12 = (bf16[2,2,128,512]{3,2,1,0:T(8,128)(2,1)}, bf16[2,2,128,512]{3,2,1,0:T(8,128)(2,1)S(1)}, u32[]{:S(2)}, u32[]{:S(2)}) collective-permute-start(bf16[2,2,128,512]{3,2,1,0:T(8,128)(2,1)} %get-tuple-element.37), channel_id=1, source_target_pairs={{0,2},{2,0},{4,6},{6,4},{8,10},{10,8},{12,14},{14,12},{1,3},{3,1},... | collective-permute-start | bytes 1572872 | tf_op jit(solution)/shard_map/ppermute | solution.py:287
  103.7 14.4 %collective-permute-start.13 = (bf16[2,2,128,512]{3,2,1,0:T(8,128)(2,1)}, bf16[2,2,128,512]{3,2,1,0:T(8,128)(2,1)S(1)}, u32[]{:S(2)}, u32[]{:S(2)}) collective-permute-start(bf16[2,2,128,512]{3,2,1,0:T(8,128)(2,1)} %get-tuple-element.38), channel_id=1, source_target_pairs={{0,14},{2,4},{4,2},{6,8},{8,6},{10,12},{12,10},{14,0},{1,15},{3,5}... | collective-permute-start | bytes 1572872 | tf_op jit(solution)/shard_map/ppermute | solution.py:287
  118.1 4.7 %copy-start.13 = (bf16[2,2,128,512]{3,2,1,0:T(8,128)(2,1)S(1)}, bf16[2,2,128,512]{3,2,1,0:T(8,128)(2,1)}, u32[]{:S(2)}) copy-start(bf16[2,2,128,512]{3,2,1,0:T(8,128)(2,1)} %get-tuple-element.35) | copy-start | bytes 1572868
  119.3 13.3 %collective-permute-start.17 = (bf16[2,2,128,512]{3,2,1,0:T(8,128)(2,1)S(1)}, bf16[2,2,128,512]{3,2,1,0:T(8,128)(2,1)S(1)}, u32[]{:S(2)}, u32[]{:S(2)}) collective-permute-start(bf16[2,2,128,512]{3,2,1,0:T(8,128)(2,1)S(1)} %add_convert_fusion.1), channel_id=1, source_target_pairs={{0,14},{2,4},{4,2},{6,8},{8,6},{10,12},{12,10},{14,0},{1,15},{3,5}... | collective-permute-start | bytes 1572872 | tf_op jit(solution)/shard_map/ppermute | solution.py:291
  122.8 2.2 %copy-start.24 = (bf16[2,128,512]{2,1,0:T(8,128)(2,1)S(1)}, bf16[2,128,512]{2,1,0:T(8,128)(2,1)}, u32[]{:S(2)}) copy-start(bf16[2,128,512]{2,1,0:T(8,128)(2,1)} %get-tuple-element.32) | copy-start | bytes 786436
  122.8 9.8 %copy-start.12 = (bf16[2,2,128,512]{3,2,1,0:T(8,128)(2,1)S(1)}, bf16[2,2,128,512]{3,2,1,0:T(8,128)(2,1)}, u32[]{:S(2)}) copy-start(bf16[2,2,128,512]{3,2,1,0:T(8,128)(2,1)} %get-tuple-element.42) | copy-start | bytes 1572868
  123.0 12.0 %collective-permute-start.14 = (bf16[2,2,128,512]{3,2,1,0:T(8,128)(2,1)S(1)}, bf16[2,2,128,512]{3,2,1,0:T(8,128)(2,1)S(1)}, u32[]{:S(2)}, u32[]{:S(2)}) collective-permute-start(bf16[2,2,128,512]{3,2,1,0:T(8,128)(2,1)S(1)} %add_convert_fusion.3), channel_id=1, source_target_pairs={{0,2},{2,0},{4,6},{6,4},{8,10},{10,8},{12,14},{14,12},{1,3},{3,1},... | collective-permute-start | bytes 1572872 | tf_op jit(solution)/shard_map/ppermute | solution.py:291
  125.0 13.4 %collective-permute-start.11 = (bf16[2,128,512]{2,1,0:T(8,128)(2,1)S(1)}, bf16[2,128,512]{2,1,0:T(8,128)(2,1)S(1)}, u32[]{:S(2)}, u32[]{:S(2)}) collective-permute-start(bf16[2,128,512]{2,1,0:T(8,128)(2,1)S(1)} %copy-done.24), channel_id=1, source_target_pairs={{0,1},{1,0},{2,3},{3,2},{4,5},{5,4},{6,7},{7,6},{8,9},{9,8},{10,11... | collective-permute-start | bytes 786440 | tf_op jit(solution)/shard_map/ppermute | solution.py:301
  132.6 2.4 %copy-start.11 = (bf16[2,2,128,512]{3,2,1,0:T(8,128)(2,1)S(1)}, bf16[2,2,128,512]{3,2,1,0:T(8,128)(2,1)}, u32[]{:S(2)}) copy-start(bf16[2,2,128,512]{3,2,1,0:T(8,128)(2,1)} %get-tuple-element.34) | copy-start | bytes 1572868
  132.8 14.3 %collective-permute-start.18 = (bf16[2,2,128,512]{3,2,1,0:T(8,128)(2,1)S(1)}, bf16[2,2,128,512]{3,2,1,0:T(8,128)(2,1)S(1)}, u32[]{:S(2)}, u32[]{:S(2)}) collective-permute-start(bf16[2,2,128,512]{3,2,1,0:T(8,128)(2,1)S(1)} %add_convert_fusion), channel_id=1, source_target_pairs={{0,2},{2,0},{4,6},{6,4},{8,10},{10,8},{12,14},{14,12},{1,3},{3,1},... | collective-permute-start | bytes 1572872 | tf_op jit(solution)/shard_map/ppermute | solution.py:294
  135.0 3.4 %copy-start.21 = (bf16[2,128,512]{2,1,0:T(8,128)(2,1)S(1)}, bf16[2,128,512]{2,1,0:T(8,128)(2,1)}, u32[]{:S(2)}) copy-start(bf16[2,128,512]{2,1,0:T(8,128)(2,1)} %get-tuple-element.31) | copy-start | bytes 786436
  135.1 15.6 %collective-permute-start.15 = (bf16[2,2,128,512]{3,2,1,0:T(8,128)(2,1)S(1)}, bf16[2,2,128,512]{3,2,1,0:T(8,128)(2,1)S(1)}, u32[]{:S(2)}, u32[]{:S(2)}) collective-permute-start(bf16[2,2,128,512]{3,2,1,0:T(8,128)(2,1)S(1)} %add_convert_fusion.2), channel_id=1, source_target_pairs={{0,14},{2,4},{4,2},{6,8},{8,6},{10,12},{12,10},{14,0},{1,15},{3,5}... | collective-permute-start | bytes 1572872 | tf_op jit(solution)/shard_map/ppermute | solution.py:294
  139.2 19.9 %copy-start.2 = (f32[2,2,128,512]{3,2,1,0:T(8,128)S(1)}, f32[2,2,128,512]{3,2,1,0:T(8,128)}, u32[]{:S(2)}) copy-start(f32[2,2,128,512]{3,2,1,0:T(8,128)} %get-tuple-element.33) | copy-start | bytes 3145732
  139.2 15.2 %all-to-all-start.1 = ((bf16[32,16,128]{2,1,0:T(8,128)(2,1)}), bf16[32,16,128]{2,1,0:T(8,128)(2,1)S(1)}, u32[]{:S(2)}, u32[]{:S(2)}) async-start(bf16[32,16,128]{2,1,0:T(8,128)(2,1)} %get-tuple-element.41), calls=%async_computation.1 | async-start | bytes 262144 | tf_op jit(solution)/shard_map/all_to_all | solution.py:289
  148.1 8.6 %collective-permute-start.19 = (bf16[2,128,512]{2,1,0:T(8,128)(2,1)S(1)}, bf16[2,128,512]{2,1,0:T(8,128)(2,1)S(1)}, u32[]{:S(2)}, u32[]{:S(2)}) collective-permute-start(bf16[2,128,512]{2,1,0:T(8,128)(2,1)S(1)} %fusion), channel_id=1, source_target_pairs={{0,14},{2,4},{4,2},{6,8},{8,6},{10,12},{12,10},{14,0},{1,15},{3,5}... | collective-permute-start | bytes 786440 | tf_op jit(solution)/shard_map/ppermute | solution.py:297
  151.7 7.4 %collective-permute-start.16 = (bf16[2,128,512]{2,1,0:T(8,128)(2,1)S(1)}, bf16[2,128,512]{2,1,0:T(8,128)(2,1)S(1)}, u32[]{:S(2)}, u32[]{:S(2)}) collective-permute-start(bf16[2,128,512]{2,1,0:T(8,128)(2,1)S(1)} %fusion.1), channel_id=1, source_target_pairs={{0,2},{2,0},{4,6},{6,4},{8,10},{10,8},{12,14},{14,12},{1,3},{3,1},... | collective-permute-start | bytes 786440 | tf_op jit(solution)/shard_map/ppermute | solution.py:297
  159.1 7.3 %copy-start.16 = (bf16[128,512]{1,0:T(8,128)(2,1)S(1)}, bf16[128,512]{1,0:T(8,128)(2,1)}, u32[]{:S(2)}) copy-start(bf16[128,512]{1,0:T(8,128)(2,1)} %get-tuple-element.54) | copy-start | bytes 393220
  159.1 7.3 %copy-start.17 = (bf16[128,512]{1,0:T(8,128)(2,1)S(1)}, bf16[128,512]{1,0:T(8,128)(2,1)}, u32[]{:S(2)}) copy-start(bf16[128,512]{1,0:T(8,128)(2,1)} %get-tuple-element.55) | copy-start | bytes 393220
  159.4 8.1 %collective-permute-start.20 = (bf16[2,128,512]{2,1,0:T(8,128)(2,1)S(1)}, bf16[2,128,512]{2,1,0:T(8,128)(2,1)S(1)}, u32[]{:S(2)}, u32[]{:S(2)}) collective-permute-start(bf16[2,128,512]{2,1,0:T(8,128)(2,1)S(1)} %get-tuple-element.47), channel_id=1, source_target_pairs={{0,1},{1,0},{2,3},{3,2},{4,5},{5,4},{6,7},{7,6},{8,9},{9,8},{10,11... | collective-permute-start | bytes 786440 | tf_op jit(solution)/shard_map/ppermute | solution.py:308

commit v4 on v2

--- a/solution.py
+++ b/solution.py
@@ -20,7 +20,7 @@
 HEADS = HALF // HEAD_DIM
 NEAR = 256
 GROWS = 4 * HEADS
-SEND_ORDER = [11, 12, 5, 4, 14, 13, 2, 3, 9, 10, 7, 6, 15, 1, 8, 0]
+SEND_ORDER = (4, 12, 11, 5, 3, 6, 10, 13, 2, 7, 9, 14, 1, 15, 8, 0)
 FKEYS = FAR * BLOCK
 SCALE = 1.0 / math.sqrt(HEAD_DIM)
 EXP_SCALE = SCALE * math.log2(math.e)
@@ -46,14 +46,14 @@
     outputs = refs[22:26]
     parts = refs[26:40]
     slots, near, fgrad, gwide, res_own, res_peer, base, gglob, spare, table, in_sem, out_sem = refs[40:]
-    my_y, my_c, my_w, my_sign = pos[0], pos[1], pos[2], pos[3]
+    my_y, my_c, my_w = pos[0], pos[1], pos[2]
     for who, far in enumerate((far_own, far_peer)):
         for row in range(BLK):
             for entry in range(FAR):
                 block = far[row, entry]
                 group = lax.shift_right_logical(block, 6)
                 offset = lax.bitwise_and(
-                    (lax.shift_right_logical(group, 1) - my_y) * my_sign, NY - 1
+                    lax.shift_right_logical(group, 1) - my_y, NY - 1
                 )
                 chain = lax.bitwise_xor(lax.bitwise_and(group, 1), my_c)
                 inner = lax.bitwise_and(block, 1)
@@ -174,10 +174,9 @@
                 if source % NY == 0:
                     base[source // NY, kind, rows, :] += value
                 else:
-                    spare[source - 1 - source // NY, kind, rows, :] = value.astype(BF16)
+                    spare[source, kind, rows, :] = value.astype(BF16)
         if source % NY:
-            index = source - 1 - source // NY
-            send(spare.at[index], parts[index])
+            send(spare.at[source], parts[source - 1 - source // NY])
     send(base, outputs[2])
     for copy in copies:
         copy.wait()
@@ -208,7 +207,7 @@
             pltpu.VMEM((2, TOK, HALF), BF16),
             pltpu.VMEM((2, 2, TOK, HALF), F32),
             pltpu.VMEM((WINDOWS, GROWS, HEAD_DIM), BF16),
-            pltpu.VMEM((2 * NY - 2, 2, TOK, HALF), BF16),
+            pltpu.VMEM((2 * NY, 2, TOK, HALF), BF16),
             pltpu.SMEM((2, 2 * NY), jnp.int32),
             pltpu.SemaphoreType.DMA((2 + 4 * NY,)),
             pltpu.SemaphoreType.DMA((2 + 2 * NY,)),
@@ -220,8 +219,9 @@
     )(pos, far_own, far_peer, qdo_own, qdo_peer, glob, *sources)
 
 
-EVEN = [(i, i ^ 1) for i in range(NY)]
-ODD = [(i, (((i + 1) ^ 1) - 1) % NY) for i in range(NY)]
+UP = [(i, (i + 1) % NY) for i in range(NY)]
+DOWN = [(i, (i - 1) % NY) for i in range(NY)]
+ROW_STEP, BACK_STEP = 1, 1
 SWAP = [(0, 1), (1, 0)]
 
 
@@ -234,8 +234,8 @@
     my_c = lax.axis_index("c")
     my_w = lax.axis_index("x") * NZ + lax.axis_index("z")
     swap = functools.partial(lax.ppermute, axis_name="c", perm=SWAP)
-    even = functools.partial(lax.ppermute, axis_name="y", perm=EVEN)
-    odd = functools.partial(lax.ppermute, axis_name="y", perm=ODD)
+    up = functools.partial(lax.ppermute, axis_name="y", perm=UP)
+    down = functools.partial(lax.ppermute, axis_name="y", perm=DOWN)
     low = my_c == 0
 
     def split(first, second):
@@ -245,36 +245,50 @@
 
     kv_own, kv_send = split(key_rows, value_rows)
     qdo_own, qdo_send = split(query_rows, out_grad)
-    a, b = {0: kv_own}, {0: swap(kv_send)}
-    row = jnp.concatenate([a[0][:, 0], b[0][:, 0]]).reshape(GROWS, HEAD_DIM)
-    glob = lax.all_to_all(
-        jnp.broadcast_to(row, (WINDOWS, GROWS, HEAD_DIM)), ("x", "z"), 0, 0, tiled=True
-    )
-    a[1], b[-1] = even(a[0]), odd(b[0])
-    a[-1], b[1] = odd(a[0]), even(b[0])
-    a[-2], b[2] = odd(a[1]), even(b[-1])
-    a[2], b[-2] = even(a[-1]), odd(b[1])
-    a[3], b[-3] = even(a[-2]), odd(b[2])
-    qdo_peer = swap(qdo_send)
-    far_peer = swap(far_blocks)
-    glob, a[2], a[3], b[-2], b[-3] = lax.optimization_barrier((glob, a[2], a[3], b[-2], b[-3]))
-    a[-3], b[3] = odd(a[2]), even(b[-2])
-    a[-4], b[4] = odd(a[3]), even(b[-3])
-    sources = [x[r] if r in x else x[r - NY] for x in (a, b) for r in range(NY)]
-    pos = jnp.stack([my_y, my_c, my_w, 1 - 2 * (my_y % 2)]).astype(jnp.int32)
+    kv_peer = swap(kv_send)
+    sources = [None] * 16
+    sources[0], sources[NY] = kv_own, kv_peer
+    row = jnp.concatenate([kv_own[:, 0], kv_peer[:, 0]]).reshape(GROWS, HEAD_DIM)
+    chains = ((0, up, 4, -1), (0, down, 3, 1), (NY, up, 3, -1), (NY, down, 4, 1))
+    held = [kv_own, kv_own, kv_peer, kv_peer]
+    for step in range(1, 5):
+        for i, (first, move, count, sign) in enumerate(chains):
+            if step <= count:
+                held[i] = move(held[i])
+        if step == ROW_STEP:
+            row, held[0] = lax.optimization_barrier((row, held[0]))
+            glob = lax.all_to_all(
+                jnp.broadcast_to(row, (WINDOWS, GROWS, HEAD_DIM)), ("x", "z"), 0, 0, tiled=True
+            )
+            qdo_peer = swap(qdo_send)
+            far_peer = swap(far_blocks)
+        if step == 3:
+            glob, qdo_peer, far_peer, held[3] = lax.optimization_barrier(
+                (glob, qdo_peer, far_peer, held[3])
+            )
+        for i, (first, move, count, sign) in enumerate(chains):
+            if step <= count:
+                sources[first + (sign * step) % NY] = held[i]
+    pos = jnp.stack([my_y, my_c, my_w]).astype(jnp.int32)
     res_own, res_peer, base, gglob, *parts = attend(
         pos, far_blocks, far_peer, qdo_own, qdo_peer, glob, sources
     )
-    a = {r: parts[r % NY - 1] for r in range(-4, 4) if r}
-    b = {r: parts[NY - 2 + r % NY] for r in range(-3, 5) if r}
-    gback = lax.all_to_all(gglob, ("x", "z"), 0, 0, tiled=True)
-    b[-2], a[2] = plus(b[-2], even(b[3])), plus(a[2], odd(a[-3]))
-    b[-3], a[3] = plus(b[-3], even(b[4])), plus(a[3], odd(a[-4]))
-    b[1], a[-1] = plus(b[1], odd(b[-2])), plus(a[-1], even(a[2]))
-    b[2], a[-2] = plus(b[2], odd(b[-3])), plus(a[-2], even(a[3]))
-    b[-1], a[1] = plus(b[-1], even(b[2])), plus(a[1], odd(a[-2]))
-    far_own = odd(a[-1]), even(a[1])
-    far_peer = even(b[1]), odd(b[-1])
+    part = parts[:7], parts[7:]
+    at = [4, 5, 3, 4]
+    held = [part[first // NY][o - 1] for o, (first, _, _, _) in zip(at, chains)]
+    for step in range(1, 5):
+        for i, (first, move, count, sign) in enumerate(chains):
+            if step <= count:
+                held[i] = move(held[i])
+        if step == BACK_STEP:
+            gglob, held[0] = lax.optimization_barrier((gglob, held[0]))
+            gback = lax.all_to_all(gglob, ("x", "z"), 0, 0, tiled=True)
+        for i, (first, move, count, sign) in enumerate(chains):
+            if step <= count:
+                at[i] = (at[i] + sign) % NY
+                if at[i]:
+                    held[i] = plus(held[i], part[first // NY][at[i] - 1])
+    far_own, far_peer = held[:2], held[2:]
     gsum = jnp.sum(gback.astype(F32), axis=0).reshape(2, 2, 1, HALF)
     res_back = swap(res_peer)
     first_row = lax.broadcasted_iota(jnp.int32, (1, TOK, 1), 1) == 0

time: 179 us -> 173 us (0.966)
  waiting for transfers between devices: 21.6 us -> 14.7 us
  starting transfers between devices: 126 us -> 128 us
    ppermute x29, waiting for transfers between devices: 21.4 us -> 12.6 us  [the longest x28 12.6 us: per_device(): held[i] = move(held[i])]
    ppermute x29, starting transfers between devices: 87.8 us -> 93.2 us  [the longest x28 84.4 us: per_device(): held[i] = move(held[i])]
    ppermute x1, starting transfers between devices: 7.22 us -> 4.96 us  [per_device(): res_back = swap(res_peer)]
    all_to_all x1, waiting for transfers between devices: 0.01 us -> 1.84 us  [per_device(): lax.all_to_all(jnp.broadcast_to(row, (WINDOWS, GROWS, HEAD_DIM)), ('x', '...]
    all_to_all x1, starting transfers between devices: 10.3 us -> 8.48 us  [per_device(): lax.all_to_all(jnp.broadcast_to(row, (WINDOWS, GROWS, HEAD_DIM)), ('x', '...]
  transfers between devices with their start and end apart: 35 -> 35, of which waited for: 10 -> 6; matrix products, arithmetic and copies ran while one was open for 3% -> 4% of each run, Pallas kernels for 0% -> 0%
where the time goes in v4:
time: 173 us; the launch traced here: 172 us
  starting transfers between devices  128 us (74%)
  Pallas kernels  18.6 us (11%)
  waiting for transfers between devices  14.7 us (8%)
  other arithmetic  6.75 us (4%)
  local copies, waits for them, and re-layouts  1.99 us (1%)
    ppermute x28, starting transfers between devices, per_device(): held[i] = move(held[i])  84.4 us
    pallas_call x1, Pallas kernels, attend(): pl.pallas_call(attend_kernel, out_shape=[piece, piece, jax.ShapeDtypeStru...  18.6 us
    ppermute x28, waiting for transfers between devices, per_device(): held[i] = move(held[i])  12.6 us
    all_to_all x1, starting transfers between devices, per_device(): gback = lax.all_to_all(gglob, ('x', 'z'), 0, 0, tiled=True)  8.88 us
    ppermute x1, starting transfers between devices, per_device(): kv_peer = swap(kv_send)  8.79 us
    all_to_all x1, starting transfers between devices, per_device(): lax.all_to_all(jnp.broadcast_to(row, (WINDOWS, GROWS, HEAD_DIM)), ('x', '...  8.48 us
    ppermute x1, starting transfers between devices, per_device(): peer_grad = swap(finish(1, far_peer))  5.95 us
    ppermute x1, starting transfers between devices, per_device(): res_back = swap(res_peer)  4.96 us
  transfers between devices with their start and end apart: 35, of which 6 were waited for; matrix products, arithmetic and copies ran while one was open for 4% of the time, Pallas kernels for 0%

profile of v4, /device:TPU:1, one launch (start us, length us, event | category | flops | bytes accessed | tf_op | source)
XLA Modules:
  0.0 171.5 jit_solution(10779052671965915744)
XLA Ops:
  0.6 1.0 select_bitcast_fusion.6
  1.8 8.8 %collective-permute-start = (bf16[2,128,512]{2,1,0:T(8,128)(2,1)S(1)}, bf16[2,128,512]{2,1,0:T(8,128)(2,1)S(1)}, u32[]{:S(2)}, u32[]{:S(2)}) collective-permute-start(bf16[2,128,512]{2,1,0:T(8,128)(2,1)S(1)} %pad_maximum_fusion.1), channel_id=1, source_target_pairs={{0,1},{1,0},{2,3},{3,2},{4,5},{5,4},{6,7},{7,6},{8,9},{9,8},{10,11... | collective-permute-start | bytes 786440 | tf_op jit(solution)/shard_map/ppermute | solution.py:248
  10.6 2.1 %collective-permute-start.1 = (bf16[2,128,512]{2,1,0:T(8,128)(2,1)S(1)}, bf16[2,128,512]{2,1,0:T(8,128)(2,1)S(1)}, u32[]{:S(2)}, u32[]{:S(2)}) collective-permute-start(bf16[2,128,512]{2,1,0:T(8,128)(2,1)S(1)} %pad_maximum_fusion.refs_6_), channel_id=1, source_target_pairs={{0,2},{2,4},{4,6},{6,8},{8,10},{10,12},{12,14},{14,0},{1,3},{3,5},... | collective-permute-start | bytes 786440 | tf_op jit(solution)/shard_map/ppermute | solution.py:257
  12.7 4.6 %collective-permute-start.7 = (bf16[2,128,512]{2,1,0:T(8,128)(2,1)S(1)}, bf16[2,128,512]{2,1,0:T(8,128)(2,1)S(1)}, u32[]{:S(2)}, u32[]{:S(2)}) collective-permute-start(bf16[2,128,512]{2,1,0:T(8,128)(2,1)S(1)} %pad_maximum_fusion.refs_6_), channel_id=1, source_target_pairs={{0,14},{2,0},{4,2},{6,4},{8,6},{10,8},{12,10},{14,12},{1,15},{3,1}... | collective-permute-start | bytes 786440 | tf_op jit(solution)/shard_map/ppermute | solution.py:257
  17.3 2.5 %collective-permute-start.3 = (s32[2,8]{1,0:T(2,128)S(1)}, s32[2,8]{1,0:T(2,128)S(1)}, u32[]{:S(2)}, u32[]{:S(2)}) collective-permute-start(s32[2,8]{1,0:T(2,128)S(1)} %copy-done.30), channel_id=1, source_target_pairs={{0,1},{1,0},{2,3},{3,2},{4,5},{5,4},{6,7},{7,6},{8,9},{9,8},{10,11... | collective-permute-start | bytes 200 | tf_op jit(solution)/shard_map/ppermute | solution.py:264
  19.8 2.1 %collective-permute-start.4 = (bf16[2,128,512]{2,1,0:T(8,128)(2,1)S(1)}, bf16[2,128,512]{2,1,0:T(8,128)(2,1)S(1)}, u32[]{:S(2)}, u32[]{:S(2)}) collective-permute-start(bf16[2,128,512]{2,1,0:T(8,128)(2,1)S(1)} %collective-permute-done.refs_14_), channel_id=1, source_target_pairs={{0,14},{2,0},{4,2},{6,4},{8,6},{10,8},{12,10},{14,12},{1,15},{3,1}... | collective-permute-start | bytes 786440 | tf_op jit(solution)/shard_map/ppermute | solution.py:257
  22.0 3.4 %collective-permute-start.10 = (bf16[2,128,512]{2,1,0:T(8,128)(2,1)S(1)}, bf16[2,128,512]{2,1,0:T(8,128)(2,1)S(1)}, u32[]{:S(2)}, u32[]{:S(2)}) collective-permute-start(bf16[2,128,512]{2,1,0:T(8,128)(2,1)S(1)} %collective-permute-done.1.refs_13_), channel_id=1, source_target_pairs={{0,2},{2,4},{4,6},{6,8},{8,10},{10,12},{12,14},{14,0},{1,3},{3,5},... | collective-permute-start | bytes 786440 | tf_op jit(solution)/shard_map/ppermute | solution.py:257
  25.4 1.9 %collective-permute-start.14 = (bf16[2,128,512]{2,1,0:T(8,128)(2,1)S(1)}, bf16[2,128,512]{2,1,0:T(8,128)(2,1)S(1)}, u32[]{:S(2)}, u32[]{:S(2)}) collective-permute-start(bf16[2,128,512]{2,1,0:T(8,128)(2,1)S(1)} %collective-permute-done.refs_14_), channel_id=1, source_target_pairs={{0,2},{2,4},{4,6},{6,8},{8,10},{10,12},{12,14},{14,0},{1,3},{3,5},... | collective-permute-start | bytes 786440 | tf_op jit(solution)/shard_map/ppermute | solution.py:257
  27.3 2.5 %collective-permute-done.4.refs_15_ = bf16[2,128,512]{2,1,0:T(8,128)(2,1)S(1)} collective-permute-done((bf16[2,128,512]{2,1,0:T(8,128)(2,1)S(1)}, bf16[2,128,512]{2,1,0:T(8,128)(2,1)S(1)}, u32[]{:S(2)}, u32[]{:S(2)}) %collective-permute-start.4) | collective-permute-done | bytes 262176 | tf_op jit(solution)/shard_map/ppermute | solution.py:257
  29.8 3.8 %collective-permute-start.5 = (bf16[2,128,512]{2,1,0:T(8,128)(2,1)S(1)}, bf16[2,128,512]{2,1,0:T(8,128)(2,1)S(1)}, u32[]{:S(2)}, u32[]{:S(2)}) collective-permute-start(bf16[2,128,512]{2,1,0:T(8,128)(2,1)S(1)} %collective-permute-done.4.refs_15_), channel_id=1, source_target_pairs={{0,14},{2,0},{4,2},{6,4},{8,6},{10,8},{12,10},{14,12},{1,15},{3,1}... | collective-permute-start | bytes 786440 | tf_op jit(solution)/shard_map/ppermute | solution.py:257
  33.7 0.7 pad_maximum_fusion.2
  34.4 1.9 %collective-permute-start.8 = (bf16[2,128,512]{2,1,0:T(8,128)(2,1)S(1)}, bf16[2,128,512]{2,1,0:T(8,128)(2,1)S(1)}, u32[]{:S(2)}, u32[]{:S(2)}) collective-permute-start(bf16[2,128,512]{2,1,0:T(8,128)(2,1)S(1)} %collective-permute-done.7.refs_7_), channel_id=1, source_target_pairs={{0,14},{2,0},{4,2},{6,4},{8,6},{10,8},{12,10},{14,12},{1,15},{3,1}... | collective-permute-start | bytes 786440 | tf_op jit(solution)/shard_map/ppermute | solution.py:257
  36.3 3.4 %collective-permute-start.11 = (bf16[2,128,512]{2,1,0:T(8,128)(2,1)S(1)}, bf16[2,128,512]{2,1,0:T(8,128)(2,1)S(1)}, u32[]{:S(2)}, u32[]{:S(2)}) collective-permute-start(bf16[2,128,512]{2,1,0:T(8,128)(2,1)S(1)} %collective-permute-done.10.refs_12_), channel_id=1, source_target_pairs={{0,2},{2,4},{4,6},{6,8},{8,10},{10,12},{12,14},{14,0},{1,3},{3,5},... | collective-permute-start | bytes 786440 | tf_op jit(solution)/shard_map/ppermute | solution.py:257
  39.7 1.9 %collective-permute-start.15 = (bf16[2,128,512]{2,1,0:T(8,128)(2,1)S(1)}, bf16[2,128,512]{2,1,0:T(8,128)(2,1)S(1)}, u32[]{:S(2)}, u32[]{:S(2)}) collective-permute-start(bf16[2,128,512]{2,1,0:T(8,128)(2,1)S(1)} %collective-permute-done.14.refs_21_), channel_id=1, source_target_pairs={{0,2},{2,4},{4,6},{6,8},{8,10},{10,12},{12,14},{14,0},{1,3},{3,5},... | collective-permute-start | bytes 786440 | tf_op jit(solution)/shard_map/ppermute | solution.py:257
  41.7 3.9 %collective-permute-start.2 = (bf16[2,128,512]{2,1,0:T(8,128)(2,1)}, bf16[2,128,512]{2,1,0:T(8,128)(2,1)S(1)}, u32[]{:S(2)}, u32[]{:S(2)}) collective-permute-start(bf16[2,128,512]{2,1,0:T(8,128)(2,1)} %pad_maximum_fusion.2), channel_id=1, source_target_pairs={{0,1},{1,0},{2,3},{3,2},{4,5},{5,4},{6,7},{7,6},{8,9},{9,8},{10,11... | collective-permute-start | bytes 786440 | tf_op jit(solution)/shard_map/ppermute | solution.py:263
  45.6 4.9 %collective-permute-start.6 = (bf16[2,128,512]{2,1,0:T(8,128)(2,1)S(1)}, bf16[2,128,512]{2,1,0:T(8,128)(2,1)S(1)}, u32[]{:S(2)}, u32[]{:S(2)}) collective-permute-start(bf16[2,128,512]{2,1,0:T(8,128)(2,1)S(1)} %collective-permute-done.5.refs_16_), channel_id=1, source_target_pairs={{0,14},{2,0},{4,2},{6,4},{8,6},{10,8},{12,10},{14,12},{1,15},{3,1}... | collective-permute-start | bytes 786440 | tf_op jit(solution)/shard_map/ppermute | solution.py:257
  51.1 8.5 %all-to-all-start = ((bf16[32,16,128]{2,1,0:T(8,128)(2,1)}), bf16[32,16,128]{2,1,0:T(8,128)(2,1)S(1)}, u32[]{:S(2)}, u32[]{:S(2)}) async-start(bf16[32,16,128]{2,1,0:T(8,128)(2,1)} %broadcast_in_dim.38), calls=%async_computation | async-start | bytes 262144 | tf_op jit(solution)/shard_map/all_to_all | solution.py:260
  59.6 1.9 %collective-permute-start.9 = (bf16[2,128,512]{2,1,0:T(8,128)(2,1)S(1)}, bf16[2,128,512]{2,1,0:T(8,128)(2,1)S(1)}, u32[]{:S(2)}, u32[]{:S(2)}) collective-permute-start(bf16[2,128,512]{2,1,0:T(8,128)(2,1)S(1)} %collective-permute-done.8.refs_8_), channel_id=1, source_target_pairs={{0,14},{2,0},{4,2},{6,4},{8,6},{10,8},{12,10},{14,12},{1,15},{3,1}... | collective-permute-start | bytes 786440 | tf_op jit(solution)/shard_map/ppermute | solution.py:257
  61.5 3.4 %collective-permute-start.12 = (bf16[2,128,512]{2,1,0:T(8,128)(2,1)S(1)}, bf16[2,128,512]{2,1,0:T(8,128)(2,1)S(1)}, u32[]{:S(2)}, u32[]{:S(2)}) collective-permute-start(bf16[2,128,512]{2,1,0:T(8,128)(2,1)S(1)} %collective-permute-done.11.refs_11_), channel_id=1, source_target_pairs={{0,2},{2,4},{4,6},{6,8},{8,10},{10,12},{12,14},{14,0},{1,3},{3,5},... | collective-permute-start | bytes 786440 | tf_op jit(solution)/shard_map/ppermute | solution.py:257
  64.9 1.9 %collective-permute-start.16 = (bf16[2,128,512]{2,1,0:T(8,128)(2,1)S(1)}, bf16[2,128,512]{2,1,0:T(8,128)(2,1)}, u32[]{:S(2)}, u32[]{:S(2)}) collective-permute-start(bf16[2,128,512]{2,1,0:T(8,128)(2,1)S(1)} %collective-permute-done.15.refs_20_), channel_id=1, source_target_pairs={{0,2},{2,4},{4,6},{6,8},{8,10},{10,12},{12,14},{14,0},{1,3},{3,5},... | collective-permute-start | bytes 786440 | tf_op jit(solution)/shard_map/ppermute | solution.py:257
  66.9 1.8 %all-to-all-done.refs_5_ = bf16[32,16,128]{2,1,0:T(8,128)(2,1)S(1)} async-done(((bf16[32,16,128]{2,1,0:T(8,128)(2,1)}), bf16[32,16,128]{2,1,0:T(8,128)(2,1)S(1)}, u32[]{:S(2)}, u32[]{:S(2)}) %all-to-all-start) | async-done | bytes 131104 | tf_op jit(solution)/shard_map/all_to_all | solution.py:260
  68.7 2.8 %collective-permute-start.13 = (bf16[2,128,512]{2,1,0:T(8,128)(2,1)S(1)}, bf16[2,128,512]{2,1,0:T(8,128)(2,1)}, u32[]{:S(2)}, u32[]{:S(2)}) collective-permute-start(bf16[2,128,512]{2,1,0:T(8,128)(2,1)S(1)} %collective-permute-done.6.refs_17_), channel_id=1, source_target_pairs={{0,14},{2,0},{4,2},{6,4},{8,6},{10,8},{12,10},{14,12},{1,15},{3,1}... | collective-permute-start | bytes 786440 | tf_op jit(solution)/shard_map/ppermute | solution.py:257
  72.1 0.7 pad_maximum_fusion.3.refs_3_
  72.9 4.6 %collective-permute-done.16.refs_19_ = bf16[2,128,512]{2,1,0:T(8,128)(2,1)} collective-permute-done((bf16[2,128,512]{2,1,0:T(8,128)(2,1)S(1)}, bf16[2,128,512]{2,1,0:T(8,128)(2,1)}, u32[]{:S(2)}, u32[]{:S(2)}) %collective-permute-start.16) | collective-permute-done | bytes 262176 | tf_op jit(solution)/shard_map/ppermute | solution.py:257
  77.6 18.6 %shard_map.84 = (bf16[2,128,512]{2,1,0:T(8,128)(2,1)}, bf16[2,128,512]{2,1,0:T(8,128)(2,1)}, f32[2,2,128,512]{3,2,1,0:T(8,128)}, bf16[32,16,128]{2,1,0:T(8,128)(...) custom-call(s32[3]{0:T(128)} %pad_add_fusion.refs_0_, ...), custom_call_target="tpu_custom_call" | custom-call | flops 1200000000 | bytes 12000000 | tf_op jit(solution)/shard_map/pallas_call | solution.py:190
  96.2 2.9 %collective-permute-start.25 = (bf16[2,128,512]{2,1,0:T(8,128)(2,1)}, bf16[2,128,512]{2,1,0:T(8,128)(2,1)S(1)}, u32[]{:S(2)}, u32[]{:S(2)}) collective-permute-start(bf16[2,128,512]{2,1,0:T(8,128)(2,1)} %get-tuple-element.49), channel_id=1, source_target_pairs={{0,2},{2,4},{4,6},{6,8},{8,10},{10,12},{12,14},{14,0},{1,3},{3,5},... | collective-permute-start | bytes 786440 | tf_op jit(solution)/shard_map/ppermute | solution.py:282
  99.1 3.6 %collective-permute-start.28 = (bf16[2,128,512]{2,1,0:T(8,128)(2,1)}, bf16[2,128,512]{2,1,0:T(8,128)(2,1)S(1)}, u32[]{:S(2)}, u32[]{:S(2)}) collective-permute-start(bf16[2,128,512]{2,1,0:T(8,128)(2,1)} %get-tuple-element.52), channel_id=1, source_target_pairs={{0,14},{2,0},{4,2},{6,4},{8,6},{10,8},{12,10},{14,12},{1,15},{3,1}... | collective-permute-start | bytes 786440 | tf_op jit(solution)/shard_map/ppermute | solution.py:282
  102.7 1.9 %collective-permute-start.18 = (bf16[2,128,512]{2,1,0:T(8,128)(2,1)}, bf16[2,128,512]{2,1,0:T(8,128)(2,1)S(1)}, u32[]{:S(2)}, u32[]{:S(2)}) collective-permute-start(bf16[2,128,512]{2,1,0:T(8,128)(2,1)} %get-tuple-element.40), channel_id=1, source_target_pairs={{0,2},{2,4},{4,6},{6,8},{8,10},{10,12},{12,14},{14,0},{1,3},{3,5},... | collective-permute-start | bytes 786440 | tf_op jit(solution)/shard_map/ppermute | solution.py:282
  104.6 4.6 %collective-permute-start.22 = (bf16[2,128,512]{2,1,0:T(8,128)(2,1)}, bf16[2,128,512]{2,1,0:T(8,128)(2,1)S(1)}, u32[]{:S(2)}, u32[]{:S(2)}) collective-permute-start(bf16[2,128,512]{2,1,0:T(8,128)(2,1)} %get-tuple-element.45), channel_id=1, source_target_pairs={{0,14},{2,0},{4,2},{6,4},{8,6},{10,8},{12,10},{14,12},{1,15},{3,1}... | collective-permute-start | bytes 786440 | tf_op jit(solution)/shard_map/ppermute | solution.py:282
  109.2 5.0 %collective-permute-start.17 = (bf16[2,128,512]{2,1,0:T(8,128)(2,1)}, bf16[2,128,512]{2,1,0:T(8,128)(2,1)S(1)}, u32[]{:S(2)}, u32[]{:S(2)}) collective-permute-start(bf16[2,128,512]{2,1,0:T(8,128)(2,1)} %get-tuple-element.37), channel_id=1, source_target_pairs={{0,1},{1,0},{2,3},{3,2},{4,5},{5,4},{6,7},{7,6},{8,9},{9,8},{10,11... | collective-permute-start | bytes 786440 | tf_op jit(solution)/shard_map/ppermute | solution.py:293
  114.2 1.0 slice_bitcast_fusion.6
  115.3 1.9 %collective-permute-start.26 = (bf16[2,128,512]{2,1,0:T(8,128)(2,1)S(1)}, bf16[2,128,512]{2,1,0:T(8,128)(2,1)S(1)}, u32[]{:S(2)}, u32[]{:S(2)}) collective-permute-start(bf16[2,128,512]{2,1,0:T(8,128)(2,1)S(1)} %add_convert_fusion.4), channel_id=1, source_target_pairs={{0,2},{2,4},{4,6},{6,8},{8,10},{10,12},{12,14},{14,0},{1,3},{3,5},... | collective-permute-start | bytes 786440 | tf_op jit(solution)/shard_map/ppermute | solution.py:282
  117.4 4.6 %collective-permute-start.29 = (bf16[2,128,512]{2,1,0:T(8,128)(2,1)S(1)}, bf16[2,128,512]{2,1,0:T(8,128)(2,1)S(1)}, u32[]{:S(2)}, u32[]{:S(2)}) collective-permute-start(bf16[2,128,512]{2,1,0:T(8,128)(2,1)S(1)} %add_convert_fusion.2), channel_id=1, source_target_pairs={{0,14},{2,0},{4,2},{6,4},{8,6},{10,8},{12,10},{14,12},{1,15},{3,1}... | collective-permute-start | bytes 786440 | tf_op jit(solution)/shard_map/ppermute | solution.py:282
  122.1 2.1 %collective-permute-start.19 = (bf16[2,128,512]{2,1,0:T(8,128)(2,1)S(1)}, bf16[2,128,512]{2,1,0:T(8,128)(2,1)S(1)}, u32[]{:S(2)}, u32[]{:S(2)}) collective-permute-start(bf16[2,128,512]{2,1,0:T(8,128)(2,1)S(1)} %add_convert_fusion.9), channel_id=1, source_target_pairs={{0,2},{2,4},{4,6},{6,8},{8,10},{10,12},{12,14},{14,0},{1,3},{3,5},... | collective-permute-start | bytes 786440 | tf_op jit(solution)/shard_map/ppermute | solution.py:282
  124.1 8.9 %all-to-all-start.1 = ((bf16[32,16,128]{2,1,0:T(8,128)(2,1)}), bf16[32,16,128]{2,1,0:T(8,128)(2,1)S(1)}, u32[]{:S(2)}, u32[]{:S(2)}) async-start(bf16[32,16,128]{2,1,0:T(8,128)(2,1)} %get-tuple-element.48), calls=%async_computation.1 | async-start | bytes 262144 | tf_op jit(solution)/shard_map/all_to_all | solution.py:285
  133.1 4.7 %collective-permute-start.23 = (bf16[2,128,512]{2,1,0:T(8,128)(2,1)S(1)}, bf16[2,128,512]{2,1,0:T(8,128)(2,1)S(1)}, u32[]{:S(2)}, u32[]{:S(2)}) collective-permute-start(bf16[2,128,512]{2,1,0:T(8,128)(2,1)S(1)} %add_convert_fusion.6), channel_id=1, source_target_pairs={{0,14},{2,0},{4,2},{6,4},{8,6},{10,8},{12,10},{14,12},{1,15},{3,1}... | collective-permute-start | bytes 786440 | tf_op jit(solution)/shard_map/ppermute | solution.py:282
  138.0 1.9 %collective-permute-start.27 = (bf16[2,128,512]{2,1,0:T(8,128)(2,1)S(1)}, bf16[2,128,512]{2,1,0:T(8,128)(2,1)S(1)}, u32[]{:S(2)}, u32[]{:S(2)}) collective-permute-start(bf16[2,128,512]{2,1,0:T(8,128)(2,1)S(1)} %add_convert_fusion.3), channel_id=1, source_target_pairs={{0,2},{2,4},{4,6},{6,8},{8,10},{10,12},{12,14},{14,0},{1,3},{3,5},... | collective-permute-start | bytes 786440 | tf_op jit(solution)/shard_map/ppermute | solution.py:282
  140.0 4.6 %collective-permute-start.30 = (bf16[2,128,512]{2,1,0:T(8,128)(2,1)S(1)}, bf16[2,128,512]{2,1,0:T(8,128)(2,1)S(1)}, u32[]{:S(2)}, u32[]{:S(2)}) collective-permute-start(bf16[2,128,512]{2,1,0:T(8,128)(2,1)S(1)} %add_convert_fusion.1), channel_id=1, source_target_pairs={{0,14},{2,0},{4,2},{6,4},{8,6},{10,8},{12,10},{14,12},{1,15},{3,1}... | collective-permute-start | bytes 786440 | tf_op jit(solution)/shard_map/ppermute | solution.py:282
  144.7 1.9 %collective-permute-start.20 = (bf16[2,128,512]{2,1,0:T(8,128)(2,1)S(1)}, bf16[2,128,512]{2,1,0:T(8,128)(2,1)S(1)}, u32[]{:S(2)}, u32[]{:S(2)}) collective-permute-start(bf16[2,128,512]{2,1,0:T(8,128)(2,1)S(1)} %add_convert_fusion.8), channel_id=1, source_target_pairs={{0,2},{2,4},{4,6},{6,8},{8,10},{10,12},{12,14},{14,0},{1,3},{3,5},... | collective-permute-start | bytes 786440 | tf_op jit(solution)/shard_map/ppermute | solution.py:282
  146.7 4.7 %collective-permute-start.24 = (bf16[2,128,512]{2,1,0:T(8,128)(2,1)S(1)}, bf16[2,128,512]{2,1,0:T(8,128)(2,1)S(1)}, u32[]{:S(2)}, u32[]{:S(2)}) collective-permute-start(bf16[2,128,512]{2,1,0:T(8,128)(2,1)S(1)} %add_convert_fusion.5), channel_id=1, source_target_pairs={{0,14},{2,0},{4,2},{6,4},{8,6},{10,8},{12,10},{14,12},{1,15},{3,1}... | collective-permute-start | bytes 786440 | tf_op jit(solution)/shard_map/ppermute | solution.py:282
  151.5 2.3 %collective-permute-start.31 = (bf16[2,128,512]{2,1,0:T(8,128)(2,1)S(1)}, bf16[2,128,512]{2,1,0:T(8,128)(2,1)S(1)}, u32[]{:S(2)}, u32[]{:S(2)}) collective-permute-start(bf16[2,128,512]{2,1,0:T(8,128)(2,1)S(1)} %add_convert_fusion), channel_id=1, source_target_pairs={{0,14},{2,0},{4,2},{6,4},{8,6},{10,8},{12,10},{14,12},{1,15},{3,1}... | collective-permute-start | bytes 786440 | tf_op jit(solution)/shard_map/ppermute | solution.py:282
  153.9 0.8 add_convert_fusion.7
  154.6 3.0 %collective-permute-start.21 = (bf16[2,128,512]{2,1,0:T(8,128)(2,1)}, bf16[2,128,512]{2,1,0:T(8,128)(2,1)S(1)}, u32[]{:S(2)}, u32[]{:S(2)}) collective-permute-start(bf16[2,128,512]{2,1,0:T(8,128)(2,1)} %add_convert_fusion.7), channel_id=1, source_target_pairs={{0,2},{2,4},{4,6},{6,8},{8,10},{10,12},{12,14},{14,0},{1,3},{3,5},... | collective-permute-start | bytes 786440 | tf_op jit(solution)/shard_map/ppermute | solution.py:282
  157.7 2.9 %collective-permute-done.31 = bf16[2,128,512]{2,1,0:T(8,128)(2,1)S(1)} collective-permute-done((bf16[2,128,512]{2,1,0:T(8,128)(2,1)S(1)}, bf16[2,128,512]{2,1,0:T(8,128)(2,1)S(1)}, u32[]{:S(2)}, u32[]{:S(2)}) %collective-permute-start.31) | collective-permute-done | bytes 262176 | tf_op jit(solution)/shard_map/ppermute | solution.py:282
  160.6 2.6 %collective-permute-done.21 = bf16[2,128,512]{2,1,0:T(8,128)(2,1)S(1)} collective-permute-done((bf16[2,128,512]{2,1,0:T(8,128)(2,1)}, bf16[2,128,512]{2,1,0:T(8,128)(2,1)S(1)}, u32[]{:S(2)}, u32[]{:S(2)}) %collective-permute-start.21) | collective-permute-done | bytes 262176 | tf_op jit(solution)/shard_map/ppermute | solution.py:282
  163.5 6.0 %collective-permute-start.32 = (bf16[2,128,512]{2,1,0:T(8,128)(2,1)S(1)}, bf16[2,128,512]{2,1,0:T(8,128)(2,1)S(1)}, u32[]{:S(2)}, u32[]{:S(2)}) collective-permute-start(bf16[2,128,512]{2,1,0:T(8,128)(2,1)S(1)} %get-tuple-element.57), channel_id=1, source_target_pairs={{0,1},{1,0},{2,3},{3,2},{4,5},{5,4},{6,7},{7,6},{8,9},{9,8},{10,11... | collective-permute-start | bytes 786440 | tf_op jit(solution)/shard_map/ppermute | solution.py:300
  169.4 0.9 maximum_select_fusion
  170.6 0.9 maximum_select_fusion.2
  (125 shorter events, 2.9 us)
Async XLA Ops:
  1.8 18.0 %collective-permute-start = (bf16[2,128,512]{2,1,0:T(8,128)(2,1)S(1)}, bf16[2,128,512]{2,1,0:T(8,128)(2,1)S(1)}, u32[]{:S(2)}, u32[]{:S(2)}) collective-permute-start(bf16[2,128,512]{2,1,0:T(8,128)(2,1)S(1)} %pad_maximum_fusion.1), channel_id=1, source_target_pairs={{0,1},{1,0},{2,3},{3,2},{4,5},{5,4},{6,7},{7,6},{8,9},{9,8},{10,11... | collective-permute-start | bytes 786440 | tf_op jit(solution)/shard_map/ppermute | solution.py:248
  10.6 11.3 %copy-start = (bf16[2,128,512]{2,1,0:T(8,128)(2,1)}, bf16[2,128,512]{2,1,0:T(8,128)(2,1)S(1)}, u32[]{:S(2)}) copy-start(bf16[2,128,512]{2,1,0:T(8,128)(2,1)S(1)} %pad_maximum_fusion.refs_6_) | copy-start | bytes 786436
  10.6 11.3 %copy-start.28 = (bf16[128,1024]{1,0:T(8,128)(2,1)S(1)}, bf16[128,1024]{1,0:T(8,128)(2,1)}, u32[]{:S(2)}) copy-start(bf16[128,1024]{1,0:T(8,128)(2,1)} %param.5) | copy-start | bytes 786436
  10.6 11.4 %collective-permute-start.1 = (bf16[2,128,512]{2,1,0:T(8,128)(2,1)S(1)}, bf16[2,128,512]{2,1,0:T(8,128)(2,1)S(1)}, u32[]{:S(2)}, u32[]{:S(2)}) collective-permute-start(bf16[2,128,512]{2,1,0:T(8,128)(2,1)S(1)} %pad_maximum_fusion.refs_6_), channel_id=1, source_target_pairs={{0,2},{2,4},{4,6},{6,8},{8,10},{10,12},{12,14},{14,0},{1,3},{3,5},... | collective-permute-start | bytes 786440 | tf_op jit(solution)/shard_map/ppermute | solution.py:257
  12.7 21.7 %collective-permute-start.7 = (bf16[2,128,512]{2,1,0:T(8,128)(2,1)S(1)}, bf16[2,128,512]{2,1,0:T(8,128)(2,1)S(1)}, u32[]{:S(2)}, u32[]{:S(2)}) collective-permute-start(bf16[2,128,512]{2,1,0:T(8,128)(2,1)S(1)} %pad_maximum_fusion.refs_6_), channel_id=1, source_target_pairs={{0,14},{2,0},{4,2},{6,4},{8,6},{10,8},{12,10},{14,12},{1,15},{3,1}... | collective-permute-start | bytes 786440 | tf_op jit(solution)/shard_map/ppermute | solution.py:257
  17.3 24.4 %collective-permute-start.3 = (s32[2,8]{1,0:T(2,128)S(1)}, s32[2,8]{1,0:T(2,128)S(1)}, u32[]{:S(2)}, u32[]{:S(2)}) collective-permute-start(s32[2,8]{1,0:T(2,128)S(1)} %copy-done.30), channel_id=1, source_target_pairs={{0,1},{1,0},{2,3},{3,2},{4,5},{5,4},{6,7},{7,6},{8,9},{9,8},{10,11... | collective-permute-start | bytes 200 | tf_op jit(solution)/shard_map/ppermute | solution.py:264
  19.8 13.8 %copy-start.29 = (bf16[128,1024]{1,0:T(8,128)(2,1)S(1)}, bf16[128,1024]{1,0:T(8,128)(2,1)}, u32[]{:S(2)}) copy-start(bf16[128,1024]{1,0:T(8,128)(2,1)} %param.8) | copy-start | bytes 786436
  19.8 10.0 %collective-permute-start.4 = (bf16[2,128,512]{2,1,0:T(8,128)(2,1)S(1)}, bf16[2,128,512]{2,1,0:T(8,128)(2,1)S(1)}, u32[]{:S(2)}, u32[]{:S(2)}) collective-permute-start(bf16[2,128,512]{2,1,0:T(8,128)(2,1)S(1)} %collective-permute-done.refs_14_), channel_id=1, source_target_pairs={{0,14},{2,0},{4,2},{6,4},{8,6},{10,8},{12,10},{14,12},{1,15},{3,1}... | collective-permute-start | bytes 786440 | tf_op jit(solution)/shard_map/ppermute | solution.py:257
  22.0 11.6 %copy-start.4 = (bf16[2,128,512]{2,1,0:T(8,128)(2,1)}, bf16[2,128,512]{2,1,0:T(8,128)(2,1)S(1)}, u32[]{:S(2)}) copy-start(bf16[2,128,512]{2,1,0:T(8,128)(2,1)S(1)} %collective-permute-done.1.refs_13_) | copy-start | bytes 786436
  22.0 14.3 %collective-permute-start.10 = (bf16[2,128,512]{2,1,0:T(8,128)(2,1)S(1)}, bf16[2,128,512]{2,1,0:T(8,128)(2,1)S(1)}, u32[]{:S(2)}, u32[]{:S(2)}) collective-permute-start(bf16[2,128,512]{2,1,0:T(8,128)(2,1)S(1)} %collective-permute-done.1.refs_13_), channel_id=1, source_target_pairs={{0,2},{2,4},{4,6},{6,8},{8,10},{10,12},{12,14},{14,0},{1,3},{3,5},... | collective-permute-start | bytes 786440 | tf_op jit(solution)/shard_map/ppermute | solution.py:257
  25.4 14.3 %collective-permute-start.14 = (bf16[2,128,512]{2,1,0:T(8,128)(2,1)S(1)}, bf16[2,128,512]{2,1,0:T(8,128)(2,1)S(1)}, u32[]{:S(2)}, u32[]{:S(2)}) collective-permute-start(bf16[2,128,512]{2,1,0:T(8,128)(2,1)S(1)} %collective-permute-done.refs_14_), channel_id=1, source_target_pairs={{0,2},{2,4},{4,6},{6,8},{8,10},{10,12},{12,14},{14,0},{1,3},{3,5},... | collective-permute-start | bytes 786440 | tf_op jit(solution)/shard_map/ppermute | solution.py:257
  29.8 15.8 %collective-permute-start.5 = (bf16[2,128,512]{2,1,0:T(8,128)(2,1)S(1)}, bf16[2,128,512]{2,1,0:T(8,128)(2,1)S(1)}, u32[]{:S(2)}, u32[]{:S(2)}) collective-permute-start(bf16[2,128,512]{2,1,0:T(8,128)(2,1)S(1)} %collective-permute-done.4.refs_15_), channel_id=1, source_target_pairs={{0,14},{2,0},{4,2},{6,4},{8,6},{10,8},{12,10},{14,12},{1,15},{3,1}... | collective-permute-start | bytes 786440 | tf_op jit(solution)/shard_map/ppermute | solution.py:257
  34.4 38.4 %copy-start.5 = (bf16[2,128,512]{2,1,0:T(8,128)(2,1)}, bf16[2,128,512]{2,1,0:T(8,128)(2,1)S(1)}, u32[]{:S(2)}) copy-start(bf16[2,128,512]{2,1,0:T(8,128)(2,1)S(1)} %collective-permute-done.7.refs_7_) | copy-start | bytes 786436
  34.4 25.2 %collective-permute-start.8 = (bf16[2,128,512]{2,1,0:T(8,128)(2,1)S(1)}, bf16[2,128,512]{2,1,0:T(8,128)(2,1)S(1)}, u32[]{:S(2)}, u32[]{:S(2)}) collective-permute-start(bf16[2,128,512]{2,1,0:T(8,128)(2,1)S(1)} %collective-permute-done.7.refs_7_), channel_id=1, source_target_pairs={{0,14},{2,0},{4,2},{6,4},{8,6},{10,8},{12,10},{14,12},{1,15},{3,1}... | collective-permute-start | bytes 786440 | tf_op jit(solution)/shard_map/ppermute | solution.py:257
  36.3 36.5 %copy-start.7 = (bf16[2,128,512]{2,1,0:T(8,128)(2,1)}, bf16[2,128,512]{2,1,0:T(8,128)(2,1)S(1)}, u32[]{:S(2)}) copy-start(bf16[2,128,512]{2,1,0:T(8,128)(2,1)S(1)} %collective-permute-done.10.refs_12_) | copy-start | bytes 786436
  36.3 25.2 %collective-permute-start.11 = (bf16[2,128,512]{2,1,0:T(8,128)(2,1)S(1)}, bf16[2,128,512]{2,1,0:T(8,128)(2,1)S(1)}, u32[]{:S(2)}, u32[]{:S(2)}) collective-permute-start(bf16[2,128,512]{2,1,0:T(8,128)(2,1)S(1)} %collective-permute-done.10.refs_12_), channel_id=1, source_target_pairs={{0,2},{2,4},{4,6},{6,8},{8,10},{10,12},{12,14},{14,0},{1,3},{3,5},... | collective-permute-start | bytes 786440 | tf_op jit(solution)/shard_map/ppermute | solution.py:257
  39.7 33.1 %copy-start.9 = (bf16[2,128,512]{2,1,0:T(8,128)(2,1)}, bf16[2,128,512]{2,1,0:T(8,128)(2,1)S(1)}, u32[]{:S(2)}) copy-start(bf16[2,128,512]{2,1,0:T(8,128)(2,1)S(1)} %collective-permute-done.14.refs_21_) | copy-start | bytes 786436
  39.7 25.2 %collective-permute-start.15 = (bf16[2,128,512]{2,1,0:T(8,128)(2,1)S(1)}, bf16[2,128,512]{2,1,0:T(8,128)(2,1)S(1)}, u32[]{:S(2)}, u32[]{:S(2)}) collective-permute-start(bf16[2,128,512]{2,1,0:T(8,128)(2,1)S(1)} %collective-permute-done.14.refs_21_), channel_id=1, source_target_pairs={{0,2},{2,4},{4,6},{6,8},{8,10},{10,12},{12,14},{14,0},{1,3},{3,5},... | collective-permute-start | bytes 786440 | tf_op jit(solution)/shard_map/ppermute | solution.py:257
  41.7 25.2 %collective-permute-start.2 = (bf16[2,128,512]{2,1,0:T(8,128)(2,1)}, bf16[2,128,512]{2,1,0:T(8,128)(2,1)S(1)}, u32[]{:S(2)}, u32[]{:S(2)}) collective-permute-start(bf16[2,128,512]{2,1,0:T(8,128)(2,1)} %pad_maximum_fusion.2), channel_id=1, source_target_pairs={{0,1},{1,0},{2,3},{3,2},{4,5},{5,4},{6,7},{7,6},{8,9},{9,8},{10,11... | collective-permute-start | bytes 786440 | tf_op jit(solution)/shard_map/ppermute | solution.py:263
  45.6 32.0 %copy-start.10 = (bf16[2,128,512]{2,1,0:T(8,128)(2,1)}, bf16[2,128,512]{2,1,0:T(8,128)(2,1)S(1)}, u32[]{:S(2)}) copy-start(bf16[2,128,512]{2,1,0:T(8,128)(2,1)S(1)} %collective-permute-done.5.refs_16_) | copy-start | bytes 786436
  45.6 23.2 %collective-permute-start.6 = (bf16[2,128,512]{2,1,0:T(8,128)(2,1)S(1)}, bf16[2,128,512]{2,1,0:T(8,128)(2,1)S(1)}, u32[]{:S(2)}, u32[]{:S(2)}) collective-permute-start(bf16[2,128,512]{2,1,0:T(8,128)(2,1)S(1)} %collective-permute-done.5.refs_16_), channel_id=1, source_target_pairs={{0,14},{2,0},{4,2},{6,4},{8,6},{10,8},{12,10},{14,12},{1,15},{3,1}... | collective-permute-start | bytes 786440 | tf_op jit(solution)/shard_map/ppermute | solution.py:257
  51.1 17.6 %all-to-all-start = ((bf16[32,16,128]{2,1,0:T(8,128)(2,1)}), bf16[32,16,128]{2,1,0:T(8,128)(2,1)S(1)}, u32[]{:S(2)}, u32[]{:S(2)}) async-start(bf16[32,16,128]{2,1,0:T(8,128)(2,1)} %broadcast_in_dim.38), calls=%async_computation | async-start | bytes 262144 | tf_op jit(solution)/shard_map/all_to_all | solution.py:260
  59.6 17.9 %copy-start.12 = (bf16[2,128,512]{2,1,0:T(8,128)(2,1)}, bf16[2,128,512]{2,1,0:T(8,128)(2,1)S(1)}, u32[]{:S(2)}) copy-start(bf16[2,128,512]{2,1,0:T(8,128)(2,1)S(1)} %collective-permute-done.8.refs_8_) | copy-start | bytes 786436
  59.6 13.2 %collective-permute-start.9 = (bf16[2,128,512]{2,1,0:T(8,128)(2,1)S(1)}, bf16[2,128,512]{2,1,0:T(8,128)(2,1)S(1)}, u32[]{:S(2)}, u32[]{:S(2)}) collective-permute-start(bf16[2,128,512]{2,1,0:T(8,128)(2,1)S(1)} %collective-permute-done.8.refs_8_), channel_id=1, source_target_pairs={{0,14},{2,0},{4,2},{6,4},{8,6},{10,8},{12,10},{14,12},{1,15},{3,1}... | collective-permute-start | bytes 786440 | tf_op jit(solution)/shard_map/ppermute | solution.py:257
  61.5 16.0 %copy-start.14 = (bf16[2,128,512]{2,1,0:T(8,128)(2,1)}, bf16[2,128,512]{2,1,0:T(8,128)(2,1)S(1)}, u32[]{:S(2)}) copy-start(bf16[2,128,512]{2,1,0:T(8,128)(2,1)S(1)} %collective-permute-done.11.refs_11_) | copy-start | bytes 786436
  61.5 11.3 %collective-permute-start.12 = (bf16[2,128,512]{2,1,0:T(8,128)(2,1)S(1)}, bf16[2,128,512]{2,1,0:T(8,128)(2,1)S(1)}, u32[]{:S(2)}, u32[]{:S(2)}) collective-permute-start(bf16[2,128,512]{2,1,0:T(8,128)(2,1)S(1)} %collective-permute-done.11.refs_11_), channel_id=1, source_target_pairs={{0,2},{2,4},{4,6},{6,8},{8,10},{10,12},{12,14},{14,0},{1,3},{3,5},... | collective-permute-start | bytes 786440 | tf_op jit(solution)/shard_map/ppermute | solution.py:257
  64.9 12.6 %copy-start.16 = (bf16[2,128,512]{2,1,0:T(8,128)(2,1)}, bf16[2,128,512]{2,1,0:T(8,128)(2,1)S(1)}, u32[]{:S(2)}) copy-start(bf16[2,128,512]{2,1,0:T(8,128)(2,1)S(1)} %collective-permute-done.15.refs_20_) | copy-start | bytes 786436
  64.9 12.6 %collective-permute-start.16 = (bf16[2,128,512]{2,1,0:T(8,128)(2,1)S(1)}, bf16[2,128,512]{2,1,0:T(8,128)(2,1)}, u32[]{:S(2)}, u32[]{:S(2)}) collective-permute-start(bf16[2,128,512]{2,1,0:T(8,128)(2,1)S(1)} %collective-permute-done.15.refs_20_), channel_id=1, source_target_pairs={{0,2},{2,4},{4,6},{6,8},{8,10},{10,12},{12,14},{14,0},{1,3},{3,5},... | collective-permute-start | bytes 786440 | tf_op jit(solution)/shard_map/ppermute | solution.py:257
  68.7 8.8 %collective-permute-start.13 = (bf16[2,128,512]{2,1,0:T(8,128)(2,1)S(1)}, bf16[2,128,512]{2,1,0:T(8,128)(2,1)}, u32[]{:S(2)}, u32[]{:S(2)}) collective-permute-start(bf16[2,128,512]{2,1,0:T(8,128)(2,1)S(1)} %collective-permute-done.6.refs_17_), channel_id=1, source_target_pairs={{0,14},{2,0},{4,2},{6,4},{8,6},{10,8},{12,10},{14,12},{1,15},{3,1}... | collective-permute-start | bytes 786440 | tf_op jit(solution)/shard_map/ppermute | solution.py:257
  96.2 19.0 %collective-permute-start.25 = (bf16[2,128,512]{2,1,0:T(8,128)(2,1)}, bf16[2,128,512]{2,1,0:T(8,128)(2,1)S(1)}, u32[]{:S(2)}, u32[]{:S(2)}) collective-permute-start(bf16[2,128,512]{2,1,0:T(8,128)(2,1)} %get-tuple-element.49), channel_id=1, source_target_pairs={{0,2},{2,4},{4,6},{6,8},{8,10},{10,12},{12,14},{14,0},{1,3},{3,5},... | collective-permute-start | bytes 786440 | tf_op jit(solution)/shard_map/ppermute | solution.py:282
  99.1 18.2 %collective-permute-start.28 = (bf16[2,128,512]{2,1,0:T(8,128)(2,1)}, bf16[2,128,512]{2,1,0:T(8,128)(2,1)S(1)}, u32[]{:S(2)}, u32[]{:S(2)}) collective-permute-start(bf16[2,128,512]{2,1,0:T(8,128)(2,1)} %get-tuple-element.52), channel_id=1, source_target_pairs={{0,14},{2,0},{4,2},{6,4},{8,6},{10,8},{12,10},{14,12},{1,15},{3,1}... | collective-permute-start | bytes 786440 | tf_op jit(solution)/shard_map/ppermute | solution.py:282
  102.7 19.2 %collective-permute-start.18 = (bf16[2,128,512]{2,1,0:T(8,128)(2,1)}, bf16[2,128,512]{2,1,0:T(8,128)(2,1)S(1)}, u32[]{:S(2)}, u32[]{:S(2)}) collective-permute-start(bf16[2,128,512]{2,1,0:T(8,128)(2,1)} %get-tuple-element.40), channel_id=1, source_target_pairs={{0,2},{2,4},{4,6},{6,8},{8,10},{10,12},{12,14},{14,0},{1,3},{3,5},... | collective-permute-start | bytes 786440 | tf_op jit(solution)/shard_map/ppermute | solution.py:282
  104.6 28.4 %collective-permute-start.22 = (bf16[2,128,512]{2,1,0:T(8,128)(2,1)}, bf16[2,128,512]{2,1,0:T(8,128)(2,1)S(1)}, u32[]{:S(2)}, u32[]{:S(2)}) collective-permute-start(bf16[2,128,512]{2,1,0:T(8,128)(2,1)} %get-tuple-element.45), channel_id=1, source_target_pairs={{0,14},{2,0},{4,2},{6,4},{8,6},{10,8},{12,10},{14,12},{1,15},{3,1}... | collective-permute-start | bytes 786440 | tf_op jit(solution)/shard_map/ppermute | solution.py:282
  109.2 28.6 %collective-permute-start.17 = (bf16[2,128,512]{2,1,0:T(8,128)(2,1)}, bf16[2,128,512]{2,1,0:T(8,128)(2,1)S(1)}, u32[]{:S(2)}, u32[]{:S(2)}) collective-permute-start(bf16[2,128,512]{2,1,0:T(8,128)(2,1)} %get-tuple-element.37), channel_id=1, source_target_pairs={{0,1},{1,0},{2,3},{3,2},{4,5},{5,4},{6,7},{7,6},{8,9},{9,8},{10,11... | collective-permute-start | bytes 786440 | tf_op jit(solution)/shard_map/ppermute | solution.py:293
  115.3 22.5 %collective-permute-start.26 = (bf16[2,128,512]{2,1,0:T(8,128)(2,1)S(1)}, bf16[2,128,512]{2,1,0:T(8,128)(2,1)S(1)}, u32[]{:S(2)}, u32[]{:S(2)}) collective-permute-start(bf16[2,128,512]{2,1,0:T(8,128)(2,1)S(1)} %add_convert_fusion.4), channel_id=1, source_target_pairs={{0,2},{2,4},{4,6},{6,8},{8,10},{10,12},{12,14},{14,0},{1,3},{3,5},... | collective-permute-start | bytes 786440 | tf_op jit(solution)/shard_map/ppermute | solution.py:282
  117.4 22.5 %collective-permute-start.29 = (bf16[2,128,512]{2,1,0:T(8,128)(2,1)S(1)}, bf16[2,128,512]{2,1,0:T(8,128)(2,1)S(1)}, u32[]{:S(2)}, u32[]{:S(2)}) collective-permute-start(bf16[2,128,512]{2,1,0:T(8,128)(2,1)S(1)} %add_convert_fusion.2), channel_id=1, source_target_pairs={{0,14},{2,0},{4,2},{6,4},{8,6},{10,8},{12,10},{14,12},{1,15},{3,1}... | collective-permute-start | bytes 786440 | tf_op jit(solution)/shard_map/ppermute | solution.py:282
  122.1 11.0 %copy-start.23 = (bf16[2,128,512]{2,1,0:T(8,128)(2,1)S(1)}, bf16[2,128,512]{2,1,0:T(8,128)(2,1)}, u32[]{:S(2)}) copy-start(bf16[2,128,512]{2,1,0:T(8,128)(2,1)} %get-tuple-element.46) | copy-start | bytes 786436
  122.1 22.5 %collective-permute-start.19 = (bf16[2,128,512]{2,1,0:T(8,128)(2,1)S(1)}, bf16[2,128,512]{2,1,0:T(8,128)(2,1)S(1)}, u32[]{:S(2)}, u32[]{:S(2)}) collective-permute-start(bf16[2,128,512]{2,1,0:T(8,128)(2,1)S(1)} %add_convert_fusion.9), channel_id=1, source_target_pairs={{0,2},{2,4},{4,6},{6,8},{8,10},{10,12},{12,14},{14,0},{1,3},{3,5},... | collective-permute-start | bytes 786440 | tf_op jit(solution)/shard_map/ppermute | solution.py:282
  124.1 33.5 %all-to-all-start.1 = ((bf16[32,16,128]{2,1,0:T(8,128)(2,1)}), bf16[32,16,128]{2,1,0:T(8,128)(2,1)S(1)}, u32[]{:S(2)}, u32[]{:S(2)}) async-start(bf16[32,16,128]{2,1,0:T(8,128)(2,1)} %get-tuple-element.48), calls=%async_computation.1 | async-start | bytes 262144 | tf_op jit(solution)/shard_map/all_to_all | solution.py:285
  133.1 13.5 %collective-permute-start.23 = (bf16[2,128,512]{2,1,0:T(8,128)(2,1)S(1)}, bf16[2,128,512]{2,1,0:T(8,128)(2,1)S(1)}, u32[]{:S(2)}, u32[]{:S(2)}) collective-permute-start(bf16[2,128,512]{2,1,0:T(8,128)(2,1)S(1)} %add_convert_fusion.6), channel_id=1, source_target_pairs={{0,14},{2,0},{4,2},{6,4},{8,6},{10,8},{12,10},{14,12},{1,15},{3,1}... | collective-permute-start | bytes 786440 | tf_op jit(solution)/shard_map/ppermute | solution.py:282
  138.0 19.7 %collective-permute-start.27 = (bf16[2,128,512]{2,1,0:T(8,128)(2,1)S(1)}, bf16[2,128,512]{2,1,0:T(8,128)(2,1)S(1)}, u32[]{:S(2)}, u32[]{:S(2)}) collective-permute-start(bf16[2,128,512]{2,1,0:T(8,128)(2,1)S(1)} %add_convert_fusion.3), channel_id=1, source_target_pairs={{0,2},{2,4},{4,6},{6,8},{8,10},{10,12},{12,14},{14,0},{1,3},{3,5},... | collective-permute-start | bytes 786440 | tf_op jit(solution)/shard_map/ppermute | solution.py:282
  140.0 11.4 %collective-permute-start.30 = (bf16[2,128,512]{2,1,0:T(8,128)(2,1)S(1)}, bf16[2,128,512]{2,1,0:T(8,128)(2,1)S(1)}, u32[]{:S(2)}, u32[]{:S(2)}) collective-permute-start(bf16[2,128,512]{2,1,0:T(8,128)(2,1)S(1)} %add_convert_fusion.1), channel_id=1, source_target_pairs={{0,14},{2,0},{4,2},{6,4},{8,6},{10,8},{12,10},{14,12},{1,15},{3,1}... | collective-permute-start | bytes 786440 | tf_op jit(solution)/shard_map/ppermute | solution.py:282
  144.7 9.2 %collective-permute-start.20 = (bf16[2,128,512]{2,1,0:T(8,128)(2,1)S(1)}, bf16[2,128,512]{2,1,0:T(8,128)(2,1)S(1)}, u32[]{:S(2)}, u32[]{:S(2)}) collective-permute-start(bf16[2,128,512]{2,1,0:T(8,128)(2,1)S(1)} %add_convert_fusion.8), channel_id=1, source_target_pairs={{0,2},{2,4},{4,6},{6,8},{8,10},{10,12},{12,14},{14,0},{1,3},{3,5},... | collective-permute-start | bytes 786440 | tf_op jit(solution)/shard_map/ppermute | solution.py:282
  146.7 16.5 %copy-start.1 = (f32[2,2,128,512]{3,2,1,0:T(8,128)S(1)}, f32[2,2,128,512]{3,2,1,0:T(8,128)}, u32[]{:S(2)}) copy-start(f32[2,2,128,512]{3,2,1,0:T(8,128)} %get-tuple-element.38) | copy-start | bytes 3145732
  146.7 11.0 %collective-permute-start.24 = (bf16[2,128,512]{2,1,0:T(8,128)(2,1)S(1)}, bf16[2,128,512]{2,1,0:T(8,128)(2,1)S(1)}, u32[]{:S(2)}, u32[]{:S(2)}) collective-permute-start(bf16[2,128,512]{2,1,0:T(8,128)(2,1)S(1)} %add_convert_fusion.5), channel_id=1, source_target_pairs={{0,14},{2,0},{4,2},{6,4},{8,6},{10,8},{12,10},{14,12},{1,15},{3,1}... | collective-permute-start | bytes 786440 | tf_op jit(solution)/shard_map/ppermute | solution.py:282
  151.5 9.0 %collective-permute-start.31 = (bf16[2,128,512]{2,1,0:T(8,128)(2,1)S(1)}, bf16[2,128,512]{2,1,0:T(8,128)(2,1)S(1)}, u32[]{:S(2)}, u32[]{:S(2)}) collective-permute-start(bf16[2,128,512]{2,1,0:T(8,128)(2,1)S(1)} %add_convert_fusion), channel_id=1, source_target_pairs={{0,14},{2,0},{4,2},{6,4},{8,6},{10,8},{12,10},{14,12},{1,15},{3,1}... | collective-permute-start | bytes 786440 | tf_op jit(solution)/shard_map/ppermute | solution.py:282
  154.6 8.5 %collective-permute-start.21 = (bf16[2,128,512]{2,1,0:T(8,128)(2,1)}, bf16[2,128,512]{2,1,0:T(8,128)(2,1)S(1)}, u32[]{:S(2)}, u32[]{:S(2)}) collective-permute-start(bf16[2,128,512]{2,1,0:T(8,128)(2,1)} %add_convert_fusion.7), channel_id=1, source_target_pairs={{0,2},{2,4},{4,6},{6,8},{8,10},{10,12},{12,14},{14,0},{1,3},{3,5},... | collective-permute-start | bytes 786440 | tf_op jit(solution)/shard_map/ppermute | solution.py:282
  163.5 7.1 %collective-permute-start.32 = (bf16[2,128,512]{2,1,0:T(8,128)(2,1)S(1)}, bf16[2,128,512]{2,1,0:T(8,128)(2,1)S(1)}, u32[]{:S(2)}, u32[]{:S(2)}) collective-permute-start(bf16[2,128,512]{2,1,0:T(8,128)(2,1)S(1)} %get-tuple-element.57), channel_id=1, source_target_pairs={{0,1},{1,0},{2,3},{3,2},{4,5},{5,4},{6,7},{7,6},{8,9},{9,8},{10,11... | collective-permute-start | bytes 786440 | tf_op jit(solution)/shard_map/ppermute | solution.py:300
  (19 other events, 93.0 us)

commit v5 on v2

v5 whole, which is shorter than its diff:
```python
import functools
import math

import jax
import jax.numpy as jnp
from jax import lax
from jax.experimental import pallas as pl
from jax.experimental.pallas import tpu as pltpu
from jax.sharding import Mesh
from jax.sharding import PartitionSpec as P

HEAD_DIM = 128
BLOCK = 64
TOK = 128
BLK = 2
FAR = 8
NX, NZ, NY, NC = 4, 8, 8, 2
WINDOWS = NX * NZ
HALF = 512
HEADS = HALF // HEAD_DIM
NEAR = 256
GROWS = 4 * HEADS
SEND_ORDER = (4, 12, 11, 3, 5, 13, 2, 10, 6, 14, 1, 9, 7, 15, 8, 0)
FKEYS = FAR * BLOCK
SCALE = 1.0 / math.sqrt(HEAD_DIM)
EXP_SCALE = SCALE * math.log2(math.e)
BF16 = jnp.bfloat16
F32 = jnp.float32


def dot_nt(a, b):
    return lax.dot_general(a, b, (((1,), (1,)), ((), ())), preferred_element_type=F32)


def dot_nn(a, b):
    return lax.dot_general(a, b, (((1,), (0,)), ((), ())), preferred_element_type=F32)


def dot_tn(a, b):
    return lax.dot_general(a, b, (((0,), (0,)), ((), ())), preferred_element_type=F32)


def attend_kernel(*refs):
    pos, far_own, far_peer, qdo_own, qdo_peer, glob = refs[:6]
    arrays = refs[6:15]
    outputs = refs[15:19]
    parts = refs[19:27]
    slots, near, fgrad, gwide, res_own, res_peer, base, gglob, spare, table, in_sem, out_sem = refs[27:]
    sources = [
        arrays[offset if offset < 4 else offset + 1].at[chain] if offset != 4 else arrays[4 + chain]
        for chain in range(2)
        for offset in range(NY)
    ]
    my_y, my_c, my_w = pos[0], pos[1], pos[2]
    for who, far in enumerate((far_own, far_peer)):
        for row in range(BLK):
            for entry in range(FAR):
                block = far[row, entry]
                group = lax.shift_right_logical(block, 6)
                chain = lax.bitwise_xor(lax.bitwise_and(group, 1), my_c)
                offset = lax.bitwise_and(
                    lax.shift_right_logical(group, 1) - my_y, NY - 1
                )
                inner = lax.bitwise_and(block, 1)
                table[who, chain * NY + offset] = (row * FAR + entry) * 2 + inner
    copies = []
    for who in range(2):
        copies.append(
            pltpu.make_async_copy(
                sources[who * NY], near.at[:, who, :TOK, :], in_sem.at[len(copies)]
            )
        )
    for source in range(2 * NY):
        for who in range(2):
            code = table[who, source]
            slot = lax.shift_right_logical(code, 1)
            inner = lax.bitwise_and(code, 1)
            at = pl.ds(pl.multiple_of(slot * BLOCK, BLOCK), BLOCK)
            rows = pl.ds(pl.multiple_of(inner * BLOCK, BLOCK), BLOCK)
            copies.append(
                pltpu.make_async_copy(
                    sources[source].at[:, rows, :],
                    slots.at[:, who, at, :],
                    in_sem.at[len(copies)],
                )
            )
    for copy in copies:
        copy.start()
    gwide[...] = glob[...].astype(F32).reshape(WINDOWS * GROWS, HEAD_DIM)
    for who in range(2):
        for kind in range(2):
            for head in range(HEADS):
                first = (who * 2 + kind) * HEADS + head
                near[kind, who, TOK : TOK + WINDOWS, head * HEAD_DIM : (head + 1) * HEAD_DIM] = (
                    gwide[pl.ds(first, WINDOWS, stride=GROWS), :].astype(BF16)
                )
            near[kind, who, TOK + WINDOWS :, :] = jnp.zeros((NEAR - TOK - WINDOWS, HALF), BF16)
    column = lax.broadcasted_iota(jnp.int32, (TOK, NEAR), 1)
    hidden = (column >= TOK + WINDOWS) | (column == TOK + my_w)
    for copy in copies:
        copy.wait()

    def head_step(head, carry):
        lanes = pl.ds(pl.multiple_of(head * HEAD_DIM, HEAD_DIM), HEAD_DIM)
        both = range(2)
        pairs = [(who, row) for who in both for row in range(BLK)]
        rows = [slice(row * BLOCK, (row + 1) * BLOCK) for row in range(BLK)]
        keys = [slice(row * FKEYS, (row + 1) * FKEYS) for row in range(BLK)]
        res = res_own, res_peer
        query = [qdo[0, :, lanes] for qdo in (qdo_own, qdo_peer)]
        grad = [qdo[1, :, lanes] for qdo in (qdo_own, qdo_peer)]
        near_score = [
            jnp.where(hidden, -1e30, dot_nt(query[who], near[0, who, :, lanes])) for who in both
        ]
        far_score = [
            dot_nt(query[who][rows[row]], slots[0, who, keys[row], lanes]) for who, row in pairs
        ]
        near_dprod = [dot_nt(grad[who], near[1, who, :, lanes]) for who in both]
        far_dprod = [
            dot_nt(grad[who][rows[row]], slots[1, who, keys[row], lanes]) for who, row in pairs
        ]
        near_weight, far_weight, near_half, far_half = [], [], [], []
        for i, (who, row) in enumerate(pairs):
            ns = near_score[who][rows[row]]
            top = jnp.maximum(
                jnp.max(ns, axis=1, keepdims=True), jnp.max(far_score[i], axis=1, keepdims=True)
            )
            near_exp = jnp.exp2((ns - top) * EXP_SCALE)
            far_exp = jnp.exp2((far_score[i] - top) * EXP_SCALE)
            inverse = 1.0 / (
                jnp.sum(near_exp, axis=1, keepdims=True) + jnp.sum(far_exp, axis=1, keepdims=True)
            )
            near_weight.append(near_exp * inverse)
            far_weight.append(far_exp * inverse)
            near_half.append(near_weight[i].astype(BF16))
            far_half.append(far_weight[i].astype(BF16))
        delta = []
        for i, (who, row) in enumerate(pairs):
            out = dot_nn(near_half[i], near[1, who, :, lanes])
            out = (out + dot_nn(far_half[i], slots[1, who, keys[row], lanes])).astype(BF16)
            res[who][0, rows[row], lanes] = out
            g = grad[who][rows[row]]
            delta.append(jnp.sum(g.astype(F32) * out.astype(F32), axis=1, keepdims=True))
        for i, (who, row) in enumerate(pairs):
            g = grad[who][rows[row]]
            fgrad[1, who, keys[row], lanes] = dot_tn(far_half[i], g).astype(BF16)
        near_dscore, far_dscore = [], []
        for i, (who, row) in enumerate(pairs):
            nd = near_weight[i] * (near_dprod[who][rows[row]] - delta[i])
            near_dscore.append(nd.astype(BF16))
            far_dscore.append((far_weight[i] * (far_dprod[i] - delta[i])).astype(BF16))
        for i, (who, row) in enumerate(pairs):
            dq = dot_nn(near_dscore[i], near[0, who, :, lanes])
            dq = (dq + dot_nn(far_dscore[i], slots[0, who, keys[row], lanes])) * SCALE
            res[who][1, rows[row], lanes] = dq.astype(BF16)
        for i, (who, row) in enumerate(pairs):
            dk = dot_tn(far_dscore[i], query[who][rows[row]]) * SCALE
            fgrad[0, who, keys[row], lanes] = dk.astype(BF16)
        for who in both:
            two = slice(who * BLK, (who + 1) * BLK)
            near_kgrad = dot_tn(jnp.concatenate(near_dscore[two], axis=0), query[who]) * SCALE
            near_vgrad = dot_tn(jnp.concatenate(near_half[two], axis=0), grad[who])
            for kind, value in enumerate((near_kgrad, near_vgrad)):
                base[who, kind, :, lanes] = value[:TOK]
                first = (who * 2 + kind) * HEADS + head
                gwide[pl.ds(first, WINDOWS, stride=GROWS), :] = value[TOK : TOK + WINDOWS]
        return carry

    lax.fori_loop(0, HEADS, head_step, 0)
    gglob[...] = gwide[...].reshape(WINDOWS, GROWS, HEAD_DIM).astype(BF16)
    copies = []

    def send(value, output):
        copy = pltpu.make_async_copy(value, output, out_sem.at[len(copies)])
        copy.start()
        copies.append(copy)

    send(gglob, outputs[3])
    send(res_peer, outputs[1])
    send(res_own, outputs[0])
    for source in SEND_ORDER:
        for kind in range(2):
            for inner in range(BLK):
                rows = slice(inner * BLOCK, (inner + 1) * BLOCK)
                value = None
                for who in range(2):
                    code = table[who, source]
                    slot = lax.shift_right_logical(code, 1)
                    at = pl.ds(pl.multiple_of(slot * BLOCK, BLOCK), BLOCK)
                    here = (lax.bitwise_and(code, 1) == inner).astype(F32)
                    term = fgrad[kind, who, at, :].astype(F32) * here
                    value = term if value is None else value + term
                if source % NY == 0:
                    base[source // NY, kind, rows, :] += value
                else:
                    spare[source, kind, rows, :] = value.astype(BF16)
        chain, offset = source // NY, source % NY
        if offset:
            index = offset - 1 if offset < 4 else offset
            send(spare.at[source], parts[3 + chain] if offset == 4 else parts[index].at[chain])
    send(base, outputs[2])
    for copy in copies:
        copy.wait()


def attend(pos, far_own, far_peer, qdo_own, qdo_peer, glob, arrays):
    smem = pl.BlockSpec(memory_space=pltpu.SMEM)
    vmem = pl.BlockSpec(memory_space=pltpu.VMEM)
    anywhere = pl.BlockSpec(memory_space=pl.ANY)
    piece = jax.ShapeDtypeStruct((2, TOK, HALF), BF16)
    double = jax.ShapeDtypeStruct((2, 2, TOK, HALF), BF16)
    return pl.pallas_call(
        attend_kernel,
        out_shape=[
            piece,
            piece,
            jax.ShapeDtypeStruct((2, 2, TOK, HALF), F32),
            jax.ShapeDtypeStruct((WINDOWS, GROWS, HEAD_DIM), BF16),
        ]
        + [double] * 3
        + [piece] * 2
        + [double] * 3,
        in_specs=[smem] * 3 + [vmem] * 3 + [anywhere] * 9,
        out_specs=[anywhere] * 12,
        scratch_shapes=[
            pltpu.VMEM((2, 2, BLK * FKEYS, HALF), BF16),
            pltpu.VMEM((2, 2, NEAR, HALF), BF16),
            pltpu.VMEM((2, 2, BLK * FKEYS, HALF), BF16),
            pltpu.VMEM((WINDOWS * GROWS, HEAD_DIM), F32),
            pltpu.VMEM((2, TOK, HALF), BF16),
            pltpu.VMEM((2, TOK, HALF), BF16),
            pltpu.VMEM((2, 2, TOK, HALF), F32),
            pltpu.VMEM((WINDOWS, GROWS, HEAD_DIM), BF16),
            pltpu.VMEM((2 * NY, 2, TOK, HALF), BF16),
            pltpu.SMEM((2, 2 * NY), jnp.int32),
            pltpu.SemaphoreType.DMA((2 + 4 * NY,)),
            pltpu.SemaphoreType.DMA((2 + 2 * NY,)),
        ],
        compiler_params=pltpu.CompilerParams(vmem_limit_bytes=60 * 1024 * 1024),
        cost_estimate=pl.CostEstimate(
            flops=1_200_000_000, bytes_accessed=12_000_000, transcendentals=800_000
        ),
    )(pos, far_own, far_peer, qdo_own, qdo_peer, glob, *arrays)


UP = [(i, (i + 1) % NY) for i in range(NY)]
DOWN = [(i, (i - 1) % NY) for i in range(NY)]
SWAP = [(0, 1), (1, 0)]


def plus(a, b):
    return (a.astype(F32) + b.astype(F32)).astype(BF16)


def per_device(query_rows, key_rows, value_rows, out_grad, far_blocks):
    my_y = lax.axis_index("y")
    my_c = lax.axis_index("c")
    my_w = lax.axis_index("x") * NZ + lax.axis_index("z")
    swap = functools.partial(lax.ppermute, axis_name="c", perm=SWAP)
    up = functools.partial(lax.ppermute, axis_name="y", perm=UP)
    down = functools.partial(lax.ppermute, axis_name="y", perm=DOWN)
    low = my_c == 0

    def split(first, second):
        mine = [jnp.where(low, a[:, :HALF], a[:, HALF:]) for a in (first, second)]
        other = [jnp.where(low, a[:, HALF:], a[:, :HALF]) for a in (first, second)]
        return jnp.stack(mine), jnp.stack(other)

    kv_own, kv_send = split(key_rows, value_rows)
    qdo_own, qdo_send = split(query_rows, out_grad)
    kv_peer = swap(kv_send)
    row = jnp.concatenate([kv_own[:, 0], kv_peer[:, 0]]).reshape(GROWS, HEAD_DIM)
    ring = [None] * NY
    ring[0] = jnp.stack([kv_own, kv_peer])
    ring[7], ring[1] = up(ring[0]), down(ring[0])
    row, ring[7], ring[1] = lax.optimization_barrier((row, ring[7], ring[1]))
    glob = lax.all_to_all(
        jnp.broadcast_to(row, (WINDOWS, GROWS, HEAD_DIM)), ("x", "z"), 0, 0, tiled=True
    )
    ring[6], ring[2] = up(ring[7]), down(ring[1])
    qdo_peer = swap(qdo_send)
    far_peer = swap(far_blocks)
    ring[5], ring[3] = up(ring[6]), down(ring[2])
    glob, ring[5], ring[3] = lax.optimization_barrier((glob, ring[5], ring[3]))
    across = up(ring[5][0]), down(ring[3][1])
    pos = jnp.stack([my_y, my_c, my_w]).astype(jnp.int32)
    arrays = [*ring[:4], *across, *ring[5:]]
    res_own, res_peer, base, gglob, *parts = attend(
        pos, far_blocks, far_peer, qdo_own, qdo_peer, glob, arrays
    )
    rise, fall = up(parts[3]), down(parts[4])
    rise = jnp.stack([plus(parts[2][0], rise), parts[2][1]])
    fall = jnp.stack([parts[5][0], plus(parts[5][1], fall)])
    rise, fall = up(rise), down(fall)
    gglob, rise, fall = lax.optimization_barrier((gglob, rise, fall))
    gback = lax.all_to_all(gglob, ("x", "z"), 0, 0, tiled=True)
    rise, fall = plus(parts[1], rise), plus(parts[6], fall)
    rise, fall = up(rise), down(fall)
    rise, fall = plus(parts[0], rise), plus(parts[7], fall)
    rise, fall = up(rise), down(fall)
    gsum = jnp.sum(gback.astype(F32), axis=0).reshape(2, 2, 1, HALF)
    res_back = swap(res_peer)
    first_row = lax.broadcasted_iota(jnp.int32, (1, TOK, 1), 1) == 0

    def finish(who):
        total = base[who] + rise[who].astype(F32) + fall[who].astype(F32)
        return (total + jnp.where(first_row, gsum[who], 0.0)).astype(BF16)

    peer_grad = swap(finish(1))
    own_grad = finish(0)

    def join(mine, other):
        return jnp.where(
            low,
            jnp.concatenate([mine, other], axis=1),
            jnp.concatenate([other, mine], axis=1),
        )

    return (
        join(res_own[0], res_back[0]),
        join(res_own[1], res_back[1]),
        join(own_grad[0], peer_grad[0]),
        join(own_grad[1], peer_grad[1]),
    )


def solution(mesh):
    fine = Mesh(mesh.devices.reshape(NX, NZ, NY, NC), ("x", "z", "y", "c"))
    spec = P(("y", "c", "x", "z"), None)
    return jax.shard_map(
        per_device, mesh=fine, in_specs=(spec,) * 5, out_specs=(spec,) * 4, check_vma=False
    )
```

time: 179 us -> 170 us (0.950)
  starting transfers between devices: 126 us -> 93.7 us
  waiting for transfers between devices: 21.6 us -> 47.5 us
  Pallas kernels: 18.6 us -> 12 us
  local copies, waits for them, and re-layouts: 3.49 us -> 5.81 us
    ppermute x30 -> x18, starting transfers between devices: 92.4 us -> 65.2 us  [the longest x6 20.5 us: per_device(): rise, fall = (up(rise), down(fall))]
    ppermute x30 -> x18, waiting for transfers between devices: 21.6 us -> 43.2 us  [the longest x6 19.7 us: per_device(): rise, fall = (up(rise), down(fall))]
    pallas_call x1, Pallas kernels: 18.6 us -> 12 us  [attend(): pl.pallas_call(attend_kernel, out_shape=[piece, piece, jax.ShapeDtypeStru...]
    all_to_all x1, starting transfers between devices: 9.7 us -> 3.85 us  [per_device(): gback = lax.all_to_all(gglob, ('x', 'z'), 0, 0, tiled=True)]
    ppermute x1, starting transfers between devices: 1.92 us -> 6.29 us  [per_device(): far_peer = swap(far_blocks)]
    all_to_all x1, waiting for transfers between devices: 0.01 us -> 3.62 us  [per_device(): lax.all_to_all(jnp.broadcast_to(row, (WINDOWS, GROWS, HEAD_DIM)), ('x', '...]
    ppermute x1, starting transfers between devices: 7.22 us -> 5.01 us  [per_device(): res_back = swap(res_peer)]
    another operation x9 -> x8, other arithmetic: 2.62 us -> 3.83 us  [split(): return (jnp.stack(mine), jnp.stack(other))]
  transfers between devices with their start and end apart: 35 -> 23, of which waited for: 10 -> 13; matrix products, arithmetic and copies ran while one was open for 3% -> 6% of each run, Pallas kernels for 0% -> 0%
where the time goes in v5:
time: 170 us; the launch traced here: 168 us
  starting transfers between devices  93.7 us (55%)
  waiting for transfers between devices  47.5 us (28%)
  Pallas kernels  12 us (7%)
  other arithmetic  7.51 us (4%)
  local copies, waits for them, and re-layouts  5.81 us (3%)
    ppermute x6, starting transfers between devices, per_device(): rise, fall = (up(rise), down(fall))  20.5 us
    ppermute x6, waiting for transfers between devices, per_device(): rise, fall = (up(rise), down(fall))  19.7 us
    pallas_call x1, Pallas kernels, attend(): pl.pallas_call(attend_kernel, out_shape=[piece, piece, jax.ShapeDtypeStru...  12 us
    ppermute x2, waiting for transfers between devices, per_device(): ring[7], ring[1] = (up(ring[0]), down(ring[0]))  10.5 us
    ppermute x1, starting transfers between devices, per_device(): kv_peer = swap(kv_send)  8.79 us
    ppermute x2, waiting for transfers between devices, per_device(): ring[6], ring[2] = (up(ring[7]), down(ring[1]))  8.77 us
    all_to_all x1, starting transfers between devices, per_device(): lax.all_to_all(jnp.broadcast_to(row, (WINDOWS, GROWS, HEAD_DIM)), ('x', '...  8.7 us
    ppermute x2, starting transfers between devices, per_device(): ring[6], ring[2] = (up(ring[7]), down(ring[1]))  7.23 us
  transfers between devices with their start and end apart: 23, of which 13 were waited for; matrix products, arithmetic and copies ran while one was open for 6% of the time, Pallas kernels for 0%

profile of v5, /device:TPU:1, one launch (start us, length us, event | category | flops | bytes accessed | tf_op | source)
XLA Modules:
  0.0 167.8 jit_solution(14692518532316520576)
XLA Ops:
  0.6 1.0 select_bitcast_fusion.2
  1.8 8.8 %collective-permute-start.2 = (bf16[2,128,512]{2,1,0:T(8,128)(2,1)S(1)}, bf16[2,128,512]{2,1,0:T(8,128)(2,1)S(1)}, u32[]{:S(2)}, u32[]{:S(2)}) collective-permute-start(bf16[2,128,512]{2,1,0:T(8,128)(2,1)S(1)} %pad_maximum_fusion.6), channel_id=1, source_target_pairs={{0,1},{1,0},{2,3},{3,2},{4,5},{5,4},{6,7},{7,6},{8,9},{9,8},{10,11... | collective-permute-start | bytes 786440 | tf_op jit(solution)/shard_map/ppermute | solution.py:271
  10.6 1.1 collective-permute-done.2
  11.8 1.9 %collective-permute-start.3 = (bf16[2,2,128,512]{3,2,1,0:T(8,128)(2,1)S(1)}, bf16[2,2,128,512]{3,2,1,0:T(8,128)(2,1)S(1)}, u32[]{:S(2)}, u32[]{:S(2)}) collective-permute-start(bf16[2,2,128,512]{3,2,1,0:T(8,128)(2,1)S(1)} %pad_maximum_fusion.refs_6_), channel_id=1, source_target_pairs={{0,2},{2,4},{4,6},{6,8},{8,10},{10,12},{12,14},{14,0},{1,3},{3,5},... | collective-permute-start | bytes 1572872 | tf_op jit(solution)/shard_map/ppermute | solution.py:275
  13.7 4.6 %collective-permute-start.4 = (bf16[2,2,128,512]{3,2,1,0:T(8,128)(2,1)S(1)}, bf16[2,2,128,512]{3,2,1,0:T(8,128)(2,1)S(1)}, u32[]{:S(2)}, u32[]{:S(2)}) collective-permute-start(bf16[2,2,128,512]{3,2,1,0:T(8,128)(2,1)S(1)} %pad_maximum_fusion.refs_6_), channel_id=1, source_target_pairs={{0,14},{2,0},{4,2},{6,4},{8,6},{10,8},{12,10},{14,12},{1,15},{3,1}... | collective-permute-start | bytes 1572872 | tf_op jit(solution)/shard_map/ppermute | solution.py:275
  18.4 9.6 %collective-permute-done.3.refs_14_ = bf16[2,2,128,512]{3,2,1,0:T(8,128)(2,1)S(1)} collective-permute-done((bf16[2,2,128,512]{3,2,1,0:T(8,128)(2,1)S(1)}, bf16[2,2,128,512]{3,2,1,0:T(8,128)(2,1)S(1)}, u32[]{:S(2)}, u32[]{:S(2)}) %collective-permute-start.3) | collective-permute-done | bytes 524320 | tf_op jit(solution)/shard_map/ppermute | solution.py:275
  28.0 0.9 collective-permute-done.4.refs_7_
  28.9 1.9 %collective-permute-start.5 = (bf16[2,2,128,512]{3,2,1,0:T(8,128)(2,1)S(1)}, bf16[2,2,128,512]{3,2,1,0:T(8,128)(2,1)S(1)}, u32[]{:S(2)}, u32[]{:S(2)}) collective-permute-start(bf16[2,2,128,512]{3,2,1,0:T(8,128)(2,1)S(1)} %collective-permute-done.3.refs_14_), channel_id=1, source_target_pairs={{0,2},{2,4},{4,6},{6,8},{8,10},{10,12},{12,14},{14,0},{1,3},{3,5},... | collective-permute-start | bytes 1572872 | tf_op jit(solution)/shard_map/ppermute | solution.py:280
  30.8 5.3 %collective-permute-start.7 = (bf16[2,2,128,512]{3,2,1,0:T(8,128)(2,1)S(1)}, bf16[2,2,128,512]{3,2,1,0:T(8,128)(2,1)}, u32[]{:S(2)}, u32[]{:S(2)}) collective-permute-start(bf16[2,2,128,512]{3,2,1,0:T(8,128)(2,1)S(1)} %collective-permute-done.4.refs_7_), channel_id=1, source_target_pairs={{0,14},{2,0},{4,2},{6,4},{8,6},{10,8},{12,10},{14,12},{1,15},{3,1}... | collective-permute-start | bytes 1572872 | tf_op jit(solution)/shard_map/ppermute | solution.py:280
  36.1 8.8 %collective-permute-done.5.refs_13_ = bf16[2,2,128,512]{3,2,1,0:T(8,128)(2,1)S(1)} collective-permute-done((bf16[2,2,128,512]{3,2,1,0:T(8,128)(2,1)S(1)}, bf16[2,2,128,512]{3,2,1,0:T(8,128)(2,1)S(1)}, u32[]{:S(2)}, u32[]{:S(2)}) %collective-permute-start.5) | collective-permute-done | bytes 524320 | tf_op jit(solution)/shard_map/ppermute | solution.py:280
  44.9 1.9 %collective-permute-start.6 = (bf16[2,2,128,512]{3,2,1,0:T(8,128)(2,1)S(1)}, bf16[2,2,128,512]{3,2,1,0:T(8,128)(2,1)S(1)}, u32[]{:S(2)}, u32[]{:S(2)}) collective-permute-start(bf16[2,2,128,512]{3,2,1,0:T(8,128)(2,1)S(1)} %collective-permute-done.5.refs_13_), channel_id=1, source_target_pairs={{0,2},{2,4},{4,6},{6,8},{8,10},{10,12},{12,14},{14,0},{1,3},{3,5},... | collective-permute-start | bytes 1572872 | tf_op jit(solution)/shard_map/ppermute | solution.py:283
  46.8 4.6 %collective-permute-start.8 = (bf16[2,2,128,512]{3,2,1,0:T(8,128)(2,1)}, bf16[2,2,128,512]{3,2,1,0:T(8,128)(2,1)S(1)}, u32[]{:S(2)}, u32[]{:S(2)}) collective-permute-start(bf16[2,2,128,512]{3,2,1,0:T(8,128)(2,1)} %collective-permute-done.7.refs_8_), channel_id=1, source_target_pairs={{0,14},{2,0},{4,2},{6,4},{8,6},{10,8},{12,10},{14,12},{1,15},{3,1}... | collective-permute-start | bytes 1572872 | tf_op jit(solution)/shard_map/ppermute | solution.py:283
  51.4 1.0 select_bitcast_fusion.5
  52.4 0.7 broadcast_in_dim.38
  53.1 8.7 %all-to-all-start = ((bf16[32,16,128]{2,1,0:T(8,128)(2,1)}), bf16[32,16,128]{2,1,0:T(8,128)(2,1)S(1)}, u32[]{:S(2)}, u32[]{:S(2)}) async-start(bf16[32,16,128]{2,1,0:T(8,128)(2,1)} %broadcast_in_dim.38), calls=%async_computation | async-start | bytes 262144 | tf_op jit(solution)/shard_map/all_to_all | solution.py:277
  61.8 1.0 select_bitcast_fusion.4
  62.8 4.6 %collective-permute-start.1 = (bf16[2,128,512]{2,1,0:T(8,128)(2,1)S(1)}, bf16[2,128,512]{2,1,0:T(8,128)(2,1)S(1)}, u32[]{:S(2)}, u32[]{:S(2)}) collective-permute-start(bf16[2,128,512]{2,1,0:T(8,128)(2,1)S(1)} %pad_maximum_fusion.5), channel_id=1, source_target_pairs={{0,1},{1,0},{2,3},{3,2},{4,5},{5,4},{6,7},{7,6},{8,9},{9,8},{10,11... | collective-permute-start | bytes 786440 | tf_op jit(solution)/shard_map/ppermute | solution.py:281
  67.4 3.6 %all-to-all-done.refs_5_ = bf16[32,16,128]{2,1,0:T(8,128)(2,1)S(1)} async-done(((bf16[32,16,128]{2,1,0:T(8,128)(2,1)}), bf16[32,16,128]{2,1,0:T(8,128)(2,1)S(1)}, u32[]{:S(2)}, u32[]{:S(2)}) %all-to-all-start) | async-done | bytes 131104 | tf_op jit(solution)/shard_map/all_to_all | solution.py:277
  71.1 2.1 %collective-permute-start.10 = (bf16[2,128,512]{2,1,0:T(8,128)(2,1)S(1)}, bf16[2,128,512]{2,1,0:T(8,128)(2,1)S(1)}, u32[]{:S(2)}, u32[]{:S(2)}) collective-permute-start(bf16[2,128,512]{2,1,0:T(8,128)(2,1)S(1)} %slice_bitcast_fusion), channel_id=1, source_target_pairs={{0,14},{2,0},{4,2},{6,4},{8,6},{10,8},{12,10},{14,12},{1,15},{3,1}... | collective-permute-start | bytes 786440 | tf_op jit(solution)/shard_map/ppermute | solution.py:285
  73.1 0.7 slice_bitcast_fusion.1
  73.9 3.4 %collective-permute-start.9 = (bf16[2,128,512]{2,1,0:T(8,128)(2,1)}, bf16[2,128,512]{2,1,0:T(8,128)(2,1)S(1)}, u32[]{:S(2)}, u32[]{:S(2)}) collective-permute-start(bf16[2,128,512]{2,1,0:T(8,128)(2,1)} %slice_bitcast_fusion.1), channel_id=1, source_target_pairs={{0,2},{2,4},{4,6},{6,8},{8,10},{10,12},{12,14},{14,0},{1,3},{3,5},... | collective-permute-start | bytes 786440 | tf_op jit(solution)/shard_map/ppermute | solution.py:285
  77.3 6.3 %collective-permute-start = (s32[2,8]{1,0:T(2,128)S(1)}, s32[2,8]{1,0:T(2,128)S(1)}, u32[]{:S(2)}, u32[]{:S(2)}) collective-permute-start(s32[2,8]{1,0:T(2,128)S(1)} %copy-done.21), channel_id=1, source_target_pairs={{0,1},{1,0},{2,3},{3,2},{4,5},{5,4},{6,7},{7,6},{8,9},{9,8},{10,11... | collective-permute-start | bytes 200 | tf_op jit(solution)/shard_map/ppermute | solution.py:282
  83.6 0.7 pad_maximum_fusion.4.refs_3_
  84.3 0.6 pad_add_fusion.refs_0_
  85.7 0.7 copy-done.18
  86.4 12.0 %shard_map.84 = (bf16[2,128,512]{2,1,0:T(8,128)(2,1)}, bf16[2,128,512]{2,1,0:T(8,128)(2,1)}, f32[2,2,128,512]{3,2,1,0:T(8,128)}, bf16[32,16,128]{2,1,0:T(8,128)(...) custom-call(s32[3]{0:T(128)} %pad_add_fusion.refs_0_, ...), custom_call_target="tpu_custom_call" | custom-call | flops 1200000000 | bytes 12000000 | tf_op jit(solution)/shard_map/pallas_call | solution.py:212
  98.5 3.4 %collective-permute-start.14 = (bf16[2,128,512]{2,1,0:T(8,128)(2,1)}, bf16[2,128,512]{2,1,0:T(8,128)(2,1)S(1)}, u32[]{:S(2)}, u32[]{:S(2)}) collective-permute-start(bf16[2,128,512]{2,1,0:T(8,128)(2,1)} %get-tuple-element.40), channel_id=1, source_target_pairs={{0,14},{2,0},{4,2},{6,4},{8,6},{10,8},{12,10},{14,12},{1,15},{3,1}... | collective-permute-start | bytes 786440 | tf_op jit(solution)/shard_map/ppermute | solution.py:291
  101.9 1.0 slice.125
  102.9 2.0 %collective-permute-start.12 = (bf16[2,128,512]{2,1,0:T(8,128)(2,1)}, bf16[2,128,512]{2,1,0:T(8,128)(2,1)S(1)}, u32[]{:S(2)}, u32[]{:S(2)}) collective-permute-start(bf16[2,128,512]{2,1,0:T(8,128)(2,1)} %get-tuple-element.38), channel_id=1, source_target_pairs={{0,2},{2,4},{4,6},{6,8},{8,10},{10,12},{12,14},{14,0},{1,3},{3,5},... | collective-permute-start | bytes 786440 | tf_op jit(solution)/shard_map/ppermute | solution.py:291
  105.0 2.4 %collective-permute-done.14 = bf16[2,128,512]{2,1,0:T(8,128)(2,1)S(1)} collective-permute-done((bf16[2,128,512]{2,1,0:T(8,128)(2,1)}, bf16[2,128,512]{2,1,0:T(8,128)(2,1)S(1)}, u32[]{:S(2)}, u32[]{:S(2)}) %collective-permute-start.14) | collective-permute-done | bytes 262176 | tf_op jit(solution)/shard_map/ppermute | solution.py:291
  107.5 5.2 %collective-permute-start.15 = (bf16[2,2,128,512]{3,2,1,0:T(8,128)(2,1)S(1)}, bf16[2,2,128,512]{3,2,1,0:T(8,128)(2,1)S(1)}, u32[]{:S(2)}, u32[]{:S(2)}) collective-permute-start(bf16[2,2,128,512]{3,2,1,0:T(8,128)(2,1)S(1)} %pad_maximum_fusion.2), channel_id=1, source_target_pairs={{0,14},{2,0},{4,2},{6,4},{8,6},{10,8},{12,10},{14,12},{1,15},{3,1}... | collective-permute-start | bytes 1572872 | tf_op jit(solution)/shard_map/ppermute | solution.py:294
  112.7 0.6 collective-permute-done.12
  113.5 2.1 %collective-permute-start.13 = (bf16[2,2,128,512]{3,2,1,0:T(8,128)(2,1)S(1)}, bf16[2,2,128,512]{3,2,1,0:T(8,128)(2,1)S(1)}, u32[]{:S(2)}, u32[]{:S(2)}) collective-permute-start(bf16[2,2,128,512]{3,2,1,0:T(8,128)(2,1)S(1)} %pad_maximum_fusion.1), channel_id=1, source_target_pairs={{0,2},{2,4},{4,6},{6,8},{8,10},{10,12},{12,14},{14,0},{1,3},{3,5},... | collective-permute-start | bytes 1572872 | tf_op jit(solution)/shard_map/ppermute | solution.py:294
  115.5 7.1 %collective-permute-done.15 = bf16[2,2,128,512]{3,2,1,0:T(8,128)(2,1)S(1)} collective-permute-done((bf16[2,2,128,512]{3,2,1,0:T(8,128)(2,1)S(1)}, bf16[2,2,128,512]{3,2,1,0:T(8,128)(2,1)S(1)}, u32[]{:S(2)}, u32[]{:S(2)}) %collective-permute-start.15) | collective-permute-done | bytes 524320 | tf_op jit(solution)/shard_map/ppermute | solution.py:294
  122.6 5.9 %collective-permute-done.13 = bf16[2,2,128,512]{3,2,1,0:T(8,128)(2,1)S(1)} collective-permute-done((bf16[2,2,128,512]{3,2,1,0:T(8,128)(2,1)S(1)}, bf16[2,2,128,512]{3,2,1,0:T(8,128)(2,1)S(1)}, u32[]{:S(2)}, u32[]{:S(2)}) %collective-permute-start.13) | collective-permute-done | bytes 524320 | tf_op jit(solution)/shard_map/ppermute | solution.py:294
  128.6 1.9 %collective-permute-start.16 = (bf16[2,2,128,512]{3,2,1,0:T(8,128)(2,1)S(1)}, bf16[2,2,128,512]{3,2,1,0:T(8,128)(2,1)S(1)}, u32[]{:S(2)}, u32[]{:S(2)}) collective-permute-start(bf16[2,2,128,512]{3,2,1,0:T(8,128)(2,1)S(1)} %add_convert_fusion.3), channel_id=1, source_target_pairs={{0,2},{2,4},{4,6},{6,8},{8,10},{10,12},{12,14},{14,0},{1,3},{3,5},... | collective-permute-start | bytes 1572872 | tf_op jit(solution)/shard_map/ppermute | solution.py:298
  130.7 4.7 %collective-permute-start.18 = (bf16[2,2,128,512]{3,2,1,0:T(8,128)(2,1)S(1)}, bf16[2,2,128,512]{3,2,1,0:T(8,128)(2,1)S(1)}, u32[]{:S(2)}, u32[]{:S(2)}) collective-permute-start(bf16[2,2,128,512]{3,2,1,0:T(8,128)(2,1)S(1)} %add_convert_fusion.1), channel_id=1, source_target_pairs={{0,14},{2,0},{4,2},{6,4},{8,6},{10,8},{12,10},{14,12},{1,15},{3,1}... | collective-permute-start | bytes 1572872 | tf_op jit(solution)/shard_map/ppermute | solution.py:298
  135.5 5.0 %collective-permute-start.11 = (bf16[2,128,512]{2,1,0:T(8,128)(2,1)}, bf16[2,128,512]{2,1,0:T(8,128)(2,1)}, u32[]{:S(2)}, u32[]{:S(2)}) collective-permute-start(bf16[2,128,512]{2,1,0:T(8,128)(2,1)} %get-tuple-element.32), channel_id=1, source_target_pairs={{0,1},{1,0},{2,3},{3,2},{4,5},{5,4},{6,7},{7,6},{8,9},{9,8},{10,11... | collective-permute-start | bytes 786440 | tf_op jit(solution)/shard_map/ppermute | solution.py:302
  140.5 3.9 %all-to-all-start.1 = ((bf16[32,16,128]{2,1,0:T(8,128)(2,1)}), bf16[32,16,128]{2,1,0:T(8,128)(2,1)S(1)}, u32[]{:S(2)}, u32[]{:S(2)}) async-start(bf16[32,16,128]{2,1,0:T(8,128)(2,1)} %get-tuple-element.45), calls=%async_computation.1 | async-start | bytes 262144 | tf_op jit(solution)/shard_map/all_to_all | solution.py:296
  144.6 1.9 %collective-permute-start.17 = (bf16[2,2,128,512]{3,2,1,0:T(8,128)(2,1)S(1)}, bf16[2,2,128,512]{3,2,1,0:T(8,128)(2,1)S(1)}, u32[]{:S(2)}, u32[]{:S(2)}) collective-permute-start(bf16[2,2,128,512]{3,2,1,0:T(8,128)(2,1)S(1)} %add_convert_fusion.2), channel_id=1, source_target_pairs={{0,2},{2,4},{4,6},{6,8},{8,10},{10,12},{12,14},{14,0},{1,3},{3,5},... | collective-permute-start | bytes 1572872 | tf_op jit(solution)/shard_map/ppermute | solution.py:300
  146.7 4.7 %collective-permute-start.19 = (bf16[2,2,128,512]{3,2,1,0:T(8,128)(2,1)S(1)}, bf16[2,2,128,512]{3,2,1,0:T(8,128)(2,1)S(1)}, u32[]{:S(2)}, u32[]{:S(2)}) collective-permute-start(bf16[2,2,128,512]{3,2,1,0:T(8,128)(2,1)S(1)} %add_convert_fusion), channel_id=1, source_target_pairs={{0,14},{2,0},{4,2},{6,4},{8,6},{10,8},{12,10},{14,12},{1,15},{3,1}... | collective-permute-start | bytes 1572872 | tf_op jit(solution)/shard_map/ppermute | solution.py:300
  151.4 1.7 %slice_bitcast_fusion.6 = (bf16[128,512]{1,0:T(8,128)(2,1)}, bf16[128,512]{1,0:T(8,128)(2,1)}) fusion(bf16[2,128,512]{2,1,0:T(8,128)(2,1)} %collective-permute-done.11), kind=kLoop, calls=%fused_computation.35 | loop fusion | bytes 524288 | tf_op jit(solution)/shard_map/squeeze | solution.py:321
  153.1 0.6 all-to-all-done.1
  153.7 5.5 %collective-permute-done.17 = bf16[2,2,128,512]{3,2,1,0:T(8,128)(2,1)S(1)} collective-permute-done((bf16[2,2,128,512]{3,2,1,0:T(8,128)(2,1)S(1)}, bf16[2,2,128,512]{3,2,1,0:T(8,128)(2,1)S(1)}, u32[]{:S(2)}, u32[]{:S(2)}) %collective-permute-start.17) | collective-permute-done | bytes 524320 | tf_op jit(solution)/shard_map/ppermute | solution.py:300
  159.3 1.2 collective-permute-done.19
  160.8 4.9 %collective-permute-start.20 = (bf16[2,128,512]{2,1,0:T(8,128)(2,1)S(1)}, bf16[2,128,512]{2,1,0:T(8,128)(2,1)S(1)}, u32[]{:S(2)}, u32[]{:S(2)}) collective-permute-start(bf16[2,128,512]{2,1,0:T(8,128)(2,1)S(1)} %get-tuple-element.47), channel_id=1, source_target_pairs={{0,1},{1,0},{2,3},{3,2},{4,5},{5,4},{6,7},{7,6},{8,9},{9,8},{10,11... | collective-permute-start | bytes 786440 | tf_op jit(solution)/shard_map/ppermute | solution.py:309
  165.7 0.9 maximum_select_fusion
  166.9 0.9 maximum_select_fusion.2
  (86 shorter events, 2.5 us)
Async XLA Ops:
  0.6 1.1 copy-start.19
  1.8 9.9 %collective-permute-start.2 = (bf16[2,128,512]{2,1,0:T(8,128)(2,1)S(1)}, bf16[2,128,512]{2,1,0:T(8,128)(2,1)S(1)}, u32[]{:S(2)}, u32[]{:S(2)}) collective-permute-start(bf16[2,128,512]{2,1,0:T(8,128)(2,1)S(1)} %pad_maximum_fusion.6), channel_id=1, source_target_pairs={{0,1},{1,0},{2,3},{3,2},{4,5},{5,4},{6,7},{7,6},{8,9},{9,8},{10,11... | collective-permute-start | bytes 786440 | tf_op jit(solution)/shard_map/ppermute | solution.py:271
  11.8 41.3 %copy-start = (bf16[2,2,128,512]{3,2,1,0:T(8,128)(2,1)}, bf16[2,2,128,512]{3,2,1,0:T(8,128)(2,1)S(1)}, u32[]{:S(2)}) copy-start(bf16[2,2,128,512]{3,2,1,0:T(8,128)(2,1)S(1)} %pad_maximum_fusion.refs_6_) | copy-start | bytes 1572868
  11.8 16.2 %collective-permute-start.3 = (bf16[2,2,128,512]{3,2,1,0:T(8,128)(2,1)S(1)}, bf16[2,2,128,512]{3,2,1,0:T(8,128)(2,1)S(1)}, u32[]{:S(2)}, u32[]{:S(2)}) collective-permute-start(bf16[2,2,128,512]{3,2,1,0:T(8,128)(2,1)S(1)} %pad_maximum_fusion.refs_6_), channel_id=1, source_target_pairs={{0,2},{2,4},{4,6},{6,8},{8,10},{10,12},{12,14},{14,0},{1,3},{3,5},... | collective-permute-start | bytes 1572872 | tf_op jit(solution)/shard_map/ppermute | solution.py:275
  13.7 15.2 %collective-permute-start.4 = (bf16[2,2,128,512]{3,2,1,0:T(8,128)(2,1)S(1)}, bf16[2,2,128,512]{3,2,1,0:T(8,128)(2,1)S(1)}, u32[]{:S(2)}, u32[]{:S(2)}) collective-permute-start(bf16[2,2,128,512]{3,2,1,0:T(8,128)(2,1)S(1)} %pad_maximum_fusion.refs_6_), channel_id=1, source_target_pairs={{0,14},{2,0},{4,2},{6,4},{8,6},{10,8},{12,10},{14,12},{1,15},{3,1}... | collective-permute-start | bytes 1572872 | tf_op jit(solution)/shard_map/ppermute | solution.py:275
  28.0 34.8 %copy-start.4 = (bf16[2,2,128,512]{3,2,1,0:T(8,128)(2,1)}, bf16[2,2,128,512]{3,2,1,0:T(8,128)(2,1)S(1)}, u32[]{:S(2)}) copy-start(bf16[2,2,128,512]{3,2,1,0:T(8,128)(2,1)S(1)} %collective-permute-done.3.refs_14_) | copy-start | bytes 1572868
  28.9 33.9 %copy-start.5 = (bf16[2,2,128,512]{3,2,1,0:T(8,128)(2,1)}, bf16[2,2,128,512]{3,2,1,0:T(8,128)(2,1)S(1)}, u32[]{:S(2)}) copy-start(bf16[2,2,128,512]{3,2,1,0:T(8,128)(2,1)S(1)} %collective-permute-done.4.refs_7_) | copy-start | bytes 1572868
  28.9 16.0 %collective-permute-start.5 = (bf16[2,2,128,512]{3,2,1,0:T(8,128)(2,1)S(1)}, bf16[2,2,128,512]{3,2,1,0:T(8,128)(2,1)S(1)}, u32[]{:S(2)}, u32[]{:S(2)}) collective-permute-start(bf16[2,2,128,512]{3,2,1,0:T(8,128)(2,1)S(1)} %collective-permute-done.3.refs_14_), channel_id=1, source_target_pairs={{0,2},{2,4},{4,6},{6,8},{8,10},{10,12},{12,14},{14,0},{1,3},{3,5},... | collective-permute-start | bytes 1572872 | tf_op jit(solution)/shard_map/ppermute | solution.py:280
  30.8 16.0 %collective-permute-start.7 = (bf16[2,2,128,512]{3,2,1,0:T(8,128)(2,1)S(1)}, bf16[2,2,128,512]{3,2,1,0:T(8,128)(2,1)}, u32[]{:S(2)}, u32[]{:S(2)}) collective-permute-start(bf16[2,2,128,512]{3,2,1,0:T(8,128)(2,1)S(1)} %collective-permute-done.4.refs_7_), channel_id=1, source_target_pairs={{0,14},{2,0},{4,2},{6,4},{8,6},{10,8},{12,10},{14,12},{1,15},{3,1}... | collective-permute-start | bytes 1572872 | tf_op jit(solution)/shard_map/ppermute | solution.py:280
  44.9 39.4 %copy-start.6 = (bf16[2,2,128,512]{3,2,1,0:T(8,128)(2,1)}, bf16[2,2,128,512]{3,2,1,0:T(8,128)(2,1)S(1)}, u32[]{:S(2)}) copy-start(bf16[2,2,128,512]{3,2,1,0:T(8,128)(2,1)S(1)} %collective-permute-done.5.refs_13_) | copy-start | bytes 1572868
  44.9 26.1 %collective-permute-start.6 = (bf16[2,2,128,512]{3,2,1,0:T(8,128)(2,1)S(1)}, bf16[2,2,128,512]{3,2,1,0:T(8,128)(2,1)S(1)}, u32[]{:S(2)}, u32[]{:S(2)}) collective-permute-start(bf16[2,2,128,512]{3,2,1,0:T(8,128)(2,1)S(1)} %collective-permute-done.5.refs_13_), channel_id=1, source_target_pairs={{0,2},{2,4},{4,6},{6,8},{8,10},{10,12},{12,14},{14,0},{1,3},{3,5},... | collective-permute-start | bytes 1572872 | tf_op jit(solution)/shard_map/ppermute | solution.py:283
  46.8 24.2 %collective-permute-start.8 = (bf16[2,2,128,512]{3,2,1,0:T(8,128)(2,1)}, bf16[2,2,128,512]{3,2,1,0:T(8,128)(2,1)S(1)}, u32[]{:S(2)}, u32[]{:S(2)}) collective-permute-start(bf16[2,2,128,512]{3,2,1,0:T(8,128)(2,1)} %collective-permute-done.7.refs_8_), channel_id=1, source_target_pairs={{0,14},{2,0},{4,2},{6,4},{8,6},{10,8},{12,10},{14,12},{1,15},{3,1}... | collective-permute-start | bytes 1572872 | tf_op jit(solution)/shard_map/ppermute | solution.py:283
  53.1 18.0 %all-to-all-start = ((bf16[32,16,128]{2,1,0:T(8,128)(2,1)}), bf16[32,16,128]{2,1,0:T(8,128)(2,1)S(1)}, u32[]{:S(2)}, u32[]{:S(2)}) async-start(bf16[32,16,128]{2,1,0:T(8,128)(2,1)} %broadcast_in_dim.38), calls=%async_computation | async-start | bytes 262144 | tf_op jit(solution)/shard_map/all_to_all | solution.py:277
  62.8 22.1 %collective-permute-start.1 = (bf16[2,128,512]{2,1,0:T(8,128)(2,1)S(1)}, bf16[2,128,512]{2,1,0:T(8,128)(2,1)S(1)}, u32[]{:S(2)}, u32[]{:S(2)}) collective-permute-start(bf16[2,128,512]{2,1,0:T(8,128)(2,1)S(1)} %pad_maximum_fusion.5), channel_id=1, source_target_pairs={{0,1},{1,0},{2,3},{3,2},{4,5},{5,4},{6,7},{7,6},{8,9},{9,8},{10,11... | collective-permute-start | bytes 786440 | tf_op jit(solution)/shard_map/ppermute | solution.py:281
  71.0 2.8 %copy-start.13 = (bf16[32,16,128]{2,1,0:T(8,128)(2,1)}, bf16[32,16,128]{2,1,0:T(8,128)(2,1)S(1)}, u32[]{:S(2)}) copy-start(bf16[32,16,128]{2,1,0:T(8,128)(2,1)S(1)} %all-to-all-done.refs_5_) | copy-start | bytes 393220
  71.0 2.8 %copy-start.1 = (bf16[2,2,128,512]{3,2,1,0:T(8,128)(2,1)}, bf16[2,2,128,512]{3,2,1,0:T(8,128)(2,1)S(1)}, u32[]{:S(2)}) copy-start(bf16[2,2,128,512]{3,2,1,0:T(8,128)(2,1)S(1)} %collective-permute-done.6.refs_12_) | copy-start | bytes 1572868
  71.0 2.8 %copy-start.2 = (bf16[2,2,128,512]{3,2,1,0:T(8,128)(2,1)}, bf16[2,2,128,512]{3,2,1,0:T(8,128)(2,1)S(1)}, u32[]{:S(2)}) copy-start(bf16[2,2,128,512]{3,2,1,0:T(8,128)(2,1)S(1)} %collective-permute-done.8.refs_9_) | copy-start | bytes 1572868
  71.1 6.2 %copy-start.21 = (s32[2,8]{1,0:T(2,128)S(1)}, s32[2,8]{1,0:T(2,128)}, u32[]{:S(2)}) copy-start(s32[2,8]{1,0:T(2,128)} %refs_1_.1) | copy-start | bytes 196
  71.1 13.8 %collective-permute-start.10 = (bf16[2,128,512]{2,1,0:T(8,128)(2,1)S(1)}, bf16[2,128,512]{2,1,0:T(8,128)(2,1)S(1)}, u32[]{:S(2)}, u32[]{:S(2)}) collective-permute-start(bf16[2,128,512]{2,1,0:T(8,128)(2,1)S(1)} %slice_bitcast_fusion), channel_id=1, source_target_pairs={{0,14},{2,0},{4,2},{6,4},{8,6},{10,8},{12,10},{14,12},{1,15},{3,1}... | collective-permute-start | bytes 786440 | tf_op jit(solution)/shard_map/ppermute | solution.py:285
  73.9 11.1 %collective-permute-start.9 = (bf16[2,128,512]{2,1,0:T(8,128)(2,1)}, bf16[2,128,512]{2,1,0:T(8,128)(2,1)S(1)}, u32[]{:S(2)}, u32[]{:S(2)}) collective-permute-start(bf16[2,128,512]{2,1,0:T(8,128)(2,1)} %slice_bitcast_fusion.1), channel_id=1, source_target_pairs={{0,2},{2,4},{4,6},{6,8},{8,10},{10,12},{12,14},{14,0},{1,3},{3,5},... | collective-permute-start | bytes 786440 | tf_op jit(solution)/shard_map/ppermute | solution.py:285
  77.3 7.7 %collective-permute-start = (s32[2,8]{1,0:T(2,128)S(1)}, s32[2,8]{1,0:T(2,128)S(1)}, u32[]{:S(2)}, u32[]{:S(2)}) collective-permute-start(s32[2,8]{1,0:T(2,128)S(1)} %copy-done.21), channel_id=1, source_target_pairs={{0,1},{1,0},{2,3},{3,2},{4,5},{5,4},{6,7},{7,6},{8,9},{9,8},{10,11... | collective-permute-start | bytes 200 | tf_op jit(solution)/shard_map/ppermute | solution.py:282
  84.9 0.5 copy-start.22
  84.9 0.7 copy-start.16
  84.9 0.8 copy-start.17
  85.7 0.7 copy-start.18
  98.5 6.5 %copy-start.11 = (bf16[2,2,128,512]{3,2,1,0:T(8,128)(2,1)S(1)}, bf16[2,2,128,512]{3,2,1,0:T(8,128)(2,1)}, u32[]{:S(2)}) copy-start(bf16[2,2,128,512]{3,2,1,0:T(8,128)(2,1)} %get-tuple-element.37) | copy-start | bytes 1572868
  98.5 8.9 %collective-permute-start.14 = (bf16[2,128,512]{2,1,0:T(8,128)(2,1)}, bf16[2,128,512]{2,1,0:T(8,128)(2,1)S(1)}, u32[]{:S(2)}, u32[]{:S(2)}) collective-permute-start(bf16[2,128,512]{2,1,0:T(8,128)(2,1)} %get-tuple-element.40), channel_id=1, source_target_pairs={{0,14},{2,0},{4,2},{6,4},{8,6},{10,8},{12,10},{14,12},{1,15},{3,1}... | collective-permute-start | bytes 786440 | tf_op jit(solution)/shard_map/ppermute | solution.py:291
  101.9 5.5 %copy-start.12 = (bf16[2,2,128,512]{3,2,1,0:T(8,128)(2,1)S(1)}, bf16[2,2,128,512]{3,2,1,0:T(8,128)(2,1)}, u32[]{:S(2)}) copy-start(bf16[2,2,128,512]{3,2,1,0:T(8,128)(2,1)} %get-tuple-element.39) | copy-start | bytes 1572868
  102.9 10.4 %collective-permute-start.12 = (bf16[2,128,512]{2,1,0:T(8,128)(2,1)}, bf16[2,128,512]{2,1,0:T(8,128)(2,1)S(1)}, u32[]{:S(2)}, u32[]{:S(2)}) collective-permute-start(bf16[2,128,512]{2,1,0:T(8,128)(2,1)} %get-tuple-element.38), channel_id=1, source_target_pairs={{0,2},{2,4},{4,6},{6,8},{8,10},{10,12},{12,14},{14,0},{1,3},{3,5},... | collective-permute-start | bytes 786440 | tf_op jit(solution)/shard_map/ppermute | solution.py:291
  107.5 15.1 %collective-permute-start.15 = (bf16[2,2,128,512]{3,2,1,0:T(8,128)(2,1)S(1)}, bf16[2,2,128,512]{3,2,1,0:T(8,128)(2,1)S(1)}, u32[]{:S(2)}, u32[]{:S(2)}) collective-permute-start(bf16[2,2,128,512]{3,2,1,0:T(8,128)(2,1)S(1)} %pad_maximum_fusion.2), channel_id=1, source_target_pairs={{0,14},{2,0},{4,2},{6,4},{8,6},{10,8},{12,10},{14,12},{1,15},{3,1}... | collective-permute-start | bytes 1572872 | tf_op jit(solution)/shard_map/ppermute | solution.py:294
  113.4 15.1 %copy-start.10 = (bf16[2,2,128,512]{3,2,1,0:T(8,128)(2,1)S(1)}, bf16[2,2,128,512]{3,2,1,0:T(8,128)(2,1)}, u32[]{:S(2)}) copy-start(bf16[2,2,128,512]{3,2,1,0:T(8,128)(2,1)} %get-tuple-element.35) | copy-start | bytes 1572868
  113.5 15.0 %collective-permute-start.13 = (bf16[2,2,128,512]{3,2,1,0:T(8,128)(2,1)S(1)}, bf16[2,2,128,512]{3,2,1,0:T(8,128)(2,1)S(1)}, u32[]{:S(2)}, u32[]{:S(2)}) collective-permute-start(bf16[2,2,128,512]{3,2,1,0:T(8,128)(2,1)S(1)} %pad_maximum_fusion.1), channel_id=1, source_target_pairs={{0,2},{2,4},{4,6},{6,8},{8,10},{10,12},{12,14},{14,0},{1,3},{3,5},... | collective-permute-start | bytes 1572872 | tf_op jit(solution)/shard_map/ppermute | solution.py:294
  128.5 2.1 %copy-start.9 = (bf16[2,2,128,512]{3,2,1,0:T(8,128)(2,1)S(1)}, bf16[2,2,128,512]{3,2,1,0:T(8,128)(2,1)}, u32[]{:S(2)}) copy-start(bf16[2,2,128,512]{3,2,1,0:T(8,128)(2,1)} %get-tuple-element.43) | copy-start | bytes 1572868
  128.6 15.8 %collective-permute-start.16 = (bf16[2,2,128,512]{3,2,1,0:T(8,128)(2,1)S(1)}, bf16[2,2,128,512]{3,2,1,0:T(8,128)(2,1)S(1)}, u32[]{:S(2)}, u32[]{:S(2)}) collective-permute-start(bf16[2,2,128,512]{3,2,1,0:T(8,128)(2,1)S(1)} %add_convert_fusion.3), channel_id=1, source_target_pairs={{0,2},{2,4},{4,6},{6,8},{8,10},{10,12},{12,14},{14,0},{1,3},{3,5},... | collective-permute-start | bytes 1572872 | tf_op jit(solution)/shard_map/ppermute | solution.py:298
  130.6 9.9 %copy-start.20 = (bf16[2,128,512]{2,1,0:T(8,128)(2,1)S(1)}, bf16[2,128,512]{2,1,0:T(8,128)(2,1)}, u32[]{:S(2)}) copy-start(bf16[2,128,512]{2,1,0:T(8,128)(2,1)} %get-tuple-element.31) | copy-start | bytes 786436
  130.7 13.7 %copy-start.8 = (bf16[2,2,128,512]{3,2,1,0:T(8,128)(2,1)S(1)}, bf16[2,2,128,512]{3,2,1,0:T(8,128)(2,1)}, u32[]{:S(2)}) copy-start(bf16[2,2,128,512]{3,2,1,0:T(8,128)(2,1)} %get-tuple-element.34) | copy-start | bytes 1572868
  130.7 15.7 %collective-permute-start.18 = (bf16[2,2,128,512]{3,2,1,0:T(8,128)(2,1)S(1)}, bf16[2,2,128,512]{3,2,1,0:T(8,128)(2,1)S(1)}, u32[]{:S(2)}, u32[]{:S(2)}) collective-permute-start(bf16[2,2,128,512]{3,2,1,0:T(8,128)(2,1)S(1)} %add_convert_fusion.1), channel_id=1, source_target_pairs={{0,14},{2,0},{4,2},{6,4},{8,6},{10,8},{12,10},{14,12},{1,15},{3,1}... | collective-permute-start | bytes 1572872 | tf_op jit(solution)/shard_map/ppermute | solution.py:298
  135.5 15.9 %collective-permute-start.11 = (bf16[2,128,512]{2,1,0:T(8,128)(2,1)}, bf16[2,128,512]{2,1,0:T(8,128)(2,1)}, u32[]{:S(2)}, u32[]{:S(2)}) collective-permute-start(bf16[2,128,512]{2,1,0:T(8,128)(2,1)} %get-tuple-element.32), channel_id=1, source_target_pairs={{0,1},{1,0},{2,3},{3,2},{4,5},{5,4},{6,7},{7,6},{8,9},{9,8},{10,11... | collective-permute-start | bytes 786440 | tf_op jit(solution)/shard_map/ppermute | solution.py:302
  140.5 13.1 %all-to-all-start.1 = ((bf16[32,16,128]{2,1,0:T(8,128)(2,1)}), bf16[32,16,128]{2,1,0:T(8,128)(2,1)S(1)}, u32[]{:S(2)}, u32[]{:S(2)}) async-start(bf16[32,16,128]{2,1,0:T(8,128)(2,1)} %get-tuple-element.45), calls=%async_computation.1 | async-start | bytes 262144 | tf_op jit(solution)/shard_map/all_to_all | solution.py:296
  144.4 2.1 %copy-start.7 = (bf16[2,2,128,512]{3,2,1,0:T(8,128)(2,1)S(1)}, bf16[2,2,128,512]{3,2,1,0:T(8,128)(2,1)}, u32[]{:S(2)}) copy-start(bf16[2,2,128,512]{3,2,1,0:T(8,128)(2,1)} %get-tuple-element.42) | copy-start | bytes 1572868
  144.6 14.7 %collective-permute-start.17 = (bf16[2,2,128,512]{3,2,1,0:T(8,128)(2,1)S(1)}, bf16[2,2,128,512]{3,2,1,0:T(8,128)(2,1)S(1)}, u32[]{:S(2)}, u32[]{:S(2)}) collective-permute-start(bf16[2,2,128,512]{3,2,1,0:T(8,128)(2,1)S(1)} %add_convert_fusion.2), channel_id=1, source_target_pairs={{0,2},{2,4},{4,6},{6,8},{8,10},{10,12},{12,14},{14,0},{1,3},{3,5},... | collective-permute-start | bytes 1572872 | tf_op jit(solution)/shard_map/ppermute | solution.py:300
  146.5 14.0 %copy-start.3 = (f32[2,2,128,512]{3,2,1,0:T(8,128)S(1)}, f32[2,2,128,512]{3,2,1,0:T(8,128)}, u32[]{:S(2)}) copy-start(f32[2,2,128,512]{3,2,1,0:T(8,128)} %get-tuple-element.33) | copy-start | bytes 3145732
  146.7 13.8 %collective-permute-start.19 = (bf16[2,2,128,512]{3,2,1,0:T(8,128)(2,1)S(1)}, bf16[2,2,128,512]{3,2,1,0:T(8,128)(2,1)S(1)}, u32[]{:S(2)}, u32[]{:S(2)}) collective-permute-start(bf16[2,2,128,512]{3,2,1,0:T(8,128)(2,1)S(1)} %add_convert_fusion), channel_id=1, source_target_pairs={{0,14},{2,0},{4,2},{6,4},{8,6},{10,8},{12,10},{14,12},{1,15},{3,1}... | collective-permute-start | bytes 1572872 | tf_op jit(solution)/shard_map/ppermute | solution.py:300
  160.5 5.2 %copy-start.14 = (bf16[128,512]{1,0:T(8,128)(2,1)S(1)}, bf16[128,512]{1,0:T(8,128)(2,1)}, u32[]{:S(2)}) copy-start(bf16[128,512]{1,0:T(8,128)(2,1)} %get-tuple-element.54) | copy-start | bytes 393220
  160.5 5.2 %copy-start.15 = (bf16[128,512]{1,0:T(8,128)(2,1)S(1)}, bf16[128,512]{1,0:T(8,128)(2,1)}, u32[]{:S(2)}) copy-start(bf16[128,512]{1,0:T(8,128)(2,1)} %get-tuple-element.55) | copy-start | bytes 393220
  160.8 6.1 %collective-permute-start.20 = (bf16[2,128,512]{2,1,0:T(8,128)(2,1)S(1)}, bf16[2,128,512]{2,1,0:T(8,128)(2,1)S(1)}, u32[]{:S(2)}, u32[]{:S(2)}) collective-permute-start(bf16[2,128,512]{2,1,0:T(8,128)(2,1)S(1)} %get-tuple-element.47), channel_id=1, source_target_pairs={{0,1},{1,0},{2,3},{3,2},{4,5},{5,4},{6,7},{7,6},{8,9},{9,8},{10,11... | collective-permute-start | bytes 786440 | tf_op jit(solution)/shard_map/ppermute | solution.py:309

commit v6 on v5

--- a/solution.py
+++ b/solution.py
@@ -20,7 +20,7 @@
 HEADS = HALF // HEAD_DIM
 NEAR = 256
 GROWS = 4 * HEADS
-SEND_ORDER = (4, 12, 11, 3, 5, 13, 2, 10, 6, 14, 1, 9, 7, 15, 8, 0)
+SEND_ORDER = (4, 12, 11, 5, 3, 6, 10, 13, 2, 7, 9, 14, 1, 15, 8, 0)
 FKEYS = FAR * BLOCK
 SCALE = 1.0 / math.sqrt(HEAD_DIM)
 EXP_SCALE = SCALE * math.log2(math.e)
@@ -42,25 +42,20 @@
 
 def attend_kernel(*refs):
     pos, far_own, far_peer, qdo_own, qdo_peer, glob = refs[:6]
-    arrays = refs[6:15]
-    outputs = refs[15:19]
-    parts = refs[19:27]
-    slots, near, fgrad, gwide, res_own, res_peer, base, gglob, spare, table, in_sem, out_sem = refs[27:]
-    sources = [
-        arrays[offset if offset < 4 else offset + 1].at[chain] if offset != 4 else arrays[4 + chain]
-        for chain in range(2)
-        for offset in range(NY)
-    ]
-    my_y, my_c, my_w = pos[0], pos[1], pos[2]
+    sources = refs[6:22]
+    outputs = refs[22:26]
+    parts = refs[26:40]
+    slots, near, fgrad, gwide, res_own, res_peer, base, gglob, spare, table, in_sem, out_sem = refs[40:]
+    my_y, my_c = pos[0], pos[1]
     for who, far in enumerate((far_own, far_peer)):
         for row in range(BLK):
             for entry in range(FAR):
                 block = far[row, entry]
                 group = lax.shift_right_logical(block, 6)
-                chain = lax.bitwise_xor(lax.bitwise_and(group, 1), my_c)
                 offset = lax.bitwise_and(
                     lax.shift_right_logical(group, 1) - my_y, NY - 1
                 )
+                chain = lax.bitwise_xor(lax.bitwise_and(group, 1), my_c)
                 inner = lax.bitwise_and(block, 1)
                 table[who, chain * NY + offset] = (row * FAR + entry) * 2 + inner
     copies = []
@@ -96,7 +91,7 @@
                 )
             near[kind, who, TOK + WINDOWS :, :] = jnp.zeros((NEAR - TOK - WINDOWS, HALF), BF16)
     column = lax.broadcasted_iota(jnp.int32, (TOK, NEAR), 1)
-    hidden = (column >= TOK + WINDOWS) | (column == TOK + my_w)
+    hidden = (column >= TOK + WINDOWS) | (column == TOK)
     for copy in copies:
         copy.wait()
 
@@ -194,21 +189,18 @@
                     base[source // NY, kind, rows, :] += value
                 else:
                     spare[source, kind, rows, :] = value.astype(BF16)
-        chain, offset = source // NY, source % NY
-        if offset:
-            index = offset - 1 if offset < 4 else offset
-            send(spare.at[source], parts[3 + chain] if offset == 4 else parts[index].at[chain])
+        if source % NY:
+            send(spare.at[source], parts[source - 1 - source // NY])
     send(base, outputs[2])
     for copy in copies:
         copy.wait()
 
 
-def attend(pos, far_own, far_peer, qdo_own, qdo_peer, glob, arrays):
+def attend(pos, far_own, far_peer, qdo_own, qdo_peer, glob, sources):
     smem = pl.BlockSpec(memory_space=pltpu.SMEM)
     vmem = pl.BlockSpec(memory_space=pltpu.VMEM)
     anywhere = pl.BlockSpec(memory_space=pl.ANY)
     piece = jax.ShapeDtypeStruct((2, TOK, HALF), BF16)
-    double = jax.ShapeDtypeStruct((2, 2, TOK, HALF), BF16)
     return pl.pallas_call(
         attend_kernel,
         out_shape=[
@@ -217,11 +209,9 @@
             jax.ShapeDtypeStruct((2, 2, TOK, HALF), F32),
             jax.ShapeDtypeStruct((WINDOWS, GROWS, HEAD_DIM), BF16),
         ]
-        + [double] * 3
-        + [piece] * 2
-        + [double] * 3,
-        in_specs=[smem] * 3 + [vmem] * 3 + [anywhere] * 9,
-        out_specs=[anywhere] * 12,
+        + [piece] * 14,
+        in_specs=[smem] * 3 + [vmem] * 3 + [anywhere] * 16,
+        out_specs=[anywhere] * 18,
         scratch_shapes=[
             pltpu.VMEM((2, 2, BLK * FKEYS, HALF), BF16),
             pltpu.VMEM((2, 2, NEAR, HALF), BF16),
@@ -240,22 +230,27 @@
         cost_estimate=pl.CostEstimate(
             flops=1_200_000_000, bytes_accessed=12_000_000, transcendentals=800_000
         ),
-    )(pos, far_own, far_peer, qdo_own, qdo_peer, glob, *arrays)
+    )(pos, far_own, far_peer, qdo_own, qdo_peer, glob, *sources)
 
 
 UP = [(i, (i + 1) % NY) for i in range(NY)]
 DOWN = [(i, (i - 1) % NY) for i in range(NY)]
+SPREAD = ((0, 1), (2, 3), (4,))
 SWAP = [(0, 1), (1, 0)]
 
 
 def plus(a, b):
     return (a.astype(F32) + b.astype(F32)).astype(BF16)
+
+
+def flip(rows, bit):
+    axis, size, step = ("z", NZ, 1 << bit) if bit < 3 else ("x", NX, 1 << (bit - 3))
+    return lax.ppermute(rows, axis, [(i, i ^ step) for i in range(size)])
 
 
 def per_device(query_rows, key_rows, value_rows, out_grad, far_blocks):
     my_y = lax.axis_index("y")
     my_c = lax.axis_index("c")
-    my_w = lax.axis_index("x") * NZ + lax.axis_index("z")
     swap = functools.partial(lax.ppermute, axis_name="c", perm=SWAP)
     up = functools.partial(lax.ppermute, axis_name="y", perm=UP)
     down = functools.partial(lax.ppermute, axis_name="y", perm=DOWN)
@@ -269,45 +264,62 @@
     kv_own, kv_send = split(key_rows, value_rows)
     qdo_own, qdo_send = split(query_rows, out_grad)
     kv_peer = swap(kv_send)
-    row = jnp.concatenate([kv_own[:, 0], kv_peer[:, 0]]).reshape(GROWS, HEAD_DIM)
-    ring = [None] * NY
-    ring[0] = jnp.stack([kv_own, kv_peer])
-    ring[7], ring[1] = up(ring[0]), down(ring[0])
-    row, ring[7], ring[1] = lax.optimization_barrier((row, ring[7], ring[1]))
-    glob = lax.all_to_all(
-        jnp.broadcast_to(row, (WINDOWS, GROWS, HEAD_DIM)), ("x", "z"), 0, 0, tiled=True
+    sources = [None] * 16
+    sources[0], sources[NY] = kv_own, kv_peer
+    glob = jnp.concatenate([kv_own[:, 0], kv_peer[:, 0]]).reshape(1, GROWS, HEAD_DIM)
+    chains = ((0, up, 4, -1), (0, down, 3, 1), (NY, up, 3, -1), (NY, down, 4, 1))
+    held = [kv_own, kv_own, kv_peer, kv_peer]
+    for step in range(1, 5):
+        for i, (first, move, count, sign) in enumerate(chains):
+            if step <= count:
+                held[i] = move(held[i])
+        if step <= 3:
+            glob, held[0] = lax.optimization_barrier((glob, held[0]))
+            for bit in SPREAD[step - 1]:
+                glob = jnp.concatenate([glob, flip(glob, bit)])
+        if step == 1:
+            qdo_peer = swap(qdo_send)
+            far_peer = swap(far_blocks)
+        if step == 3:
+            glob, qdo_peer, far_peer, held[3] = lax.optimization_barrier(
+                (glob, qdo_peer, far_peer, held[3])
+            )
+        for i, (first, move, count, sign) in enumerate(chains):
+            if step <= count:
+                sources[first + (sign * step) % NY] = held[i]
+    pos = jnp.stack([my_y, my_c]).astype(jnp.int32)
+    res_own, res_peer, base, gglob, *parts = attend(
+        pos, far_blocks, far_peer, qdo_own, qdo_peer, glob, sources
     )
-    ring[6], ring[2] = up(ring[7]), down(ring[1])
-    qdo_peer = swap(qdo_send)
-    far_peer = swap(far_blocks)
-    ring[5], ring[3] = up(ring[6]), down(ring[2])
-    glob, ring[5], ring[3] = lax.optimization_barrier((glob, ring[5], ring[3]))
-    across = up(ring[5][0]), down(ring[3][1])
-    pos = jnp.stack([my_y, my_c, my_w]).astype(jnp.int32)
-    arrays = [*ring[:4], *across, *ring[5:]]
-    res_own, res_peer, base, gglob, *parts = attend(
-        pos, far_blocks, far_peer, qdo_own, qdo_peer, glob, arrays
-    )
-    rise, fall = up(parts[3]), down(parts[4])
-    rise = jnp.stack([plus(parts[2][0], rise), parts[2][1]])
-    fall = jnp.stack([parts[5][0], plus(parts[5][1], fall)])
-    rise, fall = up(rise), down(fall)
-    gglob, rise, fall = lax.optimization_barrier((gglob, rise, fall))
-    gback = lax.all_to_all(gglob, ("x", "z"), 0, 0, tiled=True)
-    rise, fall = plus(parts[1], rise), plus(parts[6], fall)
-    rise, fall = up(rise), down(fall)
-    rise, fall = plus(parts[0], rise), plus(parts[7], fall)
-    rise, fall = up(rise), down(fall)
-    gsum = jnp.sum(gback.astype(F32), axis=0).reshape(2, 2, 1, HALF)
+    part = parts[:7], parts[7:]
+    at = [4, 5, 3, 4]
+    held = [part[first // NY][o - 1] for o, (first, _, _, _) in zip(at, chains)]
+    for step in range(1, 5):
+        for i, (first, move, count, sign) in enumerate(chains):
+            if step <= count:
+                held[i] = move(held[i])
+        if step <= 3:
+            gglob, held[0] = lax.optimization_barrier((gglob, held[0]))
+            for bit in reversed(SPREAD[3 - step]):
+                rows = 1 << bit
+                gglob = gglob[:rows].astype(F32) + flip(gglob[rows:], bit).astype(F32)
+                gglob = gglob.astype(BF16) if bit else gglob
+        for i, (first, move, count, sign) in enumerate(chains):
+            if step <= count:
+                at[i] = (at[i] + sign) % NY
+                if at[i]:
+                    held[i] = plus(held[i], part[first // NY][at[i] - 1])
+    far_own, far_peer = held[:2], held[2:]
+    gsum = gglob.reshape(2, 2, 1, HALF)
     res_back = swap(res_peer)
     first_row = lax.broadcasted_iota(jnp.int32, (1, TOK, 1), 1) == 0
 
-    def finish(who):
-        total = base[who] + rise[who].astype(F32) + fall[who].astype(F32)
+    def finish(who, far):
+        total = base[who] + far[0].astype(F32) + far[1].astype(F32)
         return (total + jnp.where(first_row, gsum[who], 0.0)).astype(BF16)
 
-    peer_grad = swap(finish(1))
-    own_grad = finish(0)
+    peer_grad = swap(finish(1, far_peer))
+    own_grad = finish(0, far_own)
 
     def join(mine, other):
         return jnp.where(

time: 170 us -> 197 us (1.16)
  starting transfers between devices: 93.7 us -> 149 us
  waiting for transfers between devices: 47.5 us -> 23.8 us
  local copies, waits for them, and re-layouts: 5.81 us -> 2.69 us
    ppermute x17 -> x39, starting transfers between devices: 56.4 us -> 126 us  [the longest x28 84.5 us: per_device(): held[i] = move(held[i])]
    ppermute x17 -> x39, waiting for transfers between devices: 42.1 us -> 23.8 us  [the longest x28 20.1 us: per_device(): held[i] = move(held[i])]
    all_to_all x2 -> x0, starting transfers between devices: 12.6 us -> none  [the longest x1 8.7 us: per_device(): lax.all_to_all(jnp.broadcast_to(row, (WINDOWS, GROWS, HEAD_DIM)), ('x', '...]
    all_to_all x2 -> x0, waiting for transfers between devices: 4.22 us -> none  [the longest x1 3.62 us: per_device(): lax.all_to_all(jnp.broadcast_to(row, (WINDOWS, GROWS, HEAD_DIM)), ('x', '...]
    ppermute x1, starting transfers between devices: 6.29 us -> 3.43 us  [per_device(): far_peer = swap(far_blocks)]
  transfers between devices with their start and end apart: 23 -> 43, of which waited for: 13 -> 6; matrix products, arithmetic and copies ran while one was open for 6% -> 3% of each run, Pallas kernels for 0% -> 0%
where the time goes in v6:
time: 197 us; the launch traced here: 196 us
  starting transfers between devices  149 us (76%)
  waiting for transfers between devices  23.8 us (12%)
  Pallas kernels  11.9 us (6%)
  other arithmetic  6.8 us (3%)
  local copies, waits for them, and re-layouts  2.69 us (1%)
  between operations  1.97 us (1%)
    ppermute x28, starting transfers between devices, per_device(): held[i] = move(held[i])  84.5 us
    ppermute x10, starting transfers between devices, flip(): return lax.ppermute(rows, axis, [(i, i ^ step) for i in range(size)])  34 us
    ppermute x28, waiting for transfers between devices, per_device(): held[i] = move(held[i])  20.1 us
    pallas_call x1, Pallas kernels, attend(): pl.pallas_call(attend_kernel, out_shape=[piece, piece, jax.ShapeDtypeStru...  11.9 us
    ppermute x1, starting transfers between devices, per_device(): kv_peer = swap(kv_send)  8.79 us
    ppermute x1, starting transfers between devices, per_device(): peer_grad = swap(finish(1, far_peer))  7.58 us
    ppermute x1, starting transfers between devices, per_device(): qdo_peer = swap(qdo_send)  5.78 us
    ppermute x1, starting transfers between devices, per_device(): res_back = swap(res_peer)  4.66 us
  transfers between devices with their start and end apart: 43, of which 6 were waited for; matrix products, arithmetic and copies ran while one was open for 3% of the time, Pallas kernels for 0%

profile of v6, /device:TPU:1, one launch (start us, length us, event | category | flops | bytes accessed | tf_op | source)
XLA Modules:
  0.0 195.9 jit_solution(4334798195810550016)
XLA Ops:
  1.8 8.8 %collective-permute-start = (bf16[2,128,512]{2,1,0:T(8,128)(2,1)S(1)}, bf16[2,128,512]{2,1,0:T(8,128)(2,1)S(1)}, u32[]{:S(2)}, u32[]{:S(2)}) collective-permute-start(bf16[2,128,512]{2,1,0:T(8,128)(2,1)S(1)} %pad_maximum_fusion.1), channel_id=1, source_target_pairs={{0,1},{1,0},{2,3},{3,2},{4,5},{5,4},{6,7},{7,6},{8,9},{9,8},{10,11... | collective-permute-start | bytes 786440 | tf_op jit(solution)/shard_map/ppermute | solution.py:266
  10.6 2.1 %collective-permute-start.1 = (bf16[2,128,512]{2,1,0:T(8,128)(2,1)S(1)}, bf16[2,128,512]{2,1,0:T(8,128)(2,1)S(1)}, u32[]{:S(2)}, u32[]{:S(2)}) collective-permute-start(bf16[2,128,512]{2,1,0:T(8,128)(2,1)S(1)} %pad_maximum_fusion.refs_6_), channel_id=1, source_target_pairs={{0,2},{2,4},{4,6},{6,8},{8,10},{10,12},{12,14},{14,0},{1,3},{3,5},... | collective-permute-start | bytes 786440 | tf_op jit(solution)/shard_map/ppermute | solution.py:275
  12.8 9.0 %collective-permute-done.1.refs_13_ = bf16[2,128,512]{2,1,0:T(8,128)(2,1)S(1)} collective-permute-done((bf16[2,128,512]{2,1,0:T(8,128)(2,1)S(1)}, bf16[2,128,512]{2,1,0:T(8,128)(2,1)S(1)}, u32[]{:S(2)}, u32[]{:S(2)}) %collective-permute-start.1) | collective-permute-done | bytes 262176 | tf_op jit(solution)/shard_map/ppermute | solution.py:275
  21.8 1.9 collective-permute-start.2
  23.7 1.9 collective-permute-start.14
  25.6 3.4 %collective-permute-start.4 = (bf16[2,128,512]{2,1,0:T(8,128)(2,1)S(1)}, bf16[2,128,512]{2,1,0:T(8,128)(2,1)S(1)}, u32[]{:S(2)}, u32[]{:S(2)}) collective-permute-start(bf16[2,128,512]{2,1,0:T(8,128)(2,1)S(1)} %collective-permute-done.1.refs_13_), channel_id=1, source_target_pairs={{0,2},{2,4},{4,6},{6,8},{8,10},{10,12},{12,14},{14,0},{1,3},{3,5},... | collective-permute-start | bytes 786440 | tf_op jit(solution)/shard_map/ppermute | solution.py:275
  29.0 3.1 %collective-permute-start.11 = (bf16[2,128,512]{2,1,0:T(8,128)(2,1)S(1)}, bf16[2,128,512]{2,1,0:T(8,128)(2,1)S(1)}, u32[]{:S(2)}, u32[]{:S(2)}) collective-permute-start(bf16[2,128,512]{2,1,0:T(8,128)(2,1)S(1)} %collective-permute-done.refs_14_), channel_id=1, source_target_pairs={{0,14},{2,0},{4,2},{6,4},{8,6},{10,8},{12,10},{14,12},{1,15},{3,1}... | collective-permute-start | bytes 786440 | tf_op jit(solution)/shard_map/ppermute | solution.py:275
  32.2 4.6 %collective-permute-start.3 = (bf16[2,16,128]{2,1,0:T(8,128)(2,1)S(1)}, bf16[2,16,128]{2,1,0:T(8,128)(2,1)S(1)}, u32[]{:S(2)}, u32[]{:S(2)}) collective-permute-start(bf16[2,16,128]{2,1,0:T(8,128)(2,1)S(1)} %pad_maximum_fusion.8), channel_id=1, source_target_pairs={{0,32},{16,48},{32,0},{48,16},{64,96},{80,112},{96,64},{112,80},{1... | collective-permute-start | bytes 24584 | tf_op jit(solution)/shard_map/ppermute | solution.py:248
  36.9 1.9 collective-permute-start.19
  38.8 7.9 %collective-permute-start.5 = (bf16[4,16,128]{2,1,0:T(8,128)(2,1)S(1)}, bf16[4,16,128]{2,1,0:T(8,128)(2,1)S(1)}, u32[]{:S(2)}, u32[]{:S(2)}) collective-permute-start(bf16[4,16,128]{2,1,0:T(8,128)(2,1)S(1)} %pad_maximum_fusion.7), channel_id=1, source_target_pairs={{0,64},{16,80},{32,96},{48,112},{64,0},{80,16},{96,32},{112,48},{1... | collective-permute-start | bytes 49160 | tf_op jit(solution)/shard_map/ppermute | solution.py:248
  46.8 4.6 %collective-permute-start.12 = (bf16[2,128,512]{2,1,0:T(8,128)(2,1)S(1)}, bf16[2,128,512]{2,1,0:T(8,128)(2,1)S(1)}, u32[]{:S(2)}, u32[]{:S(2)}) collective-permute-start(bf16[2,128,512]{2,1,0:T(8,128)(2,1)S(1)} %collective-permute-done.11.refs_15_), channel_id=1, source_target_pairs={{0,14},{2,0},{4,2},{6,4},{8,6},{10,8},{12,10},{14,12},{1,15},{3,1}... | collective-permute-start | bytes 786440 | tf_op jit(solution)/shard_map/ppermute | solution.py:275
  51.5 1.9 collective-permute-start.15
  53.4 3.4 %collective-permute-start.7 = (bf16[2,128,512]{2,1,0:T(8,128)(2,1)S(1)}, bf16[2,128,512]{2,1,0:T(8,128)(2,1)S(1)}, u32[]{:S(2)}, u32[]{:S(2)}) collective-permute-start(bf16[2,128,512]{2,1,0:T(8,128)(2,1)S(1)} %collective-permute-done.4.refs_12_), channel_id=1, source_target_pairs={{0,2},{2,4},{4,6},{6,8},{8,10},{10,12},{12,14},{14,0},{1,3},{3,5},... | collective-permute-start | bytes 786440 | tf_op jit(solution)/shard_map/ppermute | solution.py:275
  56.8 3.1 %collective-permute-start.6 = (bf16[8,16,128]{2,1,0:T(8,128)(2,1)S(1)}, bf16[8,16,128]{2,1,0:T(8,128)(2,1)S(1)}, u32[]{:S(2)}, u32[]{:S(2)}) collective-permute-start(bf16[8,16,128]{2,1,0:T(8,128)(2,1)S(1)} %pad_maximum_fusion.6), channel_id=1, source_target_pairs={{0,128},{128,0},{256,384},{384,256},{1,129},{129,1},{257,385},{385... | collective-permute-start | bytes 98312 | tf_op jit(solution)/shard_map/ppermute | solution.py:248
  60.0 5.8 %collective-permute-start.9 = (bf16[2,128,512]{2,1,0:T(8,128)(2,1)S(1)}, bf16[2,128,512]{2,1,0:T(8,128)(2,1)S(1)}, u32[]{:S(2)}, u32[]{:S(2)}) collective-permute-start(bf16[2,128,512]{2,1,0:T(8,128)(2,1)S(1)} %pad_maximum_fusion.2), channel_id=1, source_target_pairs={{0,1},{1,0},{2,3},{3,2},{4,5},{5,4},{6,7},{7,6},{8,9},{9,8},{10,11... | collective-permute-start | bytes 786440 | tf_op jit(solution)/shard_map/ppermute | solution.py:281
  65.8 1.9 collective-permute-start.20
  67.8 4.6 %collective-permute-start.13 = (bf16[2,128,512]{2,1,0:T(8,128)(2,1)S(1)}, bf16[2,128,512]{2,1,0:T(8,128)(2,1)S(1)}, u32[]{:S(2)}, u32[]{:S(2)}) collective-permute-start(bf16[2,128,512]{2,1,0:T(8,128)(2,1)S(1)} %collective-permute-done.12.refs_16_), channel_id=1, source_target_pairs={{0,14},{2,0},{4,2},{6,4},{8,6},{10,8},{12,10},{14,12},{1,15},{3,1}... | collective-permute-start | bytes 786440 | tf_op jit(solution)/shard_map/ppermute | solution.py:275
  72.4 4.4 %collective-permute-start.8 = (bf16[16,16,128]{2,1,0:T(8,128)(2,1)S(1)}, bf16[16,16,128]{2,1,0:T(8,128)(2,1)S(1)}, u32[]{:S(2)}, u32[]{:S(2)}) collective-permute-start(bf16[16,16,128]{2,1,0:T(8,128)(2,1)S(1)} %pad_maximum_fusion.5), channel_id=1, source_target_pairs={{0,256},{128,384},{256,0},{384,128},{1,257},{129,385},{257,1},{385... | collective-permute-start | bytes 196616 | tf_op jit(solution)/shard_map/ppermute | solution.py:248
  76.8 3.4 %collective-permute-start.10 = (s32[2,8]{1,0:T(2,128)S(1)}, s32[2,8]{1,0:T(2,128)S(1)}, u32[]{:S(2)}, u32[]{:S(2)}) collective-permute-start(s32[2,8]{1,0:T(2,128)S(1)} %copy-done.32), channel_id=1, source_target_pairs={{0,1},{1,0},{2,3},{3,2},{4,5},{5,4},{6,7},{7,6},{8,9},{9,8},{10,11... | collective-permute-start | bytes 200 | tf_op jit(solution)/shard_map/ppermute | solution.py:282
  80.2 1.9 collective-permute-start.16
  82.8 3.4 %collective-permute-start.17 = (bf16[2,128,512]{2,1,0:T(8,128)(2,1)S(1)}, bf16[2,128,512]{2,1,0:T(8,128)(2,1)S(1)}, u32[]{:S(2)}, u32[]{:S(2)}) collective-permute-start(bf16[2,128,512]{2,1,0:T(8,128)(2,1)S(1)} %collective-permute-done.7.refs_11_), channel_id=1, source_target_pairs={{0,2},{2,4},{4,6},{6,8},{8,10},{10,12},{12,14},{14,0},{1,3},{3,5},... | collective-permute-start | bytes 786440 | tf_op jit(solution)/shard_map/ppermute | solution.py:275
  86.2 1.9 collective-permute-start.21
  88.2 4.6 %collective-permute-start.18 = (bf16[2,128,512]{2,1,0:T(8,128)(2,1)S(1)}, bf16[2,128,512]{2,1,0:T(8,128)(2,1)S(1)}, u32[]{:S(2)}, u32[]{:S(2)}) collective-permute-start(bf16[2,128,512]{2,1,0:T(8,128)(2,1)S(1)} %collective-permute-done.13.refs_17_), channel_id=1, source_target_pairs={{0,14},{2,0},{4,2},{6,4},{8,6},{10,8},{12,10},{14,12},{1,15},{3,1}... | collective-permute-start | bytes 786440 | tf_op jit(solution)/shard_map/ppermute | solution.py:275
  94.1 4.5 %collective-permute-done.21.refs_19_ = bf16[2,128,512]{2,1,0:T(8,128)(2,1)S(1)} collective-permute-done((bf16[2,128,512]{2,1,0:T(8,128)(2,1)S(1)}, bf16[2,128,512]{2,1,0:T(8,128)(2,1)S(1)}, u32[]{:S(2)}, u32[]{:S(2)}) %collective-permute-start.21) | collective-permute-done | bytes 262176 | tf_op jit(solution)/shard_map/ppermute | solution.py:275
  100.0 11.9 %shard_map.84 = (bf16[2,128,512]{2,1,0:T(8,128)(2,1)}, bf16[2,128,512]{2,1,0:T(8,128)(2,1)}, f32[2,2,128,512]{3,2,1,0:T(8,128)}, bf16[32,16,128]{2,1,0:T(8,128)(...) custom-call(s32[2]{0:T(128)} %pad_add_fusion.refs_0_, ...), custom_call_target="tpu_custom_call" | custom-call | flops 1200000000 | bytes 12000000 | tf_op jit(solution)/shard_map/pallas_call | solution.py:204
  111.9 1.9 collective-permute-start.35
  113.9 4.6 %collective-permute-start.38 = (bf16[2,128,512]{2,1,0:T(8,128)(2,1)}, bf16[2,128,512]{2,1,0:T(8,128)(2,1)S(1)}, u32[]{:S(2)}, u32[]{:S(2)}) collective-permute-start(bf16[2,128,512]{2,1,0:T(8,128)(2,1)} %get-tuple-element.68), channel_id=1, source_target_pairs={{0,14},{2,0},{4,2},{6,4},{8,6},{10,8},{12,10},{14,12},{1,15},{3,1}... | collective-permute-start | bytes 786440 | tf_op jit(solution)/shard_map/ppermute | solution.py:300
  118.4 1.9 collective-permute-start.23
  120.4 4.6 %collective-permute-start.30 = (bf16[2,128,512]{2,1,0:T(8,128)(2,1)}, bf16[2,128,512]{2,1,0:T(8,128)(2,1)S(1)}, u32[]{:S(2)}, u32[]{:S(2)}) collective-permute-start(bf16[2,128,512]{2,1,0:T(8,128)(2,1)} %get-tuple-element.61), channel_id=1, source_target_pairs={{0,14},{2,0},{4,2},{6,4},{8,6},{10,8},{12,10},{14,12},{1,15},{3,1}... | collective-permute-start | bytes 786440 | tf_op jit(solution)/shard_map/ppermute | solution.py:300
  125.0 4.7 %collective-permute-start.22 = (bf16[2,128,512]{2,1,0:T(8,128)(2,1)}, bf16[2,128,512]{2,1,0:T(8,128)(2,1)S(1)}, u32[]{:S(2)}, u32[]{:S(2)}) collective-permute-start(bf16[2,128,512]{2,1,0:T(8,128)(2,1)} %get-tuple-element.49), channel_id=1, source_target_pairs={{0,1},{1,0},{2,3},{3,2},{4,5},{5,4},{6,7},{7,6},{8,9},{9,8},{10,11... | collective-permute-start | bytes 786440 | tf_op jit(solution)/shard_map/ppermute | solution.py:314
  130.8 1.9 collective-permute-start.36
  132.8 4.6 %collective-permute-start.39 = (bf16[2,128,512]{2,1,0:T(8,128)(2,1)S(1)}, bf16[2,128,512]{2,1,0:T(8,128)(2,1)S(1)}, u32[]{:S(2)}, u32[]{:S(2)}) collective-permute-start(bf16[2,128,512]{2,1,0:T(8,128)(2,1)S(1)} %add_convert_fusion.2), channel_id=1, source_target_pairs={{0,14},{2,0},{4,2},{6,4},{8,6},{10,8},{12,10},{14,12},{1,15},{3,1}... | collective-permute-start | bytes 786440 | tf_op jit(solution)/shard_map/ppermute | solution.py:300
  137.5 2.1 %collective-permute-start.25 = (bf16[2,128,512]{2,1,0:T(8,128)(2,1)S(1)}, bf16[2,128,512]{2,1,0:T(8,128)(2,1)S(1)}, u32[]{:S(2)}, u32[]{:S(2)}) collective-permute-start(bf16[2,128,512]{2,1,0:T(8,128)(2,1)S(1)} %add_convert_fusion.9), channel_id=1, source_target_pairs={{0,2},{2,4},{4,6},{6,8},{8,10},{10,12},{12,14},{14,0},{1,3},{3,5},... | collective-permute-start | bytes 786440 | tf_op jit(solution)/shard_map/ppermute | solution.py:300
  139.6 3.3 %collective-permute-start.24 = (bf16[16,16,128]{2,1,0:T(8,128)(2,1)S(1)}, bf16[16,16,128]{2,1,0:T(8,128)(2,1)S(1)}, u32[]{:S(2)}, u32[]{:S(2)}) collective-permute-start(bf16[16,16,128]{2,1,0:T(8,128)(2,1)S(1)} %slice.122), channel_id=1, source_target_pairs={{0,256},{128,384},{256,0},{384,128},{1,257},{129,385},{257,1},{385... | collective-permute-start | bytes 196616 | tf_op jit(solution)/shard_map/ppermute | solution.py:248
  143.0 4.7 %collective-permute-start.31 = (bf16[2,128,512]{2,1,0:T(8,128)(2,1)S(1)}, bf16[2,128,512]{2,1,0:T(8,128)(2,1)S(1)}, u32[]{:S(2)}, u32[]{:S(2)}) collective-permute-start(bf16[2,128,512]{2,1,0:T(8,128)(2,1)S(1)} %add_convert_fusion.6), channel_id=1, source_target_pairs={{0,14},{2,0},{4,2},{6,4},{8,6},{10,8},{12,10},{14,12},{1,15},{3,1}... | collective-permute-start | bytes 786440 | tf_op jit(solution)/shard_map/ppermute | solution.py:300
  147.9 1.9 collective-permute-start.37
  149.9 4.6 %collective-permute-start.40 = (bf16[2,128,512]{2,1,0:T(8,128)(2,1)S(1)}, bf16[2,128,512]{2,1,0:T(8,128)(2,1)S(1)}, u32[]{:S(2)}, u32[]{:S(2)}) collective-permute-start(bf16[2,128,512]{2,1,0:T(8,128)(2,1)S(1)} %add_convert_fusion.1), channel_id=1, source_target_pairs={{0,14},{2,0},{4,2},{6,4},{8,6},{10,8},{12,10},{14,12},{1,15},{3,1}... | collective-permute-start | bytes 786440 | tf_op jit(solution)/shard_map/ppermute | solution.py:300
  154.5 2.0 %collective-permute-start.26 = (bf16[8,16,128]{2,1,0:T(8,128)(2,1)S(1)}, bf16[8,16,128]{2,1,0:T(8,128)(2,1)S(1)}, u32[]{:S(2)}, u32[]{:S(2)}) collective-permute-start(bf16[8,16,128]{2,1,0:T(8,128)(2,1)S(1)} %slice.124), channel_id=1, source_target_pairs={{0,128},{128,0},{256,384},{384,256},{1,129},{129,1},{257,385},{385... | collective-permute-start | bytes 98312 | tf_op jit(solution)/shard_map/ppermute | solution.py:248
  156.6 1.9 collective-permute-start.28
  159.5 1.9 collective-permute-start.27
  161.6 3.8 %collective-permute-start.32 = (bf16[2,128,512]{2,1,0:T(8,128)(2,1)S(1)}, bf16[2,128,512]{2,1,0:T(8,128)(2,1)S(1)}, u32[]{:S(2)}, u32[]{:S(2)}) collective-permute-start(bf16[2,128,512]{2,1,0:T(8,128)(2,1)S(1)} %add_convert_fusion.5), channel_id=1, source_target_pairs={{0,14},{2,0},{4,2},{6,4},{8,6},{10,8},{12,10},{14,12},{1,15},{3,1}... | collective-permute-start | bytes 786440 | tf_op jit(solution)/shard_map/ppermute | solution.py:300
  165.3 2.6 %collective-permute-done.27 = bf16[4,16,128]{2,1,0:T(8,128)(2,1)S(1)} collective-permute-done((bf16[4,16,128]{2,1,0:T(8,128)(2,1)S(1)}, bf16[4,16,128]{2,1,0:T(8,128)(2,1)S(1)}, u32[]{:S(2)}, u32[]{:S(2)}) %collective-permute-start.27) | collective-permute-done | bytes 16416 | tf_op jit(solution)/shard_map/ppermute | solution.py:248
  167.9 2.7 %collective-permute-start.33 = (bf16[2,16,128]{2,1,0:T(8,128)(2,1)S(1)}, bf16[2,16,128]{2,1,0:T(8,128)(2,1)S(1)}, u32[]{:S(2)}, u32[]{:S(2)}) collective-permute-start(bf16[2,16,128]{2,1,0:T(8,128)(2,1)S(1)} %slice.128), channel_id=1, source_target_pairs={{0,32},{16,48},{32,0},{48,16},{64,96},{80,112},{96,64},{112,80},{1... | collective-permute-start | bytes 24584 | tf_op jit(solution)/shard_map/ppermute | solution.py:248
  170.7 3.7 %collective-permute-start.41 = (bf16[2,128,512]{2,1,0:T(8,128)(2,1)S(1)}, bf16[2,128,512]{2,1,0:T(8,128)(2,1)S(1)}, u32[]{:S(2)}, u32[]{:S(2)}) collective-permute-start(bf16[2,128,512]{2,1,0:T(8,128)(2,1)S(1)} %add_convert_fusion), channel_id=1, source_target_pairs={{0,14},{2,0},{4,2},{6,4},{8,6},{10,8},{12,10},{14,12},{1,15},{3,1}... | collective-permute-start | bytes 786440 | tf_op jit(solution)/shard_map/ppermute | solution.py:300
  174.4 2.2 %collective-permute-start.34 = (bf16[1,16,128]{2,1,0:T(8,128)(2,1)S(1)}, bf16[1,16,128]{2,1,0:T(8,128)(2,1)S(1)}, u32[]{:S(2)}, u32[]{:S(2)}) collective-permute-start(bf16[1,16,128]{2,1,0:T(8,128)(2,1)S(1)} %slice.146), channel_id=1, source_target_pairs={{0,16},{16,0},{32,48},{48,32},{64,80},{80,64},{96,112},{112,96},{1... | collective-permute-start | bytes 12296 | tf_op jit(solution)/shard_map/ppermute | solution.py:248
  177.4 1.9 collective-permute-start.29
  179.4 6.5 %collective-permute-done.29 = bf16[2,128,512]{2,1,0:T(8,128)(2,1)S(1)} collective-permute-done((bf16[2,128,512]{2,1,0:T(8,128)(2,1)}, bf16[2,128,512]{2,1,0:T(8,128)(2,1)S(1)}, u32[]{:S(2)}, u32[]{:S(2)}) %collective-permute-start.29) | collective-permute-done | bytes 262176 | tf_op jit(solution)/shard_map/ppermute | solution.py:300
  186.2 7.6 %collective-permute-start.42 = (bf16[2,128,512]{2,1,0:T(8,128)(2,1)S(1)}, bf16[2,128,512]{2,1,0:T(8,128)(2,1)S(1)}, u32[]{:S(2)}, u32[]{:S(2)}) collective-permute-start(bf16[2,128,512]{2,1,0:T(8,128)(2,1)S(1)} %get-tuple-element.73), channel_id=1, source_target_pairs={{0,1},{1,0},{2,3},{3,2},{4,5},{5,4},{6,7},{7,6},{8,9},{9,8},{10,11... | collective-permute-start | bytes 786440 | tf_op jit(solution)/shard_map/ppermute | solution.py:321
  (158 shorter events, 10.7 us)
Async XLA Ops:
  1.8 10.9 %collective-permute-start = (bf16[2,128,512]{2,1,0:T(8,128)(2,1)S(1)}, bf16[2,128,512]{2,1,0:T(8,128)(2,1)S(1)}, u32[]{:S(2)}, u32[]{:S(2)}) collective-permute-start(bf16[2,128,512]{2,1,0:T(8,128)(2,1)S(1)} %pad_maximum_fusion.1), channel_id=1, source_target_pairs={{0,1},{1,0},{2,3},{3,2},{4,5},{5,4},{6,7},{7,6},{8,9},{9,8},{10,11... | collective-permute-start | bytes 786440 | tf_op jit(solution)/shard_map/ppermute | solution.py:266
  10.6 26.2 %copy-start = (bf16[2,128,512]{2,1,0:T(8,128)(2,1)}, bf16[2,128,512]{2,1,0:T(8,128)(2,1)S(1)}, u32[]{:S(2)}) copy-start(bf16[2,128,512]{2,1,0:T(8,128)(2,1)S(1)} %pad_maximum_fusion.refs_6_) | copy-start | bytes 786436
  10.6 26.2 %copy-start.29 = (bf16[128,1024]{1,0:T(8,128)(2,1)S(1)}, bf16[128,1024]{1,0:T(8,128)(2,1)}, u32[]{:S(2)}) copy-start(bf16[128,1024]{1,0:T(8,128)(2,1)} %param.5) | copy-start | bytes 786436
  10.6 11.2 %collective-permute-start.1 = (bf16[2,128,512]{2,1,0:T(8,128)(2,1)S(1)}, bf16[2,128,512]{2,1,0:T(8,128)(2,1)S(1)}, u32[]{:S(2)}, u32[]{:S(2)}) collective-permute-start(bf16[2,128,512]{2,1,0:T(8,128)(2,1)S(1)} %pad_maximum_fusion.refs_6_), channel_id=1, source_target_pairs={{0,2},{2,4},{4,6},{6,8},{8,10},{10,12},{12,14},{14,0},{1,3},{3,5},... | collective-permute-start | bytes 786440 | tf_op jit(solution)/shard_map/ppermute | solution.py:275
  21.8 10.4 %collective-permute-start.2 = (bf16[1,16,128]{2,1,0:T(8,128)(2,1)S(1)}, bf16[1,16,128]{2,1,0:T(8,128)(2,1)S(1)}, u32[]{:S(2)}, u32[]{:S(2)}) collective-permute-start(bf16[1,16,128]{2,1,0:T(8,128)(2,1)S(1)} %reshape.23), channel_id=1, source_target_pairs={{0,16},{16,0},{32,48},{48,32},{64,80},{80,64},{96,112},{112,96},{1... | collective-permute-start | bytes 12296 | tf_op jit(solution)/shard_map/ppermute | solution.py:248
  23.7 27.7 %collective-permute-start.14 = (bf16[2,128,512]{2,1,0:T(8,128)(2,1)S(1)}, bf16[2,128,512]{2,1,0:T(8,128)(2,1)S(1)}, u32[]{:S(2)}, u32[]{:S(2)}) collective-permute-start(bf16[2,128,512]{2,1,0:T(8,128)(2,1)S(1)} %pad_maximum_fusion.refs_6_), channel_id=1, source_target_pairs={{0,14},{2,0},{4,2},{6,4},{8,6},{10,8},{12,10},{14,12},{1,15},{3,1}... | collective-permute-start | bytes 786440 | tf_op jit(solution)/shard_map/ppermute | solution.py:275
  25.6 13.2 %collective-permute-start.4 = (bf16[2,128,512]{2,1,0:T(8,128)(2,1)S(1)}, bf16[2,128,512]{2,1,0:T(8,128)(2,1)S(1)}, u32[]{:S(2)}, u32[]{:S(2)}) collective-permute-start(bf16[2,128,512]{2,1,0:T(8,128)(2,1)S(1)} %collective-permute-done.1.refs_13_), channel_id=1, source_target_pairs={{0,2},{2,4},{4,6},{6,8},{8,10},{10,12},{12,14},{14,0},{1,3},{3,5},... | collective-permute-start | bytes 786440 | tf_op jit(solution)/shard_map/ppermute | solution.py:275
  29.0 17.8 %collective-permute-start.11 = (bf16[2,128,512]{2,1,0:T(8,128)(2,1)S(1)}, bf16[2,128,512]{2,1,0:T(8,128)(2,1)S(1)}, u32[]{:S(2)}, u32[]{:S(2)}) collective-permute-start(bf16[2,128,512]{2,1,0:T(8,128)(2,1)S(1)} %collective-permute-done.refs_14_), channel_id=1, source_target_pairs={{0,14},{2,0},{4,2},{6,4},{8,6},{10,8},{12,10},{14,12},{1,15},{3,1}... | collective-permute-start | bytes 786440 | tf_op jit(solution)/shard_map/ppermute | solution.py:275
  32.2 6.6 %collective-permute-start.3 = (bf16[2,16,128]{2,1,0:T(8,128)(2,1)S(1)}, bf16[2,16,128]{2,1,0:T(8,128)(2,1)S(1)}, u32[]{:S(2)}, u32[]{:S(2)}) collective-permute-start(bf16[2,16,128]{2,1,0:T(8,128)(2,1)S(1)} %pad_maximum_fusion.8), channel_id=1, source_target_pairs={{0,32},{16,48},{32,0},{48,16},{64,96},{80,112},{96,64},{112,80},{1... | collective-permute-start | bytes 24584 | tf_op jit(solution)/shard_map/ppermute | solution.py:248
  36.9 23.1 %collective-permute-start.19 = (bf16[2,128,512]{2,1,0:T(8,128)(2,1)S(1)}, bf16[2,128,512]{2,1,0:T(8,128)(2,1)S(1)}, u32[]{:S(2)}, u32[]{:S(2)}) collective-permute-start(bf16[2,128,512]{2,1,0:T(8,128)(2,1)S(1)} %collective-permute-done.refs_14_), channel_id=1, source_target_pairs={{0,2},{2,4},{4,6},{6,8},{8,10},{10,12},{12,14},{14,0},{1,3},{3,5},... | collective-permute-start | bytes 786440 | tf_op jit(solution)/shard_map/ppermute | solution.py:275
  38.8 17.9 %collective-permute-start.5 = (bf16[4,16,128]{2,1,0:T(8,128)(2,1)S(1)}, bf16[4,16,128]{2,1,0:T(8,128)(2,1)S(1)}, u32[]{:S(2)}, u32[]{:S(2)}) collective-permute-start(bf16[4,16,128]{2,1,0:T(8,128)(2,1)S(1)} %pad_maximum_fusion.7), channel_id=1, source_target_pairs={{0,64},{16,80},{32,96},{48,112},{64,0},{80,16},{96,32},{112,48},{1... | collective-permute-start | bytes 49160 | tf_op jit(solution)/shard_map/ppermute | solution.py:248
  46.8 20.9 %collective-permute-start.12 = (bf16[2,128,512]{2,1,0:T(8,128)(2,1)S(1)}, bf16[2,128,512]{2,1,0:T(8,128)(2,1)S(1)}, u32[]{:S(2)}, u32[]{:S(2)}) collective-permute-start(bf16[2,128,512]{2,1,0:T(8,128)(2,1)S(1)} %collective-permute-done.11.refs_15_), channel_id=1, source_target_pairs={{0,14},{2,0},{4,2},{6,4},{8,6},{10,8},{12,10},{14,12},{1,15},{3,1}... | collective-permute-start | bytes 786440 | tf_op jit(solution)/shard_map/ppermute | solution.py:275
  51.5 25.3 %collective-permute-start.15 = (bf16[2,128,512]{2,1,0:T(8,128)(2,1)S(1)}, bf16[2,128,512]{2,1,0:T(8,128)(2,1)S(1)}, u32[]{:S(2)}, u32[]{:S(2)}) collective-permute-start(bf16[2,128,512]{2,1,0:T(8,128)(2,1)S(1)} %collective-permute-done.14.refs_7_), channel_id=1, source_target_pairs={{0,14},{2,0},{4,2},{6,4},{8,6},{10,8},{12,10},{14,12},{1,15},{3,1}... | collective-permute-start | bytes 786440 | tf_op jit(solution)/shard_map/ppermute | solution.py:275
  53.4 19.0 %collective-permute-start.7 = (bf16[2,128,512]{2,1,0:T(8,128)(2,1)S(1)}, bf16[2,128,512]{2,1,0:T(8,128)(2,1)S(1)}, u32[]{:S(2)}, u32[]{:S(2)}) collective-permute-start(bf16[2,128,512]{2,1,0:T(8,128)(2,1)S(1)} %collective-permute-done.4.refs_12_), channel_id=1, source_target_pairs={{0,2},{2,4},{4,6},{6,8},{8,10},{10,12},{12,14},{14,0},{1,3},{3,5},... | collective-permute-start | bytes 786440 | tf_op jit(solution)/shard_map/ppermute | solution.py:275
  56.8 9.0 %collective-permute-start.6 = (bf16[8,16,128]{2,1,0:T(8,128)(2,1)S(1)}, bf16[8,16,128]{2,1,0:T(8,128)(2,1)S(1)}, u32[]{:S(2)}, u32[]{:S(2)}) collective-permute-start(bf16[8,16,128]{2,1,0:T(8,128)(2,1)S(1)} %pad_maximum_fusion.6), channel_id=1, source_target_pairs={{0,128},{128,0},{256,384},{384,256},{1,129},{129,1},{257,385},{385... | collective-permute-start | bytes 98312 | tf_op jit(solution)/shard_map/ppermute | solution.py:248
  60.0 34.1 %copy-start.9 = (bf16[2,128,512]{2,1,0:T(8,128)(2,1)}, bf16[2,128,512]{2,1,0:T(8,128)(2,1)S(1)}, u32[]{:S(2)}) copy-start(bf16[2,128,512]{2,1,0:T(8,128)(2,1)S(1)} %collective-permute-done.19.refs_21_) | copy-start | bytes 786436
  60.0 28.1 %collective-permute-start.9 = (bf16[2,128,512]{2,1,0:T(8,128)(2,1)S(1)}, bf16[2,128,512]{2,1,0:T(8,128)(2,1)S(1)}, u32[]{:S(2)}, u32[]{:S(2)}) collective-permute-start(bf16[2,128,512]{2,1,0:T(8,128)(2,1)S(1)} %pad_maximum_fusion.2), channel_id=1, source_target_pairs={{0,1},{1,0},{2,3},{3,2},{4,5},{5,4},{6,7},{7,6},{8,9},{9,8},{10,11... | collective-permute-start | bytes 786440 | tf_op jit(solution)/shard_map/ppermute | solution.py:281
  65.8 20.4 %collective-permute-start.20 = (bf16[2,128,512]{2,1,0:T(8,128)(2,1)S(1)}, bf16[2,128,512]{2,1,0:T(8,128)(2,1)S(1)}, u32[]{:S(2)}, u32[]{:S(2)}) collective-permute-start(bf16[2,128,512]{2,1,0:T(8,128)(2,1)S(1)} %collective-permute-done.19.refs_21_), channel_id=1, source_target_pairs={{0,2},{2,4},{4,6},{6,8},{8,10},{10,12},{12,14},{14,0},{1,3},{3,5},... | collective-permute-start | bytes 786440 | tf_op jit(solution)/shard_map/ppermute | solution.py:275
  67.8 26.3 %copy-start.11 = (bf16[2,128,512]{2,1,0:T(8,128)(2,1)}, bf16[2,128,512]{2,1,0:T(8,128)(2,1)S(1)}, u32[]{:S(2)}) copy-start(bf16[2,128,512]{2,1,0:T(8,128)(2,1)S(1)} %collective-permute-done.12.refs_16_) | copy-start | bytes 786436
  67.8 20.4 %collective-permute-start.13 = (bf16[2,128,512]{2,1,0:T(8,128)(2,1)S(1)}, bf16[2,128,512]{2,1,0:T(8,128)(2,1)S(1)}, u32[]{:S(2)}, u32[]{:S(2)}) collective-permute-start(bf16[2,128,512]{2,1,0:T(8,128)(2,1)S(1)} %collective-permute-done.12.refs_16_), channel_id=1, source_target_pairs={{0,14},{2,0},{4,2},{6,4},{8,6},{10,8},{12,10},{14,12},{1,15},{3,1}... | collective-permute-start | bytes 786440 | tf_op jit(solution)/shard_map/ppermute | solution.py:275
  72.4 26.2 %copy-start.14 = (bf16[2,128,512]{2,1,0:T(8,128)(2,1)}, bf16[2,128,512]{2,1,0:T(8,128)(2,1)S(1)}, u32[]{:S(2)}) copy-start(bf16[2,128,512]{2,1,0:T(8,128)(2,1)S(1)} %collective-permute-done.7.refs_11_) | copy-start | bytes 786436
  72.4 7.8 %collective-permute-start.8 = (bf16[16,16,128]{2,1,0:T(8,128)(2,1)S(1)}, bf16[16,16,128]{2,1,0:T(8,128)(2,1)S(1)}, u32[]{:S(2)}, u32[]{:S(2)}) collective-permute-start(bf16[16,16,128]{2,1,0:T(8,128)(2,1)S(1)} %pad_maximum_fusion.5), channel_id=1, source_target_pairs={{0,256},{128,384},{256,0},{384,128},{1,257},{129,385},{257,1},{385... | collective-permute-start | bytes 196616 | tf_op jit(solution)/shard_map/ppermute | solution.py:248
  76.8 6.0 %collective-permute-start.10 = (s32[2,8]{1,0:T(2,128)S(1)}, s32[2,8]{1,0:T(2,128)S(1)}, u32[]{:S(2)}, u32[]{:S(2)}) collective-permute-start(s32[2,8]{1,0:T(2,128)S(1)} %copy-done.32), channel_id=1, source_target_pairs={{0,1},{1,0},{2,3},{3,2},{4,5},{5,4},{6,7},{7,6},{8,9},{9,8},{10,11... | collective-permute-start | bytes 200 | tf_op jit(solution)/shard_map/ppermute | solution.py:282
  80.2 13.9 %collective-permute-start.16 = (bf16[2,128,512]{2,1,0:T(8,128)(2,1)S(1)}, bf16[2,128,512]{2,1,0:T(8,128)(2,1)S(1)}, u32[]{:S(2)}, u32[]{:S(2)}) collective-permute-start(bf16[2,128,512]{2,1,0:T(8,128)(2,1)S(1)} %collective-permute-done.15.refs_8_), channel_id=1, source_target_pairs={{0,14},{2,0},{4,2},{6,4},{8,6},{10,8},{12,10},{14,12},{1,15},{3,1}... | collective-permute-start | bytes 786440 | tf_op jit(solution)/shard_map/ppermute | solution.py:275
  82.8 11.3 %collective-permute-start.17 = (bf16[2,128,512]{2,1,0:T(8,128)(2,1)S(1)}, bf16[2,128,512]{2,1,0:T(8,128)(2,1)S(1)}, u32[]{:S(2)}, u32[]{:S(2)}) collective-permute-start(bf16[2,128,512]{2,1,0:T(8,128)(2,1)S(1)} %collective-permute-done.7.refs_11_), channel_id=1, source_target_pairs={{0,2},{2,4},{4,6},{6,8},{8,10},{10,12},{12,14},{14,0},{1,3},{3,5},... | collective-permute-start | bytes 786440 | tf_op jit(solution)/shard_map/ppermute | solution.py:275
  86.2 12.4 %collective-permute-start.21 = (bf16[2,128,512]{2,1,0:T(8,128)(2,1)S(1)}, bf16[2,128,512]{2,1,0:T(8,128)(2,1)S(1)}, u32[]{:S(2)}, u32[]{:S(2)}) collective-permute-start(bf16[2,128,512]{2,1,0:T(8,128)(2,1)S(1)} %collective-permute-done.20.refs_20_), channel_id=1, source_target_pairs={{0,2},{2,4},{4,6},{6,8},{8,10},{10,12},{12,14},{14,0},{1,3},{3,5},... | collective-permute-start | bytes 786440 | tf_op jit(solution)/shard_map/ppermute | solution.py:275
  88.2 10.4 %collective-permute-start.18 = (bf16[2,128,512]{2,1,0:T(8,128)(2,1)S(1)}, bf16[2,128,512]{2,1,0:T(8,128)(2,1)S(1)}, u32[]{:S(2)}, u32[]{:S(2)}) collective-permute-start(bf16[2,128,512]{2,1,0:T(8,128)(2,1)S(1)} %collective-permute-done.13.refs_17_), channel_id=1, source_target_pairs={{0,14},{2,0},{4,2},{6,4},{8,6},{10,8},{12,10},{14,12},{1,15},{3,1}... | collective-permute-start | bytes 786440 | tf_op jit(solution)/shard_map/ppermute | solution.py:275
  111.9 18.7 %collective-permute-start.35 = (bf16[2,128,512]{2,1,0:T(8,128)(2,1)}, bf16[2,128,512]{2,1,0:T(8,128)(2,1)S(1)}, u32[]{:S(2)}, u32[]{:S(2)}) collective-permute-start(bf16[2,128,512]{2,1,0:T(8,128)(2,1)} %get-tuple-element.65), channel_id=1, source_target_pairs={{0,2},{2,4},{4,6},{6,8},{8,10},{10,12},{12,14},{14,0},{1,3},{3,5},... | collective-permute-start | bytes 786440 | tf_op jit(solution)/shard_map/ppermute | solution.py:300
  113.9 18.8 %collective-permute-start.38 = (bf16[2,128,512]{2,1,0:T(8,128)(2,1)}, bf16[2,128,512]{2,1,0:T(8,128)(2,1)S(1)}, u32[]{:S(2)}, u32[]{:S(2)}) collective-permute-start(bf16[2,128,512]{2,1,0:T(8,128)(2,1)} %get-tuple-element.68), channel_id=1, source_target_pairs={{0,14},{2,0},{4,2},{6,4},{8,6},{10,8},{12,10},{14,12},{1,15},{3,1}... | collective-permute-start | bytes 786440 | tf_op jit(solution)/shard_map/ppermute | solution.py:300
  118.4 18.9 %collective-permute-start.23 = (bf16[2,128,512]{2,1,0:T(8,128)(2,1)}, bf16[2,128,512]{2,1,0:T(8,128)(2,1)S(1)}, u32[]{:S(2)}, u32[]{:S(2)}) collective-permute-start(bf16[2,128,512]{2,1,0:T(8,128)(2,1)} %get-tuple-element.52), channel_id=1, source_target_pairs={{0,2},{2,4},{4,6},{6,8},{8,10},{10,12},{12,14},{14,0},{1,3},{3,5},... | collective-permute-start | bytes 786440 | tf_op jit(solution)/shard_map/ppermute | solution.py:300
  120.4 19.2 %collective-permute-start.30 = (bf16[2,128,512]{2,1,0:T(8,128)(2,1)}, bf16[2,128,512]{2,1,0:T(8,128)(2,1)S(1)}, u32[]{:S(2)}, u32[]{:S(2)}) collective-permute-start(bf16[2,128,512]{2,1,0:T(8,128)(2,1)} %get-tuple-element.61), channel_id=1, source_target_pairs={{0,14},{2,0},{4,2},{6,4},{8,6},{10,8},{12,10},{14,12},{1,15},{3,1}... | collective-permute-start | bytes 786440 | tf_op jit(solution)/shard_map/ppermute | solution.py:300
  125.0 18.1 %collective-permute-start.22 = (bf16[2,128,512]{2,1,0:T(8,128)(2,1)}, bf16[2,128,512]{2,1,0:T(8,128)(2,1)S(1)}, u32[]{:S(2)}, u32[]{:S(2)}) collective-permute-start(bf16[2,128,512]{2,1,0:T(8,128)(2,1)} %get-tuple-element.49), channel_id=1, source_target_pairs={{0,1},{1,0},{2,3},{3,2},{4,5},{5,4},{6,7},{7,6},{8,9},{9,8},{10,11... | collective-permute-start | bytes 786440 | tf_op jit(solution)/shard_map/ppermute | solution.py:314
  130.8 17.0 %collective-permute-start.36 = (bf16[2,128,512]{2,1,0:T(8,128)(2,1)S(1)}, bf16[2,128,512]{2,1,0:T(8,128)(2,1)S(1)}, u32[]{:S(2)}, u32[]{:S(2)}) collective-permute-start(bf16[2,128,512]{2,1,0:T(8,128)(2,1)S(1)} %add_convert_fusion.4), channel_id=1, source_target_pairs={{0,2},{2,4},{4,6},{6,8},{8,10},{10,12},{12,14},{14,0},{1,3},{3,5},... | collective-permute-start | bytes 786440 | tf_op jit(solution)/shard_map/ppermute | solution.py:300
  132.8 17.0 %collective-permute-start.39 = (bf16[2,128,512]{2,1,0:T(8,128)(2,1)S(1)}, bf16[2,128,512]{2,1,0:T(8,128)(2,1)S(1)}, u32[]{:S(2)}, u32[]{:S(2)}) collective-permute-start(bf16[2,128,512]{2,1,0:T(8,128)(2,1)S(1)} %add_convert_fusion.2), channel_id=1, source_target_pairs={{0,14},{2,0},{4,2},{6,4},{8,6},{10,8},{12,10},{14,12},{1,15},{3,1}... | collective-permute-start | bytes 786440 | tf_op jit(solution)/shard_map/ppermute | solution.py:300
  137.5 17.0 %collective-permute-start.25 = (bf16[2,128,512]{2,1,0:T(8,128)(2,1)S(1)}, bf16[2,128,512]{2,1,0:T(8,128)(2,1)S(1)}, u32[]{:S(2)}, u32[]{:S(2)}) collective-permute-start(bf16[2,128,512]{2,1,0:T(8,128)(2,1)S(1)} %add_convert_fusion.9), channel_id=1, source_target_pairs={{0,2},{2,4},{4,6},{6,8},{8,10},{10,12},{12,14},{14,0},{1,3},{3,5},... | collective-permute-start | bytes 786440 | tf_op jit(solution)/shard_map/ppermute | solution.py:300
  139.6 8.2 %collective-permute-start.24 = (bf16[16,16,128]{2,1,0:T(8,128)(2,1)S(1)}, bf16[16,16,128]{2,1,0:T(8,128)(2,1)S(1)}, u32[]{:S(2)}, u32[]{:S(2)}) collective-permute-start(bf16[16,16,128]{2,1,0:T(8,128)(2,1)S(1)} %slice.122), channel_id=1, source_target_pairs={{0,256},{128,384},{256,0},{384,128},{1,257},{129,385},{257,1},{385... | collective-permute-start | bytes 196616 | tf_op jit(solution)/shard_map/ppermute | solution.py:248
  143.0 18.4 %collective-permute-start.31 = (bf16[2,128,512]{2,1,0:T(8,128)(2,1)S(1)}, bf16[2,128,512]{2,1,0:T(8,128)(2,1)S(1)}, u32[]{:S(2)}, u32[]{:S(2)}) collective-permute-start(bf16[2,128,512]{2,1,0:T(8,128)(2,1)S(1)} %add_convert_fusion.6), channel_id=1, source_target_pairs={{0,14},{2,0},{4,2},{6,4},{8,6},{10,8},{12,10},{14,12},{1,15},{3,1}... | collective-permute-start | bytes 786440 | tf_op jit(solution)/shard_map/ppermute | solution.py:300
  147.9 31.5 %collective-permute-start.37 = (bf16[2,128,512]{2,1,0:T(8,128)(2,1)S(1)}, bf16[2,128,512]{2,1,0:T(8,128)(2,1)S(1)}, u32[]{:S(2)}, u32[]{:S(2)}) collective-permute-start(bf16[2,128,512]{2,1,0:T(8,128)(2,1)S(1)} %add_convert_fusion.3), channel_id=1, source_target_pairs={{0,2},{2,4},{4,6},{6,8},{8,10},{10,12},{12,14},{14,0},{1,3},{3,5},... | collective-permute-start | bytes 786440 | tf_op jit(solution)/shard_map/ppermute | solution.py:300
  149.9 20.7 %collective-permute-start.40 = (bf16[2,128,512]{2,1,0:T(8,128)(2,1)S(1)}, bf16[2,128,512]{2,1,0:T(8,128)(2,1)S(1)}, u32[]{:S(2)}, u32[]{:S(2)}) collective-permute-start(bf16[2,128,512]{2,1,0:T(8,128)(2,1)S(1)} %add_convert_fusion.1), channel_id=1, source_target_pairs={{0,14},{2,0},{4,2},{6,4},{8,6},{10,8},{12,10},{14,12},{1,15},{3,1}... | collective-permute-start | bytes 786440 | tf_op jit(solution)/shard_map/ppermute | solution.py:300
  154.5 5.0 %collective-permute-start.26 = (bf16[8,16,128]{2,1,0:T(8,128)(2,1)S(1)}, bf16[8,16,128]{2,1,0:T(8,128)(2,1)S(1)}, u32[]{:S(2)}, u32[]{:S(2)}) collective-permute-start(bf16[8,16,128]{2,1,0:T(8,128)(2,1)S(1)} %slice.124), channel_id=1, source_target_pairs={{0,128},{128,0},{256,384},{384,256},{1,129},{129,1},{257,385},{385... | collective-permute-start | bytes 98312 | tf_op jit(solution)/shard_map/ppermute | solution.py:248
  156.6 11.3 %collective-permute-start.28 = (bf16[2,128,512]{2,1,0:T(8,128)(2,1)S(1)}, bf16[2,128,512]{2,1,0:T(8,128)(2,1)S(1)}, u32[]{:S(2)}, u32[]{:S(2)}) collective-permute-start(bf16[2,128,512]{2,1,0:T(8,128)(2,1)S(1)} %add_convert_fusion.8), channel_id=1, source_target_pairs={{0,2},{2,4},{4,6},{6,8},{8,10},{10,12},{12,14},{14,0},{1,3},{3,5},... | collective-permute-start | bytes 786440 | tf_op jit(solution)/shard_map/ppermute | solution.py:300
  159.5 8.4 %collective-permute-start.27 = (bf16[4,16,128]{2,1,0:T(8,128)(2,1)S(1)}, bf16[4,16,128]{2,1,0:T(8,128)(2,1)S(1)}, u32[]{:S(2)}, u32[]{:S(2)}) collective-permute-start(bf16[4,16,128]{2,1,0:T(8,128)(2,1)S(1)} %slice.144), channel_id=1, source_target_pairs={{0,64},{16,80},{32,96},{48,112},{64,0},{80,16},{96,32},{112,48},{1... | collective-permute-start | bytes 49160 | tf_op jit(solution)/shard_map/ppermute | solution.py:248
  161.6 17.8 %collective-permute-start.32 = (bf16[2,128,512]{2,1,0:T(8,128)(2,1)S(1)}, bf16[2,128,512]{2,1,0:T(8,128)(2,1)S(1)}, u32[]{:S(2)}, u32[]{:S(2)}) collective-permute-start(bf16[2,128,512]{2,1,0:T(8,128)(2,1)S(1)} %add_convert_fusion.5), channel_id=1, source_target_pairs={{0,14},{2,0},{4,2},{6,4},{8,6},{10,8},{12,10},{14,12},{1,15},{3,1}... | collective-permute-start | bytes 786440 | tf_op jit(solution)/shard_map/ppermute | solution.py:300
  167.9 6.5 %collective-permute-start.33 = (bf16[2,16,128]{2,1,0:T(8,128)(2,1)S(1)}, bf16[2,16,128]{2,1,0:T(8,128)(2,1)S(1)}, u32[]{:S(2)}, u32[]{:S(2)}) collective-permute-start(bf16[2,16,128]{2,1,0:T(8,128)(2,1)S(1)} %slice.128), channel_id=1, source_target_pairs={{0,32},{16,48},{32,0},{48,16},{64,96},{80,112},{96,64},{112,80},{1... | collective-permute-start | bytes 24584 | tf_op jit(solution)/shard_map/ppermute | solution.py:248
  170.7 8.7 %collective-permute-start.41 = (bf16[2,128,512]{2,1,0:T(8,128)(2,1)S(1)}, bf16[2,128,512]{2,1,0:T(8,128)(2,1)S(1)}, u32[]{:S(2)}, u32[]{:S(2)}) collective-permute-start(bf16[2,128,512]{2,1,0:T(8,128)(2,1)S(1)} %add_convert_fusion), channel_id=1, source_target_pairs={{0,14},{2,0},{4,2},{6,4},{8,6},{10,8},{12,10},{14,12},{1,15},{3,1}... | collective-permute-start | bytes 786440 | tf_op jit(solution)/shard_map/ppermute | solution.py:300
  174.4 4.9 %collective-permute-start.34 = (bf16[1,16,128]{2,1,0:T(8,128)(2,1)S(1)}, bf16[1,16,128]{2,1,0:T(8,128)(2,1)S(1)}, u32[]{:S(2)}, u32[]{:S(2)}) collective-permute-start(bf16[1,16,128]{2,1,0:T(8,128)(2,1)S(1)} %slice.146), channel_id=1, source_target_pairs={{0,16},{16,0},{32,48},{48,32},{64,80},{80,64},{96,112},{112,96},{1... | collective-permute-start | bytes 12296 | tf_op jit(solution)/shard_map/ppermute | solution.py:248
  177.4 8.5 %collective-permute-start.29 = (bf16[2,128,512]{2,1,0:T(8,128)(2,1)}, bf16[2,128,512]{2,1,0:T(8,128)(2,1)S(1)}, u32[]{:S(2)}, u32[]{:S(2)}) collective-permute-start(bf16[2,128,512]{2,1,0:T(8,128)(2,1)} %add_convert_fusion.7), channel_id=1, source_target_pairs={{0,2},{2,4},{4,6},{6,8},{8,10},{10,12},{12,14},{14,0},{1,3},{3,5},... | collective-permute-start | bytes 786440 | tf_op jit(solution)/shard_map/ppermute | solution.py:300
  186.2 8.7 %collective-permute-start.42 = (bf16[2,128,512]{2,1,0:T(8,128)(2,1)S(1)}, bf16[2,128,512]{2,1,0:T(8,128)(2,1)S(1)}, u32[]{:S(2)}, u32[]{:S(2)}) collective-permute-start(bf16[2,128,512]{2,1,0:T(8,128)(2,1)S(1)} %get-tuple-element.73), channel_id=1, source_target_pairs={{0,1},{1,0},{2,3},{3,2},{4,5},{5,4},{6,7},{7,6},{8,9},{9,8},{10,11... | collective-permute-start | bytes 786440 | tf_op jit(solution)/shard_map/ppermute | solution.py:321
  (29 other events, 257.7 us)

commit v7 on v6

--- a/solution.py
+++ b/solution.py
@@ -20,7 +20,7 @@
 HEADS = HALF // HEAD_DIM
 NEAR = 256
 GROWS = 4 * HEADS
-SEND_ORDER = (4, 12, 11, 5, 3, 6, 10, 13, 2, 7, 9, 14, 1, 15, 8, 0)
+SEND_ORDER = tuple(range(NY)) + (12, 13, 11, 14, 10, 15, 9, 8)
 FKEYS = FAR * BLOCK
 SCALE = 1.0 / math.sqrt(HEAD_DIM)
 EXP_SCALE = SCALE * math.log2(math.e)
@@ -42,27 +42,32 @@
 
 def attend_kernel(*refs):
     pos, far_own, far_peer, qdo_own, qdo_peer, glob = refs[:6]
-    sources = refs[6:22]
-    outputs = refs[22:26]
-    parts = refs[26:40]
-    slots, near, fgrad, gwide, res_own, res_peer, base, gglob, spare, table, in_sem, out_sem = refs[40:]
-    my_y, my_c = pos[0], pos[1]
+    gathered = refs[6]
+    ring = refs[7:15]
+    outputs = refs[15:20]
+    scattered = refs[20]
+    parts = refs[21:28]
+    slots, near, fgrad, gwide, res_own, res_peer, base, gglob, spare, table, in_sem, out_sem = refs[28:]
+    sources = [gathered.at[y] for y in range(NY)] + list(ring)
+    my_y, my_c, my_w = pos[0], pos[1], pos[2]
     for who, far in enumerate((far_own, far_peer)):
         for row in range(BLK):
             for entry in range(FAR):
                 block = far[row, entry]
                 group = lax.shift_right_logical(block, 6)
+                chain = lax.bitwise_xor(lax.bitwise_and(group, 1), my_c)
                 offset = lax.bitwise_and(
-                    lax.shift_right_logical(group, 1) - my_y, NY - 1
+                    lax.shift_right_logical(group, 1) - my_y * chain, NY - 1
                 )
-                chain = lax.bitwise_xor(lax.bitwise_and(group, 1), my_c)
                 inner = lax.bitwise_and(block, 1)
                 table[who, chain * NY + offset] = (row * FAR + entry) * 2 + inner
     copies = []
     for who in range(2):
         copies.append(
             pltpu.make_async_copy(
-                sources[who * NY], near.at[:, who, :TOK, :], in_sem.at[len(copies)]
+                ring[0] if who else gathered.at[my_y],
+                near.at[:, who, :TOK, :],
+                in_sem.at[len(copies)],
             )
         )
     for source in range(2 * NY):
@@ -91,7 +96,7 @@
                 )
             near[kind, who, TOK + WINDOWS :, :] = jnp.zeros((NEAR - TOK - WINDOWS, HALF), BF16)
     column = lax.broadcasted_iota(jnp.int32, (TOK, NEAR), 1)
-    hidden = (column >= TOK + WINDOWS) | (column == TOK)
+    hidden = (column >= TOK + WINDOWS) | (column == TOK + my_w)
     for copy in copies:
         copy.wait()
 
@@ -170,7 +175,7 @@
         copy.start()
         copies.append(copy)
 
-    send(gglob, outputs[3])
+    send(gglob, outputs[4])
     send(res_peer, outputs[1])
     send(res_own, outputs[0])
     for source in SEND_ORDER:
@@ -185,18 +190,40 @@
                     here = (lax.bitwise_and(code, 1) == inner).astype(F32)
                     term = fgrad[kind, who, at, :].astype(F32) * here
                     value = term if value is None else value + term
-                if source % NY == 0:
-                    base[source // NY, kind, rows, :] += value
+                if source == NY:
+                    base[1, kind, rows, :] += value
                 else:
                     spare[source, kind, rows, :] = value.astype(BF16)
-        if source % NY:
-            send(spare.at[source], parts[source - 1 - source // NY])
-    send(base, outputs[2])
+        if source != NY:
+            part = scattered.at[source] if source < NY else parts[source - NY - 1]
+            send(spare.at[source], part)
+    send(base.at[1], outputs[3])
+    send(base.at[0], outputs[2])
     for copy in copies:
         copy.wait()
 
 
-def attend(pos, far_own, far_peer, qdo_own, qdo_peer, glob, sources):
+def cut_kernel(core, *refs):
+    inputs, outputs = refs[:4], refs[4:]
+    for half in range(2):
+        first = lax.bitwise_xor(core[0], half) * HALF
+        columns = pl.ds(pl.multiple_of(first, HALF), HALF)
+        for i in range(4):
+            outputs[i // 2 * 2 + half][i % 2] = inputs[i][:, columns]
+
+
+def cut(core, *inputs):
+    vmem = pl.BlockSpec(memory_space=pltpu.VMEM)
+    return pl.pallas_call(
+        cut_kernel,
+        out_shape=[jax.ShapeDtypeStruct((2, TOK, HALF), BF16)] * 4,
+        in_specs=[pl.BlockSpec(memory_space=pltpu.SMEM)] + [vmem] * 4,
+        out_specs=[vmem] * 4,
+        cost_estimate=pl.CostEstimate(flops=0, bytes_accessed=2_000_000, transcendentals=0),
+    )(core.astype(jnp.int32)[None], *inputs)
+
+
+def attend(pos, far_own, far_peer, qdo_own, qdo_peer, glob, gathered, ring):
     smem = pl.BlockSpec(memory_space=pltpu.SMEM)
     vmem = pl.BlockSpec(memory_space=pltpu.VMEM)
     anywhere = pl.BlockSpec(memory_space=pl.ANY)
@@ -206,12 +233,14 @@
         out_shape=[
             piece,
             piece,
-            jax.ShapeDtypeStruct((2, 2, TOK, HALF), F32),
+            jax.ShapeDtypeStruct((2, TOK, HALF), F32),
+            jax.ShapeDtypeStruct((2, TOK, HALF), F32),
             jax.ShapeDtypeStruct((WINDOWS, GROWS, HEAD_DIM), BF16),
         ]
-        + [piece] * 14,
-        in_specs=[smem] * 3 + [vmem] * 3 + [anywhere] * 16,
-        out_specs=[anywhere] * 18,
+        + [jax.ShapeDtypeStruct((NY, 2, TOK, HALF), BF16)]
+        + [piece] * 7,
+        in_specs=[smem] * 3 + [vmem] * 3 + [anywhere] * 9,
+        out_specs=[anywhere] * 13,
         scratch_shapes=[
             pltpu.VMEM((2, 2, BLK * FKEYS, HALF), BF16),
             pltpu.VMEM((2, 2, NEAR, HALF), BF16),
@@ -224,102 +253,91 @@
             pltpu.VMEM((2 * NY, 2, TOK, HALF), BF16),
             pltpu.SMEM((2, 2 * NY), jnp.int32),
             pltpu.SemaphoreType.DMA((2 + 4 * NY,)),
-            pltpu.SemaphoreType.DMA((2 + 2 * NY,)),
+            pltpu.SemaphoreType.DMA((5 + 2 * NY,)),
         ],
         compiler_params=pltpu.CompilerParams(vmem_limit_bytes=60 * 1024 * 1024),
         cost_estimate=pl.CostEstimate(
             flops=1_200_000_000, bytes_accessed=12_000_000, transcendentals=800_000
         ),
-    )(pos, far_own, far_peer, qdo_own, qdo_peer, glob, *sources)
+    )(pos, far_own, far_peer, qdo_own, qdo_peer, glob, gathered, *ring)
 
 
 UP = [(i, (i + 1) % NY) for i in range(NY)]
 DOWN = [(i, (i - 1) % NY) for i in range(NY)]
-SPREAD = ((0, 1), (2, 3), (4,))
+ROW_STEP, BACK_STEP = 1, 2
 SWAP = [(0, 1), (1, 0)]
 
 
 def plus(a, b):
     return (a.astype(F32) + b.astype(F32)).astype(BF16)
-
-
-def flip(rows, bit):
-    axis, size, step = ("z", NZ, 1 << bit) if bit < 3 else ("x", NX, 1 << (bit - 3))
-    return lax.ppermute(rows, axis, [(i, i ^ step) for i in range(size)])
 
 
 def per_device(query_rows, key_rows, value_rows, out_grad, far_blocks):
     my_y = lax.axis_index("y")
     my_c = lax.axis_index("c")
+    my_w = lax.axis_index("x") * NZ + lax.axis_index("z")
     swap = functools.partial(lax.ppermute, axis_name="c", perm=SWAP)
     up = functools.partial(lax.ppermute, axis_name="y", perm=UP)
     down = functools.partial(lax.ppermute, axis_name="y", perm=DOWN)
     low = my_c == 0
 
-    def split(first, second):
-        mine = [jnp.where(low, a[:, :HALF], a[:, HALF:]) for a in (first, second)]
-        other = [jnp.where(low, a[:, HALF:], a[:, :HALF]) for a in (first, second)]
-        return jnp.stack(mine), jnp.stack(other)
-
-    kv_own, kv_send = split(key_rows, value_rows)
-    qdo_own, qdo_send = split(query_rows, out_grad)
+    kv_own, kv_send, qdo_own, qdo_send = cut(my_c, key_rows, value_rows, query_rows, out_grad)
+    gathered = lax.all_gather(kv_own, "y", axis=0)
     kv_peer = swap(kv_send)
-    sources = [None] * 16
-    sources[0], sources[NY] = kv_own, kv_peer
-    glob = jnp.concatenate([kv_own[:, 0], kv_peer[:, 0]]).reshape(1, GROWS, HEAD_DIM)
-    chains = ((0, up, 4, -1), (0, down, 3, 1), (NY, up, 3, -1), (NY, down, 4, 1))
-    held = [kv_own, kv_own, kv_peer, kv_peer]
+    ring = [kv_peer] + [None] * (NY - 1)
+    row = jnp.concatenate([kv_own[:, 0], kv_peer[:, 0]]).reshape(GROWS, HEAD_DIM)
+    chains = ((up, 4, -1), (down, 3, 1))
+    held = [kv_peer, kv_peer]
     for step in range(1, 5):
-        for i, (first, move, count, sign) in enumerate(chains):
+        for i, (move, count, sign) in enumerate(chains):
             if step <= count:
                 held[i] = move(held[i])
-        if step <= 3:
-            glob, held[0] = lax.optimization_barrier((glob, held[0]))
-            for bit in SPREAD[step - 1]:
-                glob = jnp.concatenate([glob, flip(glob, bit)])
-        if step == 1:
+        if step == ROW_STEP:
+            row, held[0] = lax.optimization_barrier((row, held[0]))
+            glob = lax.all_to_all(
+                jnp.broadcast_to(row, (WINDOWS, GROWS, HEAD_DIM)), ("x", "z"), 0, 0, tiled=True
+            )
             qdo_peer = swap(qdo_send)
             far_peer = swap(far_blocks)
+        if step == 2:
+            glob, held[1] = lax.optimization_barrier((glob, held[1]))
         if step == 3:
-            glob, qdo_peer, far_peer, held[3] = lax.optimization_barrier(
-                (glob, qdo_peer, far_peer, held[3])
-            )
-        for i, (first, move, count, sign) in enumerate(chains):
+            qdo_peer, far_peer, held[0] = lax.optimization_barrier((qdo_peer, far_peer, held[0]))
+        for i, (move, count, sign) in enumerate(chains):
             if step <= count:
-                sources[first + (sign * step) % NY] = held[i]
-    pos = jnp.stack([my_y, my_c]).astype(jnp.int32)
-    res_own, res_peer, base, gglob, *parts = attend(
-        pos, far_blocks, far_peer, qdo_own, qdo_peer, glob, sources
+                ring[(sign * step) % NY] = held[i]
+    pos = jnp.stack([my_y, my_c, my_w]).astype(jnp.int32)
+    res_own, res_peer, base_own, base_peer, gglob, scattered, *parts = attend(
+        pos, far_blocks, far_peer, qdo_own, qdo_peer, glob, gathered, ring
     )
-    part = parts[:7], parts[7:]
-    at = [4, 5, 3, 4]
-    held = [part[first // NY][o - 1] for o, (first, _, _, _) in zip(at, chains)]
+    far_own = (lax.psum_scatter(scattered, "y", scatter_dimension=0),)
+    at = [4, 5]
+    held = [parts[o - 1] for o in at]
     for step in range(1, 5):
-        for i, (first, move, count, sign) in enumerate(chains):
+        for i, (move, count, sign) in enumerate(chains):
             if step <= count:
                 held[i] = move(held[i])
-        if step <= 3:
+        if step == BACK_STEP:
             gglob, held[0] = lax.optimization_barrier((gglob, held[0]))
-            for bit in reversed(SPREAD[3 - step]):
-                rows = 1 << bit
-                gglob = gglob[:rows].astype(F32) + flip(gglob[rows:], bit).astype(F32)
-                gglob = gglob.astype(BF16) if bit else gglob
-        for i, (first, move, count, sign) in enumerate(chains):
+            gback = lax.all_to_all(gglob, ("x", "z"), 0, 0, tiled=True)
+        for i, (move, count, sign) in enumerate(chains):
             if step <= count:
                 at[i] = (at[i] + sign) % NY
                 if at[i]:
-                    held[i] = plus(held[i], part[first // NY][at[i] - 1])
-    far_own, far_peer = held[:2], held[2:]
-    gsum = gglob.reshape(2, 2, 1, HALF)
+                    held[i] = plus(held[i], parts[at[i] - 1])
+    far_peer = held
+    gsum = jnp.sum(gback.astype(F32), axis=0).reshape(2, 2, 1, HALF)
     res_back = swap(res_peer)
     first_row = lax.broadcasted_iota(jnp.int32, (1, TOK, 1), 1) == 0
 
-    def finish(who, far):
-        total = base[who] + far[0].astype(F32) + far[1].astype(F32)
+    def finish(base, far, who):
+        total = base + sum(term.astype(F32) for term in far)
         return (total + jnp.where(first_row, gsum[who], 0.0)).astype(BF16)
 
-    peer_grad = swap(finish(1, far_peer))
-    own_grad = finish(0, far_own)
+    peer_grad = finish(base_peer, far_peer, 1)
+    base_own, _ = lax.optimization_barrier((base_own, peer_grad))
+    peer_grad = swap(peer_grad)
+    own_grad = finish(base_own, far_own, 0)
 
     def join(mine, other):
         return jnp.where(

time: 197 us -> 159 us (0.81)
  starting transfers between devices: 149 us -> 91.1 us
  between operations: 1.97 us -> 14.7 us
  waiting for transfers between devices: 23.8 us -> 31 us
  other arithmetic: 6.8 us -> 4.02 us
  Pallas kernels: 11.9 us -> 14.1 us
    ppermute x28 -> x14, starting transfers between devices: 84.5 us -> 45 us  [per_device(): held[i] = move(held[i])]
    ppermute x11 -> x1, starting transfers between devices: 41.6 us -> 4.98 us  [per_device(): peer_grad = swap(peer_grad)]
    all_to_all x0 -> x2, starting transfers between devices: none -> 14.4 us  [the longest x1 10.5 us: per_device(): lax.all_to_all(jnp.broadcast_to(row, (WINDOWS, GROWS, HEAD_DIM)), ('x', '...]
    all_to_all x0 -> x2, waiting for transfers between devices: none -> 5.12 us  [the longest x1 5.12 us: per_device(): lax.all_to_all(jnp.broadcast_to(row, (WINDOWS, GROWS, HEAD_DIM)), ('x', '...]
    ppermute x28 -> x14, waiting for transfers between devices: 20.1 us -> 24.3 us  [per_device(): held[i] = move(held[i])]
    ppermute x11 -> x1, waiting for transfers between devices: 3.74 us -> 0.16 us  [per_device(): peer_grad = swap(peer_grad)]
    ppermute x1, starting transfers between devices: 4.66 us -> 8.06 us  [per_device(): res_back = swap(res_peer)]
    pallas_call x0 -> x1, Pallas kernels: none -> 2.22 us  [cut(): pl.pallas_call(cut_kernel, out_shape=[jax.ShapeDtypeStruct((2, TOK, HALF)...]
  transfers between devices with their start and end apart: 43 -> 23, of which waited for: 6 -> 12; matrix products, arithmetic and copies ran while one was open for 3% -> 2% of each run, Pallas kernels for 0% -> 0%
where the time goes in v7:
time: 159 us; the launch traced here: 158 us
  starting transfers between devices  91.1 us (57%)
  waiting for transfers between devices  31 us (19%)
  between operations  14.7 us (9%)
  Pallas kernels  14.1 us (9%)
  other arithmetic  4.02 us (3%)
  local copies, waits for them, and re-layouts  3.05 us (2%)
    ppermute x14, starting transfers between devices, per_device(): held[i] = move(held[i])  45 us
    ppermute x14, waiting for transfers between devices, per_device(): held[i] = move(held[i])  24.3 us
    pallas_call x1, Pallas kernels, attend(): pl.pallas_call(attend_kernel, out_shape=[piece, piece, jax.ShapeDtypeStru...  11.9 us
    all_to_all x1, starting transfers between devices, per_device(): lax.all_to_all(jnp.broadcast_to(row, (WINDOWS, GROWS, HEAD_DIM)), ('x', '...  10.5 us
    ppermute x1, starting transfers between devices, per_device(): kv_peer = swap(kv_send)  8.79 us
    ppermute x1, starting transfers between devices, per_device(): res_back = swap(res_peer)  8.06 us
    ppermute x1, starting transfers between devices, per_device(): qdo_peer = swap(qdo_send)  5.87 us
    all_to_all x1, waiting for transfers between devices, per_device(): lax.all_to_all(jnp.broadcast_to(row, (WINDOWS, GROWS, HEAD_DIM)), ('x', '...  5.12 us
  transfers between devices with their start and end apart: 23, of which 12 were waited for; matrix products, arithmetic and copies ran while one was open for 2% of the time, Pallas kernels for 0%

profile of v7, /device:TPU:1, one launch (start us, length us, event | category | flops | bytes accessed | tf_op | source)
XLA Modules:
  0.0 158.0 jit_solution(17787297144985879449)
XLA Ops:
  7.2 2.2 %shard_map.84 = (bf16[2,128,512]{2,1,0:T(8,128)(2,1)}, bf16[2,128,512]{2,1,0:T(8,128)(2,1)}, bf16[2,128,512]{2,1,0:T(8,128)(2,1)}, bf16[2,128,512]{2,1,0:T(8,128)(2,1)}) custom-call(s32[1]{0:T(128)} %bitcast.1.core, bf16[128,1024]{1,0:T(8,128)(2,1)} %refs_0_.1, bf16[128,1024]{1,0:T(8,128)(2,1)} %refs_1_.2, bf16[128,1024]{1,0:T(8,128)(2,1)} %refs_2_.1, ...), custom_call_target="tpu_custom_call" | custom-call | bytes 2000000 | tf_op jit(solution)/shard_map/pallas_call | solution.py:217
  9.5 8.8 %collective-permute-start.2 = (bf16[2,128,512]{2,1,0:T(8,128)(2,1)}, bf16[2,128,512]{2,1,0:T(8,128)(2,1)S(1)}, u32[]{:S(2)}, u32[]{:S(2)}) collective-permute-start(bf16[2,128,512]{2,1,0:T(8,128)(2,1)} %get-tuple-element.33), channel_id=1, source_target_pairs={{0,1},{1,0},{2,3},{3,2},{4,5},{5,4},{6,7},{7,6},{8,9},{9,8},{10,11... | collective-permute-start | bytes 786440 | tf_op jit(solution)/shard_map/ppermute | solution.py:286
  18.3 1.4 collective-permute-done.2.refs_7_
  19.6 1.9 %collective-permute-start.3 = (bf16[2,128,512]{2,1,0:T(8,128)(2,1)S(1)}, bf16[2,128,512]{2,1,0:T(8,128)(2,1)S(1)}, u32[]{:S(2)}, u32[]{:S(2)}) collective-permute-start(bf16[2,128,512]{2,1,0:T(8,128)(2,1)S(1)} %collective-permute-done.2.refs_7_), channel_id=1, source_target_pairs={{0,2},{2,4},{4,6},{6,8},{8,10},{10,12},{12,14},{14,0},{1,3},{3,5},... | collective-permute-start | bytes 786440 | tf_op jit(solution)/shard_map/ppermute | solution.py:294
  21.5 0.7 slice.38
  22.3 4.6 %collective-permute-start.6 = (bf16[2,128,512]{2,1,0:T(8,128)(2,1)S(1)}, bf16[2,128,512]{2,1,0:T(8,128)(2,1)S(1)}, u32[]{:S(2)}, u32[]{:S(2)}) collective-permute-start(bf16[2,128,512]{2,1,0:T(8,128)(2,1)S(1)} %collective-permute-done.2.refs_7_), channel_id=1, source_target_pairs={{0,14},{2,0},{4,2},{6,4},{8,6},{10,8},{12,10},{14,12},{1,15},{3,1}... | collective-permute-start | bytes 786440 | tf_op jit(solution)/shard_map/ppermute | solution.py:294
  26.9 3.3 %collective-permute-done.3.refs_14_ = bf16[2,128,512]{2,1,0:T(8,128)(2,1)S(1)} collective-permute-done((bf16[2,128,512]{2,1,0:T(8,128)(2,1)S(1)}, bf16[2,128,512]{2,1,0:T(8,128)(2,1)S(1)}, u32[]{:S(2)}, u32[]{:S(2)}) %collective-permute-start.3) | collective-permute-done | bytes 262176 | tf_op jit(solution)/shard_map/ppermute | solution.py:294
  30.2 1.9 %collective-permute-start.4 = (bf16[2,128,512]{2,1,0:T(8,128)(2,1)S(1)}, bf16[2,128,512]{2,1,0:T(8,128)(2,1)S(1)}, u32[]{:S(2)}, u32[]{:S(2)}) collective-permute-start(bf16[2,128,512]{2,1,0:T(8,128)(2,1)S(1)} %collective-permute-done.3.refs_14_), channel_id=1, source_target_pairs={{0,2},{2,4},{4,6},{6,8},{8,10},{10,12},{12,14},{14,0},{1,3},{3,5},... | collective-permute-start | bytes 786440 | tf_op jit(solution)/shard_map/ppermute | solution.py:294
  32.1 0.8 collective-permute-done.6.refs_8_
  32.9 5.4 %collective-permute-start.7 = (bf16[2,128,512]{2,1,0:T(8,128)(2,1)S(1)}, bf16[2,128,512]{2,1,0:T(8,128)(2,1)S(1)}, u32[]{:S(2)}, u32[]{:S(2)}) collective-permute-start(bf16[2,128,512]{2,1,0:T(8,128)(2,1)S(1)} %collective-permute-done.6.refs_8_), channel_id=1, source_target_pairs={{0,14},{2,0},{4,2},{6,4},{8,6},{10,8},{12,10},{14,12},{1,15},{3,1}... | collective-permute-start | bytes 786440 | tf_op jit(solution)/shard_map/ppermute | solution.py:294
  38.4 5.9 %collective-permute-start = (bf16[2,128,512]{2,1,0:T(8,128)(2,1)}, bf16[2,128,512]{2,1,0:T(8,128)(2,1)S(1)}, u32[]{:S(2)}, u32[]{:S(2)}) collective-permute-start(bf16[2,128,512]{2,1,0:T(8,128)(2,1)} %get-tuple-element.31), channel_id=1, source_target_pairs={{0,1},{1,0},{2,3},{3,2},{4,5},{5,4},{6,7},{7,6},{8,9},{9,8},{10,11... | collective-permute-start | bytes 786440 | tf_op jit(solution)/shard_map/ppermute | solution.py:300
  44.2 0.2 collective-permute-done.4.refs_13_
  44.4 1.9 %collective-permute-start.5 = (bf16[2,128,512]{2,1,0:T(8,128)(2,1)S(1)}, bf16[2,128,512]{2,1,0:T(8,128)(2,1)S(1)}, u32[]{:S(2)}, u32[]{:S(2)}) collective-permute-start(bf16[2,128,512]{2,1,0:T(8,128)(2,1)S(1)} %collective-permute-done.4.refs_13_), channel_id=1, source_target_pairs={{0,2},{2,4},{4,6},{6,8},{8,10},{10,12},{12,14},{14,0},{1,3},{3,5},... | collective-permute-start | bytes 786440 | tf_op jit(solution)/shard_map/ppermute | solution.py:294
  46.4 0.7 broadcast_in_dim.39
  47.0 10.5 %all-to-all-start = ((bf16[32,16,128]{2,1,0:T(8,128)(2,1)}), bf16[32,16,128]{2,1,0:T(8,128)(2,1)S(1)}, u32[]{:S(2)}, u32[]{:S(2)}) async-start(bf16[32,16,128]{2,1,0:T(8,128)(2,1)} %broadcast_in_dim.39), calls=%async_computation | async-start | bytes 262144 | tf_op jit(solution)/shard_map/all_to_all | solution.py:297
  57.6 4.0 %collective-permute-start.1 = (s32[2,8]{1,0:T(2,128)}, s32[2,8]{1,0:T(2,128)S(1)}, u32[]{:S(2)}, u32[]{:S(2)}) collective-permute-start(s32[2,8]{1,0:T(2,128)} %refs_1_.3), channel_id=1, source_target_pairs={{0,1},{1,0},{2,3},{3,2},{4,5},{5,4},{6,7},{7,6},{8,9},{9,8},{10,11... | collective-permute-start | bytes 200 | tf_op jit(solution)/shard_map/ppermute | solution.py:301
  61.6 5.1 %all-to-all-done.refs_5_ = bf16[32,16,128]{2,1,0:T(8,128)(2,1)S(1)} async-done(((bf16[32,16,128]{2,1,0:T(8,128)(2,1)}), bf16[32,16,128]{2,1,0:T(8,128)(2,1)S(1)}, u32[]{:S(2)}, u32[]{:S(2)}) %all-to-all-start) | async-done | bytes 131104 | tf_op jit(solution)/shard_map/all_to_all | solution.py:297
  66.7 4.6 %collective-permute-start.8 = (bf16[2,128,512]{2,1,0:T(8,128)(2,1)S(1)}, bf16[2,128,512]{2,1,0:T(8,128)(2,1)S(1)}, u32[]{:S(2)}, u32[]{:S(2)}) collective-permute-start(bf16[2,128,512]{2,1,0:T(8,128)(2,1)S(1)} %collective-permute-done.7.refs_9_), channel_id=1, source_target_pairs={{0,14},{2,0},{4,2},{6,4},{8,6},{10,8},{12,10},{14,12},{1,15},{3,1}... | collective-permute-start | bytes 786440 | tf_op jit(solution)/shard_map/ppermute | solution.py:294
  71.4 1.9 %collective-permute-start.9 = (bf16[2,128,512]{2,1,0:T(8,128)(2,1)S(1)}, bf16[2,128,512]{2,1,0:T(8,128)(2,1)S(1)}, u32[]{:S(2)}, u32[]{:S(2)}) collective-permute-start(bf16[2,128,512]{2,1,0:T(8,128)(2,1)S(1)} %collective-permute-done.5.refs_12_), channel_id=1, source_target_pairs={{0,2},{2,4},{4,6},{6,8},{8,10},{10,12},{12,14},{14,0},{1,3},{3,5},... | collective-permute-start | bytes 786440 | tf_op jit(solution)/shard_map/ppermute | solution.py:294
  73.3 0.6 pad_add_fusion.refs_0_
  73.9 0.7 collective-permute-done.8.refs_10_
  74.6 5.1 %collective-permute-done.9.refs_11_ = bf16[2,128,512]{2,1,0:T(8,128)(2,1)S(1)} collective-permute-done((bf16[2,128,512]{2,1,0:T(8,128)(2,1)S(1)}, bf16[2,128,512]{2,1,0:T(8,128)(2,1)S(1)}, u32[]{:S(2)}, u32[]{:S(2)}) %collective-permute-start.9) | collective-permute-done | bytes 262176 | tf_op jit(solution)/shard_map/ppermute | solution.py:294
  79.8 0.6 copy-done.14
  80.4 11.9 %shard_map.85 = (bf16[2,128,512]{2,1,0:T(8,128)(2,1)}, bf16[2,128,512]{2,1,0:T(8,128)(2,1)}, f32[2,128,512]{2,1,0:T(8,128)}, f32[2,128,512]{2,1,0:T(8,128)}, bf1...) custom-call(s32[3]{0:T(128)} %pad_add_fusion.refs_0_, ...), custom_call_target="tpu_custom_call" | custom-call | flops 1200000000 | bytes 12000000 | tf_op jit(solution)/shard_map/pallas_call | solution.py:231
  92.4 0.8 copy-done.21
  93.2 1.9 %collective-permute-start.11 = (bf16[2,128,512]{2,1,0:T(8,128)(2,1)S(1)}, bf16[2,128,512]{2,1,0:T(8,128)(2,1)S(1)}, u32[]{:S(2)}, u32[]{:S(2)}) collective-permute-start(bf16[2,128,512]{2,1,0:T(8,128)(2,1)S(1)} %copy-done.21), channel_id=1, source_target_pairs={{0,2},{2,4},{4,6},{6,8},{8,10},{10,12},{12,14},{14,0},{1,3},{3,5},... | collective-permute-start | bytes 786440 | tf_op jit(solution)/shard_map/ppermute | solution.py:319
  95.2 4.6 %collective-permute-start.15 = (bf16[2,128,512]{2,1,0:T(8,128)(2,1)S(1)}, bf16[2,128,512]{2,1,0:T(8,128)(2,1)S(1)}, u32[]{:S(2)}, u32[]{:S(2)}) collective-permute-start(bf16[2,128,512]{2,1,0:T(8,128)(2,1)S(1)} %copy-done.20), channel_id=1, source_target_pairs={{0,14},{2,0},{4,2},{6,4},{8,6},{10,8},{12,10},{14,12},{1,15},{3,1}... | collective-permute-start | bytes 786440 | tf_op jit(solution)/shard_map/ppermute | solution.py:319
  99.7 1.8 %collective-permute-done.11 = bf16[2,128,512]{2,1,0:T(8,128)(2,1)S(1)} collective-permute-done((bf16[2,128,512]{2,1,0:T(8,128)(2,1)S(1)}, bf16[2,128,512]{2,1,0:T(8,128)(2,1)S(1)}, u32[]{:S(2)}, u32[]{:S(2)}) %collective-permute-start.11) | collective-permute-done | bytes 262176 | tf_op jit(solution)/shard_map/ppermute | solution.py:319
  101.6 0.1 add_convert_fusion.5
  101.6 2.1 %collective-permute-start.12 = (bf16[2,128,512]{2,1,0:T(8,128)(2,1)S(1)}, bf16[2,128,512]{2,1,0:T(8,128)(2,1)S(1)}, u32[]{:S(2)}, u32[]{:S(2)}) collective-permute-start(bf16[2,128,512]{2,1,0:T(8,128)(2,1)S(1)} %add_convert_fusion.5), channel_id=1, source_target_pairs={{0,2},{2,4},{4,6},{6,8},{8,10},{10,12},{12,14},{14,0},{1,3},{3,5},... | collective-permute-start | bytes 786440 | tf_op jit(solution)/shard_map/ppermute | solution.py:319
  103.7 8.1 %collective-permute-start.10 = (bf16[2,128,512]{2,1,0:T(8,128)(2,1)S(1)}, bf16[2,128,512]{2,1,0:T(8,128)(2,1)S(1)}, u32[]{:S(2)}, u32[]{:S(2)}) collective-permute-start(bf16[2,128,512]{2,1,0:T(8,128)(2,1)S(1)} %copy-done.19), channel_id=1, source_target_pairs={{0,1},{1,0},{2,3},{3,2},{4,5},{5,4},{6,7},{7,6},{8,9},{9,8},{10,11... | collective-permute-start | bytes 786440 | tf_op jit(solution)/shard_map/ppermute | solution.py:330
  111.8 0.1 add_convert_fusion.2
  111.9 4.9 %collective-permute-start.16 = (bf16[2,128,512]{2,1,0:T(8,128)(2,1)S(1)}, bf16[2,128,512]{2,1,0:T(8,128)(2,1)S(1)}, u32[]{:S(2)}, u32[]{:S(2)}) collective-permute-start(bf16[2,128,512]{2,1,0:T(8,128)(2,1)S(1)} %add_convert_fusion.2), channel_id=1, source_target_pairs={{0,14},{2,0},{4,2},{6,4},{8,6},{10,8},{12,10},{14,12},{1,15},{3,1}... | collective-permute-start | bytes 786440 | tf_op jit(solution)/shard_map/ppermute | solution.py:319
  116.8 0.1 add_convert_fusion.4
  116.8 1.9 %collective-permute-start.13 = (bf16[2,128,512]{2,1,0:T(8,128)(2,1)S(1)}, bf16[2,128,512]{2,1,0:T(8,128)(2,1)S(1)}, u32[]{:S(2)}, u32[]{:S(2)}) collective-permute-start(bf16[2,128,512]{2,1,0:T(8,128)(2,1)S(1)} %add_convert_fusion.4), channel_id=1, source_target_pairs={{0,2},{2,4},{4,6},{6,8},{8,10},{10,12},{12,14},{14,0},{1,3},{3,5},... | collective-permute-start | bytes 786440 | tf_op jit(solution)/shard_map/ppermute | solution.py:319
  118.8 3.9 %all-to-all-start.1 = ((bf16[32,16,128]{2,1,0:T(8,128)(2,1)}), bf16[32,16,128]{2,1,0:T(8,128)(2,1)S(1)}, u32[]{:S(2)}, u32[]{:S(2)}) async-start(bf16[32,16,128]{2,1,0:T(8,128)(2,1)} %get-tuple-element.55), calls=%async_computation.1 | async-start | bytes 262144 | tf_op jit(solution)/shard_map/all_to_all | solution.py:322
  122.7 5.6 %collective-permute-done.16 = bf16[2,128,512]{2,1,0:T(8,128)(2,1)S(1)} collective-permute-done((bf16[2,128,512]{2,1,0:T(8,128)(2,1)S(1)}, bf16[2,128,512]{2,1,0:T(8,128)(2,1)S(1)}, u32[]{:S(2)}, u32[]{:S(2)}) %collective-permute-start.16) | collective-permute-done | bytes 262176 | tf_op jit(solution)/shard_map/ppermute | solution.py:319
  128.4 5.4 %collective-permute-start.17 = (bf16[2,128,512]{2,1,0:T(8,128)(2,1)S(1)}, bf16[2,128,512]{2,1,0:T(8,128)(2,1)S(1)}, u32[]{:S(2)}, u32[]{:S(2)}) collective-permute-start(bf16[2,128,512]{2,1,0:T(8,128)(2,1)S(1)} %add_convert_fusion.1), channel_id=1, source_target_pairs={{0,14},{2,0},{4,2},{6,4},{8,6},{10,8},{12,10},{14,12},{1,15},{3,1}... | collective-permute-start | bytes 786440 | tf_op jit(solution)/shard_map/ppermute | solution.py:319
  133.8 0.1 add_convert_fusion.3
  133.9 2.1 %collective-permute-start.14 = (bf16[2,128,512]{2,1,0:T(8,128)(2,1)S(1)}, bf16[2,128,512]{2,1,0:T(8,128)(2,1)S(1)}, u32[]{:S(2)}, u32[]{:S(2)}) collective-permute-start(bf16[2,128,512]{2,1,0:T(8,128)(2,1)S(1)} %add_convert_fusion.3), channel_id=1, source_target_pairs={{0,2},{2,4},{4,6},{6,8},{8,10},{10,12},{12,14},{14,0},{1,3},{3,5},... | collective-permute-start | bytes 786440 | tf_op jit(solution)/shard_map/ppermute | solution.py:319
  136.0 5.5 %collective-permute-done.17 = bf16[2,128,512]{2,1,0:T(8,128)(2,1)S(1)} collective-permute-done((bf16[2,128,512]{2,1,0:T(8,128)(2,1)S(1)}, bf16[2,128,512]{2,1,0:T(8,128)(2,1)S(1)}, u32[]{:S(2)}, u32[]{:S(2)}) %collective-permute-start.17) | collective-permute-done | bytes 262176 | tf_op jit(solution)/shard_map/ppermute | solution.py:319
  141.6 1.2 collective-permute-done.14
  142.8 0.1 add_convert_fusion
  142.9 5.0 %collective-permute-start.18 = (bf16[2,128,512]{2,1,0:T(8,128)(2,1)S(1)}, bf16[2,128,512]{2,1,0:T(8,128)(2,1)S(1)}, u32[]{:S(2)}, u32[]{:S(2)}) collective-permute-start(bf16[2,128,512]{2,1,0:T(8,128)(2,1)S(1)} %add_convert_fusion), channel_id=1, source_target_pairs={{0,1},{1,0},{2,3},{3,2},{4,5},{5,4},{6,7},{7,6},{8,9},{9,8},{10,11... | collective-permute-start | bytes 786440 | tf_op jit(solution)/shard_map/ppermute | solution.py:339
  147.9 0.9 maximum_select_fusion
  148.9 0.2 collective-permute-done.18
  149.1 1.1 fusion.1
  150.2 0.9 maximum_select_fusion.2
  (72 shorter events, 0.5 us)
Async XLA Ops:
  7.2 72.5 %all-gather.3.cloned.1.call-start = ((), (), s32[]{:S(2)}) async-start(), calls=%async_computation.4 | async-start | bytes 2359296 | tf_op jit(solution)/shard_map/all_gather | solution.py:285
  9.5 10.1 %collective-permute-start.2 = (bf16[2,128,512]{2,1,0:T(8,128)(2,1)}, bf16[2,128,512]{2,1,0:T(8,128)(2,1)S(1)}, u32[]{:S(2)}, u32[]{:S(2)}) collective-permute-start(bf16[2,128,512]{2,1,0:T(8,128)(2,1)} %get-tuple-element.33), channel_id=1, source_target_pairs={{0,1},{1,0},{2,3},{3,2},{4,5},{5,4},{6,7},{7,6},{8,9},{9,8},{10,11... | collective-permute-start | bytes 786440 | tf_op jit(solution)/shard_map/ppermute | solution.py:286
  19.6 60.1 %copy-start.3 = (bf16[2,128,512]{2,1,0:T(8,128)(2,1)}, bf16[2,128,512]{2,1,0:T(8,128)(2,1)S(1)}, u32[]{:S(2)}) copy-start(bf16[2,128,512]{2,1,0:T(8,128)(2,1)S(1)} %collective-permute-done.2.refs_7_) | copy-start | bytes 786436
  19.6 10.6 %collective-permute-start.3 = (bf16[2,128,512]{2,1,0:T(8,128)(2,1)S(1)}, bf16[2,128,512]{2,1,0:T(8,128)(2,1)S(1)}, u32[]{:S(2)}, u32[]{:S(2)}) collective-permute-start(bf16[2,128,512]{2,1,0:T(8,128)(2,1)S(1)} %collective-permute-done.2.refs_7_), channel_id=1, source_target_pairs={{0,2},{2,4},{4,6},{6,8},{8,10},{10,12},{12,14},{14,0},{1,3},{3,5},... | collective-permute-start | bytes 786440 | tf_op jit(solution)/shard_map/ppermute | solution.py:294
  22.3 10.7 %collective-permute-start.6 = (bf16[2,128,512]{2,1,0:T(8,128)(2,1)S(1)}, bf16[2,128,512]{2,1,0:T(8,128)(2,1)S(1)}, u32[]{:S(2)}, u32[]{:S(2)}) collective-permute-start(bf16[2,128,512]{2,1,0:T(8,128)(2,1)S(1)} %collective-permute-done.2.refs_7_), channel_id=1, source_target_pairs={{0,14},{2,0},{4,2},{6,4},{8,6},{10,8},{12,10},{14,12},{1,15},{3,1}... | collective-permute-start | bytes 786440 | tf_op jit(solution)/shard_map/ppermute | solution.py:294
  30.2 49.5 %copy-start.4 = (bf16[2,128,512]{2,1,0:T(8,128)(2,1)}, bf16[2,128,512]{2,1,0:T(8,128)(2,1)S(1)}, u32[]{:S(2)}) copy-start(bf16[2,128,512]{2,1,0:T(8,128)(2,1)S(1)} %collective-permute-done.3.refs_14_) | copy-start | bytes 786436
  30.2 14.2 %collective-permute-start.4 = (bf16[2,128,512]{2,1,0:T(8,128)(2,1)S(1)}, bf16[2,128,512]{2,1,0:T(8,128)(2,1)S(1)}, u32[]{:S(2)}, u32[]{:S(2)}) collective-permute-start(bf16[2,128,512]{2,1,0:T(8,128)(2,1)S(1)} %collective-permute-done.3.refs_14_), channel_id=1, source_target_pairs={{0,2},{2,4},{4,6},{6,8},{8,10},{10,12},{12,14},{14,0},{1,3},{3,5},... | collective-permute-start | bytes 786440 | tf_op jit(solution)/shard_map/ppermute | solution.py:294
  32.9 46.8 %copy-start.5 = (bf16[2,128,512]{2,1,0:T(8,128)(2,1)}, bf16[2,128,512]{2,1,0:T(8,128)(2,1)S(1)}, u32[]{:S(2)}) copy-start(bf16[2,128,512]{2,1,0:T(8,128)(2,1)S(1)} %collective-permute-done.6.refs_8_) | copy-start | bytes 786436
  32.9 33.8 %collective-permute-start.7 = (bf16[2,128,512]{2,1,0:T(8,128)(2,1)S(1)}, bf16[2,128,512]{2,1,0:T(8,128)(2,1)S(1)}, u32[]{:S(2)}, u32[]{:S(2)}) collective-permute-start(bf16[2,128,512]{2,1,0:T(8,128)(2,1)S(1)} %collective-permute-done.6.refs_8_), channel_id=1, source_target_pairs={{0,14},{2,0},{4,2},{6,4},{8,6},{10,8},{12,10},{14,12},{1,15},{3,1}... | collective-permute-start | bytes 786440 | tf_op jit(solution)/shard_map/ppermute | solution.py:294
  38.4 33.0 %collective-permute-start = (bf16[2,128,512]{2,1,0:T(8,128)(2,1)}, bf16[2,128,512]{2,1,0:T(8,128)(2,1)S(1)}, u32[]{:S(2)}, u32[]{:S(2)}) collective-permute-start(bf16[2,128,512]{2,1,0:T(8,128)(2,1)} %get-tuple-element.31), channel_id=1, source_target_pairs={{0,1},{1,0},{2,3},{3,2},{4,5},{5,4},{6,7},{7,6},{8,9},{9,8},{10,11... | collective-permute-start | bytes 786440 | tf_op jit(solution)/shard_map/ppermute | solution.py:300
  44.4 35.3 %copy-start.6 = (bf16[2,128,512]{2,1,0:T(8,128)(2,1)}, bf16[2,128,512]{2,1,0:T(8,128)(2,1)S(1)}, u32[]{:S(2)}) copy-start(bf16[2,128,512]{2,1,0:T(8,128)(2,1)S(1)} %collective-permute-done.4.refs_13_) | copy-start | bytes 786436
  44.4 26.9 %collective-permute-start.5 = (bf16[2,128,512]{2,1,0:T(8,128)(2,1)S(1)}, bf16[2,128,512]{2,1,0:T(8,128)(2,1)S(1)}, u32[]{:S(2)}, u32[]{:S(2)}) collective-permute-start(bf16[2,128,512]{2,1,0:T(8,128)(2,1)S(1)} %collective-permute-done.4.refs_13_), channel_id=1, source_target_pairs={{0,2},{2,4},{4,6},{6,8},{8,10},{10,12},{12,14},{14,0},{1,3},{3,5},... | collective-permute-start | bytes 786440 | tf_op jit(solution)/shard_map/ppermute | solution.py:294
  47.0 19.6 %all-to-all-start = ((bf16[32,16,128]{2,1,0:T(8,128)(2,1)}), bf16[32,16,128]{2,1,0:T(8,128)(2,1)S(1)}, u32[]{:S(2)}, u32[]{:S(2)}) async-start(bf16[32,16,128]{2,1,0:T(8,128)(2,1)} %broadcast_in_dim.39), calls=%async_computation | async-start | bytes 262144 | tf_op jit(solution)/shard_map/all_to_all | solution.py:297
  57.5 91.6 %reduce-scatter.2.cloned.1.call-start = ((), (), s32[]{:S(2)}) async-start(), calls=%async_computation.3 | async-start | bytes 2359296 | tf_op jit(solution)/shard_map/reduce_scatter | solution.py:313
  57.6 13.7 %collective-permute-start.1 = (s32[2,8]{1,0:T(2,128)}, s32[2,8]{1,0:T(2,128)S(1)}, u32[]{:S(2)}, u32[]{:S(2)}) collective-permute-start(s32[2,8]{1,0:T(2,128)} %refs_1_.3), channel_id=1, source_target_pairs={{0,1},{1,0},{2,3},{3,2},{4,5},{5,4},{6,7},{7,6},{8,9},{9,8},{10,11... | collective-permute-start | bytes 200 | tf_op jit(solution)/shard_map/ppermute | solution.py:301
  66.7 13.0 %copy-start.1 = (bf16[32,16,128]{2,1,0:T(8,128)(2,1)}, bf16[32,16,128]{2,1,0:T(8,128)(2,1)S(1)}, u32[]{:S(2)}) copy-start(bf16[32,16,128]{2,1,0:T(8,128)(2,1)S(1)} %all-to-all-done.refs_5_) | copy-start | bytes 393220
  66.7 13.0 %copy-start.7 = (bf16[2,128,512]{2,1,0:T(8,128)(2,1)}, bf16[2,128,512]{2,1,0:T(8,128)(2,1)S(1)}, u32[]{:S(2)}) copy-start(bf16[2,128,512]{2,1,0:T(8,128)(2,1)S(1)} %collective-permute-done.7.refs_9_) | copy-start | bytes 786436
  66.7 7.9 %collective-permute-start.8 = (bf16[2,128,512]{2,1,0:T(8,128)(2,1)S(1)}, bf16[2,128,512]{2,1,0:T(8,128)(2,1)S(1)}, u32[]{:S(2)}, u32[]{:S(2)}) collective-permute-start(bf16[2,128,512]{2,1,0:T(8,128)(2,1)S(1)} %collective-permute-done.7.refs_9_), channel_id=1, source_target_pairs={{0,14},{2,0},{4,2},{6,4},{8,6},{10,8},{12,10},{14,12},{1,15},{3,1}... | collective-permute-start | bytes 786440 | tf_op jit(solution)/shard_map/ppermute | solution.py:294
  71.3 8.4 %copy-start.18 = (s32[2,8]{1,0:T(2,128)}, s32[2,8]{1,0:T(2,128)S(1)}, u32[]{:S(2)}) copy-start(s32[2,8]{1,0:T(2,128)S(1)} %collective-permute-done.1.refs_2_) | copy-start | bytes 196
  71.3 8.4 %copy-start.8 = (bf16[2,128,512]{2,1,0:T(8,128)(2,1)}, bf16[2,128,512]{2,1,0:T(8,128)(2,1)S(1)}, u32[]{:S(2)}) copy-start(bf16[2,128,512]{2,1,0:T(8,128)(2,1)S(1)} %collective-permute-done.refs_4_) | copy-start | bytes 786436
  71.3 8.4 %copy-start.10 = (bf16[2,128,512]{2,1,0:T(8,128)(2,1)}, bf16[2,128,512]{2,1,0:T(8,128)(2,1)S(1)}, u32[]{:S(2)}) copy-start(bf16[2,128,512]{2,1,0:T(8,128)(2,1)S(1)} %collective-permute-done.5.refs_12_) | copy-start | bytes 786436
  71.4 8.3 %collective-permute-start.9 = (bf16[2,128,512]{2,1,0:T(8,128)(2,1)S(1)}, bf16[2,128,512]{2,1,0:T(8,128)(2,1)S(1)}, u32[]{:S(2)}, u32[]{:S(2)}) collective-permute-start(bf16[2,128,512]{2,1,0:T(8,128)(2,1)S(1)} %collective-permute-done.5.refs_12_), channel_id=1, source_target_pairs={{0,2},{2,4},{4,6},{6,8},{8,10},{10,12},{12,14},{14,0},{1,3},{3,5},... | collective-permute-start | bytes 786440 | tf_op jit(solution)/shard_map/ppermute | solution.py:294
  74.6 5.2 %copy-start.12 = (bf16[2,128,512]{2,1,0:T(8,128)(2,1)}, bf16[2,128,512]{2,1,0:T(8,128)(2,1)S(1)}, u32[]{:S(2)}) copy-start(bf16[2,128,512]{2,1,0:T(8,128)(2,1)S(1)} %collective-permute-done.8.refs_10_) | copy-start | bytes 786436
  79.7 0.7 copy-start.14
  92.3 1.0 copy-start.21
  92.3 2.9 %copy-start.20 = (bf16[2,128,512]{2,1,0:T(8,128)(2,1)S(1)}, bf16[2,128,512]{2,1,0:T(8,128)(2,1)}, u32[]{:S(2)}) copy-start(bf16[2,128,512]{2,1,0:T(8,128)(2,1)} %get-tuple-element.52) | copy-start | bytes 786436
  92.3 9.2 %copy-start.16 = (bf16[2,128,512]{2,1,0:T(8,128)(2,1)S(1)}, bf16[2,128,512]{2,1,0:T(8,128)(2,1)}, u32[]{:S(2)}) copy-start(bf16[2,128,512]{2,1,0:T(8,128)(2,1)} %get-tuple-element.48) | copy-start | bytes 786436
  92.3 11.4 %copy-start.19 = (bf16[2,128,512]{2,1,0:T(8,128)(2,1)S(1)}, bf16[2,128,512]{2,1,0:T(8,128)(2,1)}, u32[]{:S(2)}) copy-start(bf16[2,128,512]{2,1,0:T(8,128)(2,1)} %get-tuple-element.43) | copy-start | bytes 786436
  92.3 19.5 %copy-start.15 = (bf16[2,128,512]{2,1,0:T(8,128)(2,1)S(1)}, bf16[2,128,512]{2,1,0:T(8,128)(2,1)}, u32[]{:S(2)}) copy-start(bf16[2,128,512]{2,1,0:T(8,128)(2,1)} %get-tuple-element.53) | copy-start | bytes 786436
  92.3 24.4 %copy-start.13 = (bf16[2,128,512]{2,1,0:T(8,128)(2,1)S(1)}, bf16[2,128,512]{2,1,0:T(8,128)(2,1)}, u32[]{:S(2)}) copy-start(bf16[2,128,512]{2,1,0:T(8,128)(2,1)} %get-tuple-element.50) | copy-start | bytes 786436
  92.3 26.4 %copy-start.17 = (bf16[2,128,512]{2,1,0:T(8,128)(2,1)S(1)}, bf16[2,128,512]{2,1,0:T(8,128)(2,1)}, u32[]{:S(2)}) copy-start(bf16[2,128,512]{2,1,0:T(8,128)(2,1)} %get-tuple-element.42) | copy-start | bytes 786436
  92.4 35.9 %copy-start.11 = (bf16[2,128,512]{2,1,0:T(8,128)(2,1)S(1)}, bf16[2,128,512]{2,1,0:T(8,128)(2,1)}, u32[]{:S(2)}) copy-start(bf16[2,128,512]{2,1,0:T(8,128)(2,1)} %get-tuple-element.54) | copy-start | bytes 786436
  92.4 41.4 %copy-start.9 = (bf16[2,128,512]{2,1,0:T(8,128)(2,1)S(1)}, bf16[2,128,512]{2,1,0:T(8,128)(2,1)}, u32[]{:S(2)}) copy-start(bf16[2,128,512]{2,1,0:T(8,128)(2,1)} %get-tuple-element.51) | copy-start | bytes 786436
  93.2 8.3 %collective-permute-start.11 = (bf16[2,128,512]{2,1,0:T(8,128)(2,1)S(1)}, bf16[2,128,512]{2,1,0:T(8,128)(2,1)S(1)}, u32[]{:S(2)}, u32[]{:S(2)}) collective-permute-start(bf16[2,128,512]{2,1,0:T(8,128)(2,1)S(1)} %copy-done.21), channel_id=1, source_target_pairs={{0,2},{2,4},{4,6},{6,8},{8,10},{10,12},{12,14},{14,0},{1,3},{3,5},... | collective-permute-start | bytes 786440 | tf_op jit(solution)/shard_map/ppermute | solution.py:319
  95.2 16.6 %collective-permute-start.15 = (bf16[2,128,512]{2,1,0:T(8,128)(2,1)S(1)}, bf16[2,128,512]{2,1,0:T(8,128)(2,1)S(1)}, u32[]{:S(2)}, u32[]{:S(2)}) collective-permute-start(bf16[2,128,512]{2,1,0:T(8,128)(2,1)S(1)} %copy-done.20), channel_id=1, source_target_pairs={{0,14},{2,0},{4,2},{6,4},{8,6},{10,8},{12,10},{14,12},{1,15},{3,1}... | collective-permute-start | bytes 786440 | tf_op jit(solution)/shard_map/ppermute | solution.py:319
  101.6 41.2 %copy-start = (f32[2,128,512]{2,1,0:T(8,128)S(1)}, f32[2,128,512]{2,1,0:T(8,128)}, u32[]{:S(2)}) copy-start(f32[2,128,512]{2,1,0:T(8,128)} %get-tuple-element.45) | copy-start | bytes 1572868
  101.6 15.1 %collective-permute-start.12 = (bf16[2,128,512]{2,1,0:T(8,128)(2,1)S(1)}, bf16[2,128,512]{2,1,0:T(8,128)(2,1)S(1)}, u32[]{:S(2)}, u32[]{:S(2)}) collective-permute-start(bf16[2,128,512]{2,1,0:T(8,128)(2,1)S(1)} %add_convert_fusion.5), channel_id=1, source_target_pairs={{0,2},{2,4},{4,6},{6,8},{8,10},{10,12},{12,14},{14,0},{1,3},{3,5},... | collective-permute-start | bytes 786440 | tf_op jit(solution)/shard_map/ppermute | solution.py:319
  103.7 44.2 %collective-permute-start.10 = (bf16[2,128,512]{2,1,0:T(8,128)(2,1)S(1)}, bf16[2,128,512]{2,1,0:T(8,128)(2,1)S(1)}, u32[]{:S(2)}, u32[]{:S(2)}) collective-permute-start(bf16[2,128,512]{2,1,0:T(8,128)(2,1)S(1)} %copy-done.19), channel_id=1, source_target_pairs={{0,1},{1,0},{2,3},{3,2},{4,5},{5,4},{6,7},{7,6},{8,9},{9,8},{10,11... | collective-permute-start | bytes 786440 | tf_op jit(solution)/shard_map/ppermute | solution.py:330
  111.9 16.4 %collective-permute-start.16 = (bf16[2,128,512]{2,1,0:T(8,128)(2,1)S(1)}, bf16[2,128,512]{2,1,0:T(8,128)(2,1)S(1)}, u32[]{:S(2)}, u32[]{:S(2)}) collective-permute-start(bf16[2,128,512]{2,1,0:T(8,128)(2,1)S(1)} %add_convert_fusion.2), channel_id=1, source_target_pairs={{0,14},{2,0},{4,2},{6,4},{8,6},{10,8},{12,10},{14,12},{1,15},{3,1}... | collective-permute-start | bytes 786440 | tf_op jit(solution)/shard_map/ppermute | solution.py:319
  116.8 17.0 %collective-permute-start.13 = (bf16[2,128,512]{2,1,0:T(8,128)(2,1)S(1)}, bf16[2,128,512]{2,1,0:T(8,128)(2,1)S(1)}, u32[]{:S(2)}, u32[]{:S(2)}) collective-permute-start(bf16[2,128,512]{2,1,0:T(8,128)(2,1)S(1)} %add_convert_fusion.4), channel_id=1, source_target_pairs={{0,2},{2,4},{4,6},{6,8},{8,10},{10,12},{12,14},{14,0},{1,3},{3,5},... | collective-permute-start | bytes 786440 | tf_op jit(solution)/shard_map/ppermute | solution.py:319
  118.8 17.2 %all-to-all-start.1 = ((bf16[32,16,128]{2,1,0:T(8,128)(2,1)}), bf16[32,16,128]{2,1,0:T(8,128)(2,1)S(1)}, u32[]{:S(2)}, u32[]{:S(2)}) async-start(bf16[32,16,128]{2,1,0:T(8,128)(2,1)} %get-tuple-element.55), calls=%async_computation.1 | async-start | bytes 262144 | tf_op jit(solution)/shard_map/all_to_all | solution.py:322
  128.4 13.2 %collective-permute-start.17 = (bf16[2,128,512]{2,1,0:T(8,128)(2,1)S(1)}, bf16[2,128,512]{2,1,0:T(8,128)(2,1)S(1)}, u32[]{:S(2)}, u32[]{:S(2)}) collective-permute-start(bf16[2,128,512]{2,1,0:T(8,128)(2,1)S(1)} %add_convert_fusion.1), channel_id=1, source_target_pairs={{0,14},{2,0},{4,2},{6,4},{8,6},{10,8},{12,10},{14,12},{1,15},{3,1}... | collective-permute-start | bytes 786440 | tf_op jit(solution)/shard_map/ppermute | solution.py:319
  133.8 15.3 %copy-start.2 = (f32[2,128,512]{2,1,0:T(8,128)S(1)}, f32[2,128,512]{2,1,0:T(8,128)}, u32[]{:S(2)}) copy-start(f32[2,128,512]{2,1,0:T(8,128)} %get-tuple-element.56) | copy-start | bytes 1572868
  133.9 8.9 %collective-permute-start.14 = (bf16[2,128,512]{2,1,0:T(8,128)(2,1)S(1)}, bf16[2,128,512]{2,1,0:T(8,128)(2,1)S(1)}, u32[]{:S(2)}, u32[]{:S(2)}) collective-permute-start(bf16[2,128,512]{2,1,0:T(8,128)(2,1)S(1)} %add_convert_fusion.3), channel_id=1, source_target_pairs={{0,2},{2,4},{4,6},{6,8},{8,10},{10,12},{12,14},{14,0},{1,3},{3,5},... | collective-permute-start | bytes 786440 | tf_op jit(solution)/shard_map/ppermute | solution.py:319
  142.9 6.1 %collective-permute-start.18 = (bf16[2,128,512]{2,1,0:T(8,128)(2,1)S(1)}, bf16[2,128,512]{2,1,0:T(8,128)(2,1)S(1)}, u32[]{:S(2)}, u32[]{:S(2)}) collective-permute-start(bf16[2,128,512]{2,1,0:T(8,128)(2,1)S(1)} %add_convert_fusion), channel_id=1, source_target_pairs={{0,1},{1,0},{2,3},{3,2},{4,5},{5,4},{6,7},{7,6},{8,9},{9,8},{10,11... | collective-permute-start | bytes 786440 | tf_op jit(solution)/shard_map/ppermute | solution.py:339
Sparse Core Ops, SparseCore 0:
  10.7 54.0 all-gather.2
  92.5 46.4 reduce-scatter.1

commit v8 on v7

--- a/solution.py
+++ b/solution.py
@@ -48,7 +48,6 @@
     scattered = refs[20]
     parts = refs[21:28]
     slots, near, fgrad, gwide, res_own, res_peer, base, gglob, spare, table, in_sem, out_sem = refs[28:]
-    sources = [gathered.at[y] for y in range(NY)] + list(ring)
     my_y, my_c, my_w = pos[0], pos[1], pos[2]
     for who, far in enumerate((far_own, far_peer)):
         for row in range(BLK):
@@ -62,14 +61,13 @@
                 inner = lax.bitwise_and(block, 1)
                 table[who, chain * NY + offset] = (row * FAR + entry) * 2 + inner
     copies = []
-    for who in range(2):
-        copies.append(
-            pltpu.make_async_copy(
-                ring[0] if who else gathered.at[my_y],
-                near.at[:, who, :TOK, :],
-                in_sem.at[len(copies)],
-            )
-        )
+
+    def fetch(value, output):
+        copies.append(pltpu.make_async_copy(value, output, in_sem.at[len(copies)]))
+
+    fetch(gathered.at[my_y, pl.ds(0, 2)], near.at[:, 0, :TOK, :])
+    fetch(gathered.at[my_y, 2], near.at[0, 1, :TOK, :])
+    fetch(ring[0], near.at[1, 1, :TOK, :])
     for source in range(2 * NY):
         for who in range(2):
             code = table[who, source]
@@ -77,13 +75,12 @@
             inner = lax.bitwise_and(code, 1)
             at = pl.ds(pl.multiple_of(slot * BLOCK, BLOCK), BLOCK)
             rows = pl.ds(pl.multiple_of(inner * BLOCK, BLOCK), BLOCK)
-            copies.append(
-                pltpu.make_async_copy(
-                    sources[source].at[:, rows, :],
-                    slots.at[:, who, at, :],
-                    in_sem.at[len(copies)],
-                )
-            )
+            if source < NY:
+                fetch(gathered.at[source, pl.ds(0, 2), rows, :], slots.at[:, who, at, :])
+            else:
+                their_y = lax.bitwise_and(my_y + (source - NY), NY - 1)
+                fetch(gathered.at[their_y, 2, rows, :], slots.at[0, who, at, :])
+                fetch(ring[source - NY].at[rows, :], slots.at[1, who, at, :])
     for copy in copies:
         copy.start()
     gwide[...] = glob[...].astype(F32).reshape(WINDOWS * GROWS, HEAD_DIM)
@@ -252,7 +249,7 @@
             pltpu.VMEM((WINDOWS, GROWS, HEAD_DIM), BF16),
             pltpu.VMEM((2 * NY, 2, TOK, HALF), BF16),
             pltpu.SMEM((2, 2 * NY), jnp.int32),
-            pltpu.SemaphoreType.DMA((2 + 4 * NY,)),
+            pltpu.SemaphoreType.DMA((3 + 6 * NY,)),
             pltpu.SemaphoreType.DMA((5 + 2 * NY,)),
         ],
         compiler_params=pltpu.CompilerParams(vmem_limit_bytes=60 * 1024 * 1024),
@@ -282,12 +279,12 @@
     low = my_c == 0
 
     kv_own, kv_send, qdo_own, qdo_send = cut(my_c, key_rows, value_rows, query_rows, out_grad)
-    gathered = lax.all_gather(kv_own, "y", axis=0)
     kv_peer = swap(kv_send)
-    ring = [kv_peer] + [None] * (NY - 1)
+    gathered = lax.all_gather(jnp.concatenate([kv_own, kv_peer[:1]]), "y", axis=0)
+    ring = [kv_peer[1]] + [None] * (NY - 1)
     row = jnp.concatenate([kv_own[:, 0], kv_peer[:, 0]]).reshape(GROWS, HEAD_DIM)
     chains = ((up, 4, -1), (down, 3, 1))
-    held = [kv_peer, kv_peer]
+    held = [ring[0], ring[0]]
     for step in range(1, 5):
         for i, (move, count, sign) in enumerate(chains):
             if step <= count:
@@ -299,10 +296,10 @@
             )
             qdo_peer = swap(qdo_send)
             far_peer = swap(far_blocks)
-        if step == 2:
-            glob, held[1] = lax.optimization_barrier((glob, held[1]))
         if step == 3:
-            qdo_peer, far_peer, held[0] = lax.optimization_barrier((qdo_peer, far_peer, held[0]))
+            glob, qdo_peer, far_peer, held[0] = lax.optimization_barrier(
+                (glob, qdo_peer, far_peer, held[0])
+            )
         for i, (move, count, sign) in enumerate(chains):
             if step <= count:
                 ring[(sign * step) % NY] = held[i]

time: 159 us -> 157 us (0.987)
  starting transfers between devices: 91.1 us -> 84.8 us
  other arithmetic: 4.02 us -> 7.7 us
  waiting for transfers between devices: 31 us -> 32.8 us
    all_gather x1, waiting for transfers between devices: 0.01 us -> 7.68 us  [per_device(): lax.all_gather(jnp.concatenate([kv_own, kv_peer[:1]]), 'y', axis=0)]
    all_to_all x1, waiting for transfers between devices: 5.12 us -> 0.01 us  [per_device(): lax.all_to_all(jnp.broadcast_to(row, (WINDOWS, GROWS, HEAD_DIM)), ('x', '...]
    ppermute x1, starting transfers between devices: 8.06 us -> 3.22 us  [per_device(): res_back = swap(res_peer)]
    ppermute x1, starting transfers between devices: 5.87 us -> 2.28 us  [per_device(): qdo_peer = swap(qdo_send)]
    all_to_all x1, starting transfers between devices: 3.87 us -> 7.4 us  [per_device(): gback = lax.all_to_all(gglob, ('x', 'z'), 0, 0, tiled=True)]
    all_to_all x1, starting transfers between devices: 10.5 us -> 7.75 us  [per_device(): lax.all_to_all(jnp.broadcast_to(row, (WINDOWS, GROWS, HEAD_DIM)), ('x', '...]
    ppermute x14, waiting for transfers between devices: 24.3 us -> 21.9 us  [per_device(): held[i] = move(held[i])]
    convert_element_type x5, other arithmetic: 0.33 us -> 2.23 us  [plus(): return (a.astype(F32) + b.astype(F32)).astype(BF16)]
  transfers between devices with their start and end apart: 23 -> 23, of which waited for: 12 -> 12; matrix products, arithmetic and copies ran while one was open for 2% -> 3% of each run, Pallas kernels for 0% -> 0%
where the time goes in v8:
time: 157 us; the launch traced here: 156 us
  starting transfers between devices  84.8 us (54%)
  waiting for transfers between devices  32.8 us (21%)
  between operations  14.6 us (9%)
  Pallas kernels  14.3 us (9%)
  other arithmetic  7.7 us (5%)
  local copies, waits for them, and re-layouts  1.62 us (1%)
    ppermute x14, starting transfers between devices, per_device(): held[i] = move(held[i])  45.3 us
    ppermute x14, waiting for transfers between devices, per_device(): held[i] = move(held[i])  21.9 us
    pallas_call x1, Pallas kernels, attend(): pl.pallas_call(attend_kernel, out_shape=[piece, piece, jax.ShapeDtypeStru...  12.1 us
    ppermute x1, starting transfers between devices, per_device(): kv_peer = swap(kv_send)  8.77 us
    all_to_all x1, starting transfers between devices, per_device(): lax.all_to_all(jnp.broadcast_to(row, (WINDOWS, GROWS, HEAD_DIM)), ('x', '...  7.75 us
    all_gather x1, waiting for transfers between devices, per_device(): lax.all_gather(jnp.concatenate([kv_own, kv_peer[:1]]), 'y', axis=0)  7.68 us
    all_to_all x1, starting transfers between devices, per_device(): gback = lax.all_to_all(gglob, ('x', 'z'), 0, 0, tiled=True)  7.4 us
    ppermute x1, starting transfers between devices, per_device(): peer_grad = swap(peer_grad)  6.83 us
  transfers between devices with their start and end apart: 23, of which 12 were waited for; matrix products, arithmetic and copies ran while one was open for 3% of the time, Pallas kernels for 0%

profile of v8, /device:TPU:1, one launch (start us, length us, event | category | flops | bytes accessed | tf_op | source)
XLA Modules:
  0.0 155.8 jit_solution(12425793979188021057)
XLA Ops:
  7.2 2.2 %shard_map.84 = (bf16[2,128,512]{2,1,0:T(8,128)(2,1)}, bf16[2,128,512]{2,1,0:T(8,128)(2,1)}, bf16[2,128,512]{2,1,0:T(8,128)(2,1)}, bf16[2,128,512]{2,1,0:T(8,128)(2,1)}) custom-call(s32[1]{0:T(128)} %bitcast.1.core, bf16[128,1024]{1,0:T(8,128)(2,1)} %refs_0_.1, bf16[128,1024]{1,0:T(8,128)(2,1)} %refs_1_.2, bf16[128,1024]{1,0:T(8,128)(2,1)} %refs_2_.1, ...), custom_call_target="tpu_custom_call" | custom-call | bytes 2000000 | tf_op jit(solution)/shard_map/pallas_call | solution.py:214
  9.4 8.8 %collective-permute-start = (bf16[2,128,512]{2,1,0:T(8,128)(2,1)}, bf16[2,128,512]{2,1,0:T(8,128)(2,1)S(1)}, u32[]{:S(2)}, u32[]{:S(2)}) collective-permute-start(bf16[2,128,512]{2,1,0:T(8,128)(2,1)} %get-tuple-element.31), channel_id=1, source_target_pairs={{0,1},{1,0},{2,3},{3,2},{4,5},{5,4},{6,7},{7,6},{8,9},{9,8},{10,11... | collective-permute-start | bytes 786440 | tf_op jit(solution)/shard_map/ppermute | solution.py:282
  18.2 1.4 collective-permute-done
  19.6 1.8 %pad_maximum_fusion = bf16[3,128,512]{2,1,0:T(8,128)(2,1)} fusion(bf16[1,128,512]{2,1,0:T(8,128)(2,1)S(1)} %get-tuple-element.64, bf16[2,128,512]{2,1,0:T(8,128)(2,1)} %get-tuple-element.30), kind=kLoop, calls=%fused_computation.9 | loop fusion | flops 196608 | bytes 786432 | tf_op jit(solution)/shard_map/concatenate | solution.py:283
  21.4 1.9 %collective-permute-start.1 = (bf16[128,512]{1,0:T(8,128)(2,1)S(1)}, bf16[128,512]{1,0:T(8,128)(2,1)S(1)}, u32[]{:S(2)}, u32[]{:S(2)}) collective-permute-start(bf16[128,512]{1,0:T(8,128)(2,1)S(1)} %get-tuple-element.65.refs_7_), channel_id=1, source_target_pairs={{0,2},{2,4},{4,6},{6,8},{8,10},{10,12},{12,14},{14,0},{1,3},{3,5},... | collective-permute-start | bytes 393224 | tf_op jit(solution)/shard_map/ppermute | solution.py:291
  23.4 2.3 %collective-permute-start.2 = (bf16[2,128,512]{2,1,0:T(8,128)(2,1)}, bf16[2,128,512]{2,1,0:T(8,128)(2,1)S(1)}, u32[]{:S(2)}, u32[]{:S(2)}) collective-permute-start(bf16[2,128,512]{2,1,0:T(8,128)(2,1)} %get-tuple-element.33), channel_id=1, source_target_pairs={{0,1},{1,0},{2,3},{3,2},{4,5},{5,4},{6,7},{7,6},{8,9},{9,8},{10,11... | collective-permute-start | bytes 786440 | tf_op jit(solution)/shard_map/ppermute | solution.py:297
  25.6 0.7 slice.44
  26.4 4.9 %collective-permute-start.6 = (bf16[128,512]{1,0:T(8,128)(2,1)S(1)}, bf16[128,512]{1,0:T(8,128)(2,1)S(1)}, u32[]{:S(2)}, u32[]{:S(2)}) collective-permute-start(bf16[128,512]{1,0:T(8,128)(2,1)S(1)} %get-tuple-element.65.refs_7_), channel_id=1, source_target_pairs={{0,14},{2,0},{4,2},{6,4},{8,6},{10,8},{12,10},{14,12},{1,15},{3,1}... | collective-permute-start | bytes 393224 | tf_op jit(solution)/shard_map/ppermute | solution.py:291
  31.3 1.9 %collective-permute-start.4 = (bf16[128,512]{1,0:T(8,128)(2,1)S(1)}, bf16[128,512]{1,0:T(8,128)(2,1)S(1)}, u32[]{:S(2)}, u32[]{:S(2)}) collective-permute-start(bf16[128,512]{1,0:T(8,128)(2,1)S(1)} %collective-permute-done.1.refs_14_), channel_id=1, source_target_pairs={{0,2},{2,4},{4,6},{6,8},{8,10},{10,12},{12,14},{14,0},{1,3},{3,5},... | collective-permute-start | bytes 393224 | tf_op jit(solution)/shard_map/ppermute | solution.py:291
  33.2 0.7 broadcast_in_dim.39
  33.9 7.8 %all-to-all-start = ((bf16[32,16,128]{2,1,0:T(8,128)(2,1)}), bf16[32,16,128]{2,1,0:T(8,128)(2,1)S(1)}, u32[]{:S(2)}, u32[]{:S(2)}) async-start(bf16[32,16,128]{2,1,0:T(8,128)(2,1)} %broadcast_in_dim.39), calls=%async_computation | async-start | bytes 262144 | tf_op jit(solution)/shard_map/all_to_all | solution.py:294
  41.8 4.6 %collective-permute-start.7 = (bf16[128,512]{1,0:T(8,128)(2,1)S(1)}, bf16[128,512]{1,0:T(8,128)(2,1)S(1)}, u32[]{:S(2)}, u32[]{:S(2)}) collective-permute-start(bf16[128,512]{1,0:T(8,128)(2,1)S(1)} %collective-permute-done.6.refs_8_), channel_id=1, source_target_pairs={{0,14},{2,0},{4,2},{6,4},{8,6},{10,8},{12,10},{14,12},{1,15},{3,1}... | collective-permute-start | bytes 393224 | tf_op jit(solution)/shard_map/ppermute | solution.py:291
  46.4 1.9 %collective-permute-start.5 = (bf16[128,512]{1,0:T(8,128)(2,1)S(1)}, bf16[128,512]{1,0:T(8,128)(2,1)S(1)}, u32[]{:S(2)}, u32[]{:S(2)}) collective-permute-start(bf16[128,512]{1,0:T(8,128)(2,1)S(1)} %collective-permute-done.4.refs_13_), channel_id=1, source_target_pairs={{0,2},{2,4},{4,6},{6,8},{8,10},{10,12},{12,14},{14,0},{1,3},{3,5},... | collective-permute-start | bytes 393224 | tf_op jit(solution)/shard_map/ppermute | solution.py:291
  48.3 3.2 %collective-permute-start.3 = (s32[2,8]{1,0:T(2,128)S(1)}, s32[2,8]{1,0:T(2,128)S(1)}, u32[]{:S(2)}, u32[]{:S(2)}) collective-permute-start(s32[2,8]{1,0:T(2,128)S(1)} %copy-done.16), channel_id=1, source_target_pairs={{0,1},{1,0},{2,3},{3,2},{4,5},{5,4},{6,7},{7,6},{8,9},{9,8},{10,11... | collective-permute-start | bytes 200 | tf_op jit(solution)/shard_map/ppermute | solution.py:298
  51.5 0.2 collective-permute-done.7.refs_9_
  51.7 5.4 %collective-permute-start.8 = (bf16[128,512]{1,0:T(8,128)(2,1)S(1)}, bf16[128,512]{1,0:T(8,128)(2,1)S(1)}, u32[]{:S(2)}, u32[]{:S(2)}) collective-permute-start(bf16[128,512]{1,0:T(8,128)(2,1)S(1)} %collective-permute-done.7.refs_9_), channel_id=1, source_target_pairs={{0,14},{2,0},{4,2},{6,4},{8,6},{10,8},{12,10},{14,12},{1,15},{3,1}... | collective-permute-start | bytes 393224 | tf_op jit(solution)/shard_map/ppermute | solution.py:291
  57.2 0.1 collective-permute-done.5.refs_12_
  57.3 1.9 %collective-permute-start.9 = (bf16[128,512]{1,0:T(8,128)(2,1)S(1)}, bf16[128,512]{1,0:T(8,128)(2,1)S(1)}, u32[]{:S(2)}, u32[]{:S(2)}) collective-permute-start(bf16[128,512]{1,0:T(8,128)(2,1)S(1)} %collective-permute-done.5.refs_12_), channel_id=1, source_target_pairs={{0,2},{2,4},{4,6},{6,8},{8,10},{10,12},{12,14},{14,0},{1,3},{3,5},... | collective-permute-start | bytes 393224 | tf_op jit(solution)/shard_map/ppermute | solution.py:291
  59.2 0.6 pad_add_fusion.refs_0_
  59.8 2.7 %collective-permute-done.8.refs_10_ = bf16[128,512]{1,0:T(8,128)(2,1)S(1)} collective-permute-done((bf16[128,512]{1,0:T(8,128)(2,1)S(1)}, bf16[128,512]{1,0:T(8,128)(2,1)S(1)}, u32[]{:S(2)}, u32[]{:S(2)}) %collective-permute-start.8) | collective-permute-done | bytes 131104 | tf_op jit(solution)/shard_map/ppermute | solution.py:291
  62.5 5.4 %collective-permute-done.9.refs_11_ = bf16[128,512]{1,0:T(8,128)(2,1)S(1)} collective-permute-done((bf16[128,512]{1,0:T(8,128)(2,1)S(1)}, bf16[128,512]{1,0:T(8,128)(2,1)S(1)}, u32[]{:S(2)}, u32[]{:S(2)}) %collective-permute-start.9) | collective-permute-done | bytes 131104 | tf_op jit(solution)/shard_map/ppermute | solution.py:291
  67.9 7.7 %all-gather.3.cloned.1.call-done = bf16[24,128,512]{2,1,0:T(8,128)(2,1)} async-done(((bf16[3,128,512]{2,1,0:T(8,128)(2,1)}), bf16[24,128,512]{2,1,0:T(8,128)(2,1)}) %all-gather.3.cloned.1.call-update) | async-done | bytes 3145744 | tf_op jit(solution)/shard_map/all_gather | solution.py:283
  75.7 12.1 %shard_map.85 = (bf16[2,128,512]{2,1,0:T(8,128)(2,1)}, bf16[2,128,512]{2,1,0:T(8,128)(2,1)}, f32[2,128,512]{2,1,0:T(8,128)}, f32[2,128,512]{2,1,0:T(8,128)}, bf1...) custom-call(s32[3]{0:T(128)} %pad_add_fusion.refs_0_, ...), custom_call_target="tpu_custom_call" | custom-call | flops 1200000000 | bytes 12000000 | tf_op jit(solution)/shard_map/pallas_call | solution.py:228
  87.9 2.1 %collective-permute-start.11 = (bf16[2,128,512]{2,1,0:T(8,128)(2,1)}, bf16[2,128,512]{2,1,0:T(8,128)(2,1)S(1)}, u32[]{:S(2)}, u32[]{:S(2)}) collective-permute-start(bf16[2,128,512]{2,1,0:T(8,128)(2,1)} %get-tuple-element.45), channel_id=1, source_target_pairs={{0,2},{2,4},{4,6},{6,8},{8,10},{10,12},{12,14},{14,0},{1,3},{3,5},... | collective-permute-start | bytes 786440 | tf_op jit(solution)/shard_map/ppermute | solution.py:316
  89.9 4.6 %collective-permute-start.15 = (bf16[2,128,512]{2,1,0:T(8,128)(2,1)}, bf16[2,128,512]{2,1,0:T(8,128)(2,1)S(1)}, u32[]{:S(2)}, u32[]{:S(2)}) collective-permute-start(bf16[2,128,512]{2,1,0:T(8,128)(2,1)} %get-tuple-element.50), channel_id=1, source_target_pairs={{0,14},{2,0},{4,2},{6,4},{8,6},{10,8},{12,10},{14,12},{1,15},{3,1}... | collective-permute-start | bytes 786440 | tf_op jit(solution)/shard_map/ppermute | solution.py:316
  94.5 4.2 %collective-permute-done.11 = bf16[2,128,512]{2,1,0:T(8,128)(2,1)S(1)} collective-permute-done((bf16[2,128,512]{2,1,0:T(8,128)(2,1)}, bf16[2,128,512]{2,1,0:T(8,128)(2,1)S(1)}, u32[]{:S(2)}, u32[]{:S(2)}) %collective-permute-start.11) | collective-permute-done | bytes 262176 | tf_op jit(solution)/shard_map/ppermute | solution.py:316
  98.7 1.0 add_convert_fusion.5
  99.7 1.9 %collective-permute-start.12 = (bf16[2,128,512]{2,1,0:T(8,128)(2,1)S(1)}, bf16[2,128,512]{2,1,0:T(8,128)(2,1)S(1)}, u32[]{:S(2)}, u32[]{:S(2)}) collective-permute-start(bf16[2,128,512]{2,1,0:T(8,128)(2,1)S(1)} %add_convert_fusion.5), channel_id=1, source_target_pairs={{0,2},{2,4},{4,6},{6,8},{8,10},{10,12},{12,14},{14,0},{1,3},{3,5},... | collective-permute-start | bytes 786440 | tf_op jit(solution)/shard_map/ppermute | solution.py:316
  101.7 3.2 %collective-permute-start.10 = (bf16[2,128,512]{2,1,0:T(8,128)(2,1)}, bf16[2,128,512]{2,1,0:T(8,128)(2,1)S(1)}, u32[]{:S(2)}, u32[]{:S(2)}) collective-permute-start(bf16[2,128,512]{2,1,0:T(8,128)(2,1)} %get-tuple-element.41), channel_id=1, source_target_pairs={{0,1},{1,0},{2,3},{3,2},{4,5},{5,4},{6,7},{7,6},{8,9},{9,8},{10,11... | collective-permute-start | bytes 786440 | tf_op jit(solution)/shard_map/ppermute | solution.py:327
  104.9 1.0 add_convert_fusion.2
  105.9 4.9 %collective-permute-start.16 = (bf16[2,128,512]{2,1,0:T(8,128)(2,1)S(1)}, bf16[2,128,512]{2,1,0:T(8,128)(2,1)S(1)}, u32[]{:S(2)}, u32[]{:S(2)}) collective-permute-start(bf16[2,128,512]{2,1,0:T(8,128)(2,1)S(1)} %add_convert_fusion.2), channel_id=1, source_target_pairs={{0,14},{2,0},{4,2},{6,4},{8,6},{10,8},{12,10},{14,12},{1,15},{3,1}... | collective-permute-start | bytes 786440 | tf_op jit(solution)/shard_map/ppermute | solution.py:316
  110.8 4.9 %collective-permute-done.12 = bf16[2,128,512]{2,1,0:T(8,128)(2,1)S(1)} collective-permute-done((bf16[2,128,512]{2,1,0:T(8,128)(2,1)S(1)}, bf16[2,128,512]{2,1,0:T(8,128)(2,1)S(1)}, u32[]{:S(2)}, u32[]{:S(2)}) %collective-permute-start.12) | collective-permute-done | bytes 262176 | tf_op jit(solution)/shard_map/ppermute | solution.py:316
  115.7 0.1 add_convert_fusion.4
  115.8 2.1 %collective-permute-start.13 = (bf16[2,128,512]{2,1,0:T(8,128)(2,1)S(1)}, bf16[2,128,512]{2,1,0:T(8,128)(2,1)S(1)}, u32[]{:S(2)}, u32[]{:S(2)}) collective-permute-start(bf16[2,128,512]{2,1,0:T(8,128)(2,1)S(1)} %add_convert_fusion.4), channel_id=1, source_target_pairs={{0,2},{2,4},{4,6},{6,8},{8,10},{10,12},{12,14},{14,0},{1,3},{3,5},... | collective-permute-start | bytes 786440 | tf_op jit(solution)/shard_map/ppermute | solution.py:316
  117.9 7.4 %all-to-all-start.1 = ((bf16[32,16,128]{2,1,0:T(8,128)(2,1)}), bf16[32,16,128]{2,1,0:T(8,128)(2,1)S(1)}, u32[]{:S(2)}, u32[]{:S(2)}) async-start(bf16[32,16,128]{2,1,0:T(8,128)(2,1)} %get-tuple-element.53), calls=%async_computation.1 | async-start | bytes 262144 | tf_op jit(solution)/shard_map/all_to_all | solution.py:319
  125.3 0.1 add_convert_fusion.1
  125.4 4.6 %collective-permute-start.17 = (bf16[2,128,512]{2,1,0:T(8,128)(2,1)S(1)}, bf16[2,128,512]{2,1,0:T(8,128)(2,1)S(1)}, u32[]{:S(2)}, u32[]{:S(2)}) collective-permute-start(bf16[2,128,512]{2,1,0:T(8,128)(2,1)S(1)} %add_convert_fusion.1), channel_id=1, source_target_pairs={{0,14},{2,0},{4,2},{6,4},{8,6},{10,8},{12,10},{14,12},{1,15},{3,1}... | collective-permute-start | bytes 786440 | tf_op jit(solution)/shard_map/ppermute | solution.py:316
  130.0 0.1 add_convert_fusion.3
  130.0 2.8 %collective-permute-start.14 = (bf16[2,128,512]{2,1,0:T(8,128)(2,1)S(1)}, bf16[2,128,512]{2,1,0:T(8,128)(2,1)S(1)}, u32[]{:S(2)}, u32[]{:S(2)}) collective-permute-start(bf16[2,128,512]{2,1,0:T(8,128)(2,1)S(1)} %add_convert_fusion.3), channel_id=1, source_target_pairs={{0,2},{2,4},{4,6},{6,8},{8,10},{10,12},{12,14},{14,0},{1,3},{3,5},... | collective-permute-start | bytes 786440 | tf_op jit(solution)/shard_map/ppermute | solution.py:316
  132.8 1.6 %all-to-all-done.1 = bf16[32,16,128]{2,1,0:T(8,128)(2,1)S(1)} async-done(((bf16[32,16,128]{2,1,0:T(8,128)(2,1)}), bf16[32,16,128]{2,1,0:T(8,128)(2,1)S(1)}, u32[]{:S(2)}, u32[]{:S(2)}) %all-to-all-start.1) | async-done | bytes 131104 | tf_op jit(solution)/shard_map/all_to_all | solution.py:319
  134.5 3.0 %collective-permute-done.17 = bf16[2,128,512]{2,1,0:T(8,128)(2,1)S(1)} collective-permute-done((bf16[2,128,512]{2,1,0:T(8,128)(2,1)S(1)}, bf16[2,128,512]{2,1,0:T(8,128)(2,1)S(1)}, u32[]{:S(2)}, u32[]{:S(2)}) %collective-permute-start.17) | collective-permute-done | bytes 262176 | tf_op jit(solution)/shard_map/ppermute | solution.py:316
  137.5 1.3 collective-permute-done.14
  138.8 0.1 add_convert_fusion
  138.9 6.8 %collective-permute-start.18 = (bf16[2,128,512]{2,1,0:T(8,128)(2,1)S(1)}, bf16[2,128,512]{2,1,0:T(8,128)(2,1)S(1)}, u32[]{:S(2)}, u32[]{:S(2)}) collective-permute-start(bf16[2,128,512]{2,1,0:T(8,128)(2,1)S(1)} %add_convert_fusion), channel_id=1, source_target_pairs={{0,1},{1,0},{2,3},{3,2},{4,5},{5,4},{6,7},{7,6},{8,9},{9,8},{10,11... | collective-permute-start | bytes 786440 | tf_op jit(solution)/shard_map/ppermute | solution.py:336
  145.8 0.9 maximum_select_fusion
  146.8 0.2 collective-permute-done.18
  147.0 1.1 fusion.1
  148.1 0.9 maximum_select_fusion.2
  (66 shorter events, 0.4 us)
Async XLA Ops:
  7.2 41.1 %copy-start.16 = (s32[2,8]{1,0:T(2,128)S(1)}, s32[2,8]{1,0:T(2,128)}, u32[]{:S(2)}) copy-start(s32[2,8]{1,0:T(2,128)} %refs_1_.3) | copy-start | bytes 196
  7.2 68.4 %all-gather.3.cloned.1.call-start = ((), (), s32[]{:S(2)}) async-start(), calls=%async_computation.4 | async-start | bytes 3538944 | tf_op jit(solution)/shard_map/all_gather | solution.py:283
  9.4 10.1 %collective-permute-start = (bf16[2,128,512]{2,1,0:T(8,128)(2,1)}, bf16[2,128,512]{2,1,0:T(8,128)(2,1)S(1)}, u32[]{:S(2)}, u32[]{:S(2)}) collective-permute-start(bf16[2,128,512]{2,1,0:T(8,128)(2,1)} %get-tuple-element.31), channel_id=1, source_target_pairs={{0,1},{1,0},{2,3},{3,2},{4,5},{5,4},{6,7},{7,6},{8,9},{9,8},{10,11... | collective-permute-start | bytes 786440 | tf_op jit(solution)/shard_map/ppermute | solution.py:282
  19.6 56.0 %copy-start.2 = (bf16[128,512]{1,0:T(8,128)(2,1)}, bf16[128,512]{1,0:T(8,128)(2,1)S(1)}, u32[]{:S(2)}) copy-start(bf16[128,512]{1,0:T(8,128)(2,1)S(1)} %get-tuple-element.65.refs_7_) | copy-start | bytes 393220
  21.4 9.9 %collective-permute-start.1 = (bf16[128,512]{1,0:T(8,128)(2,1)S(1)}, bf16[128,512]{1,0:T(8,128)(2,1)S(1)}, u32[]{:S(2)}, u32[]{:S(2)}) collective-permute-start(bf16[128,512]{1,0:T(8,128)(2,1)S(1)} %get-tuple-element.65.refs_7_), channel_id=1, source_target_pairs={{0,2},{2,4},{4,6},{6,8},{8,10},{10,12},{12,14},{14,0},{1,3},{3,5},... | collective-permute-start | bytes 393224 | tf_op jit(solution)/shard_map/ppermute | solution.py:291
  23.4 33.8 %collective-permute-start.2 = (bf16[2,128,512]{2,1,0:T(8,128)(2,1)}, bf16[2,128,512]{2,1,0:T(8,128)(2,1)S(1)}, u32[]{:S(2)}, u32[]{:S(2)}) collective-permute-start(bf16[2,128,512]{2,1,0:T(8,128)(2,1)} %get-tuple-element.33), channel_id=1, source_target_pairs={{0,1},{1,0},{2,3},{3,2},{4,5},{5,4},{6,7},{7,6},{8,9},{9,8},{10,11... | collective-permute-start | bytes 786440 | tf_op jit(solution)/shard_map/ppermute | solution.py:297
  26.4 15.4 %collective-permute-start.6 = (bf16[128,512]{1,0:T(8,128)(2,1)S(1)}, bf16[128,512]{1,0:T(8,128)(2,1)S(1)}, u32[]{:S(2)}, u32[]{:S(2)}) collective-permute-start(bf16[128,512]{1,0:T(8,128)(2,1)S(1)} %get-tuple-element.65.refs_7_), channel_id=1, source_target_pairs={{0,14},{2,0},{4,2},{6,4},{8,6},{10,8},{12,10},{14,12},{1,15},{3,1}... | collective-permute-start | bytes 393224 | tf_op jit(solution)/shard_map/ppermute | solution.py:291
  31.3 44.3 %copy-start.9 = (bf16[128,512]{1,0:T(8,128)(2,1)}, bf16[128,512]{1,0:T(8,128)(2,1)S(1)}, u32[]{:S(2)}) copy-start(bf16[128,512]{1,0:T(8,128)(2,1)S(1)} %collective-permute-done.1.refs_14_) | copy-start | bytes 393220
  31.3 15.0 %collective-permute-start.4 = (bf16[128,512]{1,0:T(8,128)(2,1)S(1)}, bf16[128,512]{1,0:T(8,128)(2,1)S(1)}, u32[]{:S(2)}, u32[]{:S(2)}) collective-permute-start(bf16[128,512]{1,0:T(8,128)(2,1)S(1)} %collective-permute-done.1.refs_14_), channel_id=1, source_target_pairs={{0,2},{2,4},{4,6},{6,8},{8,10},{10,12},{12,14},{14,0},{1,3},{3,5},... | collective-permute-start | bytes 393224 | tf_op jit(solution)/shard_map/ppermute | solution.py:291
  33.9 23.3 %all-to-all-start = ((bf16[32,16,128]{2,1,0:T(8,128)(2,1)}), bf16[32,16,128]{2,1,0:T(8,128)(2,1)S(1)}, u32[]{:S(2)}, u32[]{:S(2)}) async-start(bf16[32,16,128]{2,1,0:T(8,128)(2,1)} %broadcast_in_dim.39), calls=%async_computation | async-start | bytes 262144 | tf_op jit(solution)/shard_map/all_to_all | solution.py:294
  41.7 105.3 %reduce-scatter.2.cloned.1.call-start = ((), (), s32[]{:S(2)}) async-start(), calls=%async_computation.3 | async-start | bytes 2359296 | tf_op jit(solution)/shard_map/reduce_scatter | solution.py:310
  41.7 33.9 %copy-start.10 = (bf16[128,512]{1,0:T(8,128)(2,1)}, bf16[128,512]{1,0:T(8,128)(2,1)S(1)}, u32[]{:S(2)}) copy-start(bf16[128,512]{1,0:T(8,128)(2,1)S(1)} %collective-permute-done.6.refs_8_) | copy-start | bytes 393220
  41.8 10.0 %collective-permute-start.7 = (bf16[128,512]{1,0:T(8,128)(2,1)S(1)}, bf16[128,512]{1,0:T(8,128)(2,1)S(1)}, u32[]{:S(2)}, u32[]{:S(2)}) collective-permute-start(bf16[128,512]{1,0:T(8,128)(2,1)S(1)} %collective-permute-done.6.refs_8_), channel_id=1, source_target_pairs={{0,14},{2,0},{4,2},{6,4},{8,6},{10,8},{12,10},{14,12},{1,15},{3,1}... | collective-permute-start | bytes 393224 | tf_op jit(solution)/shard_map/ppermute | solution.py:291
  46.3 29.3 %copy-start.11 = (bf16[128,512]{1,0:T(8,128)(2,1)}, bf16[128,512]{1,0:T(8,128)(2,1)S(1)}, u32[]{:S(2)}) copy-start(bf16[128,512]{1,0:T(8,128)(2,1)S(1)} %collective-permute-done.4.refs_13_) | copy-start | bytes 393220
  46.4 10.9 %collective-permute-start.5 = (bf16[128,512]{1,0:T(8,128)(2,1)S(1)}, bf16[128,512]{1,0:T(8,128)(2,1)S(1)}, u32[]{:S(2)}, u32[]{:S(2)}) collective-permute-start(bf16[128,512]{1,0:T(8,128)(2,1)S(1)} %collective-permute-done.4.refs_13_), channel_id=1, source_target_pairs={{0,2},{2,4},{4,6},{6,8},{8,10},{10,12},{12,14},{14,0},{1,3},{3,5},... | collective-permute-start | bytes 393224 | tf_op jit(solution)/shard_map/ppermute | solution.py:291
  48.3 8.9 %collective-permute-start.3 = (s32[2,8]{1,0:T(2,128)S(1)}, s32[2,8]{1,0:T(2,128)S(1)}, u32[]{:S(2)}, u32[]{:S(2)}) collective-permute-start(s32[2,8]{1,0:T(2,128)S(1)} %copy-done.16), channel_id=1, source_target_pairs={{0,1},{1,0},{2,3},{3,2},{4,5},{5,4},{6,7},{7,6},{8,9},{9,8},{10,11... | collective-permute-start | bytes 200 | tf_op jit(solution)/shard_map/ppermute | solution.py:298
  51.7 23.9 %copy-start.12 = (bf16[128,512]{1,0:T(8,128)(2,1)}, bf16[128,512]{1,0:T(8,128)(2,1)S(1)}, u32[]{:S(2)}) copy-start(bf16[128,512]{1,0:T(8,128)(2,1)S(1)} %collective-permute-done.7.refs_9_) | copy-start | bytes 393220
  51.7 10.8 %collective-permute-start.8 = (bf16[128,512]{1,0:T(8,128)(2,1)S(1)}, bf16[128,512]{1,0:T(8,128)(2,1)S(1)}, u32[]{:S(2)}, u32[]{:S(2)}) collective-permute-start(bf16[128,512]{1,0:T(8,128)(2,1)S(1)} %collective-permute-done.7.refs_9_), channel_id=1, source_target_pairs={{0,14},{2,0},{4,2},{6,4},{8,6},{10,8},{12,10},{14,12},{1,15},{3,1}... | collective-permute-start | bytes 393224 | tf_op jit(solution)/shard_map/ppermute | solution.py:291
  57.2 18.5 %copy-start.17 = (s32[2,8]{1,0:T(2,128)}, s32[2,8]{1,0:T(2,128)S(1)}, u32[]{:S(2)}) copy-start(s32[2,8]{1,0:T(2,128)S(1)} %collective-permute-done.3.refs_2_) | copy-start | bytes 196
  57.2 18.5 %copy-start.4 = (bf16[2,128,512]{2,1,0:T(8,128)(2,1)}, bf16[2,128,512]{2,1,0:T(8,128)(2,1)S(1)}, u32[]{:S(2)}) copy-start(bf16[2,128,512]{2,1,0:T(8,128)(2,1)S(1)} %collective-permute-done.2.refs_4_) | copy-start | bytes 786436
  57.2 18.5 %copy-start.1 = (bf16[32,16,128]{2,1,0:T(8,128)(2,1)}, bf16[32,16,128]{2,1,0:T(8,128)(2,1)S(1)}, u32[]{:S(2)}) copy-start(bf16[32,16,128]{2,1,0:T(8,128)(2,1)S(1)} %all-to-all-done.refs_5_) | copy-start | bytes 393220
  57.3 18.4 %copy-start.13 = (bf16[128,512]{1,0:T(8,128)(2,1)}, bf16[128,512]{1,0:T(8,128)(2,1)S(1)}, u32[]{:S(2)}) copy-start(bf16[128,512]{1,0:T(8,128)(2,1)S(1)} %collective-permute-done.5.refs_12_) | copy-start | bytes 393220
  57.3 10.7 %collective-permute-start.9 = (bf16[128,512]{1,0:T(8,128)(2,1)S(1)}, bf16[128,512]{1,0:T(8,128)(2,1)S(1)}, u32[]{:S(2)}, u32[]{:S(2)}) collective-permute-start(bf16[128,512]{1,0:T(8,128)(2,1)S(1)} %collective-permute-done.5.refs_12_), channel_id=1, source_target_pairs={{0,2},{2,4},{4,6},{6,8},{8,10},{10,12},{12,14},{14,0},{1,3},{3,5},... | collective-permute-start | bytes 393224 | tf_op jit(solution)/shard_map/ppermute | solution.py:291
  62.5 13.2 %copy-start.14 = (bf16[128,512]{1,0:T(8,128)(2,1)}, bf16[128,512]{1,0:T(8,128)(2,1)S(1)}, u32[]{:S(2)}) copy-start(bf16[128,512]{1,0:T(8,128)(2,1)S(1)} %collective-permute-done.8.refs_10_) | copy-start | bytes 393220
  67.9 7.8 %copy-start.15 = (bf16[128,512]{1,0:T(8,128)(2,1)}, bf16[128,512]{1,0:T(8,128)(2,1)S(1)}, u32[]{:S(2)}) copy-start(bf16[128,512]{1,0:T(8,128)(2,1)S(1)} %collective-permute-done.9.refs_11_) | copy-start | bytes 393220
  87.8 27.9 %copy-start.7 = (bf16[2,128,512]{2,1,0:T(8,128)(2,1)S(1)}, bf16[2,128,512]{2,1,0:T(8,128)(2,1)}, u32[]{:S(2)}) copy-start(bf16[2,128,512]{2,1,0:T(8,128)(2,1)} %get-tuple-element.48) | copy-start | bytes 786436
  87.8 30.0 %copy-start.8 = (bf16[2,128,512]{2,1,0:T(8,128)(2,1)S(1)}, bf16[2,128,512]{2,1,0:T(8,128)(2,1)}, u32[]{:S(2)}) copy-start(bf16[2,128,512]{2,1,0:T(8,128)(2,1)} %get-tuple-element.40) | copy-start | bytes 786436
  87.8 37.5 %copy-start.6 = (bf16[2,128,512]{2,1,0:T(8,128)(2,1)S(1)}, bf16[2,128,512]{2,1,0:T(8,128)(2,1)}, u32[]{:S(2)}) copy-start(bf16[2,128,512]{2,1,0:T(8,128)(2,1)} %get-tuple-element.52) | copy-start | bytes 786436
  87.8 42.2 %copy-start.5 = (bf16[2,128,512]{2,1,0:T(8,128)(2,1)S(1)}, bf16[2,128,512]{2,1,0:T(8,128)(2,1)}, u32[]{:S(2)}) copy-start(bf16[2,128,512]{2,1,0:T(8,128)(2,1)} %get-tuple-element.49) | copy-start | bytes 786436
  87.8 51.0 %copy-start = (f32[2,128,512]{2,1,0:T(8,128)S(1)}, f32[2,128,512]{2,1,0:T(8,128)}, u32[]{:S(2)}) copy-start(f32[2,128,512]{2,1,0:T(8,128)} %get-tuple-element.43) | copy-start | bytes 1572868
  87.9 10.9 %collective-permute-start.11 = (bf16[2,128,512]{2,1,0:T(8,128)(2,1)}, bf16[2,128,512]{2,1,0:T(8,128)(2,1)S(1)}, u32[]{:S(2)}, u32[]{:S(2)}) collective-permute-start(bf16[2,128,512]{2,1,0:T(8,128)(2,1)} %get-tuple-element.45), channel_id=1, source_target_pairs={{0,2},{2,4},{4,6},{6,8},{8,10},{10,12},{12,14},{14,0},{1,3},{3,5},... | collective-permute-start | bytes 786440 | tf_op jit(solution)/shard_map/ppermute | solution.py:316
  89.9 15.0 %collective-permute-start.15 = (bf16[2,128,512]{2,1,0:T(8,128)(2,1)}, bf16[2,128,512]{2,1,0:T(8,128)(2,1)S(1)}, u32[]{:S(2)}, u32[]{:S(2)}) collective-permute-start(bf16[2,128,512]{2,1,0:T(8,128)(2,1)} %get-tuple-element.50), channel_id=1, source_target_pairs={{0,14},{2,0},{4,2},{6,4},{8,6},{10,8},{12,10},{14,12},{1,15},{3,1}... | collective-permute-start | bytes 786440 | tf_op jit(solution)/shard_map/ppermute | solution.py:316
  99.7 16.0 %collective-permute-start.12 = (bf16[2,128,512]{2,1,0:T(8,128)(2,1)S(1)}, bf16[2,128,512]{2,1,0:T(8,128)(2,1)S(1)}, u32[]{:S(2)}, u32[]{:S(2)}) collective-permute-start(bf16[2,128,512]{2,1,0:T(8,128)(2,1)S(1)} %add_convert_fusion.5), channel_id=1, source_target_pairs={{0,2},{2,4},{4,6},{6,8},{8,10},{10,12},{12,14},{14,0},{1,3},{3,5},... | collective-permute-start | bytes 786440 | tf_op jit(solution)/shard_map/ppermute | solution.py:316
  101.7 44.1 %collective-permute-start.10 = (bf16[2,128,512]{2,1,0:T(8,128)(2,1)}, bf16[2,128,512]{2,1,0:T(8,128)(2,1)S(1)}, u32[]{:S(2)}, u32[]{:S(2)}) collective-permute-start(bf16[2,128,512]{2,1,0:T(8,128)(2,1)} %get-tuple-element.41), channel_id=1, source_target_pairs={{0,1},{1,0},{2,3},{3,2},{4,5},{5,4},{6,7},{7,6},{8,9},{9,8},{10,11... | collective-permute-start | bytes 786440 | tf_op jit(solution)/shard_map/ppermute | solution.py:327
  105.9 19.4 %collective-permute-start.16 = (bf16[2,128,512]{2,1,0:T(8,128)(2,1)S(1)}, bf16[2,128,512]{2,1,0:T(8,128)(2,1)S(1)}, u32[]{:S(2)}, u32[]{:S(2)}) collective-permute-start(bf16[2,128,512]{2,1,0:T(8,128)(2,1)S(1)} %add_convert_fusion.2), channel_id=1, source_target_pairs={{0,14},{2,0},{4,2},{6,4},{8,6},{10,8},{12,10},{14,12},{1,15},{3,1}... | collective-permute-start | bytes 786440 | tf_op jit(solution)/shard_map/ppermute | solution.py:316
  115.8 31.2 %copy-start.3 = (f32[2,128,512]{2,1,0:T(8,128)S(1)}, f32[2,128,512]{2,1,0:T(8,128)}, u32[]{:S(2)}) copy-start(f32[2,128,512]{2,1,0:T(8,128)} %get-tuple-element.54) | copy-start | bytes 1572868
  115.8 14.2 %collective-permute-start.13 = (bf16[2,128,512]{2,1,0:T(8,128)(2,1)S(1)}, bf16[2,128,512]{2,1,0:T(8,128)(2,1)S(1)}, u32[]{:S(2)}, u32[]{:S(2)}) collective-permute-start(bf16[2,128,512]{2,1,0:T(8,128)(2,1)S(1)} %add_convert_fusion.4), channel_id=1, source_target_pairs={{0,2},{2,4},{4,6},{6,8},{8,10},{10,12},{12,14},{14,0},{1,3},{3,5},... | collective-permute-start | bytes 786440 | tf_op jit(solution)/shard_map/ppermute | solution.py:316
  117.9 16.6 %all-to-all-start.1 = ((bf16[32,16,128]{2,1,0:T(8,128)(2,1)}), bf16[32,16,128]{2,1,0:T(8,128)(2,1)S(1)}, u32[]{:S(2)}, u32[]{:S(2)}) async-start(bf16[32,16,128]{2,1,0:T(8,128)(2,1)} %get-tuple-element.53), calls=%async_computation.1 | async-start | bytes 262144 | tf_op jit(solution)/shard_map/all_to_all | solution.py:319
  125.4 12.1 %collective-permute-start.17 = (bf16[2,128,512]{2,1,0:T(8,128)(2,1)S(1)}, bf16[2,128,512]{2,1,0:T(8,128)(2,1)S(1)}, u32[]{:S(2)}, u32[]{:S(2)}) collective-permute-start(bf16[2,128,512]{2,1,0:T(8,128)(2,1)S(1)} %add_convert_fusion.1), channel_id=1, source_target_pairs={{0,14},{2,0},{4,2},{6,4},{8,6},{10,8},{12,10},{14,12},{1,15},{3,1}... | collective-permute-start | bytes 786440 | tf_op jit(solution)/shard_map/ppermute | solution.py:316
  130.0 8.8 %collective-permute-start.14 = (bf16[2,128,512]{2,1,0:T(8,128)(2,1)S(1)}, bf16[2,128,512]{2,1,0:T(8,128)(2,1)S(1)}, u32[]{:S(2)}, u32[]{:S(2)}) collective-permute-start(bf16[2,128,512]{2,1,0:T(8,128)(2,1)S(1)} %add_convert_fusion.3), channel_id=1, source_target_pairs={{0,2},{2,4},{4,6},{6,8},{8,10},{10,12},{12,14},{14,0},{1,3},{3,5},... | collective-permute-start | bytes 786440 | tf_op jit(solution)/shard_map/ppermute | solution.py:316
  138.9 8.0 %collective-permute-start.18 = (bf16[2,128,512]{2,1,0:T(8,128)(2,1)S(1)}, bf16[2,128,512]{2,1,0:T(8,128)(2,1)S(1)}, u32[]{:S(2)}, u32[]{:S(2)}) collective-permute-start(bf16[2,128,512]{2,1,0:T(8,128)(2,1)S(1)} %add_convert_fusion), channel_id=1, source_target_pairs={{0,1},{1,0},{2,3},{3,2},{4,5},{5,4},{6,7},{7,6},{8,9},{9,8},{10,11... | collective-permute-start | bytes 786440 | tf_op jit(solution)/shard_map/ppermute | solution.py:336
Sparse Core Ops, SparseCore 0:
  21.6 54.0 all-gather.2
  88.0 48.8 reduce-scatter.1

commit v9 on v8

--- a/solution.py
+++ b/solution.py
@@ -17,6 +17,7 @@
 NX, NZ, NY, NC = 4, 8, 8, 2
 WINDOWS = NX * NZ
 HALF = 512
+PIECE = 256
 HEADS = HALF // HEAD_DIM
 NEAR = 256
 GROWS = 4 * HEADS
@@ -65,9 +66,9 @@
     def fetch(value, output):
         copies.append(pltpu.make_async_copy(value, output, in_sem.at[len(copies)]))
 
-    fetch(gathered.at[my_y, pl.ds(0, 2)], near.at[:, 0, :TOK, :])
-    fetch(gathered.at[my_y, 2], near.at[0, 1, :TOK, :])
-    fetch(ring[0], near.at[1, 1, :TOK, :])
+    fetch(gathered.at[my_y, pl.ds(0, 4)], near.at[:, 0, :TOK, :])
+    fetch(gathered.at[my_y, 4], near.at[0, 1, :TOK, :])
+    fetch(ring[0], near.at[pl.ds(1, 3), 1, :TOK, :])
     for source in range(2 * NY):
         for who in range(2):
             code = table[who, source]
@@ -76,11 +77,11 @@
             at = pl.ds(pl.multiple_of(slot * BLOCK, BLOCK), BLOCK)
             rows = pl.ds(pl.multiple_of(inner * BLOCK, BLOCK), BLOCK)
             if source < NY:
-                fetch(gathered.at[source, pl.ds(0, 2), rows, :], slots.at[:, who, at, :])
+                fetch(gathered.at[source, pl.ds(0, 4), rows, :], slots.at[:, who, at, :])
             else:
                 their_y = lax.bitwise_and(my_y + (source - NY), NY - 1)
-                fetch(gathered.at[their_y, 2, rows, :], slots.at[0, who, at, :])
-                fetch(ring[source - NY].at[rows, :], slots.at[1, who, at, :])
+                fetch(gathered.at[their_y, 4, rows, :], slots.at[0, who, at, :])
+                fetch(ring[source - NY].at[:, rows, :], slots.at[pl.ds(1, 3), who, at, :])
     for copy in copies:
         copy.start()
     gwide[...] = glob[...].astype(F32).reshape(WINDOWS * GROWS, HEAD_DIM)
@@ -88,10 +89,14 @@
         for kind in range(2):
             for head in range(HEADS):
                 first = (who * 2 + kind) * HEADS + head
-                near[kind, who, TOK : TOK + WINDOWS, head * HEAD_DIM : (head + 1) * HEAD_DIM] = (
+                sub = slice(head % 2 * HEAD_DIM, (head % 2 + 1) * HEAD_DIM)
+                near[kind * 2 + head // 2, who, TOK : TOK + WINDOWS, sub] = (
                     gwide[pl.ds(first, WINDOWS, stride=GROWS), :].astype(BF16)
                 )
-            near[kind, who, TOK + WINDOWS :, :] = jnp.zeros((NEAR - TOK - WINDOWS, HALF), BF16)
+            for side in range(2):
+                near[kind * 2 + side, who, TOK + WINDOWS :, :] = jnp.zeros(
+                    (NEAR - TOK - WINDOWS, PIECE), BF16
+                )
     column = lax.broadcasted_iota(jnp.int32, (TOK, NEAR), 1)
     hidden = (column >= TOK + WINDOWS) | (column == TOK + my_w)
     for copy in copies:
@@ -99,6 +104,8 @@
 
     def head_step(head, carry):
         lanes = pl.ds(pl.multiple_of(head * HEAD_DIM, HEAD_DIM), HEAD_DIM)
+        side = lax.shift_right_logical(head, 1)
+        sub = pl.ds(pl.multiple_of(lax.bitwise_and(head, 1) * HEAD_DIM, HEAD_DIM), HEAD_DIM)
         both = range(2)
         pairs = [(who, row) for who in both for row in range(BLK)]
         rows = [slice(row * BLOCK, (row + 1) * BLOCK) for row in range(BLK)]
@@ -107,14 +114,14 @@
         query = [qdo[0, :, lanes] for qdo in (qdo_own, qdo_peer)]
         grad = [qdo[1, :, lanes] for qdo in (qdo_own, qdo_peer)]
         near_score = [
-            jnp.where(hidden, -1e30, dot_nt(query[who], near[0, who, :, lanes])) for who in both
+            jnp.where(hidden, -1e30, dot_nt(query[who], near[side, who, :, sub])) for who in both
         ]
         far_score = [
-            dot_nt(query[who][rows[row]], slots[0, who, keys[row], lanes]) for who, row in pairs
+            dot_nt(query[who][rows[row]], slots[side, who, keys[row], sub]) for who, row in pairs
         ]
-        near_dprod = [dot_nt(grad[who], near[1, who, :, lanes]) for who in both]
+        near_dprod = [dot_nt(grad[who], near[2 + side, who, :, sub]) for who in both]
         far_dprod = [
-            dot_nt(grad[who][rows[row]], slots[1, who, keys[row], lanes]) for who, row in pairs
+            dot_nt(grad[who][rows[row]], slots[2 + side, who, keys[row], sub]) for who, row in pairs
         ]
         near_weight, far_weight, near_half, far_half = [], [], [], []
         for i, (who, row) in enumerate(pairs):
@@ -133,8 +140,8 @@
             far_half.append(far_weight[i].astype(BF16))
         delta = []
         for i, (who, row) in enumerate(pairs):
-            out = dot_nn(near_half[i], near[1, who, :, lanes])
-            out = (out + dot_nn(far_half[i], slots[1, who, keys[row], lanes])).astype(BF16)
+            out = dot_nn(near_half[i], near[2 + side, who, :, sub])
+            out = (out + dot_nn(far_half[i], slots[2 + side, who, keys[row], sub])).astype(BF16)
             res[who][0, rows[row], lanes] = out
             g = grad[who][rows[row]]
             delta.append(jnp.sum(g.astype(F32) * out.astype(F32), axis=1, keepdims=True))
@@ -147,8 +154,8 @@
             near_dscore.append(nd.astype(BF16))
             far_dscore.append((far_weight[i] * (far_dprod[i] - delta[i])).astype(BF16))
         for i, (who, row) in enumerate(pairs):
-            dq = dot_nn(near_dscore[i], near[0, who, :, lanes])
-            dq = (dq + dot_nn(far_dscore[i], slots[0, who, keys[row], lanes])) * SCALE
+            dq = dot_nn(near_dscore[i], near[side, who, :, sub])
+            dq = (dq + dot_nn(far_dscore[i], slots[side, who, keys[row], sub])) * SCALE
             res[who][1, rows[row], lanes] = dq.astype(BF16)
         for i, (who, row) in enumerate(pairs):
             dk = dot_tn(far_dscore[i], query[who][rows[row]]) * SCALE
@@ -200,24 +207,29 @@
         copy.wait()
 
 
-def cut_kernel(core, *refs):
-    inputs, outputs = refs[:4], refs[4:]
-    for half in range(2):
-        first = lax.bitwise_xor(core[0], half) * HALF
-        columns = pl.ds(pl.multiple_of(first, HALF), HALF)
-        for i in range(4):
-            outputs[i // 2 * 2 + half][i % 2] = inputs[i][:, columns]
-
-
-def cut(core, *inputs):
+def cut_kernel(width, core, first, second, own, send):
+    pieces = HALF // width
+    for output, half in ((own, 0), (send, 1)):
+        start = lax.bitwise_xor(core[0], half) * HALF
+        for i in range(2):
+            for piece in range(pieces):
+                columns = pl.ds(pl.multiple_of(start + piece * width, width), width)
+                output[i * pieces + piece] = (first, second)[i][:, columns]
+
+
+def cut(core, first, second, width, room=0):
     vmem = pl.BlockSpec(memory_space=pltpu.VMEM)
+    count = 2 * HALF // width
     return pl.pallas_call(
-        cut_kernel,
-        out_shape=[jax.ShapeDtypeStruct((2, TOK, HALF), BF16)] * 4,
-        in_specs=[pl.BlockSpec(memory_space=pltpu.SMEM)] + [vmem] * 4,
-        out_specs=[vmem] * 4,
-        cost_estimate=pl.CostEstimate(flops=0, bytes_accessed=2_000_000, transcendentals=0),
-    )(core.astype(jnp.int32)[None], *inputs)
+        functools.partial(cut_kernel, width),
+        out_shape=[
+            jax.ShapeDtypeStruct((count + room, TOK, width), BF16),
+            jax.ShapeDtypeStruct((count, TOK, width), BF16),
+        ],
+        in_specs=[pl.BlockSpec(memory_space=pltpu.SMEM), vmem, vmem],
+        out_specs=[vmem] * 2,
+        cost_estimate=pl.CostEstimate(flops=0, bytes_accessed=1_000_000, transcendentals=0),
+    )(core.astype(jnp.int32)[None], first, second)
 
 
 def attend(pos, far_own, far_peer, qdo_own, qdo_peer, glob, gathered, ring):
@@ -239,8 +251,8 @@
         in_specs=[smem] * 3 + [vmem] * 3 + [anywhere] * 9,
         out_specs=[anywhere] * 13,
         scratch_shapes=[
-            pltpu.VMEM((2, 2, BLK * FKEYS, HALF), BF16),
-            pltpu.VMEM((2, 2, NEAR, HALF), BF16),
+            pltpu.VMEM((4, 2, BLK * FKEYS, PIECE), BF16),
+            pltpu.VMEM((4, 2, NEAR, PIECE), BF16),
             pltpu.VMEM((2, 2, BLK * FKEYS, HALF), BF16),
             pltpu.VMEM((WINDOWS * GROWS, HEAD_DIM), F32),
             pltpu.VMEM((2, TOK, HALF), BF16),
@@ -278,11 +290,13 @@
     down = functools.partial(lax.ppermute, axis_name="y", perm=DOWN)
     low = my_c == 0
 
-    kv_own, kv_send, qdo_own, qdo_send = cut(my_c, key_rows, value_rows, query_rows, out_grad)
+    kv_own, kv_send = cut(my_c, key_rows, value_rows, PIECE, room=1)
     kv_peer = swap(kv_send)
-    gathered = lax.all_gather(jnp.concatenate([kv_own, kv_peer[:1]]), "y", axis=0)
-    ring = [kv_peer[1]] + [None] * (NY - 1)
-    row = jnp.concatenate([kv_own[:, 0], kv_peer[:, 0]]).reshape(GROWS, HEAD_DIM)
+    kv_own = lax.dynamic_update_slice(kv_own, kv_peer[:1], (4, 0, 0))
+    gathered = lax.all_gather(kv_own, "y", axis=0)
+    ring = [kv_peer[1:]] + [None] * (NY - 1)
+    qdo_own, qdo_send = cut(my_c, query_rows, out_grad, HALF)
+    row = jnp.concatenate([kv_own[:4, 0], kv_peer[:, 0]]).reshape(GROWS, HEAD_DIM)
     chains = ((up, 4, -1), (down, 3, 1))
     held = [ring[0], ring[0]]
     for step in range(1, 5):

time: 157 us -> 153 us (0.975)
  waiting for transfers between devices: 32.8 us -> 25.4 us
  starting transfers between devices: 84.8 us -> 88.5 us
  other arithmetic: 7.7 us -> 5.01 us
    all_gather x1, waiting for transfers between devices: 7.68 us -> 0.01 us  [per_device(): gathered = lax.all_gather(kv_own, 'y', axis=0)]
    all_to_all x1, starting transfers between devices: 7.4 us -> 9.58 us  [per_device(): gback = lax.all_to_all(gglob, ('x', 'z'), 0, 0, tiled=True)]
    concatenate x2 -> x1, other arithmetic: 1.81 us -> 0.01 us  [per_device(): jnp.concatenate([kv_own[:4, 0], kv_peer[:, 0]]).reshape(GROWS, HEAD_DIM)]
    ppermute x1, starting transfers between devices: 3.22 us -> 4.83 us  [per_device(): res_back = swap(res_peer)]
    pallas_call x1 -> x2, Pallas kernels: 2.22 us -> 3.76 us  [cut(): pl.pallas_call(functools.partial(cut_kernel, width), out_shape=[jax.Shape...]
  transfers between devices with their start and end apart: 23 -> 23, of which waited for: 12 -> 10; matrix products, arithmetic and copies ran while one was open for 3% -> 3% of each run, Pallas kernels for 0% -> 1%
where the time goes in v9:
time: 153 us; the launch traced here: 152 us
  starting transfers between devices  88.5 us (58%)
  waiting for transfers between devices  25.4 us (17%)
  Pallas kernels  15.6 us (10%)
  between operations  14.7 us (10%)
  other arithmetic  5.01 us (3%)
  local copies, waits for them, and re-layouts  2.82 us (2%)
    ppermute x14, starting transfers between devices, per_device(): held[i] = move(held[i])  44.4 us
    ppermute x14, waiting for transfers between devices, per_device(): held[i] = move(held[i])  21.5 us
    pallas_call x1, Pallas kernels, attend(): pl.pallas_call(attend_kernel, out_shape=[piece, piece, jax.ShapeDtypeStru...  11.8 us
    all_to_all x1, starting transfers between devices, per_device(): gback = lax.all_to_all(gglob, ('x', 'z'), 0, 0, tiled=True)  9.58 us
    ppermute x1, starting transfers between devices, per_device(): kv_peer = swap(kv_send)  8.77 us
    all_to_all x1, starting transfers between devices, per_device(): lax.all_to_all(jnp.broadcast_to(row, (WINDOWS, GROWS, HEAD_DIM)), ('x', '...  8.04 us
    ppermute x1, starting transfers between devices, per_device(): peer_grad = swap(peer_grad)  7.18 us
    ppermute x1, starting transfers between devices, per_device(): res_back = swap(res_peer)  4.83 us
  transfers between devices with their start and end apart: 23, of which 10 were waited for; matrix products, arithmetic and copies ran while one was open for 3% of the time, Pallas kernels for 1%

profile of v9, /device:TPU:1, one launch (start us, length us, event | category | flops | bytes accessed | tf_op | source)
XLA Modules:
  0.0 152.1 jit_solution(2335480750577782934)
XLA Ops:
  7.2 1.9 %shard_map.84 = (bf16[5,128,256]{2,1,0:T(8,128)(2,1)}, bf16[4,128,256]{2,1,0:T(8,128)(2,1)}) custom-call(s32[1]{0:T(128)} %bitcast.1.core, bf16[128,1024]{1,0:T(8,128)(2,1)} %first.2, bf16[128,1024]{1,0:T(8,128)(2,1)} %second.2), custom_call_target="tpu_custom_call" | custom-call | bytes 1000000 | tf_op jit(solution)/shard_map/pallas_call | solution.py:223
  9.1 8.8 %collective-permute-start = (bf16[4,128,256]{2,1,0:T(8,128)(2,1)}, bf16[4,128,256]{2,1,0:T(8,128)(2,1)S(1)}, u32[]{:S(2)}, u32[]{:S(2)}) collective-permute-start(bf16[4,128,256]{2,1,0:T(8,128)(2,1)} %get-tuple-element.31), channel_id=1, source_target_pairs={{0,1},{1,0},{2,3},{3,2},{4,5},{5,4},{6,7},{7,6},{8,9},{9,8},{10,11... | collective-permute-start | bytes 786440 | tf_op jit(solution)/shard_map/ppermute | solution.py:294
  17.9 1.4 collective-permute-done
  19.3 0.6 slice_dynamic-update-slice_fusion
  19.9 1.9 %collective-permute-start.1 = (bf16[3,128,256]{2,1,0:T(8,128)(2,1)S(1)}, bf16[3,128,256]{2,1,0:T(8,128)(2,1)S(1)}, u32[]{:S(2)}, u32[]{:S(2)}) collective-permute-start(bf16[3,128,256]{2,1,0:T(8,128)(2,1)S(1)} %slice.61.refs_7_), channel_id=1, source_target_pairs={{0,2},{2,4},{4,6},{6,8},{8,10},{10,12},{12,14},{14,0},{1,3},{3,5},... | collective-permute-start | bytes 589832 | tf_op jit(solution)/shard_map/ppermute | solution.py:305
  21.9 0.7 slice.59
  22.6 4.6 %collective-permute-start.6 = (bf16[3,128,256]{2,1,0:T(8,128)(2,1)S(1)}, bf16[3,128,256]{2,1,0:T(8,128)(2,1)S(1)}, u32[]{:S(2)}, u32[]{:S(2)}) collective-permute-start(bf16[3,128,256]{2,1,0:T(8,128)(2,1)S(1)} %slice.61.refs_7_), channel_id=1, source_target_pairs={{0,14},{2,0},{4,2},{6,4},{8,6},{10,8},{12,10},{14,12},{1,15},{3,1}... | collective-permute-start | bytes 589832 | tf_op jit(solution)/shard_map/ppermute | solution.py:305
  27.2 1.9 %collective-permute-done.1.refs_14_ = bf16[3,128,256]{2,1,0:T(8,128)(2,1)S(1)} collective-permute-done((bf16[3,128,256]{2,1,0:T(8,128)(2,1)S(1)}, bf16[3,128,256]{2,1,0:T(8,128)(2,1)S(1)}, u32[]{:S(2)}, u32[]{:S(2)}) %collective-permute-start.1) | collective-permute-done | bytes 196640 | tf_op jit(solution)/shard_map/ppermute | solution.py:305
  29.2 1.9 %collective-permute-start.4 = (bf16[3,128,256]{2,1,0:T(8,128)(2,1)S(1)}, bf16[3,128,256]{2,1,0:T(8,128)(2,1)S(1)}, u32[]{:S(2)}, u32[]{:S(2)}) collective-permute-start(bf16[3,128,256]{2,1,0:T(8,128)(2,1)S(1)} %collective-permute-done.1.refs_14_), channel_id=1, source_target_pairs={{0,2},{2,4},{4,6},{6,8},{8,10},{10,12},{12,14},{14,0},{1,3},{3,5},... | collective-permute-start | bytes 589832 | tf_op jit(solution)/shard_map/ppermute | solution.py:305
  31.1 1.9 %shard_map.85 = (bf16[2,128,512]{2,1,0:T(8,128)(2,1)}, bf16[2,128,512]{2,1,0:T(8,128)(2,1)}) custom-call(s32[1]{0:T(128)} %bitcast.1.core, bf16[128,1024]{1,0:T(8,128)(2,1)} %first.3, bf16[128,1024]{1,0:T(8,128)(2,1)} %second.3), custom_call_target="tpu_custom_call" | custom-call | bytes 1000000 | tf_op jit(solution)/shard_map/pallas_call | solution.py:223
  32.9 3.1 %collective-permute-start.2 = (bf16[2,128,512]{2,1,0:T(8,128)(2,1)}, bf16[2,128,512]{2,1,0:T(8,128)(2,1)S(1)}, u32[]{:S(2)}, u32[]{:S(2)}) collective-permute-start(bf16[2,128,512]{2,1,0:T(8,128)(2,1)} %get-tuple-element.33), channel_id=1, source_target_pairs={{0,1},{1,0},{2,3},{3,2},{4,5},{5,4},{6,7},{7,6},{8,9},{9,8},{10,11... | collective-permute-start | bytes 786440 | tf_op jit(solution)/shard_map/ppermute | solution.py:311
  36.0 0.7 broadcast_in_dim.40
  36.7 8.0 %all-to-all-start = ((bf16[32,16,128]{2,1,0:T(8,128)(2,1)}), bf16[32,16,128]{2,1,0:T(8,128)(2,1)S(1)}, u32[]{:S(2)}, u32[]{:S(2)}) async-start(bf16[32,16,128]{2,1,0:T(8,128)(2,1)} %broadcast_in_dim.40), calls=%async_computation | async-start | bytes 262144 | tf_op jit(solution)/shard_map/all_to_all | solution.py:308
  44.8 4.9 %collective-permute-start.7 = (bf16[3,128,256]{2,1,0:T(8,128)(2,1)S(1)}, bf16[3,128,256]{2,1,0:T(8,128)(2,1)S(1)}, u32[]{:S(2)}, u32[]{:S(2)}) collective-permute-start(bf16[3,128,256]{2,1,0:T(8,128)(2,1)S(1)} %collective-permute-done.6.refs_8_), channel_id=1, source_target_pairs={{0,14},{2,0},{4,2},{6,4},{8,6},{10,8},{12,10},{14,12},{1,15},{3,1}... | collective-permute-start | bytes 589832 | tf_op jit(solution)/shard_map/ppermute | solution.py:305
  49.7 1.9 %collective-permute-start.5 = (bf16[3,128,256]{2,1,0:T(8,128)(2,1)S(1)}, bf16[3,128,256]{2,1,0:T(8,128)(2,1)S(1)}, u32[]{:S(2)}, u32[]{:S(2)}) collective-permute-start(bf16[3,128,256]{2,1,0:T(8,128)(2,1)S(1)} %collective-permute-done.4.refs_13_), channel_id=1, source_target_pairs={{0,2},{2,4},{4,6},{6,8},{8,10},{10,12},{12,14},{14,0},{1,3},{3,5},... | collective-permute-start | bytes 589832 | tf_op jit(solution)/shard_map/ppermute | solution.py:305
  51.7 2.5 %collective-permute-start.3 = (s32[2,8]{1,0:T(2,128)}, s32[2,8]{1,0:T(2,128)S(1)}, u32[]{:S(2)}, u32[]{:S(2)}) collective-permute-start(s32[2,8]{1,0:T(2,128)} %refs_1_.1), channel_id=1, source_target_pairs={{0,1},{1,0},{2,3},{3,2},{4,5},{5,4},{6,7},{7,6},{8,9},{9,8},{10,11... | collective-permute-start | bytes 200 | tf_op jit(solution)/shard_map/ppermute | solution.py:312
  54.1 4.1 %collective-permute-done.7.refs_9_ = bf16[3,128,256]{2,1,0:T(8,128)(2,1)S(1)} collective-permute-done((bf16[3,128,256]{2,1,0:T(8,128)(2,1)S(1)}, bf16[3,128,256]{2,1,0:T(8,128)(2,1)S(1)}, u32[]{:S(2)}, u32[]{:S(2)}) %collective-permute-start.7) | collective-permute-done | bytes 196640 | tf_op jit(solution)/shard_map/ppermute | solution.py:305
  58.3 5.4 %collective-permute-start.8 = (bf16[3,128,256]{2,1,0:T(8,128)(2,1)S(1)}, bf16[3,128,256]{2,1,0:T(8,128)(2,1)S(1)}, u32[]{:S(2)}, u32[]{:S(2)}) collective-permute-start(bf16[3,128,256]{2,1,0:T(8,128)(2,1)S(1)} %collective-permute-done.7.refs_9_), channel_id=1, source_target_pairs={{0,14},{2,0},{4,2},{6,4},{8,6},{10,8},{12,10},{14,12},{1,15},{3,1}... | collective-permute-start | bytes 589832 | tf_op jit(solution)/shard_map/ppermute | solution.py:305
  63.8 1.9 %collective-permute-start.9 = (bf16[3,128,256]{2,1,0:T(8,128)(2,1)S(1)}, bf16[3,128,256]{2,1,0:T(8,128)(2,1)S(1)}, u32[]{:S(2)}, u32[]{:S(2)}) collective-permute-start(bf16[3,128,256]{2,1,0:T(8,128)(2,1)S(1)} %collective-permute-done.5.refs_12_), channel_id=1, source_target_pairs={{0,2},{2,4},{4,6},{6,8},{8,10},{10,12},{12,14},{14,0},{1,3},{3,5},... | collective-permute-start | bytes 589832 | tf_op jit(solution)/shard_map/ppermute | solution.py:305
  65.7 0.6 pad_add_fusion.refs_0_
  66.3 4.5 %collective-permute-done.8.refs_10_ = bf16[3,128,256]{2,1,0:T(8,128)(2,1)S(1)} collective-permute-done((bf16[3,128,256]{2,1,0:T(8,128)(2,1)S(1)}, bf16[3,128,256]{2,1,0:T(8,128)(2,1)S(1)}, u32[]{:S(2)}, u32[]{:S(2)}) %collective-permute-start.8) | collective-permute-done | bytes 196640 | tf_op jit(solution)/shard_map/ppermute | solution.py:305
  70.8 1.4 collective-permute-done.9.refs_11_
  72.3 0.6 copy-done.16
  72.9 11.8 %shard_map.86 = (bf16[2,128,512]{2,1,0:T(8,128)(2,1)}, bf16[2,128,512]{2,1,0:T(8,128)(2,1)}, f32[2,128,512]{2,1,0:T(8,128)}, f32[2,128,512]{2,1,0:T(8,128)}, bf1...) custom-call(s32[3]{0:T(128)} %pad_add_fusion.refs_0_, ...), custom_call_target="tpu_custom_call" | custom-call | flops 1200000000 | bytes 12000000 | tf_op jit(solution)/shard_map/pallas_call | solution.py:240
  84.8 2.1 %collective-permute-start.11 = (bf16[2,128,512]{2,1,0:T(8,128)(2,1)}, bf16[2,128,512]{2,1,0:T(8,128)(2,1)S(1)}, u32[]{:S(2)}, u32[]{:S(2)}) collective-permute-start(bf16[2,128,512]{2,1,0:T(8,128)(2,1)} %get-tuple-element.45), channel_id=1, source_target_pairs={{0,2},{2,4},{4,6},{6,8},{8,10},{10,12},{12,14},{14,0},{1,3},{3,5},... | collective-permute-start | bytes 786440 | tf_op jit(solution)/shard_map/ppermute | solution.py:330
  86.9 4.5 %collective-permute-start.15 = (bf16[2,128,512]{2,1,0:T(8,128)(2,1)}, bf16[2,128,512]{2,1,0:T(8,128)(2,1)S(1)}, u32[]{:S(2)}, u32[]{:S(2)}) collective-permute-start(bf16[2,128,512]{2,1,0:T(8,128)(2,1)} %get-tuple-element.50), channel_id=1, source_target_pairs={{0,14},{2,0},{4,2},{6,4},{8,6},{10,8},{12,10},{14,12},{1,15},{3,1}... | collective-permute-start | bytes 786440 | tf_op jit(solution)/shard_map/ppermute | solution.py:330
  91.5 2.6 %collective-permute-done.11 = bf16[2,128,512]{2,1,0:T(8,128)(2,1)S(1)} collective-permute-done((bf16[2,128,512]{2,1,0:T(8,128)(2,1)}, bf16[2,128,512]{2,1,0:T(8,128)(2,1)S(1)}, u32[]{:S(2)}, u32[]{:S(2)}) %collective-permute-start.11) | collective-permute-done | bytes 262176 | tf_op jit(solution)/shard_map/ppermute | solution.py:330
  94.1 1.0 add_convert_fusion.5
  95.1 1.9 %collective-permute-start.12 = (bf16[2,128,512]{2,1,0:T(8,128)(2,1)S(1)}, bf16[2,128,512]{2,1,0:T(8,128)(2,1)S(1)}, u32[]{:S(2)}, u32[]{:S(2)}) collective-permute-start(bf16[2,128,512]{2,1,0:T(8,128)(2,1)S(1)} %add_convert_fusion.5), channel_id=1, source_target_pairs={{0,2},{2,4},{4,6},{6,8},{8,10},{10,12},{12,14},{14,0},{1,3},{3,5},... | collective-permute-start | bytes 786440 | tf_op jit(solution)/shard_map/ppermute | solution.py:330
  97.0 4.8 %collective-permute-start.10 = (bf16[2,128,512]{2,1,0:T(8,128)(2,1)S(1)}, bf16[2,128,512]{2,1,0:T(8,128)(2,1)S(1)}, u32[]{:S(2)}, u32[]{:S(2)}) collective-permute-start(bf16[2,128,512]{2,1,0:T(8,128)(2,1)S(1)} %copy-done.18), channel_id=1, source_target_pairs={{0,1},{1,0},{2,3},{3,2},{4,5},{5,4},{6,7},{7,6},{8,9},{9,8},{10,11... | collective-permute-start | bytes 786440 | tf_op jit(solution)/shard_map/ppermute | solution.py:341
  101.9 0.1 add_convert_fusion.2
  102.0 4.9 %collective-permute-start.16 = (bf16[2,128,512]{2,1,0:T(8,128)(2,1)S(1)}, bf16[2,128,512]{2,1,0:T(8,128)(2,1)S(1)}, u32[]{:S(2)}, u32[]{:S(2)}) collective-permute-start(bf16[2,128,512]{2,1,0:T(8,128)(2,1)S(1)} %add_convert_fusion.2), channel_id=1, source_target_pairs={{0,14},{2,0},{4,2},{6,4},{8,6},{10,8},{12,10},{14,12},{1,15},{3,1}... | collective-permute-start | bytes 786440 | tf_op jit(solution)/shard_map/ppermute | solution.py:330
  106.9 0.1 add_convert_fusion.4
  106.9 1.9 %collective-permute-start.13 = (bf16[2,128,512]{2,1,0:T(8,128)(2,1)S(1)}, bf16[2,128,512]{2,1,0:T(8,128)(2,1)S(1)}, u32[]{:S(2)}, u32[]{:S(2)}) collective-permute-start(bf16[2,128,512]{2,1,0:T(8,128)(2,1)S(1)} %add_convert_fusion.4), channel_id=1, source_target_pairs={{0,2},{2,4},{4,6},{6,8},{8,10},{10,12},{12,14},{14,0},{1,3},{3,5},... | collective-permute-start | bytes 786440 | tf_op jit(solution)/shard_map/ppermute | solution.py:330
  108.9 9.6 %all-to-all-start.1 = ((bf16[32,16,128]{2,1,0:T(8,128)(2,1)}), bf16[32,16,128]{2,1,0:T(8,128)(2,1)S(1)}, u32[]{:S(2)}, u32[]{:S(2)}) async-start(bf16[32,16,128]{2,1,0:T(8,128)(2,1)} %get-tuple-element.53), calls=%async_computation.1 | async-start | bytes 262144 | tf_op jit(solution)/shard_map/all_to_all | solution.py:333
  118.5 0.1 add_convert_fusion.1
  118.6 4.7 %collective-permute-start.17 = (bf16[2,128,512]{2,1,0:T(8,128)(2,1)S(1)}, bf16[2,128,512]{2,1,0:T(8,128)(2,1)S(1)}, u32[]{:S(2)}, u32[]{:S(2)}) collective-permute-start(bf16[2,128,512]{2,1,0:T(8,128)(2,1)S(1)} %add_convert_fusion.1), channel_id=1, source_target_pairs={{0,14},{2,0},{4,2},{6,4},{8,6},{10,8},{12,10},{14,12},{1,15},{3,1}... | collective-permute-start | bytes 786440 | tf_op jit(solution)/shard_map/ppermute | solution.py:330
  123.3 0.1 add_convert_fusion.3
  123.4 1.9 %collective-permute-start.14 = (bf16[2,128,512]{2,1,0:T(8,128)(2,1)S(1)}, bf16[2,128,512]{2,1,0:T(8,128)(2,1)S(1)}, u32[]{:S(2)}, u32[]{:S(2)}) collective-permute-start(bf16[2,128,512]{2,1,0:T(8,128)(2,1)S(1)} %add_convert_fusion.3), channel_id=1, source_target_pairs={{0,2},{2,4},{4,6},{6,8},{8,10},{10,12},{12,14},{14,0},{1,3},{3,5},... | collective-permute-start | bytes 786440 | tf_op jit(solution)/shard_map/ppermute | solution.py:330
  125.3 2.3 %all-to-all-done.1 = bf16[32,16,128]{2,1,0:T(8,128)(2,1)S(1)} async-done(((bf16[32,16,128]{2,1,0:T(8,128)(2,1)}), bf16[32,16,128]{2,1,0:T(8,128)(2,1)S(1)}, u32[]{:S(2)}, u32[]{:S(2)}) %all-to-all-start.1) | async-done | bytes 131104 | tf_op jit(solution)/shard_map/all_to_all | solution.py:333
  127.7 3.2 %collective-permute-done.17 = bf16[2,128,512]{2,1,0:T(8,128)(2,1)S(1)} collective-permute-done((bf16[2,128,512]{2,1,0:T(8,128)(2,1)S(1)}, bf16[2,128,512]{2,1,0:T(8,128)(2,1)S(1)}, u32[]{:S(2)}, u32[]{:S(2)}) %collective-permute-start.17) | collective-permute-done | bytes 262176 | tf_op jit(solution)/shard_map/ppermute | solution.py:330
  130.8 3.8 %collective-permute-done.14 = bf16[2,128,512]{2,1,0:T(8,128)(2,1)S(1)} collective-permute-done((bf16[2,128,512]{2,1,0:T(8,128)(2,1)S(1)}, bf16[2,128,512]{2,1,0:T(8,128)(2,1)S(1)}, u32[]{:S(2)}, u32[]{:S(2)}) %collective-permute-start.14) | collective-permute-done | bytes 262176 | tf_op jit(solution)/shard_map/ppermute | solution.py:330
  134.7 0.1 add_convert_fusion
  134.8 7.2 %collective-permute-start.18 = (bf16[2,128,512]{2,1,0:T(8,128)(2,1)S(1)}, bf16[2,128,512]{2,1,0:T(8,128)(2,1)S(1)}, u32[]{:S(2)}, u32[]{:S(2)}) collective-permute-start(bf16[2,128,512]{2,1,0:T(8,128)(2,1)S(1)} %add_convert_fusion), channel_id=1, source_target_pairs={{0,1},{1,0},{2,3},{3,2},{4,5},{5,4},{6,7},{7,6},{8,9},{9,8},{10,11... | collective-permute-start | bytes 786440 | tf_op jit(solution)/shard_map/ppermute | solution.py:350
  142.0 0.9 maximum_select_fusion
  143.0 0.2 collective-permute-done.18
  143.2 1.1 fusion.1
  144.3 0.9 maximum_select_fusion.2
  (69 shorter events, 0.4 us)
Async XLA Ops:
  7.2 65.0 %all-gather.3.cloned.1.call-start = ((), (), s32[]{:S(2)}) async-start(), calls=%async_computation.4 | async-start | bytes 2949120 | tf_op jit(solution)/shard_map/all_gather | solution.py:296
  9.1 10.1 %collective-permute-start = (bf16[4,128,256]{2,1,0:T(8,128)(2,1)}, bf16[4,128,256]{2,1,0:T(8,128)(2,1)S(1)}, u32[]{:S(2)}, u32[]{:S(2)}) collective-permute-start(bf16[4,128,256]{2,1,0:T(8,128)(2,1)} %get-tuple-element.31), channel_id=1, source_target_pairs={{0,1},{1,0},{2,3},{3,2},{4,5},{5,4},{6,7},{7,6},{8,9},{9,8},{10,11... | collective-permute-start | bytes 786440 | tf_op jit(solution)/shard_map/ppermute | solution.py:294
  19.9 52.3 %copy-start = (bf16[3,128,256]{2,1,0:T(8,128)(2,1)}, bf16[3,128,256]{2,1,0:T(8,128)(2,1)S(1)}, u32[]{:S(2)}) copy-start(bf16[3,128,256]{2,1,0:T(8,128)(2,1)S(1)} %slice.61.refs_7_) | copy-start | bytes 589828
  19.9 9.2 %collective-permute-start.1 = (bf16[3,128,256]{2,1,0:T(8,128)(2,1)S(1)}, bf16[3,128,256]{2,1,0:T(8,128)(2,1)S(1)}, u32[]{:S(2)}, u32[]{:S(2)}) collective-permute-start(bf16[3,128,256]{2,1,0:T(8,128)(2,1)S(1)} %slice.61.refs_7_), channel_id=1, source_target_pairs={{0,2},{2,4},{4,6},{6,8},{8,10},{10,12},{12,14},{14,0},{1,3},{3,5},... | collective-permute-start | bytes 589832 | tf_op jit(solution)/shard_map/ppermute | solution.py:305
  22.6 22.2 %collective-permute-start.6 = (bf16[3,128,256]{2,1,0:T(8,128)(2,1)S(1)}, bf16[3,128,256]{2,1,0:T(8,128)(2,1)S(1)}, u32[]{:S(2)}, u32[]{:S(2)}) collective-permute-start(bf16[3,128,256]{2,1,0:T(8,128)(2,1)S(1)} %slice.61.refs_7_), channel_id=1, source_target_pairs={{0,14},{2,0},{4,2},{6,4},{8,6},{10,8},{12,10},{14,12},{1,15},{3,1}... | collective-permute-start | bytes 589832 | tf_op jit(solution)/shard_map/ppermute | solution.py:305
  29.2 43.0 %copy-start.10 = (bf16[3,128,256]{2,1,0:T(8,128)(2,1)}, bf16[3,128,256]{2,1,0:T(8,128)(2,1)S(1)}, u32[]{:S(2)}) copy-start(bf16[3,128,256]{2,1,0:T(8,128)(2,1)S(1)} %collective-permute-done.1.refs_14_) | copy-start | bytes 589828
  29.2 20.5 %collective-permute-start.4 = (bf16[3,128,256]{2,1,0:T(8,128)(2,1)S(1)}, bf16[3,128,256]{2,1,0:T(8,128)(2,1)S(1)}, u32[]{:S(2)}, u32[]{:S(2)}) collective-permute-start(bf16[3,128,256]{2,1,0:T(8,128)(2,1)S(1)} %collective-permute-done.1.refs_14_), channel_id=1, source_target_pairs={{0,2},{2,4},{4,6},{6,8},{8,10},{10,12},{12,14},{14,0},{1,3},{3,5},... | collective-permute-start | bytes 589832 | tf_op jit(solution)/shard_map/ppermute | solution.py:305
  32.9 30.8 %collective-permute-start.2 = (bf16[2,128,512]{2,1,0:T(8,128)(2,1)}, bf16[2,128,512]{2,1,0:T(8,128)(2,1)S(1)}, u32[]{:S(2)}, u32[]{:S(2)}) collective-permute-start(bf16[2,128,512]{2,1,0:T(8,128)(2,1)} %get-tuple-element.33), channel_id=1, source_target_pairs={{0,1},{1,0},{2,3},{3,2},{4,5},{5,4},{6,7},{7,6},{8,9},{9,8},{10,11... | collective-permute-start | bytes 786440 | tf_op jit(solution)/shard_map/ppermute | solution.py:311
  36.7 27.0 %all-to-all-start = ((bf16[32,16,128]{2,1,0:T(8,128)(2,1)}), bf16[32,16,128]{2,1,0:T(8,128)(2,1)S(1)}, u32[]{:S(2)}, u32[]{:S(2)}) async-start(bf16[32,16,128]{2,1,0:T(8,128)(2,1)} %broadcast_in_dim.40), calls=%async_computation | async-start | bytes 262144 | tf_op jit(solution)/shard_map/all_to_all | solution.py:308
  44.8 98.4 %reduce-scatter.2.cloned.1.call-start = ((), (), s32[]{:S(2)}) async-start(), calls=%async_computation.3 | async-start | bytes 2359296 | tf_op jit(solution)/shard_map/reduce_scatter | solution.py:324
  44.8 27.4 %copy-start.11 = (bf16[3,128,256]{2,1,0:T(8,128)(2,1)}, bf16[3,128,256]{2,1,0:T(8,128)(2,1)S(1)}, u32[]{:S(2)}) copy-start(bf16[3,128,256]{2,1,0:T(8,128)(2,1)S(1)} %collective-permute-done.6.refs_8_) | copy-start | bytes 589828
  44.8 13.4 %collective-permute-start.7 = (bf16[3,128,256]{2,1,0:T(8,128)(2,1)S(1)}, bf16[3,128,256]{2,1,0:T(8,128)(2,1)S(1)}, u32[]{:S(2)}, u32[]{:S(2)}) collective-permute-start(bf16[3,128,256]{2,1,0:T(8,128)(2,1)S(1)} %collective-permute-done.6.refs_8_), channel_id=1, source_target_pairs={{0,14},{2,0},{4,2},{6,4},{8,6},{10,8},{12,10},{14,12},{1,15},{3,1}... | collective-permute-start | bytes 589832 | tf_op jit(solution)/shard_map/ppermute | solution.py:305
  49.7 22.5 %copy-start.12 = (bf16[3,128,256]{2,1,0:T(8,128)(2,1)}, bf16[3,128,256]{2,1,0:T(8,128)(2,1)S(1)}, u32[]{:S(2)}) copy-start(bf16[3,128,256]{2,1,0:T(8,128)(2,1)S(1)} %collective-permute-done.4.refs_13_) | copy-start | bytes 589828
  49.7 14.0 %collective-permute-start.5 = (bf16[3,128,256]{2,1,0:T(8,128)(2,1)S(1)}, bf16[3,128,256]{2,1,0:T(8,128)(2,1)S(1)}, u32[]{:S(2)}, u32[]{:S(2)}) collective-permute-start(bf16[3,128,256]{2,1,0:T(8,128)(2,1)S(1)} %collective-permute-done.4.refs_13_), channel_id=1, source_target_pairs={{0,2},{2,4},{4,6},{6,8},{8,10},{10,12},{12,14},{14,0},{1,3},{3,5},... | collective-permute-start | bytes 589832 | tf_op jit(solution)/shard_map/ppermute | solution.py:305
  51.7 12.0 %collective-permute-start.3 = (s32[2,8]{1,0:T(2,128)}, s32[2,8]{1,0:T(2,128)S(1)}, u32[]{:S(2)}, u32[]{:S(2)}) collective-permute-start(s32[2,8]{1,0:T(2,128)} %refs_1_.1), channel_id=1, source_target_pairs={{0,1},{1,0},{2,3},{3,2},{4,5},{5,4},{6,7},{7,6},{8,9},{9,8},{10,11... | collective-permute-start | bytes 200 | tf_op jit(solution)/shard_map/ppermute | solution.py:312
  58.3 14.0 %copy-start.13 = (bf16[3,128,256]{2,1,0:T(8,128)(2,1)}, bf16[3,128,256]{2,1,0:T(8,128)(2,1)S(1)}, u32[]{:S(2)}) copy-start(bf16[3,128,256]{2,1,0:T(8,128)(2,1)S(1)} %collective-permute-done.7.refs_9_) | copy-start | bytes 589828
  58.3 12.6 %collective-permute-start.8 = (bf16[3,128,256]{2,1,0:T(8,128)(2,1)S(1)}, bf16[3,128,256]{2,1,0:T(8,128)(2,1)S(1)}, u32[]{:S(2)}, u32[]{:S(2)}) collective-permute-start(bf16[3,128,256]{2,1,0:T(8,128)(2,1)S(1)} %collective-permute-done.7.refs_9_), channel_id=1, source_target_pairs={{0,14},{2,0},{4,2},{6,4},{8,6},{10,8},{12,10},{14,12},{1,15},{3,1}... | collective-permute-start | bytes 589832 | tf_op jit(solution)/shard_map/ppermute | solution.py:305
  63.7 8.5 %copy-start.17 = (s32[2,8]{1,0:T(2,128)}, s32[2,8]{1,0:T(2,128)S(1)}, u32[]{:S(2)}) copy-start(s32[2,8]{1,0:T(2,128)S(1)} %collective-permute-done.3.refs_2_) | copy-start | bytes 196
  63.7 8.5 %copy-start.4 = (bf16[2,128,512]{2,1,0:T(8,128)(2,1)}, bf16[2,128,512]{2,1,0:T(8,128)(2,1)S(1)}, u32[]{:S(2)}) copy-start(bf16[2,128,512]{2,1,0:T(8,128)(2,1)S(1)} %collective-permute-done.2.refs_4_) | copy-start | bytes 786436
  63.7 8.5 %copy-start.2 = (bf16[32,16,128]{2,1,0:T(8,128)(2,1)}, bf16[32,16,128]{2,1,0:T(8,128)(2,1)S(1)}, u32[]{:S(2)}) copy-start(bf16[32,16,128]{2,1,0:T(8,128)(2,1)S(1)} %all-to-all-done.refs_5_) | copy-start | bytes 393220
  63.8 8.5 %copy-start.14 = (bf16[3,128,256]{2,1,0:T(8,128)(2,1)}, bf16[3,128,256]{2,1,0:T(8,128)(2,1)S(1)}, u32[]{:S(2)}) copy-start(bf16[3,128,256]{2,1,0:T(8,128)(2,1)S(1)} %collective-permute-done.5.refs_12_) | copy-start | bytes 589828
  63.8 8.4 %collective-permute-start.9 = (bf16[3,128,256]{2,1,0:T(8,128)(2,1)S(1)}, bf16[3,128,256]{2,1,0:T(8,128)(2,1)S(1)}, u32[]{:S(2)}, u32[]{:S(2)}) collective-permute-start(bf16[3,128,256]{2,1,0:T(8,128)(2,1)S(1)} %collective-permute-done.5.refs_12_), channel_id=1, source_target_pairs={{0,2},{2,4},{4,6},{6,8},{8,10},{10,12},{12,14},{14,0},{1,3},{3,5},... | collective-permute-start | bytes 589832 | tf_op jit(solution)/shard_map/ppermute | solution.py:305
  70.8 1.5 copy-start.15
  72.2 0.7 copy-start.16
  84.7 12.3 %copy-start.18 = (bf16[2,128,512]{2,1,0:T(8,128)(2,1)S(1)}, bf16[2,128,512]{2,1,0:T(8,128)(2,1)}, u32[]{:S(2)}) copy-start(bf16[2,128,512]{2,1,0:T(8,128)(2,1)} %get-tuple-element.41) | copy-start | bytes 786436
  84.7 17.2 %copy-start.8 = (bf16[2,128,512]{2,1,0:T(8,128)(2,1)S(1)}, bf16[2,128,512]{2,1,0:T(8,128)(2,1)}, u32[]{:S(2)}) copy-start(bf16[2,128,512]{2,1,0:T(8,128)(2,1)} %get-tuple-element.51) | copy-start | bytes 786436
  84.7 22.1 %copy-start.7 = (bf16[2,128,512]{2,1,0:T(8,128)(2,1)S(1)}, bf16[2,128,512]{2,1,0:T(8,128)(2,1)}, u32[]{:S(2)}) copy-start(bf16[2,128,512]{2,1,0:T(8,128)(2,1)} %get-tuple-element.48) | copy-start | bytes 786436
  84.8 24.1 %copy-start.9 = (bf16[2,128,512]{2,1,0:T(8,128)(2,1)S(1)}, bf16[2,128,512]{2,1,0:T(8,128)(2,1)}, u32[]{:S(2)}) copy-start(bf16[2,128,512]{2,1,0:T(8,128)(2,1)} %get-tuple-element.40) | copy-start | bytes 786436
  84.8 33.7 %copy-start.6 = (bf16[2,128,512]{2,1,0:T(8,128)(2,1)S(1)}, bf16[2,128,512]{2,1,0:T(8,128)(2,1)}, u32[]{:S(2)}) copy-start(bf16[2,128,512]{2,1,0:T(8,128)(2,1)} %get-tuple-element.52) | copy-start | bytes 786436
  84.8 38.5 %copy-start.5 = (bf16[2,128,512]{2,1,0:T(8,128)(2,1)S(1)}, bf16[2,128,512]{2,1,0:T(8,128)(2,1)}, u32[]{:S(2)}) copy-start(bf16[2,128,512]{2,1,0:T(8,128)(2,1)} %get-tuple-element.49) | copy-start | bytes 786436
  84.8 49.9 %copy-start.1 = (f32[2,128,512]{2,1,0:T(8,128)S(1)}, f32[2,128,512]{2,1,0:T(8,128)}, u32[]{:S(2)}) copy-start(f32[2,128,512]{2,1,0:T(8,128)} %get-tuple-element.43) | copy-start | bytes 1572868
  84.8 9.2 %collective-permute-start.11 = (bf16[2,128,512]{2,1,0:T(8,128)(2,1)}, bf16[2,128,512]{2,1,0:T(8,128)(2,1)S(1)}, u32[]{:S(2)}, u32[]{:S(2)}) collective-permute-start(bf16[2,128,512]{2,1,0:T(8,128)(2,1)} %get-tuple-element.45), channel_id=1, source_target_pairs={{0,2},{2,4},{4,6},{6,8},{8,10},{10,12},{12,14},{14,0},{1,3},{3,5},... | collective-permute-start | bytes 786440 | tf_op jit(solution)/shard_map/ppermute | solution.py:330
  86.9 15.0 %collective-permute-start.15 = (bf16[2,128,512]{2,1,0:T(8,128)(2,1)}, bf16[2,128,512]{2,1,0:T(8,128)(2,1)S(1)}, u32[]{:S(2)}, u32[]{:S(2)}) collective-permute-start(bf16[2,128,512]{2,1,0:T(8,128)(2,1)} %get-tuple-element.50), channel_id=1, source_target_pairs={{0,14},{2,0},{4,2},{6,4},{8,6},{10,8},{12,10},{14,12},{1,15},{3,1}... | collective-permute-start | bytes 786440 | tf_op jit(solution)/shard_map/ppermute | solution.py:330
  95.1 11.7 %collective-permute-start.12 = (bf16[2,128,512]{2,1,0:T(8,128)(2,1)S(1)}, bf16[2,128,512]{2,1,0:T(8,128)(2,1)S(1)}, u32[]{:S(2)}, u32[]{:S(2)}) collective-permute-start(bf16[2,128,512]{2,1,0:T(8,128)(2,1)S(1)} %add_convert_fusion.5), channel_id=1, source_target_pairs={{0,2},{2,4},{4,6},{6,8},{8,10},{10,12},{12,14},{14,0},{1,3},{3,5},... | collective-permute-start | bytes 786440 | tf_op jit(solution)/shard_map/ppermute | solution.py:330
  97.0 45.0 %collective-permute-start.10 = (bf16[2,128,512]{2,1,0:T(8,128)(2,1)S(1)}, bf16[2,128,512]{2,1,0:T(8,128)(2,1)S(1)}, u32[]{:S(2)}, u32[]{:S(2)}) collective-permute-start(bf16[2,128,512]{2,1,0:T(8,128)(2,1)S(1)} %copy-done.18), channel_id=1, source_target_pairs={{0,1},{1,0},{2,3},{3,2},{4,5},{5,4},{6,7},{7,6},{8,9},{9,8},{10,11... | collective-permute-start | bytes 786440 | tf_op jit(solution)/shard_map/ppermute | solution.py:341
  102.0 16.5 %collective-permute-start.16 = (bf16[2,128,512]{2,1,0:T(8,128)(2,1)S(1)}, bf16[2,128,512]{2,1,0:T(8,128)(2,1)S(1)}, u32[]{:S(2)}, u32[]{:S(2)}) collective-permute-start(bf16[2,128,512]{2,1,0:T(8,128)(2,1)S(1)} %add_convert_fusion.2), channel_id=1, source_target_pairs={{0,14},{2,0},{4,2},{6,4},{8,6},{10,8},{12,10},{14,12},{1,15},{3,1}... | collective-permute-start | bytes 786440 | tf_op jit(solution)/shard_map/ppermute | solution.py:330
  106.9 16.4 %collective-permute-start.13 = (bf16[2,128,512]{2,1,0:T(8,128)(2,1)S(1)}, bf16[2,128,512]{2,1,0:T(8,128)(2,1)S(1)}, u32[]{:S(2)}, u32[]{:S(2)}) collective-permute-start(bf16[2,128,512]{2,1,0:T(8,128)(2,1)S(1)} %add_convert_fusion.4), channel_id=1, source_target_pairs={{0,2},{2,4},{4,6},{6,8},{8,10},{10,12},{12,14},{14,0},{1,3},{3,5},... | collective-permute-start | bytes 786440 | tf_op jit(solution)/shard_map/ppermute | solution.py:330
  108.9 18.7 %all-to-all-start.1 = ((bf16[32,16,128]{2,1,0:T(8,128)(2,1)}), bf16[32,16,128]{2,1,0:T(8,128)(2,1)S(1)}, u32[]{:S(2)}, u32[]{:S(2)}) async-start(bf16[32,16,128]{2,1,0:T(8,128)(2,1)} %get-tuple-element.53), calls=%async_computation.1 | async-start | bytes 262144 | tf_op jit(solution)/shard_map/all_to_all | solution.py:333
  118.5 24.7 %copy-start.3 = (f32[2,128,512]{2,1,0:T(8,128)S(1)}, f32[2,128,512]{2,1,0:T(8,128)}, u32[]{:S(2)}) copy-start(f32[2,128,512]{2,1,0:T(8,128)} %get-tuple-element.54) | copy-start | bytes 1572868
  118.6 12.3 %collective-permute-start.17 = (bf16[2,128,512]{2,1,0:T(8,128)(2,1)S(1)}, bf16[2,128,512]{2,1,0:T(8,128)(2,1)S(1)}, u32[]{:S(2)}, u32[]{:S(2)}) collective-permute-start(bf16[2,128,512]{2,1,0:T(8,128)(2,1)S(1)} %add_convert_fusion.1), channel_id=1, source_target_pairs={{0,14},{2,0},{4,2},{6,4},{8,6},{10,8},{12,10},{14,12},{1,15},{3,1}... | collective-permute-start | bytes 786440 | tf_op jit(solution)/shard_map/ppermute | solution.py:330
  123.4 11.3 %collective-permute-start.14 = (bf16[2,128,512]{2,1,0:T(8,128)(2,1)S(1)}, bf16[2,128,512]{2,1,0:T(8,128)(2,1)S(1)}, u32[]{:S(2)}, u32[]{:S(2)}) collective-permute-start(bf16[2,128,512]{2,1,0:T(8,128)(2,1)S(1)} %add_convert_fusion.3), channel_id=1, source_target_pairs={{0,2},{2,4},{4,6},{6,8},{8,10},{10,12},{12,14},{14,0},{1,3},{3,5},... | collective-permute-start | bytes 786440 | tf_op jit(solution)/shard_map/ppermute | solution.py:330
  134.8 8.3 %collective-permute-start.18 = (bf16[2,128,512]{2,1,0:T(8,128)(2,1)S(1)}, bf16[2,128,512]{2,1,0:T(8,128)(2,1)S(1)}, u32[]{:S(2)}, u32[]{:S(2)}) collective-permute-start(bf16[2,128,512]{2,1,0:T(8,128)(2,1)S(1)} %add_convert_fusion), channel_id=1, source_target_pairs={{0,1},{1,0},{2,3},{3,2},{4,5},{5,4},{6,7},{7,6},{8,9},{9,8},{10,11... | collective-permute-start | bytes 786440 | tf_op jit(solution)/shard_map/ppermute | solution.py:350
Sparse Core Ops, SparseCore 0:
  20.0 50.9 all-gather.2
  84.9 49.7 reduce-scatter.1

commit v10 on v9

--- a/solution.py
+++ b/solution.py
@@ -273,7 +273,7 @@
 
 UP = [(i, (i + 1) % NY) for i in range(NY)]
 DOWN = [(i, (i - 1) % NY) for i in range(NY)]
-ROW_STEP, BACK_STEP = 1, 2
+ROW_STEP, BACK_STEP = 2, 2
 SWAP = [(0, 1), (1, 0)]
 
 

time: 153 us -> 156 us (1.020)
  waiting for transfers between devices: 25.4 us -> 29.5 us
    ppermute x14, waiting for transfers between devices: 21.5 us -> 25.8 us  [per_device(): held[i] = move(held[i])]
    ppermute x1, starting transfers between devices: 7.18 us -> 4.17 us  [per_device(): peer_grad = swap(peer_grad)]
    ppermute x14, starting transfers between devices: 44.4 us -> 41.4 us  [per_device(): held[i] = move(held[i])]
    ppermute x1, starting transfers between devices: 2.48 us -> 4.89 us  [per_device(): far_peer = swap(far_blocks)]
    ppermute x1, starting transfers between devices: 4.83 us -> 6.98 us  [per_device(): res_back = swap(res_peer)]
where the time goes in v10:
time: 156 us; the launch traced here: 155 us
  starting transfers between devices  87.7 us (56%)
  waiting for transfers between devices  29.5 us (19%)
  Pallas kernels  15.6 us (10%)
  between operations  14.7 us (9%)
  other arithmetic  5.01 us (3%)
  local copies, waits for them, and re-layouts  2.86 us (2%)
    ppermute x14, starting transfers between devices, per_device(): held[i] = move(held[i])  41.4 us
    ppermute x14, waiting for transfers between devices, per_device(): held[i] = move(held[i])  25.8 us
    pallas_call x1, Pallas kernels, attend(): pl.pallas_call(attend_kernel, out_shape=[piece, piece, jax.ShapeDtypeStru...  11.8 us
    all_to_all x1, starting transfers between devices, per_device(): gback = lax.all_to_all(gglob, ('x', 'z'), 0, 0, tiled=True)  9.68 us
    ppermute x1, starting transfers between devices, per_device(): kv_peer = swap(kv_send)  8.77 us
    all_to_all x1, starting transfers between devices, per_device(): lax.all_to_all(jnp.broadcast_to(row, (WINDOWS, GROWS, HEAD_DIM)), ('x', '...  8.04 us
    ppermute x1, starting transfers between devices, per_device(): res_back = swap(res_peer)  6.98 us
    ppermute x1, starting transfers between devices, per_device(): far_peer = swap(far_blocks)  4.89 us
  transfers between devices with their start and end apart: 23, of which 10 were waited for; matrix products, arithmetic and copies ran while one was open for 3% of the time, Pallas kernels for 1%

profile of v10, /device:TPU:1, one launch (start us, length us, event | category | flops | bytes accessed | tf_op | source)
XLA Modules:
  0.0 155.4 jit_solution(9096863386283675256)
XLA Ops:
  7.2 1.9 %shard_map.84 = (bf16[5,128,256]{2,1,0:T(8,128)(2,1)}, bf16[4,128,256]{2,1,0:T(8,128)(2,1)}) custom-call(s32[1]{0:T(128)} %bitcast.1.core, bf16[128,1024]{1,0:T(8,128)(2,1)} %first.2, bf16[128,1024]{1,0:T(8,128)(2,1)} %second.2), custom_call_target="tpu_custom_call" | custom-call | bytes 1000000 | tf_op jit(solution)/shard_map/pallas_call | solution.py:223
  9.1 8.8 %collective-permute-start = (bf16[4,128,256]{2,1,0:T(8,128)(2,1)}, bf16[4,128,256]{2,1,0:T(8,128)(2,1)S(1)}, u32[]{:S(2)}, u32[]{:S(2)}) collective-permute-start(bf16[4,128,256]{2,1,0:T(8,128)(2,1)} %get-tuple-element.31), channel_id=1, source_target_pairs={{0,1},{1,0},{2,3},{3,2},{4,5},{5,4},{6,7},{7,6},{8,9},{9,8},{10,11... | collective-permute-start | bytes 786440 | tf_op jit(solution)/shard_map/ppermute | solution.py:294
  17.9 1.4 collective-permute-done
  19.3 0.6 slice_dynamic-update-slice_fusion
  19.9 1.9 %collective-permute-start.1 = (bf16[3,128,256]{2,1,0:T(8,128)(2,1)S(1)}, bf16[3,128,256]{2,1,0:T(8,128)(2,1)S(1)}, u32[]{:S(2)}, u32[]{:S(2)}) collective-permute-start(bf16[3,128,256]{2,1,0:T(8,128)(2,1)S(1)} %slice.61.refs_7_), channel_id=1, source_target_pairs={{0,2},{2,4},{4,6},{6,8},{8,10},{10,12},{12,14},{14,0},{1,3},{3,5},... | collective-permute-start | bytes 589832 | tf_op jit(solution)/shard_map/ppermute | solution.py:305
  21.9 7.3 %collective-permute-done.1.refs_14_ = bf16[3,128,256]{2,1,0:T(8,128)(2,1)S(1)} collective-permute-done((bf16[3,128,256]{2,1,0:T(8,128)(2,1)S(1)}, bf16[3,128,256]{2,1,0:T(8,128)(2,1)S(1)}, u32[]{:S(2)}, u32[]{:S(2)}) %collective-permute-start.1) | collective-permute-done | bytes 196640 | tf_op jit(solution)/shard_map/ppermute | solution.py:305
  29.2 1.9 %collective-permute-start.2 = (bf16[3,128,256]{2,1,0:T(8,128)(2,1)S(1)}, bf16[3,128,256]{2,1,0:T(8,128)(2,1)S(1)}, u32[]{:S(2)}, u32[]{:S(2)}) collective-permute-start(bf16[3,128,256]{2,1,0:T(8,128)(2,1)S(1)} %collective-permute-done.1.refs_14_), channel_id=1, source_target_pairs={{0,2},{2,4},{4,6},{6,8},{8,10},{10,12},{12,14},{14,0},{1,3},{3,5},... | collective-permute-start | bytes 589832 | tf_op jit(solution)/shard_map/ppermute | solution.py:305
  31.1 4.6 %collective-permute-start.6 = (bf16[3,128,256]{2,1,0:T(8,128)(2,1)S(1)}, bf16[3,128,256]{2,1,0:T(8,128)(2,1)S(1)}, u32[]{:S(2)}, u32[]{:S(2)}) collective-permute-start(bf16[3,128,256]{2,1,0:T(8,128)(2,1)S(1)} %slice.61.refs_7_), channel_id=1, source_target_pairs={{0,14},{2,0},{4,2},{6,4},{8,6},{10,8},{12,10},{14,12},{1,15},{3,1}... | collective-permute-start | bytes 589832 | tf_op jit(solution)/shard_map/ppermute | solution.py:305
  35.7 1.9 %shard_map.85 = (bf16[2,128,512]{2,1,0:T(8,128)(2,1)}, bf16[2,128,512]{2,1,0:T(8,128)(2,1)}) custom-call(s32[1]{0:T(128)} %bitcast.1.core, bf16[128,1024]{1,0:T(8,128)(2,1)} %first.3, bf16[128,1024]{1,0:T(8,128)(2,1)} %second.3), custom_call_target="tpu_custom_call" | custom-call | bytes 1000000 | tf_op jit(solution)/shard_map/pallas_call | solution.py:223
  37.5 3.7 %collective-permute-start.3 = (bf16[2,128,512]{2,1,0:T(8,128)(2,1)}, bf16[2,128,512]{2,1,0:T(8,128)(2,1)S(1)}, u32[]{:S(2)}, u32[]{:S(2)}) collective-permute-start(bf16[2,128,512]{2,1,0:T(8,128)(2,1)} %get-tuple-element.33), channel_id=1, source_target_pairs={{0,1},{1,0},{2,3},{3,2},{4,5},{5,4},{6,7},{7,6},{8,9},{9,8},{10,11... | collective-permute-start | bytes 786440 | tf_op jit(solution)/shard_map/ppermute | solution.py:311
  41.2 0.7 slice.59
  42.0 0.7 broadcast_in_dim.40
  42.7 8.0 %all-to-all-start = ((bf16[32,16,128]{2,1,0:T(8,128)(2,1)}), bf16[32,16,128]{2,1,0:T(8,128)(2,1)S(1)}, u32[]{:S(2)}, u32[]{:S(2)}) async-start(bf16[32,16,128]{2,1,0:T(8,128)(2,1)} %broadcast_in_dim.40), calls=%async_computation | async-start | bytes 262144 | tf_op jit(solution)/shard_map/all_to_all | solution.py:308
  50.8 2.2 %collective-permute-start.7 = (bf16[3,128,256]{2,1,0:T(8,128)(2,1)S(1)}, bf16[3,128,256]{2,1,0:T(8,128)(2,1)S(1)}, u32[]{:S(2)}, u32[]{:S(2)}) collective-permute-start(bf16[3,128,256]{2,1,0:T(8,128)(2,1)S(1)} %collective-permute-done.6.refs_8_), channel_id=1, source_target_pairs={{0,14},{2,0},{4,2},{6,4},{8,6},{10,8},{12,10},{14,12},{1,15},{3,1}... | collective-permute-start | bytes 589832 | tf_op jit(solution)/shard_map/ppermute | solution.py:305
  53.0 3.1 %collective-permute-start.5 = (bf16[3,128,256]{2,1,0:T(8,128)(2,1)S(1)}, bf16[3,128,256]{2,1,0:T(8,128)(2,1)S(1)}, u32[]{:S(2)}, u32[]{:S(2)}) collective-permute-start(bf16[3,128,256]{2,1,0:T(8,128)(2,1)S(1)} %collective-permute-done.2.refs_13_), channel_id=1, source_target_pairs={{0,2},{2,4},{4,6},{6,8},{8,10},{10,12},{12,14},{14,0},{1,3},{3,5},... | collective-permute-start | bytes 589832 | tf_op jit(solution)/shard_map/ppermute | solution.py:305
  56.1 4.9 %collective-permute-start.4 = (s32[2,8]{1,0:T(2,128)}, s32[2,8]{1,0:T(2,128)S(1)}, u32[]{:S(2)}, u32[]{:S(2)}) collective-permute-start(s32[2,8]{1,0:T(2,128)} %refs_1_.1), channel_id=1, source_target_pairs={{0,1},{1,0},{2,3},{3,2},{4,5},{5,4},{6,7},{7,6},{8,9},{9,8},{10,11... | collective-permute-start | bytes 200 | tf_op jit(solution)/shard_map/ppermute | solution.py:312
  61.0 1.7 %collective-permute-done.7.refs_9_ = bf16[3,128,256]{2,1,0:T(8,128)(2,1)S(1)} collective-permute-done((bf16[3,128,256]{2,1,0:T(8,128)(2,1)S(1)}, bf16[3,128,256]{2,1,0:T(8,128)(2,1)S(1)}, u32[]{:S(2)}, u32[]{:S(2)}) %collective-permute-start.7) | collective-permute-done | bytes 196640 | tf_op jit(solution)/shard_map/ppermute | solution.py:305
  62.7 3.6 %collective-permute-start.8 = (bf16[3,128,256]{2,1,0:T(8,128)(2,1)S(1)}, bf16[3,128,256]{2,1,0:T(8,128)(2,1)S(1)}, u32[]{:S(2)}, u32[]{:S(2)}) collective-permute-start(bf16[3,128,256]{2,1,0:T(8,128)(2,1)S(1)} %collective-permute-done.7.refs_9_), channel_id=1, source_target_pairs={{0,14},{2,0},{4,2},{6,4},{8,6},{10,8},{12,10},{14,12},{1,15},{3,1}... | collective-permute-start | bytes 589832 | tf_op jit(solution)/shard_map/ppermute | solution.py:305
  66.5 1.9 %collective-permute-start.9 = (bf16[3,128,256]{2,1,0:T(8,128)(2,1)S(1)}, bf16[3,128,256]{2,1,0:T(8,128)(2,1)S(1)}, u32[]{:S(2)}, u32[]{:S(2)}) collective-permute-start(bf16[3,128,256]{2,1,0:T(8,128)(2,1)S(1)} %collective-permute-done.5.refs_12_), channel_id=1, source_target_pairs={{0,2},{2,4},{4,6},{6,8},{8,10},{10,12},{12,14},{14,0},{1,3},{3,5},... | collective-permute-start | bytes 589832 | tf_op jit(solution)/shard_map/ppermute | solution.py:305
  68.4 0.6 pad_add_fusion.refs_0_
  69.0 1.0 collective-permute-done.8.refs_10_
  70.0 4.1 %collective-permute-done.9.refs_11_ = bf16[3,128,256]{2,1,0:T(8,128)(2,1)S(1)} collective-permute-done((bf16[3,128,256]{2,1,0:T(8,128)(2,1)S(1)}, bf16[3,128,256]{2,1,0:T(8,128)(2,1)S(1)}, u32[]{:S(2)}, u32[]{:S(2)}) %collective-permute-start.9) | collective-permute-done | bytes 196640 | tf_op jit(solution)/shard_map/ppermute | solution.py:305
  74.2 0.6 copy-done.16
  74.8 11.8 %shard_map.86 = (bf16[2,128,512]{2,1,0:T(8,128)(2,1)}, bf16[2,128,512]{2,1,0:T(8,128)(2,1)}, f32[2,128,512]{2,1,0:T(8,128)}, f32[2,128,512]{2,1,0:T(8,128)}, bf1...) custom-call(s32[3]{0:T(128)} %pad_add_fusion.refs_0_, ...), custom_call_target="tpu_custom_call" | custom-call | flops 1200000000 | bytes 12000000 | tf_op jit(solution)/shard_map/pallas_call | solution.py:240
  86.7 2.1 %collective-permute-start.11 = (bf16[2,128,512]{2,1,0:T(8,128)(2,1)}, bf16[2,128,512]{2,1,0:T(8,128)(2,1)S(1)}, u32[]{:S(2)}, u32[]{:S(2)}) collective-permute-start(bf16[2,128,512]{2,1,0:T(8,128)(2,1)} %get-tuple-element.45), channel_id=1, source_target_pairs={{0,2},{2,4},{4,6},{6,8},{8,10},{10,12},{12,14},{14,0},{1,3},{3,5},... | collective-permute-start | bytes 786440 | tf_op jit(solution)/shard_map/ppermute | solution.py:330
  88.8 4.6 %collective-permute-start.15 = (bf16[2,128,512]{2,1,0:T(8,128)(2,1)}, bf16[2,128,512]{2,1,0:T(8,128)(2,1)S(1)}, u32[]{:S(2)}, u32[]{:S(2)}) collective-permute-start(bf16[2,128,512]{2,1,0:T(8,128)(2,1)} %get-tuple-element.50), channel_id=1, source_target_pairs={{0,14},{2,0},{4,2},{6,4},{8,6},{10,8},{12,10},{14,12},{1,15},{3,1}... | collective-permute-start | bytes 786440 | tf_op jit(solution)/shard_map/ppermute | solution.py:330
  93.3 2.0 %collective-permute-done.11 = bf16[2,128,512]{2,1,0:T(8,128)(2,1)S(1)} collective-permute-done((bf16[2,128,512]{2,1,0:T(8,128)(2,1)}, bf16[2,128,512]{2,1,0:T(8,128)(2,1)S(1)}, u32[]{:S(2)}, u32[]{:S(2)}) %collective-permute-start.11) | collective-permute-done | bytes 262176 | tf_op jit(solution)/shard_map/ppermute | solution.py:330
  95.4 1.0 add_convert_fusion.5
  96.4 1.9 %collective-permute-start.12 = (bf16[2,128,512]{2,1,0:T(8,128)(2,1)S(1)}, bf16[2,128,512]{2,1,0:T(8,128)(2,1)S(1)}, u32[]{:S(2)}, u32[]{:S(2)}) collective-permute-start(bf16[2,128,512]{2,1,0:T(8,128)(2,1)S(1)} %add_convert_fusion.5), channel_id=1, source_target_pairs={{0,2},{2,4},{4,6},{6,8},{8,10},{10,12},{12,14},{14,0},{1,3},{3,5},... | collective-permute-start | bytes 786440 | tf_op jit(solution)/shard_map/ppermute | solution.py:330
  98.4 7.0 %collective-permute-start.10 = (bf16[2,128,512]{2,1,0:T(8,128)(2,1)S(1)}, bf16[2,128,512]{2,1,0:T(8,128)(2,1)S(1)}, u32[]{:S(2)}, u32[]{:S(2)}) collective-permute-start(bf16[2,128,512]{2,1,0:T(8,128)(2,1)S(1)} %copy-done.18), channel_id=1, source_target_pairs={{0,1},{1,0},{2,3},{3,2},{4,5},{5,4},{6,7},{7,6},{8,9},{9,8},{10,11... | collective-permute-start | bytes 786440 | tf_op jit(solution)/shard_map/ppermute | solution.py:341
  105.4 0.1 add_convert_fusion.2
  105.4 4.9 %collective-permute-start.16 = (bf16[2,128,512]{2,1,0:T(8,128)(2,1)S(1)}, bf16[2,128,512]{2,1,0:T(8,128)(2,1)S(1)}, u32[]{:S(2)}, u32[]{:S(2)}) collective-permute-start(bf16[2,128,512]{2,1,0:T(8,128)(2,1)S(1)} %add_convert_fusion.2), channel_id=1, source_target_pairs={{0,14},{2,0},{4,2},{6,4},{8,6},{10,8},{12,10},{14,12},{1,15},{3,1}... | collective-permute-start | bytes 786440 | tf_op jit(solution)/shard_map/ppermute | solution.py:330
  110.3 0.1 add_convert_fusion.4
  110.4 1.9 %collective-permute-start.13 = (bf16[2,128,512]{2,1,0:T(8,128)(2,1)S(1)}, bf16[2,128,512]{2,1,0:T(8,128)(2,1)S(1)}, u32[]{:S(2)}, u32[]{:S(2)}) collective-permute-start(bf16[2,128,512]{2,1,0:T(8,128)(2,1)S(1)} %add_convert_fusion.4), channel_id=1, source_target_pairs={{0,2},{2,4},{4,6},{6,8},{8,10},{10,12},{12,14},{14,0},{1,3},{3,5},... | collective-permute-start | bytes 786440 | tf_op jit(solution)/shard_map/ppermute | solution.py:330
  112.4 9.7 %all-to-all-start.1 = ((bf16[32,16,128]{2,1,0:T(8,128)(2,1)}), bf16[32,16,128]{2,1,0:T(8,128)(2,1)S(1)}, u32[]{:S(2)}, u32[]{:S(2)}) async-start(bf16[32,16,128]{2,1,0:T(8,128)(2,1)} %get-tuple-element.53), calls=%async_computation.1 | async-start | bytes 262144 | tf_op jit(solution)/shard_map/all_to_all | solution.py:333
  122.1 0.1 add_convert_fusion.1
  122.1 5.0 %collective-permute-start.17 = (bf16[2,128,512]{2,1,0:T(8,128)(2,1)S(1)}, bf16[2,128,512]{2,1,0:T(8,128)(2,1)S(1)}, u32[]{:S(2)}, u32[]{:S(2)}) collective-permute-start(bf16[2,128,512]{2,1,0:T(8,128)(2,1)S(1)} %add_convert_fusion.1), channel_id=1, source_target_pairs={{0,14},{2,0},{4,2},{6,4},{8,6},{10,8},{12,10},{14,12},{1,15},{3,1}... | collective-permute-start | bytes 786440 | tf_op jit(solution)/shard_map/ppermute | solution.py:330
  127.1 0.1 add_convert_fusion.3
  127.2 1.9 %collective-permute-start.14 = (bf16[2,128,512]{2,1,0:T(8,128)(2,1)S(1)}, bf16[2,128,512]{2,1,0:T(8,128)(2,1)S(1)}, u32[]{:S(2)}, u32[]{:S(2)}) collective-permute-start(bf16[2,128,512]{2,1,0:T(8,128)(2,1)S(1)} %add_convert_fusion.3), channel_id=1, source_target_pairs={{0,2},{2,4},{4,6},{6,8},{8,10},{10,12},{12,14},{14,0},{1,3},{3,5},... | collective-permute-start | bytes 786440 | tf_op jit(solution)/shard_map/ppermute | solution.py:330
  129.1 2.1 %all-to-all-done.1 = bf16[32,16,128]{2,1,0:T(8,128)(2,1)S(1)} async-done(((bf16[32,16,128]{2,1,0:T(8,128)(2,1)}), bf16[32,16,128]{2,1,0:T(8,128)(2,1)S(1)}, u32[]{:S(2)}, u32[]{:S(2)}) %all-to-all-start.1) | async-done | bytes 131104 | tf_op jit(solution)/shard_map/all_to_all | solution.py:333
  131.3 5.7 %collective-permute-done.17 = bf16[2,128,512]{2,1,0:T(8,128)(2,1)S(1)} collective-permute-done((bf16[2,128,512]{2,1,0:T(8,128)(2,1)S(1)}, bf16[2,128,512]{2,1,0:T(8,128)(2,1)S(1)}, u32[]{:S(2)}, u32[]{:S(2)}) %collective-permute-start.17) | collective-permute-done | bytes 262176 | tf_op jit(solution)/shard_map/ppermute | solution.py:330
  137.0 4.0 %collective-permute-done.14 = bf16[2,128,512]{2,1,0:T(8,128)(2,1)S(1)} collective-permute-done((bf16[2,128,512]{2,1,0:T(8,128)(2,1)S(1)}, bf16[2,128,512]{2,1,0:T(8,128)(2,1)S(1)}, u32[]{:S(2)}, u32[]{:S(2)}) %collective-permute-start.14) | collective-permute-done | bytes 262176 | tf_op jit(solution)/shard_map/ppermute | solution.py:330
  141.0 0.1 add_convert_fusion
  141.1 4.2 %collective-permute-start.18 = (bf16[2,128,512]{2,1,0:T(8,128)(2,1)S(1)}, bf16[2,128,512]{2,1,0:T(8,128)(2,1)S(1)}, u32[]{:S(2)}, u32[]{:S(2)}) collective-permute-start(bf16[2,128,512]{2,1,0:T(8,128)(2,1)S(1)} %add_convert_fusion), channel_id=1, source_target_pairs={{0,1},{1,0},{2,3},{3,2},{4,5},{5,4},{6,7},{7,6},{8,9},{9,8},{10,11... | collective-permute-start | bytes 786440 | tf_op jit(solution)/shard_map/ppermute | solution.py:350
  145.3 0.9 maximum_select_fusion
  146.3 0.2 collective-permute-done.18
  146.5 1.1 fusion.1
  147.6 0.9 maximum_select_fusion.2
  (69 shorter events, 0.4 us)
Async XLA Ops:
  7.2 66.9 %all-gather.3.cloned.1.call-start = ((), (), s32[]{:S(2)}) async-start(), calls=%async_computation.4 | async-start | bytes 2949120 | tf_op jit(solution)/shard_map/all_gather | solution.py:296
  9.1 10.1 %collective-permute-start = (bf16[4,128,256]{2,1,0:T(8,128)(2,1)}, bf16[4,128,256]{2,1,0:T(8,128)(2,1)S(1)}, u32[]{:S(2)}, u32[]{:S(2)}) collective-permute-start(bf16[4,128,256]{2,1,0:T(8,128)(2,1)} %get-tuple-element.31), channel_id=1, source_target_pairs={{0,1},{1,0},{2,3},{3,2},{4,5},{5,4},{6,7},{7,6},{8,9},{9,8},{10,11... | collective-permute-start | bytes 786440 | tf_op jit(solution)/shard_map/ppermute | solution.py:294
  19.9 54.2 %copy-start = (bf16[3,128,256]{2,1,0:T(8,128)(2,1)}, bf16[3,128,256]{2,1,0:T(8,128)(2,1)S(1)}, u32[]{:S(2)}) copy-start(bf16[3,128,256]{2,1,0:T(8,128)(2,1)S(1)} %slice.61.refs_7_) | copy-start | bytes 589828
  19.9 9.2 %collective-permute-start.1 = (bf16[3,128,256]{2,1,0:T(8,128)(2,1)S(1)}, bf16[3,128,256]{2,1,0:T(8,128)(2,1)S(1)}, u32[]{:S(2)}, u32[]{:S(2)}) collective-permute-start(bf16[3,128,256]{2,1,0:T(8,128)(2,1)S(1)} %slice.61.refs_7_), channel_id=1, source_target_pairs={{0,2},{2,4},{4,6},{6,8},{8,10},{10,12},{12,14},{14,0},{1,3},{3,5},... | collective-permute-start | bytes 589832 | tf_op jit(solution)/shard_map/ppermute | solution.py:305
  29.2 44.9 %copy-start.10 = (bf16[3,128,256]{2,1,0:T(8,128)(2,1)}, bf16[3,128,256]{2,1,0:T(8,128)(2,1)S(1)}, u32[]{:S(2)}) copy-start(bf16[3,128,256]{2,1,0:T(8,128)(2,1)S(1)} %collective-permute-done.1.refs_14_) | copy-start | bytes 589828
  29.2 12.8 %collective-permute-start.2 = (bf16[3,128,256]{2,1,0:T(8,128)(2,1)S(1)}, bf16[3,128,256]{2,1,0:T(8,128)(2,1)S(1)}, u32[]{:S(2)}, u32[]{:S(2)}) collective-permute-start(bf16[3,128,256]{2,1,0:T(8,128)(2,1)S(1)} %collective-permute-done.1.refs_14_), channel_id=1, source_target_pairs={{0,2},{2,4},{4,6},{6,8},{8,10},{10,12},{12,14},{14,0},{1,3},{3,5},... | collective-permute-start | bytes 589832 | tf_op jit(solution)/shard_map/ppermute | solution.py:305
  31.1 19.7 %collective-permute-start.6 = (bf16[3,128,256]{2,1,0:T(8,128)(2,1)S(1)}, bf16[3,128,256]{2,1,0:T(8,128)(2,1)S(1)}, u32[]{:S(2)}, u32[]{:S(2)}) collective-permute-start(bf16[3,128,256]{2,1,0:T(8,128)(2,1)S(1)} %slice.61.refs_7_), channel_id=1, source_target_pairs={{0,14},{2,0},{4,2},{6,4},{8,6},{10,8},{12,10},{14,12},{1,15},{3,1}... | collective-permute-start | bytes 589832 | tf_op jit(solution)/shard_map/ppermute | solution.py:305
  37.5 28.9 %collective-permute-start.3 = (bf16[2,128,512]{2,1,0:T(8,128)(2,1)}, bf16[2,128,512]{2,1,0:T(8,128)(2,1)S(1)}, u32[]{:S(2)}, u32[]{:S(2)}) collective-permute-start(bf16[2,128,512]{2,1,0:T(8,128)(2,1)} %get-tuple-element.33), channel_id=1, source_target_pairs={{0,1},{1,0},{2,3},{3,2},{4,5},{5,4},{6,7},{7,6},{8,9},{9,8},{10,11... | collective-permute-start | bytes 786440 | tf_op jit(solution)/shard_map/ppermute | solution.py:311
  42.0 32.1 %copy-start.11 = (bf16[3,128,256]{2,1,0:T(8,128)(2,1)}, bf16[3,128,256]{2,1,0:T(8,128)(2,1)S(1)}, u32[]{:S(2)}) copy-start(bf16[3,128,256]{2,1,0:T(8,128)(2,1)S(1)} %collective-permute-done.2.refs_13_) | copy-start | bytes 589828
  42.7 23.7 %all-to-all-start = ((bf16[32,16,128]{2,1,0:T(8,128)(2,1)}), bf16[32,16,128]{2,1,0:T(8,128)(2,1)S(1)}, u32[]{:S(2)}, u32[]{:S(2)}) async-start(bf16[32,16,128]{2,1,0:T(8,128)(2,1)} %broadcast_in_dim.40), calls=%async_computation | async-start | bytes 262144 | tf_op jit(solution)/shard_map/all_to_all | solution.py:308
  50.7 95.7 %reduce-scatter.2.cloned.1.call-start = ((), (), s32[]{:S(2)}) async-start(), calls=%async_computation.3 | async-start | bytes 2359296 | tf_op jit(solution)/shard_map/reduce_scatter | solution.py:324
  50.8 23.3 %copy-start.12 = (bf16[3,128,256]{2,1,0:T(8,128)(2,1)}, bf16[3,128,256]{2,1,0:T(8,128)(2,1)S(1)}, u32[]{:S(2)}) copy-start(bf16[3,128,256]{2,1,0:T(8,128)(2,1)S(1)} %collective-permute-done.6.refs_8_) | copy-start | bytes 589828
  50.8 11.9 %collective-permute-start.7 = (bf16[3,128,256]{2,1,0:T(8,128)(2,1)S(1)}, bf16[3,128,256]{2,1,0:T(8,128)(2,1)S(1)}, u32[]{:S(2)}, u32[]{:S(2)}) collective-permute-start(bf16[3,128,256]{2,1,0:T(8,128)(2,1)S(1)} %collective-permute-done.6.refs_8_), channel_id=1, source_target_pairs={{0,14},{2,0},{4,2},{6,4},{8,6},{10,8},{12,10},{14,12},{1,15},{3,1}... | collective-permute-start | bytes 589832 | tf_op jit(solution)/shard_map/ppermute | solution.py:305
  53.0 13.4 %collective-permute-start.5 = (bf16[3,128,256]{2,1,0:T(8,128)(2,1)S(1)}, bf16[3,128,256]{2,1,0:T(8,128)(2,1)S(1)}, u32[]{:S(2)}, u32[]{:S(2)}) collective-permute-start(bf16[3,128,256]{2,1,0:T(8,128)(2,1)S(1)} %collective-permute-done.2.refs_13_), channel_id=1, source_target_pairs={{0,2},{2,4},{4,6},{6,8},{8,10},{10,12},{12,14},{14,0},{1,3},{3,5},... | collective-permute-start | bytes 589832 | tf_op jit(solution)/shard_map/ppermute | solution.py:305
  56.1 10.3 %collective-permute-start.4 = (s32[2,8]{1,0:T(2,128)}, s32[2,8]{1,0:T(2,128)S(1)}, u32[]{:S(2)}, u32[]{:S(2)}) collective-permute-start(s32[2,8]{1,0:T(2,128)} %refs_1_.1), channel_id=1, source_target_pairs={{0,1},{1,0},{2,3},{3,2},{4,5},{5,4},{6,7},{7,6},{8,9},{9,8},{10,11... | collective-permute-start | bytes 200 | tf_op jit(solution)/shard_map/ppermute | solution.py:312
  62.7 11.4 %copy-start.13 = (bf16[3,128,256]{2,1,0:T(8,128)(2,1)}, bf16[3,128,256]{2,1,0:T(8,128)(2,1)S(1)}, u32[]{:S(2)}) copy-start(bf16[3,128,256]{2,1,0:T(8,128)(2,1)S(1)} %collective-permute-done.7.refs_9_) | copy-start | bytes 589828
  62.7 7.3 %collective-permute-start.8 = (bf16[3,128,256]{2,1,0:T(8,128)(2,1)S(1)}, bf16[3,128,256]{2,1,0:T(8,128)(2,1)S(1)}, u32[]{:S(2)}, u32[]{:S(2)}) collective-permute-start(bf16[3,128,256]{2,1,0:T(8,128)(2,1)S(1)} %collective-permute-done.7.refs_9_), channel_id=1, source_target_pairs={{0,14},{2,0},{4,2},{6,4},{8,6},{10,8},{12,10},{14,12},{1,15},{3,1}... | collective-permute-start | bytes 589832 | tf_op jit(solution)/shard_map/ppermute | solution.py:305
  66.4 7.7 %copy-start.17 = (s32[2,8]{1,0:T(2,128)}, s32[2,8]{1,0:T(2,128)S(1)}, u32[]{:S(2)}) copy-start(s32[2,8]{1,0:T(2,128)S(1)} %collective-permute-done.4.refs_2_) | copy-start | bytes 196
  66.4 7.7 %copy-start.4 = (bf16[2,128,512]{2,1,0:T(8,128)(2,1)}, bf16[2,128,512]{2,1,0:T(8,128)(2,1)S(1)}, u32[]{:S(2)}) copy-start(bf16[2,128,512]{2,1,0:T(8,128)(2,1)S(1)} %collective-permute-done.3.refs_4_) | copy-start | bytes 786436
  66.4 7.7 %copy-start.14 = (bf16[3,128,256]{2,1,0:T(8,128)(2,1)}, bf16[3,128,256]{2,1,0:T(8,128)(2,1)S(1)}, u32[]{:S(2)}) copy-start(bf16[3,128,256]{2,1,0:T(8,128)(2,1)S(1)} %collective-permute-done.5.refs_12_) | copy-start | bytes 589828
  66.4 7.7 %copy-start.2 = (bf16[32,16,128]{2,1,0:T(8,128)(2,1)}, bf16[32,16,128]{2,1,0:T(8,128)(2,1)S(1)}, u32[]{:S(2)}) copy-start(bf16[32,16,128]{2,1,0:T(8,128)(2,1)S(1)} %all-to-all-done.refs_5_) | copy-start | bytes 393220
  66.5 7.6 %collective-permute-start.9 = (bf16[3,128,256]{2,1,0:T(8,128)(2,1)S(1)}, bf16[3,128,256]{2,1,0:T(8,128)(2,1)S(1)}, u32[]{:S(2)}, u32[]{:S(2)}) collective-permute-start(bf16[3,128,256]{2,1,0:T(8,128)(2,1)S(1)} %collective-permute-done.5.refs_12_), channel_id=1, source_target_pairs={{0,2},{2,4},{4,6},{6,8},{8,10},{10,12},{12,14},{14,0},{1,3},{3,5},... | collective-permute-start | bytes 589832 | tf_op jit(solution)/shard_map/ppermute | solution.py:305
  70.0 4.1 %copy-start.15 = (bf16[3,128,256]{2,1,0:T(8,128)(2,1)}, bf16[3,128,256]{2,1,0:T(8,128)(2,1)S(1)}, u32[]{:S(2)}) copy-start(bf16[3,128,256]{2,1,0:T(8,128)(2,1)S(1)} %collective-permute-done.8.refs_10_) | copy-start | bytes 589828
  74.1 0.7 copy-start.16
  86.6 11.7 %copy-start.18 = (bf16[2,128,512]{2,1,0:T(8,128)(2,1)S(1)}, bf16[2,128,512]{2,1,0:T(8,128)(2,1)}, u32[]{:S(2)}) copy-start(bf16[2,128,512]{2,1,0:T(8,128)(2,1)} %get-tuple-element.41) | copy-start | bytes 786436
  86.6 18.7 %copy-start.8 = (bf16[2,128,512]{2,1,0:T(8,128)(2,1)S(1)}, bf16[2,128,512]{2,1,0:T(8,128)(2,1)}, u32[]{:S(2)}) copy-start(bf16[2,128,512]{2,1,0:T(8,128)(2,1)} %get-tuple-element.51) | copy-start | bytes 786436
  86.6 23.7 %copy-start.7 = (bf16[2,128,512]{2,1,0:T(8,128)(2,1)S(1)}, bf16[2,128,512]{2,1,0:T(8,128)(2,1)}, u32[]{:S(2)}) copy-start(bf16[2,128,512]{2,1,0:T(8,128)(2,1)} %get-tuple-element.48) | copy-start | bytes 786436
  86.6 25.7 %copy-start.9 = (bf16[2,128,512]{2,1,0:T(8,128)(2,1)S(1)}, bf16[2,128,512]{2,1,0:T(8,128)(2,1)}, u32[]{:S(2)}) copy-start(bf16[2,128,512]{2,1,0:T(8,128)(2,1)} %get-tuple-element.40) | copy-start | bytes 786436
  86.7 35.4 %copy-start.6 = (bf16[2,128,512]{2,1,0:T(8,128)(2,1)S(1)}, bf16[2,128,512]{2,1,0:T(8,128)(2,1)}, u32[]{:S(2)}) copy-start(bf16[2,128,512]{2,1,0:T(8,128)(2,1)} %get-tuple-element.52) | copy-start | bytes 786436
  86.7 40.5 %copy-start.5 = (bf16[2,128,512]{2,1,0:T(8,128)(2,1)S(1)}, bf16[2,128,512]{2,1,0:T(8,128)(2,1)}, u32[]{:S(2)}) copy-start(bf16[2,128,512]{2,1,0:T(8,128)(2,1)} %get-tuple-element.49) | copy-start | bytes 786436
  86.7 54.3 %copy-start.1 = (f32[2,128,512]{2,1,0:T(8,128)S(1)}, f32[2,128,512]{2,1,0:T(8,128)}, u32[]{:S(2)}) copy-start(f32[2,128,512]{2,1,0:T(8,128)} %get-tuple-element.43) | copy-start | bytes 1572868
  86.7 8.7 %collective-permute-start.11 = (bf16[2,128,512]{2,1,0:T(8,128)(2,1)}, bf16[2,128,512]{2,1,0:T(8,128)(2,1)S(1)}, u32[]{:S(2)}, u32[]{:S(2)}) collective-permute-start(bf16[2,128,512]{2,1,0:T(8,128)(2,1)} %get-tuple-element.45), channel_id=1, source_target_pairs={{0,2},{2,4},{4,6},{6,8},{8,10},{10,12},{12,14},{14,0},{1,3},{3,5},... | collective-permute-start | bytes 786440 | tf_op jit(solution)/shard_map/ppermute | solution.py:330
  88.8 16.6 %collective-permute-start.15 = (bf16[2,128,512]{2,1,0:T(8,128)(2,1)}, bf16[2,128,512]{2,1,0:T(8,128)(2,1)S(1)}, u32[]{:S(2)}, u32[]{:S(2)}) collective-permute-start(bf16[2,128,512]{2,1,0:T(8,128)(2,1)} %get-tuple-element.50), channel_id=1, source_target_pairs={{0,14},{2,0},{4,2},{6,4},{8,6},{10,8},{12,10},{14,12},{1,15},{3,1}... | collective-permute-start | bytes 786440 | tf_op jit(solution)/shard_map/ppermute | solution.py:330
  96.4 13.9 %collective-permute-start.12 = (bf16[2,128,512]{2,1,0:T(8,128)(2,1)S(1)}, bf16[2,128,512]{2,1,0:T(8,128)(2,1)S(1)}, u32[]{:S(2)}, u32[]{:S(2)}) collective-permute-start(bf16[2,128,512]{2,1,0:T(8,128)(2,1)S(1)} %add_convert_fusion.5), channel_id=1, source_target_pairs={{0,2},{2,4},{4,6},{6,8},{8,10},{10,12},{12,14},{14,0},{1,3},{3,5},... | collective-permute-start | bytes 786440 | tf_op jit(solution)/shard_map/ppermute | solution.py:330
  98.4 46.9 %collective-permute-start.10 = (bf16[2,128,512]{2,1,0:T(8,128)(2,1)S(1)}, bf16[2,128,512]{2,1,0:T(8,128)(2,1)S(1)}, u32[]{:S(2)}, u32[]{:S(2)}) collective-permute-start(bf16[2,128,512]{2,1,0:T(8,128)(2,1)S(1)} %copy-done.18), channel_id=1, source_target_pairs={{0,1},{1,0},{2,3},{3,2},{4,5},{5,4},{6,7},{7,6},{8,9},{9,8},{10,11... | collective-permute-start | bytes 786440 | tf_op jit(solution)/shard_map/ppermute | solution.py:341
  105.4 16.6 %collective-permute-start.16 = (bf16[2,128,512]{2,1,0:T(8,128)(2,1)S(1)}, bf16[2,128,512]{2,1,0:T(8,128)(2,1)S(1)}, u32[]{:S(2)}, u32[]{:S(2)}) collective-permute-start(bf16[2,128,512]{2,1,0:T(8,128)(2,1)S(1)} %add_convert_fusion.2), channel_id=1, source_target_pairs={{0,14},{2,0},{4,2},{6,4},{8,6},{10,8},{12,10},{14,12},{1,15},{3,1}... | collective-permute-start | bytes 786440 | tf_op jit(solution)/shard_map/ppermute | solution.py:330
  110.4 16.7 %collective-permute-start.13 = (bf16[2,128,512]{2,1,0:T(8,128)(2,1)S(1)}, bf16[2,128,512]{2,1,0:T(8,128)(2,1)S(1)}, u32[]{:S(2)}, u32[]{:S(2)}) collective-permute-start(bf16[2,128,512]{2,1,0:T(8,128)(2,1)S(1)} %add_convert_fusion.4), channel_id=1, source_target_pairs={{0,2},{2,4},{4,6},{6,8},{8,10},{10,12},{12,14},{14,0},{1,3},{3,5},... | collective-permute-start | bytes 786440 | tf_op jit(solution)/shard_map/ppermute | solution.py:330
  112.4 18.9 %all-to-all-start.1 = ((bf16[32,16,128]{2,1,0:T(8,128)(2,1)}), bf16[32,16,128]{2,1,0:T(8,128)(2,1)S(1)}, u32[]{:S(2)}, u32[]{:S(2)}) async-start(bf16[32,16,128]{2,1,0:T(8,128)(2,1)} %get-tuple-element.53), calls=%async_computation.1 | async-start | bytes 262144 | tf_op jit(solution)/shard_map/all_to_all | solution.py:333
  122.0 24.4 %copy-start.3 = (f32[2,128,512]{2,1,0:T(8,128)S(1)}, f32[2,128,512]{2,1,0:T(8,128)}, u32[]{:S(2)}) copy-start(f32[2,128,512]{2,1,0:T(8,128)} %get-tuple-element.54) | copy-start | bytes 1572868
  122.1 14.9 %collective-permute-start.17 = (bf16[2,128,512]{2,1,0:T(8,128)(2,1)S(1)}, bf16[2,128,512]{2,1,0:T(8,128)(2,1)S(1)}, u32[]{:S(2)}, u32[]{:S(2)}) collective-permute-start(bf16[2,128,512]{2,1,0:T(8,128)(2,1)S(1)} %add_convert_fusion.1), channel_id=1, source_target_pairs={{0,14},{2,0},{4,2},{6,4},{8,6},{10,8},{12,10},{14,12},{1,15},{3,1}... | collective-permute-start | bytes 786440 | tf_op jit(solution)/shard_map/ppermute | solution.py:330
  127.2 13.8 %collective-permute-start.14 = (bf16[2,128,512]{2,1,0:T(8,128)(2,1)S(1)}, bf16[2,128,512]{2,1,0:T(8,128)(2,1)S(1)}, u32[]{:S(2)}, u32[]{:S(2)}) collective-permute-start(bf16[2,128,512]{2,1,0:T(8,128)(2,1)S(1)} %add_convert_fusion.3), channel_id=1, source_target_pairs={{0,2},{2,4},{4,6},{6,8},{8,10},{10,12},{12,14},{14,0},{1,3},{3,5},... | collective-permute-start | bytes 786440 | tf_op jit(solution)/shard_map/ppermute | solution.py:330
  141.1 5.3 %collective-permute-start.18 = (bf16[2,128,512]{2,1,0:T(8,128)(2,1)S(1)}, bf16[2,128,512]{2,1,0:T(8,128)(2,1)S(1)}, u32[]{:S(2)}, u32[]{:S(2)}) collective-permute-start(bf16[2,128,512]{2,1,0:T(8,128)(2,1)S(1)} %add_convert_fusion), channel_id=1, source_target_pairs={{0,1},{1,0},{2,3},{3,2},{4,5},{5,4},{6,7},{7,6},{8,9},{9,8},{10,11... | collective-permute-start | bytes 786440 | tf_op jit(solution)/shard_map/ppermute | solution.py:350
Sparse Core Ops, SparseCore 0:
  20.0 47.6 all-gather.2
  86.8 53.0 reduce-scatter.1

commit v11 on v10

--- a/solution.py
+++ b/solution.py
@@ -273,7 +273,7 @@
 
 UP = [(i, (i + 1) % NY) for i in range(NY)]
 DOWN = [(i, (i - 1) % NY) for i in range(NY)]
-ROW_STEP, BACK_STEP = 2, 2
+BACK_STEP = 2
 SWAP = [(0, 1), (1, 0)]
 
 
@@ -303,13 +303,16 @@
         for i, (move, count, sign) in enumerate(chains):
             if step <= count:
                 held[i] = move(held[i])
-        if step == ROW_STEP:
+        if step == 1:
+            row, held[1] = lax.optimization_barrier((row, held[1]))
+            qdo_peer = swap(qdo_send)
+            far_peer = swap(far_blocks)
+        if step == 2:
             row, held[0] = lax.optimization_barrier((row, held[0]))
+            row, held[1] = lax.optimization_barrier((row, held[1]))
             glob = lax.all_to_all(
                 jnp.broadcast_to(row, (WINDOWS, GROWS, HEAD_DIM)), ("x", "z"), 0, 0, tiled=True
             )
-            qdo_peer = swap(qdo_send)
-            far_peer = swap(far_blocks)
         if step == 3:
             glob, qdo_peer, far_peer, held[0] = lax.optimization_barrier(
                 (glob, qdo_peer, far_peer, held[0])

time: 156 us -> 156 us (level)
  waiting for transfers between devices: 29.5 us -> 26.1 us
  starting transfers between devices: 87.7 us -> 90.2 us
    ppermute x14, starting transfers between devices: 41.4 us -> 44.6 us  [per_device(): held[i] = move(held[i])]
    ppermute x14, waiting for transfers between devices: 25.8 us -> 22.9 us  [per_device(): held[i] = move(held[i])]
  transfers between devices with their start and end apart: 23 -> 23, of which waited for: 10 -> 11; matrix products, arithmetic and copies ran while one was open for 3% -> 3% of each run, Pallas kernels for 1% -> 1%
where the time goes in v11:
time: 156 us; the launch traced here: 155 us
  starting transfers between devices  90.2 us (58%)
  waiting for transfers between devices  26.1 us (17%)
  Pallas kernels  15.6 us (10%)
  between operations  14.7 us (9%)
  other arithmetic  5.01 us (3%)
  local copies, waits for them, and re-layouts  2.87 us (2%)
    ppermute x14, starting transfers between devices, per_device(): held[i] = move(held[i])  44.6 us
    ppermute x14, waiting for transfers between devices, per_device(): held[i] = move(held[i])  22.9 us
    pallas_call x1, Pallas kernels, attend(): pl.pallas_call(attend_kernel, out_shape=[piece, piece, jax.ShapeDtypeStru...  11.9 us
    all_to_all x1, starting transfers between devices, per_device(): gback = lax.all_to_all(gglob, ('x', 'z'), 0, 0, tiled=True)  9.25 us
    ppermute x1, starting transfers between devices, per_device(): kv_peer = swap(kv_send)  8.77 us
    all_to_all x1, starting transfers between devices, per_device(): lax.all_to_all(jnp.broadcast_to(row, (WINDOWS, GROWS, HEAD_DIM)), ('x', '...  8.65 us
    ppermute x1, starting transfers between devices, per_device(): res_back = swap(res_peer)  6.38 us
    ppermute x1, starting transfers between devices, per_device(): peer_grad = swap(peer_grad)  4.57 us
  transfers between devices with their start and end apart: 23, of which 11 were waited for; matrix products, arithmetic and copies ran while one was open for 3% of the time, Pallas kernels for 1%

profile of v11, /device:TPU:1, one launch (start us, length us, event | category | flops | bytes accessed | tf_op | source)
XLA Modules:
  0.0 154.5 jit_solution(11896324697854164489)
XLA Ops:
  7.2 1.9 %shard_map.84 = (bf16[5,128,256]{2,1,0:T(8,128)(2,1)}, bf16[4,128,256]{2,1,0:T(8,128)(2,1)}) custom-call(s32[1]{0:T(128)} %bitcast.1.core, bf16[128,1024]{1,0:T(8,128)(2,1)} %first.2, bf16[128,1024]{1,0:T(8,128)(2,1)} %second.2), custom_call_target="tpu_custom_call" | custom-call | bytes 1000000 | tf_op jit(solution)/shard_map/pallas_call | solution.py:223
  9.1 8.8 %collective-permute-start = (bf16[4,128,256]{2,1,0:T(8,128)(2,1)}, bf16[4,128,256]{2,1,0:T(8,128)(2,1)S(1)}, u32[]{:S(2)}, u32[]{:S(2)}) collective-permute-start(bf16[4,128,256]{2,1,0:T(8,128)(2,1)} %get-tuple-element.35), channel_id=1, source_target_pairs={{0,1},{1,0},{2,3},{3,2},{4,5},{5,4},{6,7},{7,6},{8,9},{9,8},{10,11... | collective-permute-start | bytes 786440 | tf_op jit(solution)/shard_map/ppermute | solution.py:294
  17.9 1.4 collective-permute-done
  19.3 0.6 slice_dynamic-update-slice_fusion
  19.9 1.9 %collective-permute-start.2 = (bf16[3,128,256]{2,1,0:T(8,128)(2,1)S(1)}, bf16[3,128,256]{2,1,0:T(8,128)(2,1)S(1)}, u32[]{:S(2)}, u32[]{:S(2)}) collective-permute-start(bf16[3,128,256]{2,1,0:T(8,128)(2,1)S(1)} %slice.61.refs_7_), channel_id=1, source_target_pairs={{0,2},{2,4},{4,6},{6,8},{8,10},{10,12},{12,14},{14,0},{1,3},{3,5},... | collective-permute-start | bytes 589832 | tf_op jit(solution)/shard_map/ppermute | solution.py:305
  21.9 4.6 %collective-permute-start.1 = (bf16[3,128,256]{2,1,0:T(8,128)(2,1)S(1)}, bf16[3,128,256]{2,1,0:T(8,128)(2,1)S(1)}, u32[]{:S(2)}, u32[]{:S(2)}) collective-permute-start(bf16[3,128,256]{2,1,0:T(8,128)(2,1)S(1)} %slice.61.refs_7_), channel_id=1, source_target_pairs={{0,14},{2,0},{4,2},{6,4},{8,6},{10,8},{12,10},{14,12},{1,15},{3,1}... | collective-permute-start | bytes 589832 | tf_op jit(solution)/shard_map/ppermute | solution.py:305
  26.4 0.7 slice.59
  27.2 1.9 %collective-permute-done.2.refs_14_ = bf16[3,128,256]{2,1,0:T(8,128)(2,1)S(1)} collective-permute-done((bf16[3,128,256]{2,1,0:T(8,128)(2,1)S(1)}, bf16[3,128,256]{2,1,0:T(8,128)(2,1)S(1)}, u32[]{:S(2)}, u32[]{:S(2)}) %collective-permute-start.2) | collective-permute-done | bytes 196640 | tf_op jit(solution)/shard_map/ppermute | solution.py:305
  29.2 1.9 %collective-permute-start.3 = (bf16[3,128,256]{2,1,0:T(8,128)(2,1)S(1)}, bf16[3,128,256]{2,1,0:T(8,128)(2,1)S(1)}, u32[]{:S(2)}, u32[]{:S(2)}) collective-permute-start(bf16[3,128,256]{2,1,0:T(8,128)(2,1)S(1)} %collective-permute-done.2.refs_14_), channel_id=1, source_target_pairs={{0,2},{2,4},{4,6},{6,8},{8,10},{10,12},{12,14},{14,0},{1,3},{3,5},... | collective-permute-start | bytes 589832 | tf_op jit(solution)/shard_map/ppermute | solution.py:305
  31.1 4.6 %collective-permute-start.4 = (bf16[3,128,256]{2,1,0:T(8,128)(2,1)S(1)}, bf16[3,128,256]{2,1,0:T(8,128)(2,1)S(1)}, u32[]{:S(2)}, u32[]{:S(2)}) collective-permute-start(bf16[3,128,256]{2,1,0:T(8,128)(2,1)S(1)} %collective-permute-done.1.refs_8_), channel_id=1, source_target_pairs={{0,14},{2,0},{4,2},{6,4},{8,6},{10,8},{12,10},{14,12},{1,15},{3,1}... | collective-permute-start | bytes 589832 | tf_op jit(solution)/shard_map/ppermute | solution.py:305
  35.7 1.9 %shard_map.85 = (bf16[2,128,512]{2,1,0:T(8,128)(2,1)}, bf16[2,128,512]{2,1,0:T(8,128)(2,1)}) custom-call(s32[1]{0:T(128)} %bitcast.1.core, bf16[128,1024]{1,0:T(8,128)(2,1)} %first.3, bf16[128,1024]{1,0:T(8,128)(2,1)} %second.3), custom_call_target="tpu_custom_call" | custom-call | bytes 1000000 | tf_op jit(solution)/shard_map/pallas_call | solution.py:223
  37.5 3.7 %collective-permute-start.5 = (bf16[2,128,512]{2,1,0:T(8,128)(2,1)}, bf16[2,128,512]{2,1,0:T(8,128)(2,1)S(1)}, u32[]{:S(2)}, u32[]{:S(2)}) collective-permute-start(bf16[2,128,512]{2,1,0:T(8,128)(2,1)} %get-tuple-element.40), channel_id=1, source_target_pairs={{0,1},{1,0},{2,3},{3,2},{4,5},{5,4},{6,7},{7,6},{8,9},{9,8},{10,11... | collective-permute-start | bytes 786440 | tf_op jit(solution)/shard_map/ppermute | solution.py:308
  41.2 2.0 %collective-permute-done.4.refs_9_ = bf16[3,128,256]{2,1,0:T(8,128)(2,1)S(1)} collective-permute-done((bf16[3,128,256]{2,1,0:T(8,128)(2,1)S(1)}, bf16[3,128,256]{2,1,0:T(8,128)(2,1)S(1)}, u32[]{:S(2)}, u32[]{:S(2)}) %collective-permute-start.4) | collective-permute-done | bytes 196640 | tf_op jit(solution)/shard_map/ppermute | solution.py:305
  43.3 0.7 broadcast_in_dim.40
  44.0 8.7 %all-to-all-start = ((bf16[32,16,128]{2,1,0:T(8,128)(2,1)}), bf16[32,16,128]{2,1,0:T(8,128)(2,1)S(1)}, u32[]{:S(2)}, u32[]{:S(2)}) async-start(bf16[32,16,128]{2,1,0:T(8,128)(2,1)} %broadcast_in_dim.40), calls=%async_computation | async-start | bytes 262144 | tf_op jit(solution)/shard_map/all_to_all | solution.py:313
  52.7 3.3 %collective-permute-start.7 = (bf16[3,128,256]{2,1,0:T(8,128)(2,1)S(1)}, bf16[3,128,256]{2,1,0:T(8,128)(2,1)S(1)}, u32[]{:S(2)}, u32[]{:S(2)}) collective-permute-start(bf16[3,128,256]{2,1,0:T(8,128)(2,1)S(1)} %collective-permute-done.3.refs_13_), channel_id=1, source_target_pairs={{0,2},{2,4},{4,6},{6,8},{8,10},{10,12},{12,14},{14,0},{1,3},{3,5},... | collective-permute-start | bytes 589832 | tf_op jit(solution)/shard_map/ppermute | solution.py:305
  56.0 4.3 %collective-permute-start.6 = (s32[2,8]{1,0:T(2,128)}, s32[2,8]{1,0:T(2,128)S(1)}, u32[]{:S(2)}, u32[]{:S(2)}) collective-permute-start(s32[2,8]{1,0:T(2,128)} %refs_1_.1), channel_id=1, source_target_pairs={{0,1},{1,0},{2,3},{3,2},{4,5},{5,4},{6,7},{7,6},{8,9},{9,8},{10,11... | collective-permute-start | bytes 200 | tf_op jit(solution)/shard_map/ppermute | solution.py:309
  60.3 3.8 %collective-permute-start.8 = (bf16[3,128,256]{2,1,0:T(8,128)(2,1)S(1)}, bf16[3,128,256]{2,1,0:T(8,128)(2,1)S(1)}, u32[]{:S(2)}, u32[]{:S(2)}) collective-permute-start(bf16[3,128,256]{2,1,0:T(8,128)(2,1)S(1)} %collective-permute-done.4.refs_9_), channel_id=1, source_target_pairs={{0,14},{2,0},{4,2},{6,4},{8,6},{10,8},{12,10},{14,12},{1,15},{3,1}... | collective-permute-start | bytes 589832 | tf_op jit(solution)/shard_map/ppermute | solution.py:305
  64.2 2.4 %collective-permute-done.7.refs_12_ = bf16[3,128,256]{2,1,0:T(8,128)(2,1)S(1)} collective-permute-done((bf16[3,128,256]{2,1,0:T(8,128)(2,1)S(1)}, bf16[3,128,256]{2,1,0:T(8,128)(2,1)S(1)}, u32[]{:S(2)}, u32[]{:S(2)}) %collective-permute-start.7) | collective-permute-done | bytes 196640 | tf_op jit(solution)/shard_map/ppermute | solution.py:305
  66.6 1.9 %collective-permute-start.9 = (bf16[3,128,256]{2,1,0:T(8,128)(2,1)S(1)}, bf16[3,128,256]{2,1,0:T(8,128)(2,1)S(1)}, u32[]{:S(2)}, u32[]{:S(2)}) collective-permute-start(bf16[3,128,256]{2,1,0:T(8,128)(2,1)S(1)} %collective-permute-done.7.refs_12_), channel_id=1, source_target_pairs={{0,2},{2,4},{4,6},{6,8},{8,10},{10,12},{12,14},{14,0},{1,3},{3,5},... | collective-permute-start | bytes 589832 | tf_op jit(solution)/shard_map/ppermute | solution.py:305
  68.5 0.6 pad_add_fusion.refs_0_
  69.2 1.6 %collective-permute-done.8.refs_10_ = bf16[3,128,256]{2,1,0:T(8,128)(2,1)S(1)} collective-permute-done((bf16[3,128,256]{2,1,0:T(8,128)(2,1)S(1)}, bf16[3,128,256]{2,1,0:T(8,128)(2,1)S(1)}, u32[]{:S(2)}, u32[]{:S(2)}) %collective-permute-start.8) | collective-permute-done | bytes 196640 | tf_op jit(solution)/shard_map/ppermute | solution.py:305
  70.7 3.5 %collective-permute-done.9.refs_11_ = bf16[3,128,256]{2,1,0:T(8,128)(2,1)S(1)} collective-permute-done((bf16[3,128,256]{2,1,0:T(8,128)(2,1)S(1)}, bf16[3,128,256]{2,1,0:T(8,128)(2,1)S(1)}, u32[]{:S(2)}, u32[]{:S(2)}) %collective-permute-start.9) | collective-permute-done | bytes 196640 | tf_op jit(solution)/shard_map/ppermute | solution.py:305
  74.3 0.6 copy-done.16
  74.9 11.9 %shard_map.86 = (bf16[2,128,512]{2,1,0:T(8,128)(2,1)}, bf16[2,128,512]{2,1,0:T(8,128)(2,1)}, f32[2,128,512]{2,1,0:T(8,128)}, f32[2,128,512]{2,1,0:T(8,128)}, bf1...) custom-call(s32[3]{0:T(128)} %pad_add_fusion.refs_0_, ...), custom_call_target="tpu_custom_call" | custom-call | flops 1200000000 | bytes 12000000 | tf_op jit(solution)/shard_map/pallas_call | solution.py:240
  86.9 2.1 %collective-permute-start.11 = (bf16[2,128,512]{2,1,0:T(8,128)(2,1)}, bf16[2,128,512]{2,1,0:T(8,128)(2,1)S(1)}, u32[]{:S(2)}, u32[]{:S(2)}) collective-permute-start(bf16[2,128,512]{2,1,0:T(8,128)(2,1)} %get-tuple-element.53), channel_id=1, source_target_pairs={{0,2},{2,4},{4,6},{6,8},{8,10},{10,12},{12,14},{14,0},{1,3},{3,5},... | collective-permute-start | bytes 786440 | tf_op jit(solution)/shard_map/ppermute | solution.py:333
  88.9 4.6 %collective-permute-start.15 = (bf16[2,128,512]{2,1,0:T(8,128)(2,1)}, bf16[2,128,512]{2,1,0:T(8,128)(2,1)S(1)}, u32[]{:S(2)}, u32[]{:S(2)}) collective-permute-start(bf16[2,128,512]{2,1,0:T(8,128)(2,1)} %get-tuple-element.58), channel_id=1, source_target_pairs={{0,14},{2,0},{4,2},{6,4},{8,6},{10,8},{12,10},{14,12},{1,15},{3,1}... | collective-permute-start | bytes 786440 | tf_op jit(solution)/shard_map/ppermute | solution.py:333
  93.5 2.0 %collective-permute-done.11 = bf16[2,128,512]{2,1,0:T(8,128)(2,1)S(1)} collective-permute-done((bf16[2,128,512]{2,1,0:T(8,128)(2,1)}, bf16[2,128,512]{2,1,0:T(8,128)(2,1)S(1)}, u32[]{:S(2)}, u32[]{:S(2)}) %collective-permute-start.11) | collective-permute-done | bytes 262176 | tf_op jit(solution)/shard_map/ppermute | solution.py:333
  95.5 1.0 add_convert_fusion.5
  96.5 1.9 %collective-permute-start.12 = (bf16[2,128,512]{2,1,0:T(8,128)(2,1)S(1)}, bf16[2,128,512]{2,1,0:T(8,128)(2,1)S(1)}, u32[]{:S(2)}, u32[]{:S(2)}) collective-permute-start(bf16[2,128,512]{2,1,0:T(8,128)(2,1)S(1)} %add_convert_fusion.5), channel_id=1, source_target_pairs={{0,2},{2,4},{4,6},{6,8},{8,10},{10,12},{12,14},{14,0},{1,3},{3,5},... | collective-permute-start | bytes 786440 | tf_op jit(solution)/shard_map/ppermute | solution.py:333
  98.5 6.4 %collective-permute-start.10 = (bf16[2,128,512]{2,1,0:T(8,128)(2,1)S(1)}, bf16[2,128,512]{2,1,0:T(8,128)(2,1)S(1)}, u32[]{:S(2)}, u32[]{:S(2)}) collective-permute-start(bf16[2,128,512]{2,1,0:T(8,128)(2,1)S(1)} %copy-done.18), channel_id=1, source_target_pairs={{0,1},{1,0},{2,3},{3,2},{4,5},{5,4},{6,7},{7,6},{8,9},{9,8},{10,11... | collective-permute-start | bytes 786440 | tf_op jit(solution)/shard_map/ppermute | solution.py:344
  104.9 0.1 add_convert_fusion.2
  105.0 4.9 %collective-permute-start.16 = (bf16[2,128,512]{2,1,0:T(8,128)(2,1)S(1)}, bf16[2,128,512]{2,1,0:T(8,128)(2,1)S(1)}, u32[]{:S(2)}, u32[]{:S(2)}) collective-permute-start(bf16[2,128,512]{2,1,0:T(8,128)(2,1)S(1)} %add_convert_fusion.2), channel_id=1, source_target_pairs={{0,14},{2,0},{4,2},{6,4},{8,6},{10,8},{12,10},{14,12},{1,15},{3,1}... | collective-permute-start | bytes 786440 | tf_op jit(solution)/shard_map/ppermute | solution.py:333
  109.9 0.1 add_convert_fusion.4
  109.9 1.9 %collective-permute-start.13 = (bf16[2,128,512]{2,1,0:T(8,128)(2,1)S(1)}, bf16[2,128,512]{2,1,0:T(8,128)(2,1)S(1)}, u32[]{:S(2)}, u32[]{:S(2)}) collective-permute-start(bf16[2,128,512]{2,1,0:T(8,128)(2,1)S(1)} %add_convert_fusion.4), channel_id=1, source_target_pairs={{0,2},{2,4},{4,6},{6,8},{8,10},{10,12},{12,14},{14,0},{1,3},{3,5},... | collective-permute-start | bytes 786440 | tf_op jit(solution)/shard_map/ppermute | solution.py:333
  111.9 9.3 %all-to-all-start.1 = ((bf16[32,16,128]{2,1,0:T(8,128)(2,1)}), bf16[32,16,128]{2,1,0:T(8,128)(2,1)S(1)}, u32[]{:S(2)}, u32[]{:S(2)}) async-start(bf16[32,16,128]{2,1,0:T(8,128)(2,1)} %get-tuple-element.61), calls=%async_computation.1 | async-start | bytes 262144 | tf_op jit(solution)/shard_map/all_to_all | solution.py:336
  121.3 5.3 %collective-permute-start.17 = (bf16[2,128,512]{2,1,0:T(8,128)(2,1)S(1)}, bf16[2,128,512]{2,1,0:T(8,128)(2,1)S(1)}, u32[]{:S(2)}, u32[]{:S(2)}) collective-permute-start(bf16[2,128,512]{2,1,0:T(8,128)(2,1)S(1)} %add_convert_fusion.1), channel_id=1, source_target_pairs={{0,14},{2,0},{4,2},{6,4},{8,6},{10,8},{12,10},{14,12},{1,15},{3,1}... | collective-permute-start | bytes 786440 | tf_op jit(solution)/shard_map/ppermute | solution.py:333
  126.6 0.1 add_convert_fusion.3
  126.7 1.9 %collective-permute-start.14 = (bf16[2,128,512]{2,1,0:T(8,128)(2,1)S(1)}, bf16[2,128,512]{2,1,0:T(8,128)(2,1)S(1)}, u32[]{:S(2)}, u32[]{:S(2)}) collective-permute-start(bf16[2,128,512]{2,1,0:T(8,128)(2,1)S(1)} %add_convert_fusion.3), channel_id=1, source_target_pairs={{0,2},{2,4},{4,6},{6,8},{8,10},{10,12},{12,14},{14,0},{1,3},{3,5},... | collective-permute-start | bytes 786440 | tf_op jit(solution)/shard_map/ppermute | solution.py:333
  128.6 1.7 %all-to-all-done.1 = bf16[32,16,128]{2,1,0:T(8,128)(2,1)S(1)} async-done(((bf16[32,16,128]{2,1,0:T(8,128)(2,1)}), bf16[32,16,128]{2,1,0:T(8,128)(2,1)S(1)}, u32[]{:S(2)}, u32[]{:S(2)}) %all-to-all-start.1) | async-done | bytes 131104 | tf_op jit(solution)/shard_map/all_to_all | solution.py:336
  130.4 6.2 %collective-permute-done.17 = bf16[2,128,512]{2,1,0:T(8,128)(2,1)S(1)} collective-permute-done((bf16[2,128,512]{2,1,0:T(8,128)(2,1)S(1)}, bf16[2,128,512]{2,1,0:T(8,128)(2,1)S(1)}, u32[]{:S(2)}, u32[]{:S(2)}) %collective-permute-start.17) | collective-permute-done | bytes 262176 | tf_op jit(solution)/shard_map/ppermute | solution.py:333
  136.5 3.2 %collective-permute-done.14 = bf16[2,128,512]{2,1,0:T(8,128)(2,1)S(1)} collective-permute-done((bf16[2,128,512]{2,1,0:T(8,128)(2,1)S(1)}, bf16[2,128,512]{2,1,0:T(8,128)(2,1)S(1)}, u32[]{:S(2)}, u32[]{:S(2)}) %collective-permute-start.14) | collective-permute-done | bytes 262176 | tf_op jit(solution)/shard_map/ppermute | solution.py:333
  139.7 0.1 add_convert_fusion
  139.9 4.6 %collective-permute-start.18 = (bf16[2,128,512]{2,1,0:T(8,128)(2,1)S(1)}, bf16[2,128,512]{2,1,0:T(8,128)(2,1)S(1)}, u32[]{:S(2)}, u32[]{:S(2)}) collective-permute-start(bf16[2,128,512]{2,1,0:T(8,128)(2,1)S(1)} %add_convert_fusion), channel_id=1, source_target_pairs={{0,1},{1,0},{2,3},{3,2},{4,5},{5,4},{6,7},{7,6},{8,9},{9,8},{10,11... | collective-permute-start | bytes 786440 | tf_op jit(solution)/shard_map/ppermute | solution.py:353
  144.5 0.9 maximum_select_fusion
  145.4 0.2 collective-permute-done.18
  145.7 1.1 fusion.1
  146.8 0.9 maximum_select_fusion.2
  (69 shorter events, 0.5 us)
Async XLA Ops:
  7.2 67.1 %all-gather.3.cloned.1.call-start = ((), (), s32[]{:S(2)}) async-start(), calls=%async_computation.4 | async-start | bytes 2949120 | tf_op jit(solution)/shard_map/all_gather | solution.py:296
  9.1 10.1 %collective-permute-start = (bf16[4,128,256]{2,1,0:T(8,128)(2,1)}, bf16[4,128,256]{2,1,0:T(8,128)(2,1)S(1)}, u32[]{:S(2)}, u32[]{:S(2)}) collective-permute-start(bf16[4,128,256]{2,1,0:T(8,128)(2,1)} %get-tuple-element.35), channel_id=1, source_target_pairs={{0,1},{1,0},{2,3},{3,2},{4,5},{5,4},{6,7},{7,6},{8,9},{9,8},{10,11... | collective-permute-start | bytes 786440 | tf_op jit(solution)/shard_map/ppermute | solution.py:294
  19.9 54.3 %copy-start = (bf16[3,128,256]{2,1,0:T(8,128)(2,1)}, bf16[3,128,256]{2,1,0:T(8,128)(2,1)S(1)}, u32[]{:S(2)}) copy-start(bf16[3,128,256]{2,1,0:T(8,128)(2,1)S(1)} %slice.61.refs_7_) | copy-start | bytes 589828
  19.9 9.2 %collective-permute-start.2 = (bf16[3,128,256]{2,1,0:T(8,128)(2,1)S(1)}, bf16[3,128,256]{2,1,0:T(8,128)(2,1)S(1)}, u32[]{:S(2)}, u32[]{:S(2)}) collective-permute-start(bf16[3,128,256]{2,1,0:T(8,128)(2,1)S(1)} %slice.61.refs_7_), channel_id=1, source_target_pairs={{0,2},{2,4},{4,6},{6,8},{8,10},{10,12},{12,14},{14,0},{1,3},{3,5},... | collective-permute-start | bytes 589832 | tf_op jit(solution)/shard_map/ppermute | solution.py:305
  21.9 9.2 %collective-permute-start.1 = (bf16[3,128,256]{2,1,0:T(8,128)(2,1)S(1)}, bf16[3,128,256]{2,1,0:T(8,128)(2,1)S(1)}, u32[]{:S(2)}, u32[]{:S(2)}) collective-permute-start(bf16[3,128,256]{2,1,0:T(8,128)(2,1)S(1)} %slice.61.refs_7_), channel_id=1, source_target_pairs={{0,14},{2,0},{4,2},{6,4},{8,6},{10,8},{12,10},{14,12},{1,15},{3,1}... | collective-permute-start | bytes 589832 | tf_op jit(solution)/shard_map/ppermute | solution.py:305
  29.2 45.1 %copy-start.10 = (bf16[3,128,256]{2,1,0:T(8,128)(2,1)}, bf16[3,128,256]{2,1,0:T(8,128)(2,1)S(1)}, u32[]{:S(2)}) copy-start(bf16[3,128,256]{2,1,0:T(8,128)(2,1)S(1)} %collective-permute-done.2.refs_14_) | copy-start | bytes 589828
  29.2 12.0 %collective-permute-start.3 = (bf16[3,128,256]{2,1,0:T(8,128)(2,1)S(1)}, bf16[3,128,256]{2,1,0:T(8,128)(2,1)S(1)}, u32[]{:S(2)}, u32[]{:S(2)}) collective-permute-start(bf16[3,128,256]{2,1,0:T(8,128)(2,1)S(1)} %collective-permute-done.2.refs_14_), channel_id=1, source_target_pairs={{0,2},{2,4},{4,6},{6,8},{8,10},{10,12},{12,14},{14,0},{1,3},{3,5},... | collective-permute-start | bytes 589832 | tf_op jit(solution)/shard_map/ppermute | solution.py:305
  31.1 43.2 %copy-start.11 = (bf16[3,128,256]{2,1,0:T(8,128)(2,1)}, bf16[3,128,256]{2,1,0:T(8,128)(2,1)S(1)}, u32[]{:S(2)}) copy-start(bf16[3,128,256]{2,1,0:T(8,128)(2,1)S(1)} %collective-permute-done.1.refs_8_) | copy-start | bytes 589828
  31.1 12.2 %collective-permute-start.4 = (bf16[3,128,256]{2,1,0:T(8,128)(2,1)S(1)}, bf16[3,128,256]{2,1,0:T(8,128)(2,1)S(1)}, u32[]{:S(2)}, u32[]{:S(2)}) collective-permute-start(bf16[3,128,256]{2,1,0:T(8,128)(2,1)S(1)} %collective-permute-done.1.refs_8_), channel_id=1, source_target_pairs={{0,14},{2,0},{4,2},{6,4},{8,6},{10,8},{12,10},{14,12},{1,15},{3,1}... | collective-permute-start | bytes 589832 | tf_op jit(solution)/shard_map/ppermute | solution.py:305
  37.5 26.6 %collective-permute-start.5 = (bf16[2,128,512]{2,1,0:T(8,128)(2,1)}, bf16[2,128,512]{2,1,0:T(8,128)(2,1)S(1)}, u32[]{:S(2)}, u32[]{:S(2)}) collective-permute-start(bf16[2,128,512]{2,1,0:T(8,128)(2,1)} %get-tuple-element.40), channel_id=1, source_target_pairs={{0,1},{1,0},{2,3},{3,2},{4,5},{5,4},{6,7},{7,6},{8,9},{9,8},{10,11... | collective-permute-start | bytes 786440 | tf_op jit(solution)/shard_map/ppermute | solution.py:308
  41.2 33.0 %copy-start.12 = (bf16[3,128,256]{2,1,0:T(8,128)(2,1)}, bf16[3,128,256]{2,1,0:T(8,128)(2,1)S(1)}, u32[]{:S(2)}) copy-start(bf16[3,128,256]{2,1,0:T(8,128)(2,1)S(1)} %collective-permute-done.3.refs_13_) | copy-start | bytes 589828
  43.3 31.0 %copy-start.13 = (bf16[3,128,256]{2,1,0:T(8,128)(2,1)}, bf16[3,128,256]{2,1,0:T(8,128)(2,1)S(1)}, u32[]{:S(2)}) copy-start(bf16[3,128,256]{2,1,0:T(8,128)(2,1)S(1)} %collective-permute-done.4.refs_9_) | copy-start | bytes 589828
  44.0 22.6 %all-to-all-start = ((bf16[32,16,128]{2,1,0:T(8,128)(2,1)}), bf16[32,16,128]{2,1,0:T(8,128)(2,1)S(1)}, u32[]{:S(2)}, u32[]{:S(2)}) async-start(bf16[32,16,128]{2,1,0:T(8,128)(2,1)} %broadcast_in_dim.40), calls=%async_computation | async-start | bytes 262144 | tf_op jit(solution)/shard_map/all_to_all | solution.py:313
  52.7 93.0 %reduce-scatter.2.cloned.1.call-start = ((), (), s32[]{:S(2)}) async-start(), calls=%async_computation.3 | async-start | bytes 2359296 | tf_op jit(solution)/shard_map/reduce_scatter | solution.py:327
  52.7 13.9 %collective-permute-start.7 = (bf16[3,128,256]{2,1,0:T(8,128)(2,1)S(1)}, bf16[3,128,256]{2,1,0:T(8,128)(2,1)S(1)}, u32[]{:S(2)}, u32[]{:S(2)}) collective-permute-start(bf16[3,128,256]{2,1,0:T(8,128)(2,1)S(1)} %collective-permute-done.3.refs_13_), channel_id=1, source_target_pairs={{0,2},{2,4},{4,6},{6,8},{8,10},{10,12},{12,14},{14,0},{1,3},{3,5},... | collective-permute-start | bytes 589832 | tf_op jit(solution)/shard_map/ppermute | solution.py:305
  56.0 8.2 %collective-permute-start.6 = (s32[2,8]{1,0:T(2,128)}, s32[2,8]{1,0:T(2,128)S(1)}, u32[]{:S(2)}, u32[]{:S(2)}) collective-permute-start(s32[2,8]{1,0:T(2,128)} %refs_1_.1), channel_id=1, source_target_pairs={{0,1},{1,0},{2,3},{3,2},{4,5},{5,4},{6,7},{7,6},{8,9},{9,8},{10,11... | collective-permute-start | bytes 200 | tf_op jit(solution)/shard_map/ppermute | solution.py:309
  60.3 10.5 %collective-permute-start.8 = (bf16[3,128,256]{2,1,0:T(8,128)(2,1)S(1)}, bf16[3,128,256]{2,1,0:T(8,128)(2,1)S(1)}, u32[]{:S(2)}, u32[]{:S(2)}) collective-permute-start(bf16[3,128,256]{2,1,0:T(8,128)(2,1)S(1)} %collective-permute-done.4.refs_9_), channel_id=1, source_target_pairs={{0,14},{2,0},{4,2},{6,4},{8,6},{10,8},{12,10},{14,12},{1,15},{3,1}... | collective-permute-start | bytes 589832 | tf_op jit(solution)/shard_map/ppermute | solution.py:305
  64.1 10.1 %copy-start.17 = (s32[2,8]{1,0:T(2,128)}, s32[2,8]{1,0:T(2,128)S(1)}, u32[]{:S(2)}) copy-start(s32[2,8]{1,0:T(2,128)S(1)} %collective-permute-done.6.refs_2_) | copy-start | bytes 196
  64.2 10.1 %copy-start.4 = (bf16[2,128,512]{2,1,0:T(8,128)(2,1)}, bf16[2,128,512]{2,1,0:T(8,128)(2,1)S(1)}, u32[]{:S(2)}) copy-start(bf16[2,128,512]{2,1,0:T(8,128)(2,1)S(1)} %collective-permute-done.5.refs_4_) | copy-start | bytes 786436
  66.6 7.7 %copy-start.14 = (bf16[3,128,256]{2,1,0:T(8,128)(2,1)}, bf16[3,128,256]{2,1,0:T(8,128)(2,1)S(1)}, u32[]{:S(2)}) copy-start(bf16[3,128,256]{2,1,0:T(8,128)(2,1)S(1)} %collective-permute-done.7.refs_12_) | copy-start | bytes 589828
  66.6 7.7 %copy-start.2 = (bf16[32,16,128]{2,1,0:T(8,128)(2,1)}, bf16[32,16,128]{2,1,0:T(8,128)(2,1)S(1)}, u32[]{:S(2)}) copy-start(bf16[32,16,128]{2,1,0:T(8,128)(2,1)S(1)} %all-to-all-done.refs_5_) | copy-start | bytes 393220
  66.6 7.6 %collective-permute-start.9 = (bf16[3,128,256]{2,1,0:T(8,128)(2,1)S(1)}, bf16[3,128,256]{2,1,0:T(8,128)(2,1)S(1)}, u32[]{:S(2)}, u32[]{:S(2)}) collective-permute-start(bf16[3,128,256]{2,1,0:T(8,128)(2,1)S(1)} %collective-permute-done.7.refs_12_), channel_id=1, source_target_pairs={{0,2},{2,4},{4,6},{6,8},{8,10},{10,12},{12,14},{14,0},{1,3},{3,5},... | collective-permute-start | bytes 589832 | tf_op jit(solution)/shard_map/ppermute | solution.py:305
  70.7 3.6 %copy-start.15 = (bf16[3,128,256]{2,1,0:T(8,128)(2,1)}, bf16[3,128,256]{2,1,0:T(8,128)(2,1)S(1)}, u32[]{:S(2)}) copy-start(bf16[3,128,256]{2,1,0:T(8,128)(2,1)S(1)} %collective-permute-done.8.refs_10_) | copy-start | bytes 589828
  74.2 0.7 copy-start.16
  86.8 11.7 %copy-start.18 = (bf16[2,128,512]{2,1,0:T(8,128)(2,1)S(1)}, bf16[2,128,512]{2,1,0:T(8,128)(2,1)}, u32[]{:S(2)}) copy-start(bf16[2,128,512]{2,1,0:T(8,128)(2,1)} %get-tuple-element.49) | copy-start | bytes 786436
  86.8 18.1 %copy-start.8 = (bf16[2,128,512]{2,1,0:T(8,128)(2,1)S(1)}, bf16[2,128,512]{2,1,0:T(8,128)(2,1)}, u32[]{:S(2)}) copy-start(bf16[2,128,512]{2,1,0:T(8,128)(2,1)} %get-tuple-element.59) | copy-start | bytes 786436
  86.8 23.1 %copy-start.7 = (bf16[2,128,512]{2,1,0:T(8,128)(2,1)S(1)}, bf16[2,128,512]{2,1,0:T(8,128)(2,1)}, u32[]{:S(2)}) copy-start(bf16[2,128,512]{2,1,0:T(8,128)(2,1)} %get-tuple-element.56) | copy-start | bytes 786436
  86.8 25.1 %copy-start.9 = (bf16[2,128,512]{2,1,0:T(8,128)(2,1)S(1)}, bf16[2,128,512]{2,1,0:T(8,128)(2,1)}, u32[]{:S(2)}) copy-start(bf16[2,128,512]{2,1,0:T(8,128)(2,1)} %get-tuple-element.48) | copy-start | bytes 786436
  86.8 34.4 %copy-start.6 = (bf16[2,128,512]{2,1,0:T(8,128)(2,1)S(1)}, bf16[2,128,512]{2,1,0:T(8,128)(2,1)}, u32[]{:S(2)}) copy-start(bf16[2,128,512]{2,1,0:T(8,128)(2,1)} %get-tuple-element.60) | copy-start | bytes 786436
  86.8 39.8 %copy-start.5 = (bf16[2,128,512]{2,1,0:T(8,128)(2,1)S(1)}, bf16[2,128,512]{2,1,0:T(8,128)(2,1)}, u32[]{:S(2)}) copy-start(bf16[2,128,512]{2,1,0:T(8,128)(2,1)} %get-tuple-element.57) | copy-start | bytes 786436
  86.8 52.9 %copy-start.1 = (f32[2,128,512]{2,1,0:T(8,128)S(1)}, f32[2,128,512]{2,1,0:T(8,128)}, u32[]{:S(2)}) copy-start(f32[2,128,512]{2,1,0:T(8,128)} %get-tuple-element.51) | copy-start | bytes 1572868
  86.9 8.7 %collective-permute-start.11 = (bf16[2,128,512]{2,1,0:T(8,128)(2,1)}, bf16[2,128,512]{2,1,0:T(8,128)(2,1)S(1)}, u32[]{:S(2)}, u32[]{:S(2)}) collective-permute-start(bf16[2,128,512]{2,1,0:T(8,128)(2,1)} %get-tuple-element.53), channel_id=1, source_target_pairs={{0,2},{2,4},{4,6},{6,8},{8,10},{10,12},{12,14},{14,0},{1,3},{3,5},... | collective-permute-start | bytes 786440 | tf_op jit(solution)/shard_map/ppermute | solution.py:333
  88.9 16.0 %collective-permute-start.15 = (bf16[2,128,512]{2,1,0:T(8,128)(2,1)}, bf16[2,128,512]{2,1,0:T(8,128)(2,1)S(1)}, u32[]{:S(2)}, u32[]{:S(2)}) collective-permute-start(bf16[2,128,512]{2,1,0:T(8,128)(2,1)} %get-tuple-element.58), channel_id=1, source_target_pairs={{0,14},{2,0},{4,2},{6,4},{8,6},{10,8},{12,10},{14,12},{1,15},{3,1}... | collective-permute-start | bytes 786440 | tf_op jit(solution)/shard_map/ppermute | solution.py:333
  96.5 13.3 %collective-permute-start.12 = (bf16[2,128,512]{2,1,0:T(8,128)(2,1)S(1)}, bf16[2,128,512]{2,1,0:T(8,128)(2,1)S(1)}, u32[]{:S(2)}, u32[]{:S(2)}) collective-permute-start(bf16[2,128,512]{2,1,0:T(8,128)(2,1)S(1)} %add_convert_fusion.5), channel_id=1, source_target_pairs={{0,2},{2,4},{4,6},{6,8},{8,10},{10,12},{12,14},{14,0},{1,3},{3,5},... | collective-permute-start | bytes 786440 | tf_op jit(solution)/shard_map/ppermute | solution.py:333
  98.5 46.0 %collective-permute-start.10 = (bf16[2,128,512]{2,1,0:T(8,128)(2,1)S(1)}, bf16[2,128,512]{2,1,0:T(8,128)(2,1)S(1)}, u32[]{:S(2)}, u32[]{:S(2)}) collective-permute-start(bf16[2,128,512]{2,1,0:T(8,128)(2,1)S(1)} %copy-done.18), channel_id=1, source_target_pairs={{0,1},{1,0},{2,3},{3,2},{4,5},{5,4},{6,7},{7,6},{8,9},{9,8},{10,11... | collective-permute-start | bytes 786440 | tf_op jit(solution)/shard_map/ppermute | solution.py:344
  105.0 16.2 %collective-permute-start.16 = (bf16[2,128,512]{2,1,0:T(8,128)(2,1)S(1)}, bf16[2,128,512]{2,1,0:T(8,128)(2,1)S(1)}, u32[]{:S(2)}, u32[]{:S(2)}) collective-permute-start(bf16[2,128,512]{2,1,0:T(8,128)(2,1)S(1)} %add_convert_fusion.2), channel_id=1, source_target_pairs={{0,14},{2,0},{4,2},{6,4},{8,6},{10,8},{12,10},{14,12},{1,15},{3,1}... | collective-permute-start | bytes 786440 | tf_op jit(solution)/shard_map/ppermute | solution.py:333
  109.9 16.7 %collective-permute-start.13 = (bf16[2,128,512]{2,1,0:T(8,128)(2,1)S(1)}, bf16[2,128,512]{2,1,0:T(8,128)(2,1)S(1)}, u32[]{:S(2)}, u32[]{:S(2)}) collective-permute-start(bf16[2,128,512]{2,1,0:T(8,128)(2,1)S(1)} %add_convert_fusion.4), channel_id=1, source_target_pairs={{0,2},{2,4},{4,6},{6,8},{8,10},{10,12},{12,14},{14,0},{1,3},{3,5},... | collective-permute-start | bytes 786440 | tf_op jit(solution)/shard_map/ppermute | solution.py:333
  111.9 18.4 %all-to-all-start.1 = ((bf16[32,16,128]{2,1,0:T(8,128)(2,1)}), bf16[32,16,128]{2,1,0:T(8,128)(2,1)S(1)}, u32[]{:S(2)}, u32[]{:S(2)}) async-start(bf16[32,16,128]{2,1,0:T(8,128)(2,1)} %get-tuple-element.61), calls=%async_computation.1 | async-start | bytes 262144 | tf_op jit(solution)/shard_map/all_to_all | solution.py:336
  121.2 24.5 %copy-start.3 = (f32[2,128,512]{2,1,0:T(8,128)S(1)}, f32[2,128,512]{2,1,0:T(8,128)}, u32[]{:S(2)}) copy-start(f32[2,128,512]{2,1,0:T(8,128)} %get-tuple-element.62) | copy-start | bytes 1572868
  121.3 15.3 %collective-permute-start.17 = (bf16[2,128,512]{2,1,0:T(8,128)(2,1)S(1)}, bf16[2,128,512]{2,1,0:T(8,128)(2,1)S(1)}, u32[]{:S(2)}, u32[]{:S(2)}) collective-permute-start(bf16[2,128,512]{2,1,0:T(8,128)(2,1)S(1)} %add_convert_fusion.1), channel_id=1, source_target_pairs={{0,14},{2,0},{4,2},{6,4},{8,6},{10,8},{12,10},{14,12},{1,15},{3,1}... | collective-permute-start | bytes 786440 | tf_op jit(solution)/shard_map/ppermute | solution.py:333
  126.7 13.0 %collective-permute-start.14 = (bf16[2,128,512]{2,1,0:T(8,128)(2,1)S(1)}, bf16[2,128,512]{2,1,0:T(8,128)(2,1)S(1)}, u32[]{:S(2)}, u32[]{:S(2)}) collective-permute-start(bf16[2,128,512]{2,1,0:T(8,128)(2,1)S(1)} %add_convert_fusion.3), channel_id=1, source_target_pairs={{0,2},{2,4},{4,6},{6,8},{8,10},{10,12},{12,14},{14,0},{1,3},{3,5},... | collective-permute-start | bytes 786440 | tf_op jit(solution)/shard_map/ppermute | solution.py:333
  139.9 5.7 %collective-permute-start.18 = (bf16[2,128,512]{2,1,0:T(8,128)(2,1)S(1)}, bf16[2,128,512]{2,1,0:T(8,128)(2,1)S(1)}, u32[]{:S(2)}, u32[]{:S(2)}) collective-permute-start(bf16[2,128,512]{2,1,0:T(8,128)(2,1)S(1)} %add_convert_fusion), channel_id=1, source_target_pairs={{0,1},{1,0},{2,3},{3,2},{4,5},{5,4},{6,7},{7,6},{8,9},{9,8},{10,11... | collective-permute-start | bytes 786440 | tf_op jit(solution)/shard_map/ppermute | solution.py:353
Sparse Core Ops, SparseCore 0:
  20.0 47.2 all-gather.2
  87.0 52.2 reduce-scatter.1

commit v12 on v10

--- a/solution.py
+++ b/solution.py
@@ -273,7 +273,7 @@
 
 UP = [(i, (i + 1) % NY) for i in range(NY)]
 DOWN = [(i, (i - 1) % NY) for i in range(NY)]
-ROW_STEP, BACK_STEP = 2, 2
+ROW_STEP, BACK_STEP = 1, 1
 SWAP = [(0, 1), (1, 0)]
 
 
@@ -289,6 +289,12 @@
     up = functools.partial(lax.ppermute, axis_name="y", perm=UP)
     down = functools.partial(lax.ppermute, axis_name="y", perm=DOWN)
     low = my_c == 0
+
+    def home(terms, sign):
+        pairs = [
+            (2 * y + c, (y - sign) % NY * 2 + 1 - c) for y in range(NY) for c in range(NC)
+        ]
+        return lax.ppermute(terms, ("y", "c"), pairs)
 
     kv_own, kv_send = cut(my_c, key_rows, value_rows, PIECE, room=1)
     kv_peer = swap(kv_send)
@@ -321,13 +327,16 @@
     res_own, res_peer, base_own, base_peer, gglob, scattered, *parts = attend(
         pos, far_blocks, far_peer, qdo_own, qdo_peer, glob, gathered, ring
     )
+    base_other = swap(base_peer)
     far_own = (lax.psum_scatter(scattered, "y", scatter_dimension=0),)
     at = [4, 5]
     held = [parts[o - 1] for o in at]
     for step in range(1, 5):
         for i, (move, count, sign) in enumerate(chains):
-            if step <= count:
+            if step < count:
                 held[i] = move(held[i])
+            elif step == count:
+                held[i] = home(held[i], sign)
         if step == BACK_STEP:
             gglob, held[0] = lax.optimization_barrier((gglob, held[0]))
             gback = lax.all_to_all(gglob, ("x", "z"), 0, 0, tiled=True)
@@ -338,6 +347,7 @@
                     held[i] = plus(held[i], parts[at[i] - 1])
     far_peer = held
     gsum = jnp.sum(gback.astype(F32), axis=0).reshape(2, 2, 1, HALF)
+    gsum = gsum[0], swap(gsum[1])
     res_back = swap(res_peer)
     first_row = lax.broadcasted_iota(jnp.int32, (1, TOK, 1), 1) == 0
 
@@ -345,9 +355,7 @@
         total = base + sum(term.astype(F32) for term in far)
         return (total + jnp.where(first_row, gsum[who], 0.0)).astype(BF16)
 
-    peer_grad = finish(base_peer, far_peer, 1)
-    base_own, _ = lax.optimization_barrier((base_own, peer_grad))
-    peer_grad = swap(peer_grad)
+    other_grad = finish(base_other, far_peer, 1)
     own_grad = finish(base_own, far_own, 0)
 
     def join(mine, other):
@@ -360,8 +368,8 @@
     return (
         join(res_own[0], res_back[0]),
         join(res_own[1], res_back[1]),
-        join(own_grad[0], peer_grad[0]),
-        join(own_grad[1], peer_grad[1]),
+        join(own_grad[0], other_grad[0]),
+        join(own_grad[1], other_grad[1]),
     )
 
 

time: 156 us -> 153 us (0.981)
  waiting for transfers between devices: 29.5 us -> 26.2 us
  local copies, waits for them, and re-layouts: 2.86 us -> 4.75 us
  starting transfers between devices: 87.7 us -> 85.9 us
    ppermute x1 -> x4, starting transfers between devices: 4.17 us -> 14.9 us  [the longest x2 7.09 us: home(): return lax.ppermute(terms, ('y', 'c'), pairs)]
    ppermute x14 -> x12, waiting for transfers between devices: 25.8 us -> 15.8 us  [per_device(): held[i] = move(held[i])]
    ppermute x1, starting transfers between devices: 6.98 us -> 1.92 us  [per_device(): res_back = swap(res_peer)]
    all_to_all x1, waiting for transfers between devices: 2.09 us -> 6.15 us  [per_device(): gback = lax.all_to_all(gglob, ('x', 'z'), 0, 0, tiled=True)]
    ppermute x14 -> x12, starting transfers between devices: 41.4 us -> 37.7 us  [per_device(): held[i] = move(held[i])]
    ppermute x1 -> x4, waiting for transfers between devices: 0.16 us -> 2.81 us  [the longest x2 2.8 us: home(): return lax.ppermute(terms, ('y', 'c'), pairs)]
    ppermute x1, starting transfers between devices: 4.89 us -> 2.48 us  [per_device(): far_peer = swap(far_blocks)]
  transfers between devices with their start and end apart: 23 -> 24, of which waited for: 10 -> 8; matrix products, arithmetic and copies ran while one was open for 3% -> 4% of each run, Pallas kernels for 1% -> 1%
where the time goes in v12:
time: 153 us; the launch traced here: 151 us
  starting transfers between devices  85.9 us (56%)
  waiting for transfers between devices  26.2 us (17%)
  Pallas kernels  15.6 us (10%)
  between operations  14.7 us (10%)
  local copies, waits for them, and re-layouts  4.75 us (3%)
  other arithmetic  4.08 us (3%)
    ppermute x12, starting transfers between devices, per_device(): held[i] = move(held[i])  37.7 us
    ppermute x12, waiting for transfers between devices, per_device(): held[i] = move(held[i])  15.8 us
    pallas_call x1, Pallas kernels, attend(): pl.pallas_call(attend_kernel, out_shape=[piece, piece, jax.ShapeDtypeStru...  11.8 us
    all_to_all x1, starting transfers between devices, per_device(): gback = lax.all_to_all(gglob, ('x', 'z'), 0, 0, tiled=True)  8.83 us
    ppermute x1, starting transfers between devices, per_device(): kv_peer = swap(kv_send)  8.77 us
    all_to_all x1, starting transfers between devices, per_device(): lax.all_to_all(jnp.broadcast_to(row, (WINDOWS, GROWS, HEAD_DIM)), ('x', '...  8.04 us
    ppermute x2, starting transfers between devices, home(): return lax.ppermute(terms, ('y', 'c'), pairs)  7.09 us
    all_to_all x1, waiting for transfers between devices, per_device(): gback = lax.all_to_all(gglob, ('x', 'z'), 0, 0, tiled=True)  6.15 us
  transfers between devices with their start and end apart: 24, of which 8 were waited for; matrix products, arithmetic and copies ran while one was open for 4% of the time, Pallas kernels for 1%

profile of v12, /device:TPU:1, one launch (start us, length us, event | category | flops | bytes accessed | tf_op | source)
XLA Modules:
  0.0 151.1 jit_solution(11380517421023749224)
XLA Ops:
  7.2 1.9 %shard_map.84 = (bf16[5,128,256]{2,1,0:T(8,128)(2,1)}, bf16[4,128,256]{2,1,0:T(8,128)(2,1)}) custom-call(s32[1]{0:T(128)} %bitcast.1.core, bf16[128,1024]{1,0:T(8,128)(2,1)} %first.2, bf16[128,1024]{1,0:T(8,128)(2,1)} %second.2), custom_call_target="tpu_custom_call" | custom-call | bytes 1000000 | tf_op jit(solution)/shard_map/pallas_call | solution.py:223
  9.1 8.8 %collective-permute-start = (bf16[4,128,256]{2,1,0:T(8,128)(2,1)}, bf16[4,128,256]{2,1,0:T(8,128)(2,1)S(1)}, u32[]{:S(2)}, u32[]{:S(2)}) collective-permute-start(bf16[4,128,256]{2,1,0:T(8,128)(2,1)} %get-tuple-element.30), channel_id=1, source_target_pairs={{0,1},{1,0},{2,3},{3,2},{4,5},{5,4},{6,7},{7,6},{8,9},{9,8},{10,11... | collective-permute-start | bytes 786440 | tf_op jit(solution)/shard_map/ppermute | solution.py:300
  17.9 1.4 collective-permute-done
  19.3 0.6 slice_dynamic-update-slice_fusion
  19.9 1.9 %collective-permute-start.1 = (bf16[3,128,256]{2,1,0:T(8,128)(2,1)S(1)}, bf16[3,128,256]{2,1,0:T(8,128)(2,1)S(1)}, u32[]{:S(2)}, u32[]{:S(2)}) collective-permute-start(bf16[3,128,256]{2,1,0:T(8,128)(2,1)S(1)} %slice.61.refs_7_), channel_id=1, source_target_pairs={{0,2},{2,4},{4,6},{6,8},{8,10},{10,12},{12,14},{14,0},{1,3},{3,5},... | collective-permute-start | bytes 589832 | tf_op jit(solution)/shard_map/ppermute | solution.py:311
  21.9 0.7 slice.59
  22.6 4.6 %collective-permute-start.6 = (bf16[3,128,256]{2,1,0:T(8,128)(2,1)S(1)}, bf16[3,128,256]{2,1,0:T(8,128)(2,1)S(1)}, u32[]{:S(2)}, u32[]{:S(2)}) collective-permute-start(bf16[3,128,256]{2,1,0:T(8,128)(2,1)S(1)} %slice.61.refs_7_), channel_id=1, source_target_pairs={{0,14},{2,0},{4,2},{6,4},{8,6},{10,8},{12,10},{14,12},{1,15},{3,1}... | collective-permute-start | bytes 589832 | tf_op jit(solution)/shard_map/ppermute | solution.py:311
  27.2 1.9 %collective-permute-done.1.refs_14_ = bf16[3,128,256]{2,1,0:T(8,128)(2,1)S(1)} collective-permute-done((bf16[3,128,256]{2,1,0:T(8,128)(2,1)S(1)}, bf16[3,128,256]{2,1,0:T(8,128)(2,1)S(1)}, u32[]{:S(2)}, u32[]{:S(2)}) %collective-permute-start.1) | collective-permute-done | bytes 196640 | tf_op jit(solution)/shard_map/ppermute | solution.py:311
  29.2 1.9 %collective-permute-start.4 = (bf16[3,128,256]{2,1,0:T(8,128)(2,1)S(1)}, bf16[3,128,256]{2,1,0:T(8,128)(2,1)S(1)}, u32[]{:S(2)}, u32[]{:S(2)}) collective-permute-start(bf16[3,128,256]{2,1,0:T(8,128)(2,1)S(1)} %collective-permute-done.1.refs_14_), channel_id=1, source_target_pairs={{0,2},{2,4},{4,6},{6,8},{8,10},{10,12},{12,14},{14,0},{1,3},{3,5},... | collective-permute-start | bytes 589832 | tf_op jit(solution)/shard_map/ppermute | solution.py:311
  31.1 1.9 %shard_map.85 = (bf16[2,128,512]{2,1,0:T(8,128)(2,1)}, bf16[2,128,512]{2,1,0:T(8,128)(2,1)}) custom-call(s32[1]{0:T(128)} %bitcast.1.core, bf16[128,1024]{1,0:T(8,128)(2,1)} %first.3, bf16[128,1024]{1,0:T(8,128)(2,1)} %second.3), custom_call_target="tpu_custom_call" | custom-call | bytes 1000000 | tf_op jit(solution)/shard_map/pallas_call | solution.py:223
  32.9 3.1 %collective-permute-start.2 = (bf16[2,128,512]{2,1,0:T(8,128)(2,1)}, bf16[2,128,512]{2,1,0:T(8,128)(2,1)S(1)}, u32[]{:S(2)}, u32[]{:S(2)}) collective-permute-start(bf16[2,128,512]{2,1,0:T(8,128)(2,1)} %get-tuple-element.32), channel_id=1, source_target_pairs={{0,1},{1,0},{2,3},{3,2},{4,5},{5,4},{6,7},{7,6},{8,9},{9,8},{10,11... | collective-permute-start | bytes 786440 | tf_op jit(solution)/shard_map/ppermute | solution.py:317
  36.0 0.7 broadcast_in_dim.40
  36.7 8.0 %all-to-all-start = ((bf16[32,16,128]{2,1,0:T(8,128)(2,1)}), bf16[32,16,128]{2,1,0:T(8,128)(2,1)S(1)}, u32[]{:S(2)}, u32[]{:S(2)}) async-start(bf16[32,16,128]{2,1,0:T(8,128)(2,1)} %broadcast_in_dim.40), calls=%async_computation | async-start | bytes 262144 | tf_op jit(solution)/shard_map/all_to_all | solution.py:314
  44.8 4.9 %collective-permute-start.7 = (bf16[3,128,256]{2,1,0:T(8,128)(2,1)S(1)}, bf16[3,128,256]{2,1,0:T(8,128)(2,1)S(1)}, u32[]{:S(2)}, u32[]{:S(2)}) collective-permute-start(bf16[3,128,256]{2,1,0:T(8,128)(2,1)S(1)} %collective-permute-done.6.refs_8_), channel_id=1, source_target_pairs={{0,14},{2,0},{4,2},{6,4},{8,6},{10,8},{12,10},{14,12},{1,15},{3,1}... | collective-permute-start | bytes 589832 | tf_op jit(solution)/shard_map/ppermute | solution.py:311
  49.7 1.9 %collective-permute-start.5 = (bf16[3,128,256]{2,1,0:T(8,128)(2,1)S(1)}, bf16[3,128,256]{2,1,0:T(8,128)(2,1)S(1)}, u32[]{:S(2)}, u32[]{:S(2)}) collective-permute-start(bf16[3,128,256]{2,1,0:T(8,128)(2,1)S(1)} %collective-permute-done.4.refs_13_), channel_id=1, source_target_pairs={{0,2},{2,4},{4,6},{6,8},{8,10},{10,12},{12,14},{14,0},{1,3},{3,5},... | collective-permute-start | bytes 589832 | tf_op jit(solution)/shard_map/ppermute | solution.py:311
  51.7 2.5 %collective-permute-start.3 = (s32[2,8]{1,0:T(2,128)}, s32[2,8]{1,0:T(2,128)S(1)}, u32[]{:S(2)}, u32[]{:S(2)}) collective-permute-start(s32[2,8]{1,0:T(2,128)} %refs_1_.1), channel_id=1, source_target_pairs={{0,1},{1,0},{2,3},{3,2},{4,5},{5,4},{6,7},{7,6},{8,9},{9,8},{10,11... | collective-permute-start | bytes 200 | tf_op jit(solution)/shard_map/ppermute | solution.py:318
  54.1 4.1 %collective-permute-done.7.refs_9_ = bf16[3,128,256]{2,1,0:T(8,128)(2,1)S(1)} collective-permute-done((bf16[3,128,256]{2,1,0:T(8,128)(2,1)S(1)}, bf16[3,128,256]{2,1,0:T(8,128)(2,1)S(1)}, u32[]{:S(2)}, u32[]{:S(2)}) %collective-permute-start.7) | collective-permute-done | bytes 196640 | tf_op jit(solution)/shard_map/ppermute | solution.py:311
  58.3 5.4 %collective-permute-start.8 = (bf16[3,128,256]{2,1,0:T(8,128)(2,1)S(1)}, bf16[3,128,256]{2,1,0:T(8,128)(2,1)S(1)}, u32[]{:S(2)}, u32[]{:S(2)}) collective-permute-start(bf16[3,128,256]{2,1,0:T(8,128)(2,1)S(1)} %collective-permute-done.7.refs_9_), channel_id=1, source_target_pairs={{0,14},{2,0},{4,2},{6,4},{8,6},{10,8},{12,10},{14,12},{1,15},{3,1}... | collective-permute-start | bytes 589832 | tf_op jit(solution)/shard_map/ppermute | solution.py:311
  63.8 1.9 %collective-permute-start.9 = (bf16[3,128,256]{2,1,0:T(8,128)(2,1)S(1)}, bf16[3,128,256]{2,1,0:T(8,128)(2,1)S(1)}, u32[]{:S(2)}, u32[]{:S(2)}) collective-permute-start(bf16[3,128,256]{2,1,0:T(8,128)(2,1)S(1)} %collective-permute-done.5.refs_12_), channel_id=1, source_target_pairs={{0,2},{2,4},{4,6},{6,8},{8,10},{10,12},{12,14},{14,0},{1,3},{3,5},... | collective-permute-start | bytes 589832 | tf_op jit(solution)/shard_map/ppermute | solution.py:311
  65.7 0.6 pad_add_fusion.refs_0_
  66.3 4.5 %collective-permute-done.8.refs_10_ = bf16[3,128,256]{2,1,0:T(8,128)(2,1)S(1)} collective-permute-done((bf16[3,128,256]{2,1,0:T(8,128)(2,1)S(1)}, bf16[3,128,256]{2,1,0:T(8,128)(2,1)S(1)}, u32[]{:S(2)}, u32[]{:S(2)}) %collective-permute-start.8) | collective-permute-done | bytes 196640 | tf_op jit(solution)/shard_map/ppermute | solution.py:311
  70.8 1.4 collective-permute-done.9.refs_11_
  72.3 0.6 copy-done.15
  72.9 11.8 %shard_map.86 = (bf16[2,128,512]{2,1,0:T(8,128)(2,1)}, bf16[2,128,512]{2,1,0:T(8,128)(2,1)}, f32[2,128,512]{2,1,0:T(8,128)}, f32[2,128,512]{2,1,0:T(8,128)}, bf1...) custom-call(s32[3]{0:T(128)} %pad_add_fusion.refs_0_, ...), custom_call_target="tpu_custom_call" | custom-call | flops 1200000000 | bytes 12000000 | tf_op jit(solution)/shard_map/pallas_call | solution.py:240
  84.8 2.1 %collective-permute-start.11 = (bf16[2,128,512]{2,1,0:T(8,128)(2,1)}, bf16[2,128,512]{2,1,0:T(8,128)(2,1)S(1)}, u32[]{:S(2)}, u32[]{:S(2)}) collective-permute-start(bf16[2,128,512]{2,1,0:T(8,128)(2,1)} %get-tuple-element.44), channel_id=1, source_target_pairs={{0,2},{2,4},{4,6},{6,8},{8,10},{10,12},{12,14},{14,0},{1,3},{3,5},... | collective-permute-start | bytes 786440 | tf_op jit(solution)/shard_map/ppermute | solution.py:337
  86.9 4.6 %collective-permute-start.16 = (bf16[2,128,512]{2,1,0:T(8,128)(2,1)}, bf16[2,128,512]{2,1,0:T(8,128)(2,1)S(1)}, u32[]{:S(2)}, u32[]{:S(2)}) collective-permute-start(bf16[2,128,512]{2,1,0:T(8,128)(2,1)} %get-tuple-element.51), channel_id=1, source_target_pairs={{0,14},{2,0},{4,2},{6,4},{8,6},{10,8},{12,10},{14,12},{1,15},{3,1}... | collective-permute-start | bytes 786440 | tf_op jit(solution)/shard_map/ppermute | solution.py:337
  91.5 4.7 %collective-permute-start.12 = (f32[2,128,512]{2,1,0:T(8,128)}, f32[2,128,512]{2,1,0:T(8,128)S(1)}, u32[]{:S(2)}, u32[]{:S(2)}) collective-permute-start(f32[2,128,512]{2,1,0:T(8,128)} %get-tuple-element.46), channel_id=1, source_target_pairs={{0,1},{1,0},{2,3},{3,2},{4,5},{5,4},{6,7},{7,6},{8,9},{9,8},{10,11... | collective-permute-start | bytes 1572872 | tf_op jit(solution)/shard_map/ppermute | solution.py:330
  96.1 1.9 %collective-permute-start.10 = (bf16[2,128,512]{2,1,0:T(8,128)(2,1)}, bf16[2,128,512]{2,1,0:T(8,128)(2,1)}, u32[]{:S(2)}, u32[]{:S(2)}) collective-permute-start(bf16[2,128,512]{2,1,0:T(8,128)(2,1)} %get-tuple-element.40), channel_id=1, source_target_pairs={{0,1},{1,0},{2,3},{3,2},{4,5},{5,4},{6,7},{7,6},{8,9},{9,8},{10,11... | collective-permute-start | bytes 786440 | tf_op jit(solution)/shard_map/ppermute | solution.py:351
  98.0 1.0 slice_bitcast_fusion.6
  99.1 0.1 add_convert_fusion.5
  99.1 2.1 %collective-permute-start.13 = (bf16[2,128,512]{2,1,0:T(8,128)(2,1)S(1)}, bf16[2,128,512]{2,1,0:T(8,128)(2,1)S(1)}, u32[]{:S(2)}, u32[]{:S(2)}) collective-permute-start(bf16[2,128,512]{2,1,0:T(8,128)(2,1)S(1)} %add_convert_fusion.5), channel_id=1, source_target_pairs={{0,2},{2,4},{4,6},{6,8},{8,10},{10,12},{12,14},{14,0},{1,3},{3,5},... | collective-permute-start | bytes 786440 | tf_op jit(solution)/shard_map/ppermute | solution.py:337
  101.2 0.1 add_convert_fusion.2
  101.3 4.6 %collective-permute-start.17 = (bf16[2,128,512]{2,1,0:T(8,128)(2,1)S(1)}, bf16[2,128,512]{2,1,0:T(8,128)(2,1)S(1)}, u32[]{:S(2)}, u32[]{:S(2)}) collective-permute-start(bf16[2,128,512]{2,1,0:T(8,128)(2,1)S(1)} %add_convert_fusion.2), channel_id=1, source_target_pairs={{0,14},{2,0},{4,2},{6,4},{8,6},{10,8},{12,10},{14,12},{1,15},{3,1}... | collective-permute-start | bytes 786440 | tf_op jit(solution)/shard_map/ppermute | solution.py:337
  105.9 8.8 %all-to-all-start.1 = ((bf16[32,16,128]{2,1,0:T(8,128)(2,1)}), bf16[32,16,128]{2,1,0:T(8,128)(2,1)S(1)}, u32[]{:S(2)}, u32[]{:S(2)}) async-start(bf16[32,16,128]{2,1,0:T(8,128)(2,1)} %get-tuple-element.45), calls=%async_computation.2 | async-start | bytes 262144 | tf_op jit(solution)/shard_map/all_to_all | solution.py:342
  114.7 1.0 slice_bitcast_fusion.4
  115.7 0.1 add_convert_fusion.4
  115.8 1.9 %collective-permute-start.14 = (bf16[2,128,512]{2,1,0:T(8,128)(2,1)S(1)}, bf16[2,128,512]{2,1,0:T(8,128)(2,1)S(1)}, u32[]{:S(2)}, u32[]{:S(2)}) collective-permute-start(bf16[2,128,512]{2,1,0:T(8,128)(2,1)S(1)} %add_convert_fusion.4), channel_id=1, source_target_pairs={{0,2},{2,4},{4,6},{6,8},{8,10},{10,12},{12,14},{14,0},{1,3},{3,5},... | collective-permute-start | bytes 786440 | tf_op jit(solution)/shard_map/ppermute | solution.py:337
  117.7 6.2 %all-to-all-done.1 = bf16[32,16,128]{2,1,0:T(8,128)(2,1)S(1)} async-done(((bf16[32,16,128]{2,1,0:T(8,128)(2,1)}), bf16[32,16,128]{2,1,0:T(8,128)(2,1)S(1)}, u32[]{:S(2)}, u32[]{:S(2)}) %all-to-all-start.1) | async-done | bytes 131104 | tf_op jit(solution)/shard_map/all_to_all | solution.py:342
  124.0 0.1 add_convert_fusion.1
  124.0 4.0 %collective-permute-start.18 = (bf16[2,128,512]{2,1,0:T(8,128)(2,1)S(1)}, bf16[2,128,512]{2,1,0:T(8,128)(2,1)S(1)}, u32[]{:S(2)}, u32[]{:S(2)}) collective-permute-start(bf16[2,128,512]{2,1,0:T(8,128)(2,1)S(1)} %add_convert_fusion.1), channel_id=1, source_target_pairs={{0,15},{1,14},{2,1},{3,0},{4,3},{5,2},{6,5},{7,4},{8,7},{9,6},{10,... | collective-permute-start | bytes 786440 | tf_op jit(solution)/shard_map/ppermute | solution.py:297
  128.0 3.9 %collective-permute-done.14 = bf16[2,128,512]{2,1,0:T(8,128)(2,1)S(1)} collective-permute-done((bf16[2,128,512]{2,1,0:T(8,128)(2,1)S(1)}, bf16[2,128,512]{2,1,0:T(8,128)(2,1)S(1)}, u32[]{:S(2)}, u32[]{:S(2)}) %collective-permute-start.14) | collective-permute-done | bytes 262176 | tf_op jit(solution)/shard_map/ppermute | solution.py:337
  131.9 0.1 add_convert_fusion.3
  131.9 3.1 %collective-permute-start.15 = (bf16[2,128,512]{2,1,0:T(8,128)(2,1)S(1)}, bf16[2,128,512]{2,1,0:T(8,128)(2,1)S(1)}, u32[]{:S(2)}, u32[]{:S(2)}) collective-permute-start(bf16[2,128,512]{2,1,0:T(8,128)(2,1)S(1)} %add_convert_fusion.3), channel_id=1, source_target_pairs={{0,3},{1,2},{2,5},{3,4},{4,7},{5,6},{6,9},{7,8},{8,11},{9,10},{10,... | collective-permute-start | bytes 786440 | tf_op jit(solution)/shard_map/ppermute | solution.py:297
  135.1 3.2 %collective-permute-start.19 = (f32[2,1,512]{2,0,1:T(2,128)S(1)}, f32[2,1,512]{2,0,1:T(2,128)S(1)}, u32[]{:S(2)}, u32[]{:S(2)}) collective-permute-start(f32[2,1,512]{2,0,1:T(2,128)S(1)} %squeeze.41), channel_id=1, source_target_pairs={{0,1},{1,0},{2,3},{3,2},{4,5},{5,4},{6,7},{7,6},{8,9},{9,8},{10,11... | collective-permute-start | bytes 12296 | tf_op jit(solution)/shard_map/ppermute | solution.py:350
  138.3 0.9 maximum_select_fusion
  139.3 2.8 %collective-permute-done.15 = bf16[2,128,512]{2,1,0:T(8,128)(2,1)S(1)} collective-permute-done((bf16[2,128,512]{2,1,0:T(8,128)(2,1)S(1)}, bf16[2,128,512]{2,1,0:T(8,128)(2,1)S(1)}, u32[]{:S(2)}, u32[]{:S(2)}) %collective-permute-start.15) | collective-permute-done | bytes 262176 | tf_op jit(solution)/shard_map/ppermute | solution.py:297
  142.1 1.2 fusion.1
  143.3 0.9 maximum_select_fusion.2
  (66 shorter events, 0.4 us)
Async XLA Ops:
  7.2 65.0 %all-gather.3.cloned.1.call-start = ((), (), s32[]{:S(2)}) async-start(), calls=%async_computation.4 | async-start | bytes 2949120 | tf_op jit(solution)/shard_map/all_gather | solution.py:302
  9.1 10.1 %collective-permute-start = (bf16[4,128,256]{2,1,0:T(8,128)(2,1)}, bf16[4,128,256]{2,1,0:T(8,128)(2,1)S(1)}, u32[]{:S(2)}, u32[]{:S(2)}) collective-permute-start(bf16[4,128,256]{2,1,0:T(8,128)(2,1)} %get-tuple-element.30), channel_id=1, source_target_pairs={{0,1},{1,0},{2,3},{3,2},{4,5},{5,4},{6,7},{7,6},{8,9},{9,8},{10,11... | collective-permute-start | bytes 786440 | tf_op jit(solution)/shard_map/ppermute | solution.py:300
  19.9 52.3 %copy-start = (bf16[3,128,256]{2,1,0:T(8,128)(2,1)}, bf16[3,128,256]{2,1,0:T(8,128)(2,1)S(1)}, u32[]{:S(2)}) copy-start(bf16[3,128,256]{2,1,0:T(8,128)(2,1)S(1)} %slice.61.refs_7_) | copy-start | bytes 589828
  19.9 9.2 %collective-permute-start.1 = (bf16[3,128,256]{2,1,0:T(8,128)(2,1)S(1)}, bf16[3,128,256]{2,1,0:T(8,128)(2,1)S(1)}, u32[]{:S(2)}, u32[]{:S(2)}) collective-permute-start(bf16[3,128,256]{2,1,0:T(8,128)(2,1)S(1)} %slice.61.refs_7_), channel_id=1, source_target_pairs={{0,2},{2,4},{4,6},{6,8},{8,10},{10,12},{12,14},{14,0},{1,3},{3,5},... | collective-permute-start | bytes 589832 | tf_op jit(solution)/shard_map/ppermute | solution.py:311
  22.6 22.2 %collective-permute-start.6 = (bf16[3,128,256]{2,1,0:T(8,128)(2,1)S(1)}, bf16[3,128,256]{2,1,0:T(8,128)(2,1)S(1)}, u32[]{:S(2)}, u32[]{:S(2)}) collective-permute-start(bf16[3,128,256]{2,1,0:T(8,128)(2,1)S(1)} %slice.61.refs_7_), channel_id=1, source_target_pairs={{0,14},{2,0},{4,2},{6,4},{8,6},{10,8},{12,10},{14,12},{1,15},{3,1}... | collective-permute-start | bytes 589832 | tf_op jit(solution)/shard_map/ppermute | solution.py:311
  29.2 43.0 %copy-start.9 = (bf16[3,128,256]{2,1,0:T(8,128)(2,1)}, bf16[3,128,256]{2,1,0:T(8,128)(2,1)S(1)}, u32[]{:S(2)}) copy-start(bf16[3,128,256]{2,1,0:T(8,128)(2,1)S(1)} %collective-permute-done.1.refs_14_) | copy-start | bytes 589828
  29.2 20.5 %collective-permute-start.4 = (bf16[3,128,256]{2,1,0:T(8,128)(2,1)S(1)}, bf16[3,128,256]{2,1,0:T(8,128)(2,1)S(1)}, u32[]{:S(2)}, u32[]{:S(2)}) collective-permute-start(bf16[3,128,256]{2,1,0:T(8,128)(2,1)S(1)} %collective-permute-done.1.refs_14_), channel_id=1, source_target_pairs={{0,2},{2,4},{4,6},{6,8},{8,10},{10,12},{12,14},{14,0},{1,3},{3,5},... | collective-permute-start | bytes 589832 | tf_op jit(solution)/shard_map/ppermute | solution.py:311
  32.9 30.8 %collective-permute-start.2 = (bf16[2,128,512]{2,1,0:T(8,128)(2,1)}, bf16[2,128,512]{2,1,0:T(8,128)(2,1)S(1)}, u32[]{:S(2)}, u32[]{:S(2)}) collective-permute-start(bf16[2,128,512]{2,1,0:T(8,128)(2,1)} %get-tuple-element.32), channel_id=1, source_target_pairs={{0,1},{1,0},{2,3},{3,2},{4,5},{5,4},{6,7},{7,6},{8,9},{9,8},{10,11... | collective-permute-start | bytes 786440 | tf_op jit(solution)/shard_map/ppermute | solution.py:317
  36.7 27.0 %all-to-all-start = ((bf16[32,16,128]{2,1,0:T(8,128)(2,1)}), bf16[32,16,128]{2,1,0:T(8,128)(2,1)S(1)}, u32[]{:S(2)}, u32[]{:S(2)}) async-start(bf16[32,16,128]{2,1,0:T(8,128)(2,1)} %broadcast_in_dim.40), calls=%async_computation | async-start | bytes 262144 | tf_op jit(solution)/shard_map/all_to_all | solution.py:314
  44.8 97.3 %reduce-scatter.2.cloned.1.call-start = ((), (), s32[]{:S(2)}) async-start(), calls=%async_computation.3 | async-start | bytes 2359296 | tf_op jit(solution)/shard_map/reduce_scatter | solution.py:331
  44.8 27.4 %copy-start.10 = (bf16[3,128,256]{2,1,0:T(8,128)(2,1)}, bf16[3,128,256]{2,1,0:T(8,128)(2,1)S(1)}, u32[]{:S(2)}) copy-start(bf16[3,128,256]{2,1,0:T(8,128)(2,1)S(1)} %collective-permute-done.6.refs_8_) | copy-start | bytes 589828
  44.8 13.4 %collective-permute-start.7 = (bf16[3,128,256]{2,1,0:T(8,128)(2,1)S(1)}, bf16[3,128,256]{2,1,0:T(8,128)(2,1)S(1)}, u32[]{:S(2)}, u32[]{:S(2)}) collective-permute-start(bf16[3,128,256]{2,1,0:T(8,128)(2,1)S(1)} %collective-permute-done.6.refs_8_), channel_id=1, source_target_pairs={{0,14},{2,0},{4,2},{6,4},{8,6},{10,8},{12,10},{14,12},{1,15},{3,1}... | collective-permute-start | bytes 589832 | tf_op jit(solution)/shard_map/ppermute | solution.py:311
  49.7 22.5 %copy-start.11 = (bf16[3,128,256]{2,1,0:T(8,128)(2,1)}, bf16[3,128,256]{2,1,0:T(8,128)(2,1)S(1)}, u32[]{:S(2)}) copy-start(bf16[3,128,256]{2,1,0:T(8,128)(2,1)S(1)} %collective-permute-done.4.refs_13_) | copy-start | bytes 589828
  49.7 14.0 %collective-permute-start.5 = (bf16[3,128,256]{2,1,0:T(8,128)(2,1)S(1)}, bf16[3,128,256]{2,1,0:T(8,128)(2,1)S(1)}, u32[]{:S(2)}, u32[]{:S(2)}) collective-permute-start(bf16[3,128,256]{2,1,0:T(8,128)(2,1)S(1)} %collective-permute-done.4.refs_13_), channel_id=1, source_target_pairs={{0,2},{2,4},{4,6},{6,8},{8,10},{10,12},{12,14},{14,0},{1,3},{3,5},... | collective-permute-start | bytes 589832 | tf_op jit(solution)/shard_map/ppermute | solution.py:311
  51.7 12.0 %collective-permute-start.3 = (s32[2,8]{1,0:T(2,128)}, s32[2,8]{1,0:T(2,128)S(1)}, u32[]{:S(2)}, u32[]{:S(2)}) collective-permute-start(s32[2,8]{1,0:T(2,128)} %refs_1_.1), channel_id=1, source_target_pairs={{0,1},{1,0},{2,3},{3,2},{4,5},{5,4},{6,7},{7,6},{8,9},{9,8},{10,11... | collective-permute-start | bytes 200 | tf_op jit(solution)/shard_map/ppermute | solution.py:318
  58.3 14.0 %copy-start.12 = (bf16[3,128,256]{2,1,0:T(8,128)(2,1)}, bf16[3,128,256]{2,1,0:T(8,128)(2,1)S(1)}, u32[]{:S(2)}) copy-start(bf16[3,128,256]{2,1,0:T(8,128)(2,1)S(1)} %collective-permute-done.7.refs_9_) | copy-start | bytes 589828
  58.3 12.6 %collective-permute-start.8 = (bf16[3,128,256]{2,1,0:T(8,128)(2,1)S(1)}, bf16[3,128,256]{2,1,0:T(8,128)(2,1)S(1)}, u32[]{:S(2)}, u32[]{:S(2)}) collective-permute-start(bf16[3,128,256]{2,1,0:T(8,128)(2,1)S(1)} %collective-permute-done.7.refs_9_), channel_id=1, source_target_pairs={{0,14},{2,0},{4,2},{6,4},{8,6},{10,8},{12,10},{14,12},{1,15},{3,1}... | collective-permute-start | bytes 589832 | tf_op jit(solution)/shard_map/ppermute | solution.py:311
  63.7 8.5 %copy-start.16 = (s32[2,8]{1,0:T(2,128)}, s32[2,8]{1,0:T(2,128)S(1)}, u32[]{:S(2)}) copy-start(s32[2,8]{1,0:T(2,128)S(1)} %collective-permute-done.3.refs_2_) | copy-start | bytes 196
  63.7 8.5 %copy-start.4 = (bf16[2,128,512]{2,1,0:T(8,128)(2,1)}, bf16[2,128,512]{2,1,0:T(8,128)(2,1)S(1)}, u32[]{:S(2)}) copy-start(bf16[2,128,512]{2,1,0:T(8,128)(2,1)S(1)} %collective-permute-done.2.refs_4_) | copy-start | bytes 786436
  63.7 8.5 %copy-start.1 = (bf16[32,16,128]{2,1,0:T(8,128)(2,1)}, bf16[32,16,128]{2,1,0:T(8,128)(2,1)S(1)}, u32[]{:S(2)}) copy-start(bf16[32,16,128]{2,1,0:T(8,128)(2,1)S(1)} %all-to-all-done.refs_5_) | copy-start | bytes 393220
  63.8 8.5 %copy-start.13 = (bf16[3,128,256]{2,1,0:T(8,128)(2,1)}, bf16[3,128,256]{2,1,0:T(8,128)(2,1)S(1)}, u32[]{:S(2)}) copy-start(bf16[3,128,256]{2,1,0:T(8,128)(2,1)S(1)} %collective-permute-done.5.refs_12_) | copy-start | bytes 589828
  63.8 8.4 %collective-permute-start.9 = (bf16[3,128,256]{2,1,0:T(8,128)(2,1)S(1)}, bf16[3,128,256]{2,1,0:T(8,128)(2,1)S(1)}, u32[]{:S(2)}, u32[]{:S(2)}) collective-permute-start(bf16[3,128,256]{2,1,0:T(8,128)(2,1)S(1)} %collective-permute-done.5.refs_12_), channel_id=1, source_target_pairs={{0,2},{2,4},{4,6},{6,8},{8,10},{10,12},{12,14},{14,0},{1,3},{3,5},... | collective-permute-start | bytes 589832 | tf_op jit(solution)/shard_map/ppermute | solution.py:311
  70.8 1.5 copy-start.14
  72.2 0.7 copy-start.15
  84.7 14.3 %copy-start.8 = (bf16[2,128,512]{2,1,0:T(8,128)(2,1)S(1)}, bf16[2,128,512]{2,1,0:T(8,128)(2,1)}, u32[]{:S(2)}) copy-start(bf16[2,128,512]{2,1,0:T(8,128)(2,1)} %get-tuple-element.48) | copy-start | bytes 786436
  84.7 16.5 %copy-start.7 = (bf16[2,128,512]{2,1,0:T(8,128)(2,1)S(1)}, bf16[2,128,512]{2,1,0:T(8,128)(2,1)}, u32[]{:S(2)}) copy-start(bf16[2,128,512]{2,1,0:T(8,128)(2,1)} %get-tuple-element.52) | copy-start | bytes 786436
  84.7 31.0 %copy-start.6 = (bf16[2,128,512]{2,1,0:T(8,128)(2,1)S(1)}, bf16[2,128,512]{2,1,0:T(8,128)(2,1)}, u32[]{:S(2)}) copy-start(bf16[2,128,512]{2,1,0:T(8,128)(2,1)} %get-tuple-element.49) | copy-start | bytes 786436
  84.8 39.2 %copy-start.5 = (bf16[2,128,512]{2,1,0:T(8,128)(2,1)S(1)}, bf16[2,128,512]{2,1,0:T(8,128)(2,1)}, u32[]{:S(2)}) copy-start(bf16[2,128,512]{2,1,0:T(8,128)(2,1)} %get-tuple-element.53) | copy-start | bytes 786436
  84.8 47.1 %copy-start.3 = (bf16[2,128,512]{2,1,0:T(8,128)(2,1)S(1)}, bf16[2,128,512]{2,1,0:T(8,128)(2,1)}, u32[]{:S(2)}) copy-start(bf16[2,128,512]{2,1,0:T(8,128)(2,1)} %get-tuple-element.50) | copy-start | bytes 786436
  84.8 14.2 %collective-permute-start.11 = (bf16[2,128,512]{2,1,0:T(8,128)(2,1)}, bf16[2,128,512]{2,1,0:T(8,128)(2,1)S(1)}, u32[]{:S(2)}, u32[]{:S(2)}) collective-permute-start(bf16[2,128,512]{2,1,0:T(8,128)(2,1)} %get-tuple-element.44), channel_id=1, source_target_pairs={{0,2},{2,4},{4,6},{6,8},{8,10},{10,12},{12,14},{14,0},{1,3},{3,5},... | collective-permute-start | bytes 786440 | tf_op jit(solution)/shard_map/ppermute | solution.py:337
  86.9 14.3 %collective-permute-start.16 = (bf16[2,128,512]{2,1,0:T(8,128)(2,1)}, bf16[2,128,512]{2,1,0:T(8,128)(2,1)S(1)}, u32[]{:S(2)}, u32[]{:S(2)}) collective-permute-start(bf16[2,128,512]{2,1,0:T(8,128)(2,1)} %get-tuple-element.51), channel_id=1, source_target_pairs={{0,14},{2,0},{4,2},{6,4},{8,6},{10,8},{12,10},{14,12},{1,15},{3,1}... | collective-permute-start | bytes 786440 | tf_op jit(solution)/shard_map/ppermute | solution.py:337
  91.5 47.8 %collective-permute-start.12 = (f32[2,128,512]{2,1,0:T(8,128)}, f32[2,128,512]{2,1,0:T(8,128)S(1)}, u32[]{:S(2)}, u32[]{:S(2)}) collective-permute-start(f32[2,128,512]{2,1,0:T(8,128)} %get-tuple-element.46), channel_id=1, source_target_pairs={{0,1},{1,0},{2,3},{3,2},{4,5},{5,4},{6,7},{7,6},{8,9},{9,8},{10,11... | collective-permute-start | bytes 1572872 | tf_op jit(solution)/shard_map/ppermute | solution.py:330
  96.1 18.6 %collective-permute-start.10 = (bf16[2,128,512]{2,1,0:T(8,128)(2,1)}, bf16[2,128,512]{2,1,0:T(8,128)(2,1)}, u32[]{:S(2)}, u32[]{:S(2)}) collective-permute-start(bf16[2,128,512]{2,1,0:T(8,128)(2,1)} %get-tuple-element.40), channel_id=1, source_target_pairs={{0,1},{1,0},{2,3},{3,2},{4,5},{5,4},{6,7},{7,6},{8,9},{9,8},{10,11... | collective-permute-start | bytes 786440 | tf_op jit(solution)/shard_map/ppermute | solution.py:351
  99.1 42.9 %copy-start.2 = (f32[2,128,512]{2,1,0:T(8,128)S(1)}, f32[2,128,512]{2,1,0:T(8,128)}, u32[]{:S(2)}) copy-start(f32[2,128,512]{2,1,0:T(8,128)} %get-tuple-element.41) | copy-start | bytes 1572868
  99.1 16.6 %collective-permute-start.13 = (bf16[2,128,512]{2,1,0:T(8,128)(2,1)S(1)}, bf16[2,128,512]{2,1,0:T(8,128)(2,1)S(1)}, u32[]{:S(2)}, u32[]{:S(2)}) collective-permute-start(bf16[2,128,512]{2,1,0:T(8,128)(2,1)S(1)} %add_convert_fusion.5), channel_id=1, source_target_pairs={{0,2},{2,4},{4,6},{6,8},{8,10},{10,12},{12,14},{14,0},{1,3},{3,5},... | collective-permute-start | bytes 786440 | tf_op jit(solution)/shard_map/ppermute | solution.py:337
  101.3 22.6 %collective-permute-start.17 = (bf16[2,128,512]{2,1,0:T(8,128)(2,1)S(1)}, bf16[2,128,512]{2,1,0:T(8,128)(2,1)S(1)}, u32[]{:S(2)}, u32[]{:S(2)}) collective-permute-start(bf16[2,128,512]{2,1,0:T(8,128)(2,1)S(1)} %add_convert_fusion.2), channel_id=1, source_target_pairs={{0,14},{2,0},{4,2},{6,4},{8,6},{10,8},{12,10},{14,12},{1,15},{3,1}... | collective-permute-start | bytes 786440 | tf_op jit(solution)/shard_map/ppermute | solution.py:337
  105.9 18.0 %all-to-all-start.1 = ((bf16[32,16,128]{2,1,0:T(8,128)(2,1)}), bf16[32,16,128]{2,1,0:T(8,128)(2,1)S(1)}, u32[]{:S(2)}, u32[]{:S(2)}) async-start(bf16[32,16,128]{2,1,0:T(8,128)(2,1)} %get-tuple-element.45), calls=%async_computation.2 | async-start | bytes 262144 | tf_op jit(solution)/shard_map/all_to_all | solution.py:342
  115.8 16.0 %collective-permute-start.14 = (bf16[2,128,512]{2,1,0:T(8,128)(2,1)S(1)}, bf16[2,128,512]{2,1,0:T(8,128)(2,1)S(1)}, u32[]{:S(2)}, u32[]{:S(2)}) collective-permute-start(bf16[2,128,512]{2,1,0:T(8,128)(2,1)S(1)} %add_convert_fusion.4), channel_id=1, source_target_pairs={{0,2},{2,4},{4,6},{6,8},{8,10},{10,12},{12,14},{14,0},{1,3},{3,5},... | collective-permute-start | bytes 786440 | tf_op jit(solution)/shard_map/ppermute | solution.py:337
  124.0 15.2 %collective-permute-start.18 = (bf16[2,128,512]{2,1,0:T(8,128)(2,1)S(1)}, bf16[2,128,512]{2,1,0:T(8,128)(2,1)S(1)}, u32[]{:S(2)}, u32[]{:S(2)}) collective-permute-start(bf16[2,128,512]{2,1,0:T(8,128)(2,1)S(1)} %add_convert_fusion.1), channel_id=1, source_target_pairs={{0,15},{1,14},{2,1},{3,0},{4,3},{5,2},{6,5},{7,4},{8,7},{9,6},{10,... | collective-permute-start | bytes 786440 | tf_op jit(solution)/shard_map/ppermute | solution.py:297
  131.9 10.1 %collective-permute-start.15 = (bf16[2,128,512]{2,1,0:T(8,128)(2,1)S(1)}, bf16[2,128,512]{2,1,0:T(8,128)(2,1)S(1)}, u32[]{:S(2)}, u32[]{:S(2)}) collective-permute-start(bf16[2,128,512]{2,1,0:T(8,128)(2,1)S(1)} %add_convert_fusion.3), channel_id=1, source_target_pairs={{0,3},{1,2},{2,5},{3,4},{4,7},{5,6},{6,9},{7,8},{8,11},{9,10},{10,... | collective-permute-start | bytes 786440 | tf_op jit(solution)/shard_map/ppermute | solution.py:297
  135.1 4.2 %collective-permute-start.19 = (f32[2,1,512]{2,0,1:T(2,128)S(1)}, f32[2,1,512]{2,0,1:T(2,128)S(1)}, u32[]{:S(2)}, u32[]{:S(2)}) collective-permute-start(f32[2,1,512]{2,0,1:T(2,128)S(1)} %squeeze.41), channel_id=1, source_target_pairs={{0,1},{1,0},{2,3},{3,2},{4,5},{5,4},{6,7},{7,6},{8,9},{9,8},{10,11... | collective-permute-start | bytes 12296 | tf_op jit(solution)/shard_map/ppermute | solution.py:350
Sparse Core Ops, SparseCore 0:
  20.0 50.9 all-gather.2
  84.9 51.4 reduce-scatter.1

commit v13 on v12

--- a/solution.py
+++ b/solution.py
@@ -170,7 +170,7 @@
                 gwide[pl.ds(first, WINDOWS, stride=GROWS), :] = value[TOK : TOK + WINDOWS]
         return carry
 
-    lax.fori_loop(0, HEADS, head_step, 0)
+    lax.fori_loop(0, HEADS, head_step, 0, unroll=True)
     gglob[...] = gwide[...].reshape(WINDOWS, GROWS, HEAD_DIM).astype(BF16)
     copies = []
 

time: 153 us -> 153 us (level)
  no operation moved by 1% of the time
where the time goes in v13:
time: 153 us; the launch traced here: 151 us
  starting transfers between devices  85.4 us (56%)
  waiting for transfers between devices  27.2 us (18%)
  Pallas kernels  15.4 us (10%)
  between operations  14.7 us (10%)
  local copies, waits for them, and re-layouts  4.75 us (3%)
  other arithmetic  4.08 us (3%)
    ppermute x12, starting transfers between devices, per_device(): held[i] = move(held[i])  37.7 us
    ppermute x12, waiting for transfers between devices, per_device(): held[i] = move(held[i])  16.1 us
    pallas_call x1, Pallas kernels, attend(): pl.pallas_call(attend_kernel, out_shape=[piece, piece, jax.ShapeDtypeStru...  11.6 us
    all_to_all x1, starting transfers between devices, per_device(): gback = lax.all_to_all(gglob, ('x', 'z'), 0, 0, tiled=True)  8.94 us
    ppermute x1, starting transfers between devices, per_device(): kv_peer = swap(kv_send)  8.77 us
    all_to_all x1, starting transfers between devices, per_device(): lax.all_to_all(jnp.broadcast_to(row, (WINDOWS, GROWS, HEAD_DIM)), ('x', '...  8.04 us
    ppermute x2, starting transfers between devices, home(): return lax.ppermute(terms, ('y', 'c'), pairs)  6.65 us
    all_to_all x1, waiting for transfers between devices, per_device(): gback = lax.all_to_all(gglob, ('x', 'z'), 0, 0, tiled=True)  6.15 us
  transfers between devices with their start and end apart: 24, of which 8 were waited for; matrix products, arithmetic and copies ran while one was open for 4% of the time, Pallas kernels for 1%

profile of v13, /device:TPU:1, one launch (start us, length us, event | category | flops | bytes accessed | tf_op | source)
XLA Modules:
  0.0 151.4 jit_solution(12519659955710890185)
XLA Ops:
  7.2 1.9 %shard_map.84 = (bf16[5,128,256]{2,1,0:T(8,128)(2,1)}, bf16[4,128,256]{2,1,0:T(8,128)(2,1)}) custom-call(s32[1]{0:T(128)} %bitcast.1.core, bf16[128,1024]{1,0:T(8,128)(2,1)} %first.2, bf16[128,1024]{1,0:T(8,128)(2,1)} %second.2), custom_call_target="tpu_custom_call" | custom-call | bytes 1000000 | tf_op jit(solution)/shard_map/pallas_call | solution.py:223
  9.1 8.8 %collective-permute-start = (bf16[4,128,256]{2,1,0:T(8,128)(2,1)}, bf16[4,128,256]{2,1,0:T(8,128)(2,1)S(1)}, u32[]{:S(2)}, u32[]{:S(2)}) collective-permute-start(bf16[4,128,256]{2,1,0:T(8,128)(2,1)} %get-tuple-element.30), channel_id=1, source_target_pairs={{0,1},{1,0},{2,3},{3,2},{4,5},{5,4},{6,7},{7,6},{8,9},{9,8},{10,11... | collective-permute-start | bytes 786440 | tf_op jit(solution)/shard_map/ppermute | solution.py:300
  17.9 1.4 collective-permute-done
  19.3 0.6 slice_dynamic-update-slice_fusion
  19.9 1.9 %collective-permute-start.1 = (bf16[3,128,256]{2,1,0:T(8,128)(2,1)S(1)}, bf16[3,128,256]{2,1,0:T(8,128)(2,1)S(1)}, u32[]{:S(2)}, u32[]{:S(2)}) collective-permute-start(bf16[3,128,256]{2,1,0:T(8,128)(2,1)S(1)} %slice.61.refs_7_), channel_id=1, source_target_pairs={{0,2},{2,4},{4,6},{6,8},{8,10},{10,12},{12,14},{14,0},{1,3},{3,5},... | collective-permute-start | bytes 589832 | tf_op jit(solution)/shard_map/ppermute | solution.py:311
  21.9 0.7 slice.59
  22.6 4.6 %collective-permute-start.6 = (bf16[3,128,256]{2,1,0:T(8,128)(2,1)S(1)}, bf16[3,128,256]{2,1,0:T(8,128)(2,1)S(1)}, u32[]{:S(2)}, u32[]{:S(2)}) collective-permute-start(bf16[3,128,256]{2,1,0:T(8,128)(2,1)S(1)} %slice.61.refs_7_), channel_id=1, source_target_pairs={{0,14},{2,0},{4,2},{6,4},{8,6},{10,8},{12,10},{14,12},{1,15},{3,1}... | collective-permute-start | bytes 589832 | tf_op jit(solution)/shard_map/ppermute | solution.py:311
  27.2 1.9 %collective-permute-done.1.refs_14_ = bf16[3,128,256]{2,1,0:T(8,128)(2,1)S(1)} collective-permute-done((bf16[3,128,256]{2,1,0:T(8,128)(2,1)S(1)}, bf16[3,128,256]{2,1,0:T(8,128)(2,1)S(1)}, u32[]{:S(2)}, u32[]{:S(2)}) %collective-permute-start.1) | collective-permute-done | bytes 196640 | tf_op jit(solution)/shard_map/ppermute | solution.py:311
  29.2 1.9 %collective-permute-start.4 = (bf16[3,128,256]{2,1,0:T(8,128)(2,1)S(1)}, bf16[3,128,256]{2,1,0:T(8,128)(2,1)S(1)}, u32[]{:S(2)}, u32[]{:S(2)}) collective-permute-start(bf16[3,128,256]{2,1,0:T(8,128)(2,1)S(1)} %collective-permute-done.1.refs_14_), channel_id=1, source_target_pairs={{0,2},{2,4},{4,6},{6,8},{8,10},{10,12},{12,14},{14,0},{1,3},{3,5},... | collective-permute-start | bytes 589832 | tf_op jit(solution)/shard_map/ppermute | solution.py:311
  31.1 1.9 %shard_map.85 = (bf16[2,128,512]{2,1,0:T(8,128)(2,1)}, bf16[2,128,512]{2,1,0:T(8,128)(2,1)}) custom-call(s32[1]{0:T(128)} %bitcast.1.core, bf16[128,1024]{1,0:T(8,128)(2,1)} %first.3, bf16[128,1024]{1,0:T(8,128)(2,1)} %second.3), custom_call_target="tpu_custom_call" | custom-call | bytes 1000000 | tf_op jit(solution)/shard_map/pallas_call | solution.py:223
  32.9 3.1 %collective-permute-start.2 = (bf16[2,128,512]{2,1,0:T(8,128)(2,1)}, bf16[2,128,512]{2,1,0:T(8,128)(2,1)S(1)}, u32[]{:S(2)}, u32[]{:S(2)}) collective-permute-start(bf16[2,128,512]{2,1,0:T(8,128)(2,1)} %get-tuple-element.32), channel_id=1, source_target_pairs={{0,1},{1,0},{2,3},{3,2},{4,5},{5,4},{6,7},{7,6},{8,9},{9,8},{10,11... | collective-permute-start | bytes 786440 | tf_op jit(solution)/shard_map/ppermute | solution.py:317
  36.0 0.7 broadcast_in_dim.40
  36.7 8.0 %all-to-all-start = ((bf16[32,16,128]{2,1,0:T(8,128)(2,1)}), bf16[32,16,128]{2,1,0:T(8,128)(2,1)S(1)}, u32[]{:S(2)}, u32[]{:S(2)}) async-start(bf16[32,16,128]{2,1,0:T(8,128)(2,1)} %broadcast_in_dim.40), calls=%async_computation | async-start | bytes 262144 | tf_op jit(solution)/shard_map/all_to_all | solution.py:314
  44.8 4.9 %collective-permute-start.7 = (bf16[3,128,256]{2,1,0:T(8,128)(2,1)S(1)}, bf16[3,128,256]{2,1,0:T(8,128)(2,1)S(1)}, u32[]{:S(2)}, u32[]{:S(2)}) collective-permute-start(bf16[3,128,256]{2,1,0:T(8,128)(2,1)S(1)} %collective-permute-done.6.refs_8_), channel_id=1, source_target_pairs={{0,14},{2,0},{4,2},{6,4},{8,6},{10,8},{12,10},{14,12},{1,15},{3,1}... | collective-permute-start | bytes 589832 | tf_op jit(solution)/shard_map/ppermute | solution.py:311
  49.7 1.9 %collective-permute-start.5 = (bf16[3,128,256]{2,1,0:T(8,128)(2,1)S(1)}, bf16[3,128,256]{2,1,0:T(8,128)(2,1)S(1)}, u32[]{:S(2)}, u32[]{:S(2)}) collective-permute-start(bf16[3,128,256]{2,1,0:T(8,128)(2,1)S(1)} %collective-permute-done.4.refs_13_), channel_id=1, source_target_pairs={{0,2},{2,4},{4,6},{6,8},{8,10},{10,12},{12,14},{14,0},{1,3},{3,5},... | collective-permute-start | bytes 589832 | tf_op jit(solution)/shard_map/ppermute | solution.py:311
  51.7 2.5 %collective-permute-start.3 = (s32[2,8]{1,0:T(2,128)}, s32[2,8]{1,0:T(2,128)S(1)}, u32[]{:S(2)}, u32[]{:S(2)}) collective-permute-start(s32[2,8]{1,0:T(2,128)} %refs_1_.1), channel_id=1, source_target_pairs={{0,1},{1,0},{2,3},{3,2},{4,5},{5,4},{6,7},{7,6},{8,9},{9,8},{10,11... | collective-permute-start | bytes 200 | tf_op jit(solution)/shard_map/ppermute | solution.py:318
  54.1 4.1 %collective-permute-done.7.refs_9_ = bf16[3,128,256]{2,1,0:T(8,128)(2,1)S(1)} collective-permute-done((bf16[3,128,256]{2,1,0:T(8,128)(2,1)S(1)}, bf16[3,128,256]{2,1,0:T(8,128)(2,1)S(1)}, u32[]{:S(2)}, u32[]{:S(2)}) %collective-permute-start.7) | collective-permute-done | bytes 196640 | tf_op jit(solution)/shard_map/ppermute | solution.py:311
  58.3 5.4 %collective-permute-start.8 = (bf16[3,128,256]{2,1,0:T(8,128)(2,1)S(1)}, bf16[3,128,256]{2,1,0:T(8,128)(2,1)S(1)}, u32[]{:S(2)}, u32[]{:S(2)}) collective-permute-start(bf16[3,128,256]{2,1,0:T(8,128)(2,1)S(1)} %collective-permute-done.7.refs_9_), channel_id=1, source_target_pairs={{0,14},{2,0},{4,2},{6,4},{8,6},{10,8},{12,10},{14,12},{1,15},{3,1}... | collective-permute-start | bytes 589832 | tf_op jit(solution)/shard_map/ppermute | solution.py:311
  63.8 1.9 %collective-permute-start.9 = (bf16[3,128,256]{2,1,0:T(8,128)(2,1)S(1)}, bf16[3,128,256]{2,1,0:T(8,128)(2,1)S(1)}, u32[]{:S(2)}, u32[]{:S(2)}) collective-permute-start(bf16[3,128,256]{2,1,0:T(8,128)(2,1)S(1)} %collective-permute-done.5.refs_12_), channel_id=1, source_target_pairs={{0,2},{2,4},{4,6},{6,8},{8,10},{10,12},{12,14},{14,0},{1,3},{3,5},... | collective-permute-start | bytes 589832 | tf_op jit(solution)/shard_map/ppermute | solution.py:311
  65.7 0.6 pad_add_fusion.refs_0_
  66.3 4.5 %collective-permute-done.8.refs_10_ = bf16[3,128,256]{2,1,0:T(8,128)(2,1)S(1)} collective-permute-done((bf16[3,128,256]{2,1,0:T(8,128)(2,1)S(1)}, bf16[3,128,256]{2,1,0:T(8,128)(2,1)S(1)}, u32[]{:S(2)}, u32[]{:S(2)}) %collective-permute-start.8) | collective-permute-done | bytes 196640 | tf_op jit(solution)/shard_map/ppermute | solution.py:311
  70.8 1.4 collective-permute-done.9.refs_11_
  72.3 0.6 copy-done.15
  72.9 11.6 %shard_map.86 = (bf16[2,128,512]{2,1,0:T(8,128)(2,1)}, bf16[2,128,512]{2,1,0:T(8,128)(2,1)}, f32[2,128,512]{2,1,0:T(8,128)}, f32[2,128,512]{2,1,0:T(8,128)}, bf1...) custom-call(s32[3]{0:T(128)} %pad_add_fusion.refs_0_, ...), custom_call_target="tpu_custom_call" | custom-call | flops 1200000000 | bytes 12000000 | tf_op jit(solution)/shard_map/pallas_call | solution.py:240
  84.6 2.1 %collective-permute-start.11 = (bf16[2,128,512]{2,1,0:T(8,128)(2,1)}, bf16[2,128,512]{2,1,0:T(8,128)(2,1)S(1)}, u32[]{:S(2)}, u32[]{:S(2)}) collective-permute-start(bf16[2,128,512]{2,1,0:T(8,128)(2,1)} %get-tuple-element.44), channel_id=1, source_target_pairs={{0,2},{2,4},{4,6},{6,8},{8,10},{10,12},{12,14},{14,0},{1,3},{3,5},... | collective-permute-start | bytes 786440 | tf_op jit(solution)/shard_map/ppermute | solution.py:337
  86.6 4.6 %collective-permute-start.16 = (bf16[2,128,512]{2,1,0:T(8,128)(2,1)}, bf16[2,128,512]{2,1,0:T(8,128)(2,1)S(1)}, u32[]{:S(2)}, u32[]{:S(2)}) collective-permute-start(bf16[2,128,512]{2,1,0:T(8,128)(2,1)} %get-tuple-element.51), channel_id=1, source_target_pairs={{0,14},{2,0},{4,2},{6,4},{8,6},{10,8},{12,10},{14,12},{1,15},{3,1}... | collective-permute-start | bytes 786440 | tf_op jit(solution)/shard_map/ppermute | solution.py:337
  91.2 4.4 %collective-permute-start.12 = (f32[2,128,512]{2,1,0:T(8,128)}, f32[2,128,512]{2,1,0:T(8,128)S(1)}, u32[]{:S(2)}, u32[]{:S(2)}) collective-permute-start(f32[2,128,512]{2,1,0:T(8,128)} %get-tuple-element.46), channel_id=1, source_target_pairs={{0,1},{1,0},{2,3},{3,2},{4,5},{5,4},{6,7},{7,6},{8,9},{9,8},{10,11... | collective-permute-start | bytes 1572872 | tf_op jit(solution)/shard_map/ppermute | solution.py:330
  95.7 1.9 %collective-permute-start.10 = (bf16[2,128,512]{2,1,0:T(8,128)(2,1)}, bf16[2,128,512]{2,1,0:T(8,128)(2,1)}, u32[]{:S(2)}, u32[]{:S(2)}) collective-permute-start(bf16[2,128,512]{2,1,0:T(8,128)(2,1)} %get-tuple-element.40), channel_id=1, source_target_pairs={{0,1},{1,0},{2,3},{3,2},{4,5},{5,4},{6,7},{7,6},{8,9},{9,8},{10,11... | collective-permute-start | bytes 786440 | tf_op jit(solution)/shard_map/ppermute | solution.py:351
  97.6 1.0 slice_bitcast_fusion.6
  98.6 0.1 add_convert_fusion.5
  98.7 2.1 %collective-permute-start.13 = (bf16[2,128,512]{2,1,0:T(8,128)(2,1)S(1)}, bf16[2,128,512]{2,1,0:T(8,128)(2,1)S(1)}, u32[]{:S(2)}, u32[]{:S(2)}) collective-permute-start(bf16[2,128,512]{2,1,0:T(8,128)(2,1)S(1)} %add_convert_fusion.5), channel_id=1, source_target_pairs={{0,2},{2,4},{4,6},{6,8},{8,10},{10,12},{12,14},{14,0},{1,3},{3,5},... | collective-permute-start | bytes 786440 | tf_op jit(solution)/shard_map/ppermute | solution.py:337
  100.8 0.1 add_convert_fusion.2
  100.8 4.6 %collective-permute-start.17 = (bf16[2,128,512]{2,1,0:T(8,128)(2,1)S(1)}, bf16[2,128,512]{2,1,0:T(8,128)(2,1)S(1)}, u32[]{:S(2)}, u32[]{:S(2)}) collective-permute-start(bf16[2,128,512]{2,1,0:T(8,128)(2,1)S(1)} %add_convert_fusion.2), channel_id=1, source_target_pairs={{0,14},{2,0},{4,2},{6,4},{8,6},{10,8},{12,10},{14,12},{1,15},{3,1}... | collective-permute-start | bytes 786440 | tf_op jit(solution)/shard_map/ppermute | solution.py:337
  105.4 8.9 %all-to-all-start.1 = ((bf16[32,16,128]{2,1,0:T(8,128)(2,1)}), bf16[32,16,128]{2,1,0:T(8,128)(2,1)S(1)}, u32[]{:S(2)}, u32[]{:S(2)}) async-start(bf16[32,16,128]{2,1,0:T(8,128)(2,1)} %get-tuple-element.45), calls=%async_computation.2 | async-start | bytes 262144 | tf_op jit(solution)/shard_map/all_to_all | solution.py:342
  114.4 1.0 slice_bitcast_fusion.4
  115.4 0.1 add_convert_fusion.4
  115.5 1.9 %collective-permute-start.14 = (bf16[2,128,512]{2,1,0:T(8,128)(2,1)S(1)}, bf16[2,128,512]{2,1,0:T(8,128)(2,1)S(1)}, u32[]{:S(2)}, u32[]{:S(2)}) collective-permute-start(bf16[2,128,512]{2,1,0:T(8,128)(2,1)S(1)} %add_convert_fusion.4), channel_id=1, source_target_pairs={{0,2},{2,4},{4,6},{6,8},{8,10},{10,12},{12,14},{14,0},{1,3},{3,5},... | collective-permute-start | bytes 786440 | tf_op jit(solution)/shard_map/ppermute | solution.py:337
  117.4 6.1 %all-to-all-done.1 = bf16[32,16,128]{2,1,0:T(8,128)(2,1)S(1)} async-done(((bf16[32,16,128]{2,1,0:T(8,128)(2,1)}), bf16[32,16,128]{2,1,0:T(8,128)(2,1)S(1)}, u32[]{:S(2)}, u32[]{:S(2)}) %all-to-all-start.1) | async-done | bytes 131104 | tf_op jit(solution)/shard_map/all_to_all | solution.py:342
  123.6 0.1 add_convert_fusion.1
  123.7 4.0 %collective-permute-start.18 = (bf16[2,128,512]{2,1,0:T(8,128)(2,1)S(1)}, bf16[2,128,512]{2,1,0:T(8,128)(2,1)S(1)}, u32[]{:S(2)}, u32[]{:S(2)}) collective-permute-start(bf16[2,128,512]{2,1,0:T(8,128)(2,1)S(1)} %add_convert_fusion.1), channel_id=1, source_target_pairs={{0,15},{1,14},{2,1},{3,0},{4,3},{5,2},{6,5},{7,4},{8,7},{9,6},{10,... | collective-permute-start | bytes 786440 | tf_op jit(solution)/shard_map/ppermute | solution.py:297
  127.6 4.2 %collective-permute-done.14 = bf16[2,128,512]{2,1,0:T(8,128)(2,1)S(1)} collective-permute-done((bf16[2,128,512]{2,1,0:T(8,128)(2,1)S(1)}, bf16[2,128,512]{2,1,0:T(8,128)(2,1)S(1)}, u32[]{:S(2)}, u32[]{:S(2)}) %collective-permute-start.14) | collective-permute-done | bytes 262176 | tf_op jit(solution)/shard_map/ppermute | solution.py:337
  131.8 0.1 add_convert_fusion.3
  131.9 2.7 %collective-permute-start.15 = (bf16[2,128,512]{2,1,0:T(8,128)(2,1)S(1)}, bf16[2,128,512]{2,1,0:T(8,128)(2,1)S(1)}, u32[]{:S(2)}, u32[]{:S(2)}) collective-permute-start(bf16[2,128,512]{2,1,0:T(8,128)(2,1)S(1)} %add_convert_fusion.3), channel_id=1, source_target_pairs={{0,3},{1,2},{2,5},{3,4},{4,7},{5,6},{6,9},{7,8},{8,11},{9,10},{10,... | collective-permute-start | bytes 786440 | tf_op jit(solution)/shard_map/ppermute | solution.py:297
  134.6 3.3 %collective-permute-start.19 = (f32[2,1,512]{2,0,1:T(2,128)S(1)}, f32[2,1,512]{2,0,1:T(2,128)S(1)}, u32[]{:S(2)}, u32[]{:S(2)}) collective-permute-start(f32[2,1,512]{2,0,1:T(2,128)S(1)} %squeeze.41), channel_id=1, source_target_pairs={{0,1},{1,0},{2,3},{3,2},{4,5},{5,4},{6,7},{7,6},{8,9},{9,8},{10,11... | collective-permute-start | bytes 12296 | tf_op jit(solution)/shard_map/ppermute | solution.py:350
  137.9 0.9 maximum_select_fusion
  138.9 3.5 %collective-permute-done.15 = bf16[2,128,512]{2,1,0:T(8,128)(2,1)S(1)} collective-permute-done((bf16[2,128,512]{2,1,0:T(8,128)(2,1)S(1)}, bf16[2,128,512]{2,1,0:T(8,128)(2,1)S(1)}, u32[]{:S(2)}, u32[]{:S(2)}) %collective-permute-start.15) | collective-permute-done | bytes 262176 | tf_op jit(solution)/shard_map/ppermute | solution.py:297
  142.4 1.2 fusion.1
  143.7 0.9 maximum_select_fusion.2
  (66 shorter events, 0.4 us)
Async XLA Ops:
  7.2 65.0 %all-gather.3.cloned.1.call-start = ((), (), s32[]{:S(2)}) async-start(), calls=%async_computation.4 | async-start | bytes 2949120 | tf_op jit(solution)/shard_map/all_gather | solution.py:302
  9.1 10.1 %collective-permute-start = (bf16[4,128,256]{2,1,0:T(8,128)(2,1)}, bf16[4,128,256]{2,1,0:T(8,128)(2,1)S(1)}, u32[]{:S(2)}, u32[]{:S(2)}) collective-permute-start(bf16[4,128,256]{2,1,0:T(8,128)(2,1)} %get-tuple-element.30), channel_id=1, source_target_pairs={{0,1},{1,0},{2,3},{3,2},{4,5},{5,4},{6,7},{7,6},{8,9},{9,8},{10,11... | collective-permute-start | bytes 786440 | tf_op jit(solution)/shard_map/ppermute | solution.py:300
  19.9 52.3 %copy-start = (bf16[3,128,256]{2,1,0:T(8,128)(2,1)}, bf16[3,128,256]{2,1,0:T(8,128)(2,1)S(1)}, u32[]{:S(2)}) copy-start(bf16[3,128,256]{2,1,0:T(8,128)(2,1)S(1)} %slice.61.refs_7_) | copy-start | bytes 589828
  19.9 9.2 %collective-permute-start.1 = (bf16[3,128,256]{2,1,0:T(8,128)(2,1)S(1)}, bf16[3,128,256]{2,1,0:T(8,128)(2,1)S(1)}, u32[]{:S(2)}, u32[]{:S(2)}) collective-permute-start(bf16[3,128,256]{2,1,0:T(8,128)(2,1)S(1)} %slice.61.refs_7_), channel_id=1, source_target_pairs={{0,2},{2,4},{4,6},{6,8},{8,10},{10,12},{12,14},{14,0},{1,3},{3,5},... | collective-permute-start | bytes 589832 | tf_op jit(solution)/shard_map/ppermute | solution.py:311
  22.6 22.2 %collective-permute-start.6 = (bf16[3,128,256]{2,1,0:T(8,128)(2,1)S(1)}, bf16[3,128,256]{2,1,0:T(8,128)(2,1)S(1)}, u32[]{:S(2)}, u32[]{:S(2)}) collective-permute-start(bf16[3,128,256]{2,1,0:T(8,128)(2,1)S(1)} %slice.61.refs_7_), channel_id=1, source_target_pairs={{0,14},{2,0},{4,2},{6,4},{8,6},{10,8},{12,10},{14,12},{1,15},{3,1}... | collective-permute-start | bytes 589832 | tf_op jit(solution)/shard_map/ppermute | solution.py:311
  29.2 43.0 %copy-start.9 = (bf16[3,128,256]{2,1,0:T(8,128)(2,1)}, bf16[3,128,256]{2,1,0:T(8,128)(2,1)S(1)}, u32[]{:S(2)}) copy-start(bf16[3,128,256]{2,1,0:T(8,128)(2,1)S(1)} %collective-permute-done.1.refs_14_) | copy-start | bytes 589828
  29.2 20.5 %collective-permute-start.4 = (bf16[3,128,256]{2,1,0:T(8,128)(2,1)S(1)}, bf16[3,128,256]{2,1,0:T(8,128)(2,1)S(1)}, u32[]{:S(2)}, u32[]{:S(2)}) collective-permute-start(bf16[3,128,256]{2,1,0:T(8,128)(2,1)S(1)} %collective-permute-done.1.refs_14_), channel_id=1, source_target_pairs={{0,2},{2,4},{4,6},{6,8},{8,10},{10,12},{12,14},{14,0},{1,3},{3,5},... | collective-permute-start | bytes 589832 | tf_op jit(solution)/shard_map/ppermute | solution.py:311
  32.9 30.8 %collective-permute-start.2 = (bf16[2,128,512]{2,1,0:T(8,128)(2,1)}, bf16[2,128,512]{2,1,0:T(8,128)(2,1)S(1)}, u32[]{:S(2)}, u32[]{:S(2)}) collective-permute-start(bf16[2,128,512]{2,1,0:T(8,128)(2,1)} %get-tuple-element.32), channel_id=1, source_target_pairs={{0,1},{1,0},{2,3},{3,2},{4,5},{5,4},{6,7},{7,6},{8,9},{9,8},{10,11... | collective-permute-start | bytes 786440 | tf_op jit(solution)/shard_map/ppermute | solution.py:317
  36.7 27.0 %all-to-all-start = ((bf16[32,16,128]{2,1,0:T(8,128)(2,1)}), bf16[32,16,128]{2,1,0:T(8,128)(2,1)S(1)}, u32[]{:S(2)}, u32[]{:S(2)}) async-start(bf16[32,16,128]{2,1,0:T(8,128)(2,1)} %broadcast_in_dim.40), calls=%async_computation | async-start | bytes 262144 | tf_op jit(solution)/shard_map/all_to_all | solution.py:314
  44.8 97.6 %reduce-scatter.2.cloned.1.call-start = ((), (), s32[]{:S(2)}) async-start(), calls=%async_computation.3 | async-start | bytes 2359296 | tf_op jit(solution)/shard_map/reduce_scatter | solution.py:331
  44.8 27.4 %copy-start.10 = (bf16[3,128,256]{2,1,0:T(8,128)(2,1)}, bf16[3,128,256]{2,1,0:T(8,128)(2,1)S(1)}, u32[]{:S(2)}) copy-start(bf16[3,128,256]{2,1,0:T(8,128)(2,1)S(1)} %collective-permute-done.6.refs_8_) | copy-start | bytes 589828
  44.8 13.4 %collective-permute-start.7 = (bf16[3,128,256]{2,1,0:T(8,128)(2,1)S(1)}, bf16[3,128,256]{2,1,0:T(8,128)(2,1)S(1)}, u32[]{:S(2)}, u32[]{:S(2)}) collective-permute-start(bf16[3,128,256]{2,1,0:T(8,128)(2,1)S(1)} %collective-permute-done.6.refs_8_), channel_id=1, source_target_pairs={{0,14},{2,0},{4,2},{6,4},{8,6},{10,8},{12,10},{14,12},{1,15},{3,1}... | collective-permute-start | bytes 589832 | tf_op jit(solution)/shard_map/ppermute | solution.py:311
  49.7 22.5 %copy-start.11 = (bf16[3,128,256]{2,1,0:T(8,128)(2,1)}, bf16[3,128,256]{2,1,0:T(8,128)(2,1)S(1)}, u32[]{:S(2)}) copy-start(bf16[3,128,256]{2,1,0:T(8,128)(2,1)S(1)} %collective-permute-done.4.refs_13_) | copy-start | bytes 589828
  49.7 14.0 %collective-permute-start.5 = (bf16[3,128,256]{2,1,0:T(8,128)(2,1)S(1)}, bf16[3,128,256]{2,1,0:T(8,128)(2,1)S(1)}, u32[]{:S(2)}, u32[]{:S(2)}) collective-permute-start(bf16[3,128,256]{2,1,0:T(8,128)(2,1)S(1)} %collective-permute-done.4.refs_13_), channel_id=1, source_target_pairs={{0,2},{2,4},{4,6},{6,8},{8,10},{10,12},{12,14},{14,0},{1,3},{3,5},... | collective-permute-start | bytes 589832 | tf_op jit(solution)/shard_map/ppermute | solution.py:311
  51.7 12.0 %collective-permute-start.3 = (s32[2,8]{1,0:T(2,128)}, s32[2,8]{1,0:T(2,128)S(1)}, u32[]{:S(2)}, u32[]{:S(2)}) collective-permute-start(s32[2,8]{1,0:T(2,128)} %refs_1_.1), channel_id=1, source_target_pairs={{0,1},{1,0},{2,3},{3,2},{4,5},{5,4},{6,7},{7,6},{8,9},{9,8},{10,11... | collective-permute-start | bytes 200 | tf_op jit(solution)/shard_map/ppermute | solution.py:318
  58.3 14.0 %copy-start.12 = (bf16[3,128,256]{2,1,0:T(8,128)(2,1)}, bf16[3,128,256]{2,1,0:T(8,128)(2,1)S(1)}, u32[]{:S(2)}) copy-start(bf16[3,128,256]{2,1,0:T(8,128)(2,1)S(1)} %collective-permute-done.7.refs_9_) | copy-start | bytes 589828
  58.3 12.6 %collective-permute-start.8 = (bf16[3,128,256]{2,1,0:T(8,128)(2,1)S(1)}, bf16[3,128,256]{2,1,0:T(8,128)(2,1)S(1)}, u32[]{:S(2)}, u32[]{:S(2)}) collective-permute-start(bf16[3,128,256]{2,1,0:T(8,128)(2,1)S(1)} %collective-permute-done.7.refs_9_), channel_id=1, source_target_pairs={{0,14},{2,0},{4,2},{6,4},{8,6},{10,8},{12,10},{14,12},{1,15},{3,1}... | collective-permute-start | bytes 589832 | tf_op jit(solution)/shard_map/ppermute | solution.py:311
  63.7 8.5 %copy-start.16 = (s32[2,8]{1,0:T(2,128)}, s32[2,8]{1,0:T(2,128)S(1)}, u32[]{:S(2)}) copy-start(s32[2,8]{1,0:T(2,128)S(1)} %collective-permute-done.3.refs_2_) | copy-start | bytes 196
  63.7 8.5 %copy-start.4 = (bf16[2,128,512]{2,1,0:T(8,128)(2,1)}, bf16[2,128,512]{2,1,0:T(8,128)(2,1)S(1)}, u32[]{:S(2)}) copy-start(bf16[2,128,512]{2,1,0:T(8,128)(2,1)S(1)} %collective-permute-done.2.refs_4_) | copy-start | bytes 786436
  63.7 8.5 %copy-start.1 = (bf16[32,16,128]{2,1,0:T(8,128)(2,1)}, bf16[32,16,128]{2,1,0:T(8,128)(2,1)S(1)}, u32[]{:S(2)}) copy-start(bf16[32,16,128]{2,1,0:T(8,128)(2,1)S(1)} %all-to-all-done.refs_5_) | copy-start | bytes 393220
  63.8 8.5 %copy-start.13 = (bf16[3,128,256]{2,1,0:T(8,128)(2,1)}, bf16[3,128,256]{2,1,0:T(8,128)(2,1)S(1)}, u32[]{:S(2)}) copy-start(bf16[3,128,256]{2,1,0:T(8,128)(2,1)S(1)} %collective-permute-done.5.refs_12_) | copy-start | bytes 589828
  63.8 8.4 %collective-permute-start.9 = (bf16[3,128,256]{2,1,0:T(8,128)(2,1)S(1)}, bf16[3,128,256]{2,1,0:T(8,128)(2,1)S(1)}, u32[]{:S(2)}, u32[]{:S(2)}) collective-permute-start(bf16[3,128,256]{2,1,0:T(8,128)(2,1)S(1)} %collective-permute-done.5.refs_12_), channel_id=1, source_target_pairs={{0,2},{2,4},{4,6},{6,8},{8,10},{10,12},{12,14},{14,0},{1,3},{3,5},... | collective-permute-start | bytes 589832 | tf_op jit(solution)/shard_map/ppermute | solution.py:311
  70.8 1.5 copy-start.14
  72.2 0.7 copy-start.15
  84.5 14.1 %copy-start.8 = (bf16[2,128,512]{2,1,0:T(8,128)(2,1)S(1)}, bf16[2,128,512]{2,1,0:T(8,128)(2,1)}, u32[]{:S(2)}) copy-start(bf16[2,128,512]{2,1,0:T(8,128)(2,1)} %get-tuple-element.48) | copy-start | bytes 786436
  84.5 16.3 %copy-start.7 = (bf16[2,128,512]{2,1,0:T(8,128)(2,1)S(1)}, bf16[2,128,512]{2,1,0:T(8,128)(2,1)}, u32[]{:S(2)}) copy-start(bf16[2,128,512]{2,1,0:T(8,128)(2,1)} %get-tuple-element.52) | copy-start | bytes 786436
  84.5 30.9 %copy-start.6 = (bf16[2,128,512]{2,1,0:T(8,128)(2,1)S(1)}, bf16[2,128,512]{2,1,0:T(8,128)(2,1)}, u32[]{:S(2)}) copy-start(bf16[2,128,512]{2,1,0:T(8,128)(2,1)} %get-tuple-element.49) | copy-start | bytes 786436
  84.5 39.1 %copy-start.5 = (bf16[2,128,512]{2,1,0:T(8,128)(2,1)S(1)}, bf16[2,128,512]{2,1,0:T(8,128)(2,1)}, u32[]{:S(2)}) copy-start(bf16[2,128,512]{2,1,0:T(8,128)(2,1)} %get-tuple-element.53) | copy-start | bytes 786436
  84.5 47.3 %copy-start.3 = (bf16[2,128,512]{2,1,0:T(8,128)(2,1)S(1)}, bf16[2,128,512]{2,1,0:T(8,128)(2,1)}, u32[]{:S(2)}) copy-start(bf16[2,128,512]{2,1,0:T(8,128)(2,1)} %get-tuple-element.50) | copy-start | bytes 786436
  84.6 14.0 %collective-permute-start.11 = (bf16[2,128,512]{2,1,0:T(8,128)(2,1)}, bf16[2,128,512]{2,1,0:T(8,128)(2,1)S(1)}, u32[]{:S(2)}, u32[]{:S(2)}) collective-permute-start(bf16[2,128,512]{2,1,0:T(8,128)(2,1)} %get-tuple-element.44), channel_id=1, source_target_pairs={{0,2},{2,4},{4,6},{6,8},{8,10},{10,12},{12,14},{14,0},{1,3},{3,5},... | collective-permute-start | bytes 786440 | tf_op jit(solution)/shard_map/ppermute | solution.py:337
  86.6 14.1 %collective-permute-start.16 = (bf16[2,128,512]{2,1,0:T(8,128)(2,1)}, bf16[2,128,512]{2,1,0:T(8,128)(2,1)S(1)}, u32[]{:S(2)}, u32[]{:S(2)}) collective-permute-start(bf16[2,128,512]{2,1,0:T(8,128)(2,1)} %get-tuple-element.51), channel_id=1, source_target_pairs={{0,14},{2,0},{4,2},{6,4},{8,6},{10,8},{12,10},{14,12},{1,15},{3,1}... | collective-permute-start | bytes 786440 | tf_op jit(solution)/shard_map/ppermute | solution.py:337
  91.2 47.6 %collective-permute-start.12 = (f32[2,128,512]{2,1,0:T(8,128)}, f32[2,128,512]{2,1,0:T(8,128)S(1)}, u32[]{:S(2)}, u32[]{:S(2)}) collective-permute-start(f32[2,128,512]{2,1,0:T(8,128)} %get-tuple-element.46), channel_id=1, source_target_pairs={{0,1},{1,0},{2,3},{3,2},{4,5},{5,4},{6,7},{7,6},{8,9},{9,8},{10,11... | collective-permute-start | bytes 1572872 | tf_op jit(solution)/shard_map/ppermute | solution.py:330
  95.7 18.7 %collective-permute-start.10 = (bf16[2,128,512]{2,1,0:T(8,128)(2,1)}, bf16[2,128,512]{2,1,0:T(8,128)(2,1)}, u32[]{:S(2)}, u32[]{:S(2)}) collective-permute-start(bf16[2,128,512]{2,1,0:T(8,128)(2,1)} %get-tuple-element.40), channel_id=1, source_target_pairs={{0,1},{1,0},{2,3},{3,2},{4,5},{5,4},{6,7},{7,6},{8,9},{9,8},{10,11... | collective-permute-start | bytes 786440 | tf_op jit(solution)/shard_map/ppermute | solution.py:351
  98.7 43.7 %copy-start.2 = (f32[2,128,512]{2,1,0:T(8,128)S(1)}, f32[2,128,512]{2,1,0:T(8,128)}, u32[]{:S(2)}) copy-start(f32[2,128,512]{2,1,0:T(8,128)} %get-tuple-element.41) | copy-start | bytes 1572868
  98.7 16.7 %collective-permute-start.13 = (bf16[2,128,512]{2,1,0:T(8,128)(2,1)S(1)}, bf16[2,128,512]{2,1,0:T(8,128)(2,1)S(1)}, u32[]{:S(2)}, u32[]{:S(2)}) collective-permute-start(bf16[2,128,512]{2,1,0:T(8,128)(2,1)S(1)} %add_convert_fusion.5), channel_id=1, source_target_pairs={{0,2},{2,4},{4,6},{6,8},{8,10},{10,12},{12,14},{14,0},{1,3},{3,5},... | collective-permute-start | bytes 786440 | tf_op jit(solution)/shard_map/ppermute | solution.py:337
  100.8 22.8 %collective-permute-start.17 = (bf16[2,128,512]{2,1,0:T(8,128)(2,1)S(1)}, bf16[2,128,512]{2,1,0:T(8,128)(2,1)S(1)}, u32[]{:S(2)}, u32[]{:S(2)}) collective-permute-start(bf16[2,128,512]{2,1,0:T(8,128)(2,1)S(1)} %add_convert_fusion.2), channel_id=1, source_target_pairs={{0,14},{2,0},{4,2},{6,4},{8,6},{10,8},{12,10},{14,12},{1,15},{3,1}... | collective-permute-start | bytes 786440 | tf_op jit(solution)/shard_map/ppermute | solution.py:337
  105.4 18.1 %all-to-all-start.1 = ((bf16[32,16,128]{2,1,0:T(8,128)(2,1)}), bf16[32,16,128]{2,1,0:T(8,128)(2,1)S(1)}, u32[]{:S(2)}, u32[]{:S(2)}) async-start(bf16[32,16,128]{2,1,0:T(8,128)(2,1)} %get-tuple-element.45), calls=%async_computation.2 | async-start | bytes 262144 | tf_op jit(solution)/shard_map/all_to_all | solution.py:342
  115.5 16.4 %collective-permute-start.14 = (bf16[2,128,512]{2,1,0:T(8,128)(2,1)S(1)}, bf16[2,128,512]{2,1,0:T(8,128)(2,1)S(1)}, u32[]{:S(2)}, u32[]{:S(2)}) collective-permute-start(bf16[2,128,512]{2,1,0:T(8,128)(2,1)S(1)} %add_convert_fusion.4), channel_id=1, source_target_pairs={{0,2},{2,4},{4,6},{6,8},{8,10},{10,12},{12,14},{14,0},{1,3},{3,5},... | collective-permute-start | bytes 786440 | tf_op jit(solution)/shard_map/ppermute | solution.py:337
  123.7 15.2 %collective-permute-start.18 = (bf16[2,128,512]{2,1,0:T(8,128)(2,1)S(1)}, bf16[2,128,512]{2,1,0:T(8,128)(2,1)S(1)}, u32[]{:S(2)}, u32[]{:S(2)}) collective-permute-start(bf16[2,128,512]{2,1,0:T(8,128)(2,1)S(1)} %add_convert_fusion.1), channel_id=1, source_target_pairs={{0,15},{1,14},{2,1},{3,0},{4,3},{5,2},{6,5},{7,4},{8,7},{9,6},{10,... | collective-permute-start | bytes 786440 | tf_op jit(solution)/shard_map/ppermute | solution.py:297
  131.9 10.5 %collective-permute-start.15 = (bf16[2,128,512]{2,1,0:T(8,128)(2,1)S(1)}, bf16[2,128,512]{2,1,0:T(8,128)(2,1)S(1)}, u32[]{:S(2)}, u32[]{:S(2)}) collective-permute-start(bf16[2,128,512]{2,1,0:T(8,128)(2,1)S(1)} %add_convert_fusion.3), channel_id=1, source_target_pairs={{0,3},{1,2},{2,5},{3,4},{4,7},{5,6},{6,9},{7,8},{8,11},{9,10},{10,... | collective-permute-start | bytes 786440 | tf_op jit(solution)/shard_map/ppermute | solution.py:297
  134.6 4.2 %collective-permute-start.19 = (f32[2,1,512]{2,0,1:T(2,128)S(1)}, f32[2,1,512]{2,0,1:T(2,128)S(1)}, u32[]{:S(2)}, u32[]{:S(2)}) collective-permute-start(f32[2,1,512]{2,0,1:T(2,128)S(1)} %squeeze.41), channel_id=1, source_target_pairs={{0,1},{1,0},{2,3},{3,2},{4,5},{5,4},{6,7},{7,6},{8,9},{9,8},{10,11... | collective-permute-start | bytes 12296 | tf_op jit(solution)/shard_map/ppermute | solution.py:350
Sparse Core Ops, SparseCore 0:
  20.0 50.9 all-gather.2
  84.7 51.4 reduce-scatter.1
